TPU v7x, 32 devices: a whole 2x2x4 slice. The times are simulated.
32 devices in a mesh: section: 2 (over y), dp: 4 (over z), tensor: 4 (over x, core).
Axes of the slice: x: 2, y: 2, z: 4, core: 2. Of those that a mesh axis runs over, the one named last changes fastest.
Arguments:
- block_input: bfloat16 [2, 8192, 1024], P(None, ('dp', 'tensor')), may hold values from -6 to 6
- segment_ids: int32 [2, 8192], P(None, 'dp'), may hold values from 0 to 2, as said below
- cotangent: bfloat16 [2, 8192, 1024], P(None, ('dp', 'tensor')), may hold values from -6 to 6
- norm_one_gain: float32 [2, 1024], P('section'), may hold values from 0.1 to 1.9
- qkv_weight: float32 [2, 1024, 16, 192], P('section', 'dp', 'tensor'), may hold values from -0.1875 to 0.1875
- out_weight: float32 [2, 16, 64, 1024], P('section', 'tensor', None, 'dp'), may hold values from -5 to 5
- norm_two_gain: float32 [2, 1024], P('section'), may hold values from 0.1 to 1.9
- up_weight: float32 [2, 1024, 4096], P('section', 'dp', 'tensor'), may hold values from -0.1875 to 0.1875
- down_weight: float32 [2, 4096, 1024], P('section', 'tensor', 'dp'), may hold values from -0.09375 to 0.09375
Outputs:
- layer_outputs: bfloat16 [2, 2, 8192, 1024], P('section', None, ('dp', 'tensor'))
- input_grads: bfloat16 [2, 2, 8192, 1024], P('section', None, ('dp', 'tensor'))
- norm_one_grad: float32 [2, 1024], P('section')
- qkv_grad: float32 [2, 1024, 16, 192], P('section', 'dp', 'tensor')
- out_grad: float32 [2, 16, 64, 1024], P('section', 'tensor', None, 'dp')
- norm_two_grad: float32 [2, 1024], P('section')
- up_grad: float32 [2, 1024, 4096], P('section', 'dp', 'tensor')
- down_grad: float32 [2, 4096, 1024], P('section', 'tensor', 'dp')
Inputs may be any that keep to these rules, and one draw needn't show every extreme that they name: `segment_ids`: within each replica's micro-batch of 2048 tokens, scene numbers run 0, 1, 2 in order, each scene nonempty; scene 1 begins within the first 512 tokens and ends within the last 512 tokens.
All inputs are finite; a program needn't handle non-finite values.
Results may differ from a plain program's by a relative error of at most 0.033.
Values may be sent and summed in bfloat16 or wider, within the bound.
A program may use at most 384 MiB of HBM per device.

v0:
```python
import jax
import jax.numpy as jnp
from jax import lax
from jax.sharding import PartitionSpec as P


def shifted(value, axis, by):
    devices = lax.axis_size(axis)
    pairs = [(i, i + by) for i in range(devices) if 0 <= i + by < devices]
    return lax.ppermute(value, axis, pairs)


def layer_norm(source, gain_vec):
    center = source - jnp.mean(source, axis=-1, keepdims=True)
    spread_sq = jnp.mean(center * center, axis=-1, keepdims=True)
    return center * lax.rsqrt(spread_sq + 1e-05) * gain_vec


def exact_gelu(source):
    return jax.nn.gelu(source, approximate=False)


def spread_rows(source):
    return lax.all_gather(source, "tensor", axis=0, tiled=True)


def collect_rows(source):
    return lax.psum_scatter(
        source.astype(jnp.bfloat16), "tensor", scatter_dimension=0, tiled=True
    ).astype(jnp.float32)


def spread_grads(source):
    return lax.all_gather(source, "tensor", axis=0, tiled=True)


def collect_grads(source):
    return lax.psum_scatter(
        source.astype(jnp.bfloat16), "tensor", scatter_dimension=0, tiled=True
    ).astype(jnp.float32)


def masked_scores(query_block, key_rows, query_segs, segments, score_scale):
    raw_scores = jnp.einsum(
        "hqd,hkd->hqk", query_block, key_rows, preferred_element_type=jnp.float32
    )
    same_scene = (query_segs[:, None] == segments[None, :])[None]
    return jnp.where(same_scene, raw_scores * score_scale, -1e30)


def attend(queries, key_rows, value_rows, segments):
    head_count, length, head_dim = queries.shape
    block_rows = min(512, length)
    score_scale = head_dim ** (-0.5)

    def one_block(start):
        query_block = lax.dynamic_slice_in_dim(queries, start, block_rows, 1)
        query_segs = lax.dynamic_slice_in_dim(segments, start, block_rows, 0)
        scores = masked_scores(query_block, key_rows, query_segs, segments, score_scale)
        row_max = jnp.max(scores, axis=-1, keepdims=True)
        exponents = jnp.exp(scores - row_max)
        row_total = jnp.sum(exponents, axis=-1, keepdims=True)
        attn_probs = (exponents / row_total).astype(jnp.bfloat16)
        context = jnp.einsum(
            "hqk,hkd->hqd", attn_probs, value_rows, preferred_element_type=jnp.float32
        )
        return (context, (row_max + jnp.log(row_total))[..., 0])

    starts = jnp.arange(length // block_rows, dtype=jnp.int32) * block_rows
    context, logsum = lax.map(one_block, starts)
    context = jnp.moveaxis(context, 0, 1).reshape(head_count, length, head_dim)
    logsum = jnp.moveaxis(logsum, 0, 1).reshape(head_count, length)
    return (context, logsum)


def attend_back(queries, key_rows, value_rows, segments, logsum, d_context):
    head_count, length, head_dim = queries.shape
    block_rows = min(512, length)
    score_scale = head_dim ** (-0.5)

    def one_block(carry, start):
        d_keys, d_values = carry
        query_block = lax.dynamic_slice_in_dim(queries, start, block_rows, 1)
        query_segs = lax.dynamic_slice_in_dim(segments, start, block_rows, 0)
        lse_block = lax.dynamic_slice_in_dim(logsum, start, block_rows, 1)
        d_ctx_block = lax.dynamic_slice_in_dim(d_context, start, block_rows, 1)
        scores = masked_scores(query_block, key_rows, query_segs, segments, score_scale)
        attn_probs = jnp.exp(scores - lse_block[..., None])
        d_values = d_values + jnp.einsum(
            "hqk,hqd->hkd",
            attn_probs.astype(jnp.bfloat16),
            d_ctx_block,
            preferred_element_type=jnp.float32,
        )
        d_probs = jnp.einsum(
            "hqd,hkd->hqk", d_ctx_block, value_rows, preferred_element_type=jnp.float32
        )
        d_scores = attn_probs * (d_probs - jnp.sum(d_probs * attn_probs, axis=-1, keepdims=True))
        d_raw = (d_scores * score_scale).astype(jnp.bfloat16)
        d_query = jnp.einsum("hqk,hkd->hqd", d_raw, key_rows, preferred_element_type=jnp.float32)
        d_keys = d_keys + jnp.einsum(
            "hqk,hqd->hkd", d_raw, query_block, preferred_element_type=jnp.float32
        )
        return ((d_keys, d_values), d_query)

    starts = jnp.arange(length // block_rows, dtype=jnp.int32) * block_rows
    zeros_init = jnp.zeros(key_rows.shape, jnp.float32)
    (d_keys, d_values), d_queries = lax.scan(one_block, (zeros_init, zeros_init), starts)
    d_queries = jnp.moveaxis(d_queries, 0, 1).reshape(head_count, length, head_dim)
    return (d_queries, d_keys, d_values)


def shards(
    block_input,
    segment_ids,
    cotangent,
    norm_one_gain,
    qkv_weight,
    out_weight,
    norm_two_gain,
    up_weight,
    down_weight,
):
    section_index = lax.axis_index("section")
    micro_count = block_input.shape[0]
    row_count = block_input.shape[1]
    model_width = block_input.shape[2]
    w_qkv, w_out, w_up, w_down = (
        lax.all_gather(qkv_weight.astype(jnp.bfloat16), "dp", axis=1, tiled=True),
        lax.all_gather(out_weight.astype(jnp.bfloat16), "dp", axis=3, tiled=True),
        lax.all_gather(up_weight.astype(jnp.bfloat16), "dp", axis=1, tiled=True),
        lax.all_gather(down_weight.astype(jnp.bfloat16), "dp", axis=2, tiled=True),
    )
    w_qkv = w_qkv[0]
    w_out = w_out[0]
    w_up = w_up[0]
    w_down = w_down[0]
    gain_one = norm_one_gain[0]
    gain_two = norm_two_gain[0]
    head_dim = w_qkv.shape[2] // 3
    incoming = jnp.zeros((row_count, model_width), jnp.bfloat16)
    results = []
    kept_list = []
    for time_step in range(micro_count + 1):
        micro_index = jnp.clip(time_step - section_index, 0, micro_count - 1)
        segments = lax.dynamic_index_in_dim(segment_ids, micro_index, 0, keepdims=False)
        feed_rows = jnp.where(
            section_index == 0, block_input[min(time_step, micro_count - 1)], incoming
        )
        forward_resid = feed_rows.astype(jnp.float32)
        forward_normed_one = spread_rows(layer_norm(forward_resid, gain_one).astype(jnp.bfloat16))
        forward_qkv_all = jnp.einsum(
            "sd,dhe->hse", forward_normed_one, w_qkv, preferred_element_type=jnp.float32
        ).astype(jnp.bfloat16)
        forward_context, forward_logsum = attend(
            forward_qkv_all[..., :head_dim],
            forward_qkv_all[..., head_dim : 2 * head_dim],
            forward_qkv_all[..., 2 * head_dim :],
            segments,
        )
        forward_context = forward_context.astype(jnp.bfloat16)
        attn_out = collect_rows(
            jnp.einsum("hse,hed->sd", forward_context, w_out, preferred_element_type=jnp.float32)
        )
        forward_resid_mid = forward_resid + attn_out
        forward_normed_two = layer_norm(forward_resid_mid, gain_two).astype(jnp.bfloat16)
        forward_normed_two = spread_rows(forward_normed_two)
        forward_up_proj = jnp.dot(forward_normed_two, w_up, preferred_element_type=jnp.float32)
        forward_hidden = exact_gelu(forward_up_proj).astype(jnp.bfloat16)
        mlp_out = jnp.dot(forward_hidden, w_down, preferred_element_type=jnp.float32)
        mlp_out = collect_rows(mlp_out)
        result = (forward_resid_mid + mlp_out).astype(jnp.bfloat16)
        result, saved = (
            result,
            (
                forward_resid,
                forward_normed_one,
                forward_qkv_all,
                forward_logsum,
                forward_context,
                forward_resid_mid,
                forward_normed_two,
                forward_up_proj,
            ),
        )
        results.append(result)
        kept_list.append(saved)
        if time_step < micro_count:
            incoming = shifted(result, "section", 1)
    kept_stack = jax.tree.map(lambda *arrays: jnp.stack(arrays), *kept_list)
    totals = (
        jnp.zeros(gain_one.shape, jnp.float32),
        jnp.zeros(w_qkv.shape, jnp.float32),
        jnp.zeros(w_out.shape, jnp.float32),
        jnp.zeros(gain_two.shape, jnp.float32),
        jnp.zeros(w_up.shape, jnp.float32),
        jnp.zeros(w_down.shape, jnp.float32),
    )
    returning = jnp.zeros((row_count, model_width), jnp.bfloat16)
    grads_list = []
    for time_step in range(micro_count + 1):
        micro_index = time_step - 1 + section_index
        live_step = (micro_index >= 0) & (micro_index < micro_count)
        clipped = jnp.clip(micro_index, 0, micro_count - 1)
        kept_index = jnp.clip(micro_index + section_index, 0, micro_count)
        from_cot = lax.dynamic_index_in_dim(cotangent, clipped, 0, keepdims=False)
        from_cot = jnp.where(live_step, from_cot, jnp.zeros_like(from_cot))
        grad_in = jnp.where(section_index == 1, from_cot, returning).astype(jnp.float32)
        segments = lax.dynamic_index_in_dim(segment_ids, clipped, 0, keepdims=False)
        saved = jax.tree.map(
            lambda arrays: lax.dynamic_index_in_dim(arrays, kept_index, 0, keepdims=False),
            kept_stack,
        )
        resid, normed_one, qkv_all, logsum, context, resid_mid, normed_two, up_proj = saved
        grad_low = grad_in.astype(jnp.bfloat16)
        grad_low = spread_grads(grad_low)
        hidden, gelu_back = jax.vjp(exact_gelu, up_proj)
        grad_down = jnp.einsum(
            "sf,sd->fd", hidden.astype(jnp.bfloat16), grad_low, preferred_element_type=jnp.float32
        )
        d_hidden = jnp.einsum("sd,fd->sf", grad_low, w_down, preferred_element_type=jnp.float32)
        d_up = gelu_back(d_hidden)[0].astype(jnp.bfloat16)
        grad_up = jnp.einsum("sd,sf->df", normed_two, d_up, preferred_element_type=jnp.float32)
        d_normed = jnp.einsum("sf,df->sd", d_up, w_up, preferred_element_type=jnp.float32)
        d_normed = collect_grads(d_normed)
        norm_back = jax.vjp(layer_norm, resid_mid, gain_two)[1]
        d_mid, d_gain_two = norm_back(d_normed)
        d_mid = d_mid + grad_in
        d_attn = spread_grads(d_mid.astype(jnp.bfloat16))
        grad_out_w = jnp.einsum("hse,sd->hed", context, d_attn, preferred_element_type=jnp.float32)
        d_context = jnp.einsum(
            "sd,hed->hse", d_attn, w_out, preferred_element_type=jnp.float32
        ).astype(jnp.bfloat16)
        d_query, d_key, d_value = attend_back(
            qkv_all[..., :head_dim],
            qkv_all[..., head_dim : 2 * head_dim],
            qkv_all[..., 2 * head_dim :],
            segments,
            logsum,
            d_context,
        )
        d_qkv = jnp.concatenate([d_query, d_key, d_value], axis=-1).astype(jnp.bfloat16)
        grad_qkv = jnp.einsum("sd,hse->dhe", normed_one, d_qkv, preferred_element_type=jnp.float32)
        d_first = collect_grads(
            jnp.einsum("hse,dhe->sd", d_qkv, w_qkv, preferred_element_type=jnp.float32)
        )
        norm_back = jax.vjp(layer_norm, resid, gain_one)[1]
        d_resid, d_gain_one = norm_back(d_first)
        d_input = d_resid + d_mid
        d_input, grads = (
            d_input,
            (d_gain_one, grad_qkv, grad_out_w, d_gain_two, grad_up, grad_down),
        )
        d_low = d_input.astype(jnp.bfloat16)
        grads_list.append(d_low)
        totals = jax.tree.map(jnp.add, totals, grads)
        if time_step < micro_count:
            returning = shifted(d_low, "section", -1)
    layer_out = lax.dynamic_slice_in_dim(jnp.stack(results), section_index, micro_count, 0)[None]
    input_out = lax.dynamic_slice_in_dim(jnp.stack(grads_list), 1 - section_index, micro_count, 0)[
        None
    ]
    gain_grad_one, gain_grad_two = lax.psum((totals[0], totals[3]), ("dp", "tensor"))
    grad_up_all = totals[4]
    grad_down_all = totals[5]
    qkv_grad, out_grad, up_grad, down_grad = (
        lax.psum_scatter(
            totals[1][None].astype(jnp.bfloat16), "dp", scatter_dimension=1, tiled=True
        ).astype(jnp.float32),
        lax.psum_scatter(
            totals[2][None].astype(jnp.bfloat16), "dp", scatter_dimension=3, tiled=True
        ).astype(jnp.float32),
        lax.psum_scatter(
            grad_up_all[None].astype(jnp.bfloat16), "dp", scatter_dimension=1, tiled=True
        ).astype(jnp.float32),
        lax.psum_scatter(
            grad_down_all[None].astype(jnp.bfloat16), "dp", scatter_dimension=2, tiled=True
        ).astype(jnp.float32),
    )
    return (
        layer_out,
        input_out,
        gain_grad_one[None],
        qkv_grad,
        out_grad,
        gain_grad_two[None],
        up_grad,
        down_grad,
    )


def solution(mesh):
    return jax.shard_map(
        shards,
        mesh=mesh,
        in_specs=(
            P(None, ("dp", "tensor"), None),
            P(None, "dp"),
            P(None, ("dp", "tensor"), None),
            P("section", None),
            P("section", "dp", "tensor", None),
            P("section", "tensor", None, "dp"),
            P("section", None),
            P("section", "dp", "tensor"),
            P("section", "tensor", "dp"),
        ),
        out_specs=(
            P("section", None, ("dp", "tensor"), None),
            P("section", None, ("dp", "tensor"), None),
            P("section", None),
            P("section", "dp", "tensor", None),
            P("section", "tensor", None, "dp"),
            P("section", None),
            P("section", "dp", "tensor"),
            P("section", "tensor", "dp"),
        ),
        check_vma=False,
    )
```

profile of v0, /device:TPU:0, one launch (start us, length us, event | category | flops | bytes accessed | tf_op | source)
XLA Modules:
  0.0 3032.9 jit_solution(10924792900351240160)
XLA Ops:
  16.1 25.5 all_gather.50
  56.6 37.1 %all-gather.17.cloned.1.call-done = bf16[2048,1024]{1,0:T(8,128)(2,1)} async-done(((bf16[512,1024]{1,0:T(8,128)(2,1)}), bf16[2048,1024]{1,0:T(8,128)(2,1)}) %all-gather.17.cloned.1.call-update) | async-done | bytes 4194320 | tf_op jit(solution)/shard_map/all_gather | solution.py:24
  103.2 63.8 %while.81 = (s32[]{:T(128)}, bf16[4,4,512,64]{2,3,1,0:T(8,128)(2,1)S(1)}, f32[4,4,512]{2,1,0:T(4,128)S(1)}, s32[4]{0:T(128)S(1)}, s32[2048]{0:T(1024)S(1)}, /*in...) while((s32[]{:T(128)}, ...), condition=%wide.region_5.6_spmd, body=%wide.region_2.5_spmd.sunk | while | flops 1125120000 | bytes 61683920 | solution.py:70
  173.9 43.3 %reduce-scatter.17.cloned.1.call-done = bf16[512,1024]{1,0:T(8,128)(2,1)} async-done(((bf16[2048,1024]{1,0:T(8,128)(2,1)}), bf16[512,1024]{1,0:T(8,128)(2,1)}) %reduce-scatter.17.cloned.1.call-update) | async-done | bytes 1048592 | tf_op jit(solution)/shard_map/reduce_scatter | solution.py:28
  225.6 39.7 %all-gather.23.cloned.1.call-done = bf16[1,1024,1024]{2,1,0:T(8,128)(2,1)} async-done(((bf16[1,256,1024]{2,1,0:T(8,128)(2,1)}), bf16[1,1024,1024]{2,1,0:T(8,128)(2,1)}) %all-gather.23.cloned.1.call-update) | async-done | bytes 2097168 | tf_op jit(solution)/shard_map/all_gather | solution.py:131
  265.2 35.3 %all-gather.21.cloned.1.call-done = bf16[2048,1024]{1,0:T(8,128)(2,1)} async-done(((bf16[512,1024]{1,0:T(8,128)(2,1)}), bf16[2048,1024]{1,0:T(8,128)(2,1)}) %all-gather.21.cloned.1.call-update) | async-done | bytes 4194320 | tf_op jit(solution)/shard_map/all_gather | solution.py:24
  311.3 37.6 %all-gather.25.cloned.1.call-done = bf16[1,1024,1024]{2,1,0:T(8,128)(2,1)} async-done(((bf16[1,1024,256]{2,1,0:T(8,128)(2,1)}), bf16[1,1024,1024]{2,1,0:T(8,128)(2,1)}) %all-gather.25.cloned.1.call-update) | async-done | bytes 2097168 | tf_op jit(solution)/shard_map/all_gather | solution.py:132
  348.9 24.6 fusion.363
  373.6 42.8 %reduce-scatter.19.cloned.1.call-done = bf16[512,1024]{1,0:T(8,128)(2,1)} async-done(((bf16[2048,1024]{1,0:T(8,128)(2,1)}), bf16[512,1024]{1,0:T(8,128)(2,1)}) %reduce-scatter.19.cloned.1.call-update) | async-done | bytes 1048592 | tf_op jit(solution)/shard_map/reduce_scatter | solution.py:28
  421.9 22.1 collective-permute-done
  448.0 35.6 %all-gather.27.cloned.1.call-done = bf16[2048,1024]{1,0:T(8,128)(2,1)} async-done(((bf16[512,1024]{1,0:T(8,128)(2,1)}), bf16[2048,1024]{1,0:T(8,128)(2,1)}) %all-gather.27.cloned.1.call-update) | async-done | bytes 4194320 | tf_op jit(solution)/shard_map/all_gather | solution.py:24
  493.2 63.8 %while.82 = (s32[]{:T(128)}, bf16[4,4,512,64]{2,3,1,0:T(8,128)(2,1)S(1)}, f32[4,4,512]{2,1,0:T(4,128)S(1)}, s32[4]{0:T(128)S(1)}, s32[2048]{0:T(1024)S(1)}, /*in...) while((s32[]{:T(128)}, ...), condition=%wide.region_15.16_spmd, body=%wide.region_12.15_spmd.sunk | while | flops 1125120000 | bytes 61683920 | solution.py:70
  562.2 44.4 %reduce-scatter.21.cloned.1.call-done = bf16[512,1024]{1,0:T(8,128)(2,1)} async-done(((bf16[2048,1024]{1,0:T(8,128)(2,1)}), bf16[512,1024]{1,0:T(8,128)(2,1)}) %reduce-scatter.21.cloned.1.call-update) | async-done | bytes 1048592 | tf_op jit(solution)/shard_map/reduce_scatter | solution.py:28
  613.9 34.6 %all-gather.29.cloned.1.call-done = bf16[2048,1024]{1,0:T(8,128)(2,1)} async-done(((bf16[512,1024]{1,0:T(8,128)(2,1)}), bf16[2048,1024]{1,0:T(8,128)(2,1)}) %all-gather.29.cloned.1.call-update) | async-done | bytes 4194320 | tf_op jit(solution)/shard_map/all_gather | solution.py:24
  658.6 22.9 fusion.366
  681.6 44.6 %reduce-scatter.23.cloned.1.call-done = bf16[512,1024]{1,0:T(8,128)(2,1)} async-done(((bf16[2048,1024]{1,0:T(8,128)(2,1)}), bf16[512,1024]{1,0:T(8,128)(2,1)}) %reduce-scatter.23.cloned.1.call-update) | async-done | bytes 1048592 | tf_op jit(solution)/shard_map/reduce_scatter | solution.py:28
  731.8 22.3 collective-permute-done.1
  758.5 35.2 %all-gather.31.cloned.1.call-done = bf16[2048,1024]{1,0:T(8,128)(2,1)} async-done(((bf16[512,1024]{1,0:T(8,128)(2,1)}), bf16[2048,1024]{1,0:T(8,128)(2,1)}) %all-gather.31.cloned.1.call-update) | async-done | bytes 4194320 | tf_op jit(solution)/shard_map/all_gather | solution.py:24
  803.3 63.8 %while.83 = (s32[]{:T(128)}, bf16[4,4,512,64]{2,3,1,0:T(8,128)(2,1)S(1)}, f32[4,4,512]{2,1,0:T(4,128)S(1)}, s32[4]{0:T(128)S(1)}, s32[2048]{0:T(1024)S(1)}, /*in...) while((s32[]{:T(128)}, ...), condition=%wide.region_25.26_spmd, body=%wide.region_22.25_spmd.sunk | while | flops 1125120000 | bytes 61683920 | solution.py:70
  872.8 44.4 %reduce-scatter.25.cloned.1.call-done = bf16[512,1024]{1,0:T(8,128)(2,1)} async-done(((bf16[2048,1024]{1,0:T(8,128)(2,1)}), bf16[512,1024]{1,0:T(8,128)(2,1)}) %reduce-scatter.25.cloned.1.call-update) | async-done | bytes 1048592 | tf_op jit(solution)/shard_map/reduce_scatter | solution.py:28
  925.7 33.4 %all-gather.33.cloned.1.call-done = bf16[2048,1024]{1,0:T(8,128)(2,1)} async-done(((bf16[512,1024]{1,0:T(8,128)(2,1)}), bf16[2048,1024]{1,0:T(8,128)(2,1)}) %all-gather.33.cloned.1.call-update) | async-done | bytes 4194320 | tf_op jit(solution)/shard_map/all_gather | solution.py:24
  985.5 52.9 %fusion.233 = (f32[2048,1024]{1,0:T(8,128)}, f32[2048,1024]{1,0:T(8,128)}, f32[2048,1024]{1,0:T(8,128)}) fusion(f32[3,2048,1024]{2,1,0:T(8,128)S(1)} %pad_maximum_fusion, s32[]{:T(128)S(6)} %min.36, s32[]{:T(128)S(6)} %min.32, s32[]{:T(128)S(6)} %min.34), kind=kLoop, calls=%fused_computation.192 | loop fusion | flops 390070272 | bytes 50331660 | tf_op jit(solution)/shard_map/jvp()/erfc | solution.py:20
  1069.4 34.8 %reduce-scatter.29.cloned.1.call-done = bf16[512,1024]{1,0:T(8,128)(2,1)} async-done(((bf16[2048,1024]{1,0:T(8,128)(2,1)}), bf16[512,1024]{1,0:T(8,128)(2,1)}) %reduce-scatter.29.cloned.1.call-update) | async-done | bytes 1048592 | tf_op jit(solution)/shard_map/reduce_scatter | solution.py:38
  1127.0 21.4 all-gather.35.cloned.1.call-done
  1153.9 367.7 %while.84 = (s32[]{:T(128)}, f32[4,2048,64]{1,2,0:T(8,128)}, f32[4,2048,64]{1,2,0:T(8,128)}, bf16[4,4,512,64]{2,3,1,0:T(8,128)(2,1)}, s32[4]{0:T(128)S(1)}, /*in...) while((s32[]{:T(128)}, f32[4,2048,64]{1,2,0:T(8,128)}, ...), condition=%wide.region_37.38_spmd.clone, body=%wide.region_35.37_spmd.clone.sunk | while | flops 2796560384 | bytes 271128832 | solution.py:108
  1179.9 31.2 %fusion.754 = bf16[4,4,512,64]{2,3,1,0:T(8,128)(2,1)} fusion(bf16[4,4,512,64]{2,3,1,0:T(8,128)(2,1)} %get-tuple-element.1125, s32[]{:T(128)S(6)} %copy.75, bf16[4,2048,64]{1,2,0:T(8,128)(2,1)S(1)} %get-tuple-element.1143, f32[4,512,2048]{2,1,0:T(8,128)} %fusion.750, f32[4,512,2048]{2,1,0:T(8,128)} %copy-done, ...), kind=kOutput, calls=%fused_computation.67.clone.1 | convolution fusion | flops 583012352 | bytes 70795264 | tf_op jit(solution)/shard_map/while/body/eval_jaxpr/hqk,hkd->hqd/dot_general | solution.py:100
  1211.2 34.0 %fusion.752 = f32[4,2048,64]{1,2,0:T(8,128)} fusion(f32[4,512,2048]{2,1,0:T(8,128)} %fusion.750, f32[4,512,2048]{2,1,0:T(8,128)} %copy-done, f32[4,512]{1,0:T(4,128)S(1)} %constant_dynamic-slice_fusion.12, pred[512,2048]{1,0:T(8,128)(4,1)} %broadcast_compare_fusion.15, f32[4,2048,64]{1,2,0:T(8,128)} %get-tuple-element.1123, pred[]{:T(512)S(6)} %compare.9, ...), kind=kOutput, calls=%fused_computation.64.clone.1 | convolution fusion | flops 584060928 | bytes 73678856 | tf_op jit(solution)/shard_map/while/body/eval_jaxpr/hqk,hqd->hkd/dot_general | solution.py:101
  1271.9 31.2 %fusion.754 = bf16[4,4,512,64]{2,3,1,0:T(8,128)(2,1)} fusion(bf16[4,4,512,64]{2,3,1,0:T(8,128)(2,1)} %get-tuple-element.1125, s32[]{:T(128)S(6)} %copy.75, bf16[4,2048,64]{1,2,0:T(8,128)(2,1)S(1)} %get-tuple-element.1143, f32[4,512,2048]{2,1,0:T(8,128)} %fusion.750, f32[4,512,2048]{2,1,0:T(8,128)} %copy-done, ...), kind=kOutput, calls=%fused_computation.67.clone.1 | convolution fusion | flops 583012352 | bytes 70795264 | tf_op jit(solution)/shard_map/while/body/eval_jaxpr/hqk,hkd->hqd/dot_general | solution.py:100
  1303.1 34.2 %fusion.752 = f32[4,2048,64]{1,2,0:T(8,128)} fusion(f32[4,512,2048]{2,1,0:T(8,128)} %fusion.750, f32[4,512,2048]{2,1,0:T(8,128)} %copy-done, f32[4,512]{1,0:T(4,128)S(1)} %constant_dynamic-slice_fusion.12, pred[512,2048]{1,0:T(8,128)(4,1)} %broadcast_compare_fusion.15, f32[4,2048,64]{1,2,0:T(8,128)} %get-tuple-element.1123, pred[]{:T(512)S(6)} %compare.9, ...), kind=kOutput, calls=%fused_computation.64.clone.1 | convolution fusion | flops 584060928 | bytes 73678856 | tf_op jit(solution)/shard_map/while/body/eval_jaxpr/hqk,hqd->hkd/dot_general | solution.py:101
  1364.0 31.2 %fusion.754 = bf16[4,4,512,64]{2,3,1,0:T(8,128)(2,1)} fusion(bf16[4,4,512,64]{2,3,1,0:T(8,128)(2,1)} %get-tuple-element.1125, s32[]{:T(128)S(6)} %copy.75, bf16[4,2048,64]{1,2,0:T(8,128)(2,1)S(1)} %get-tuple-element.1143, f32[4,512,2048]{2,1,0:T(8,128)} %fusion.750, f32[4,512,2048]{2,1,0:T(8,128)} %copy-done, ...), kind=kOutput, calls=%fused_computation.67.clone.1 | convolution fusion | flops 583012352 | bytes 70795264 | tf_op jit(solution)/shard_map/while/body/eval_jaxpr/hqk,hkd->hqd/dot_general | solution.py:100
  1395.2 34.2 %fusion.752 = f32[4,2048,64]{1,2,0:T(8,128)} fusion(f32[4,512,2048]{2,1,0:T(8,128)} %fusion.750, f32[4,512,2048]{2,1,0:T(8,128)} %copy-done, f32[4,512]{1,0:T(4,128)S(1)} %constant_dynamic-slice_fusion.12, pred[512,2048]{1,0:T(8,128)(4,1)} %broadcast_compare_fusion.15, f32[4,2048,64]{1,2,0:T(8,128)} %get-tuple-element.1123, pred[]{:T(512)S(6)} %compare.9, ...), kind=kOutput, calls=%fused_computation.64.clone.1 | convolution fusion | flops 584060928 | bytes 73678856 | tf_op jit(solution)/shard_map/while/body/eval_jaxpr/hqk,hqd->hkd/dot_general | solution.py:101
  1456.0 31.2 %fusion.754 = bf16[4,4,512,64]{2,3,1,0:T(8,128)(2,1)} fusion(bf16[4,4,512,64]{2,3,1,0:T(8,128)(2,1)} %get-tuple-element.1125, s32[]{:T(128)S(6)} %copy.75, bf16[4,2048,64]{1,2,0:T(8,128)(2,1)S(1)} %get-tuple-element.1143, f32[4,512,2048]{2,1,0:T(8,128)} %fusion.750, f32[4,512,2048]{2,1,0:T(8,128)} %copy-done, ...), kind=kOutput, calls=%fused_computation.67.clone.1 | convolution fusion | flops 583012352 | bytes 70795264 | tf_op jit(solution)/shard_map/while/body/eval_jaxpr/hqk,hkd->hqd/dot_general | solution.py:100
  1487.2 34.2 %fusion.752 = f32[4,2048,64]{1,2,0:T(8,128)} fusion(f32[4,512,2048]{2,1,0:T(8,128)} %fusion.750, f32[4,512,2048]{2,1,0:T(8,128)} %copy-done, f32[4,512]{1,0:T(4,128)S(1)} %constant_dynamic-slice_fusion.12, pred[512,2048]{1,0:T(8,128)(4,1)} %broadcast_compare_fusion.15, f32[4,2048,64]{1,2,0:T(8,128)} %get-tuple-element.1123, pred[]{:T(512)S(6)} %compare.9, ...), kind=kOutput, calls=%fused_computation.64.clone.1 | convolution fusion | flops 584060928 | bytes 73678856 | tf_op jit(solution)/shard_map/while/body/eval_jaxpr/hqk,hqd->hkd/dot_general | solution.py:101
  1533.6 44.6 %reduce-scatter.31.cloned.1.call-done = bf16[512,1024]{1,0:T(8,128)(2,1)} async-done(((bf16[2048,1024]{1,0:T(8,128)(2,1)}), bf16[512,1024]{1,0:T(8,128)(2,1)}) %reduce-scatter.31.cloned.1.call-update) | async-done | bytes 1048592 | tf_op jit(solution)/shard_map/reduce_scatter | solution.py:38
  1588.4 25.5 collective-permute-done.2
  1616.4 33.7 %all-gather.37.cloned.1.call-done = bf16[2048,1024]{1,0:T(8,128)(2,1)} async-done(((bf16[512,1024]{1,0:T(8,128)(2,1)}), bf16[2048,1024]{1,0:T(8,128)(2,1)}) %all-gather.37.cloned.1.call-update) | async-done | bytes 4194320 | tf_op jit(solution)/shard_map/all_gather | solution.py:34
  1671.4 44.6 %reduce-scatter.33.cloned.1.call-done = bf16[512,1024]{1,0:T(8,128)(2,1)} async-done(((bf16[2048,1024]{1,0:T(8,128)(2,1)}), bf16[512,1024]{1,0:T(8,128)(2,1)}) %reduce-scatter.33.cloned.1.call-update) | async-done | bytes 1048592 | tf_op jit(solution)/shard_map/reduce_scatter | solution.py:38
  1728.7 31.4 %all-gather.39.cloned.1.call-done = bf16[2048,1024]{1,0:T(8,128)(2,1)} async-done(((bf16[512,1024]{1,0:T(8,128)(2,1)}), bf16[2048,1024]{1,0:T(8,128)(2,1)}) %all-gather.39.cloned.1.call-update) | async-done | bytes 4194320 | tf_op jit(solution)/shard_map/all_gather | solution.py:34
  1765.7 369.9 %while.85 = (s32[]{:T(128)}, f32[4,2048,64]{1,2,0:T(8,128)}, f32[4,2048,64]{1,2,0:T(8,128)}, bf16[4,4,512,64]{2,3,1,0:T(8,128)(2,1)}, s32[4]{0:T(128)S(1)}, /*in...) while((s32[]{:T(128)}, f32[4,2048,64]{1,2,0:T(8,128)}, ...), condition=%wide.region_50.51_spmd.clone, body=%wide.region_48.50_spmd.clone.sunk | while | flops 2796560384 | bytes 271128832 | solution.py:108
  1792.5 31.2 %fusion.769 = bf16[4,4,512,64]{2,3,1,0:T(8,128)(2,1)} fusion(bf16[4,4,512,64]{2,3,1,0:T(8,128)(2,1)} %get-tuple-element.1167, s32[]{:T(128)S(6)} %copy.87, bf16[4,2048,64]{1,2,0:T(8,128)(2,1)S(1)} %get-tuple-element.1185, f32[4,512,2048]{2,1,0:T(8,128)} %fusion.765, f32[4,512,2048]{2,1,0:T(8,128)} %copy-done.1, ...), kind=kOutput, calls=%fused_computation.109.clone.1 | convolution fusion | flops 583012352 | bytes 70795264 | tf_op jit(solution)/shard_map/while/body/eval_jaxpr/hqk,hkd->hqd/dot_general | solution.py:100
  1823.7 33.9 %fusion.767 = f32[4,2048,64]{1,2,0:T(8,128)} fusion(f32[4,512,2048]{2,1,0:T(8,128)} %fusion.765, f32[4,512,2048]{2,1,0:T(8,128)} %copy-done.1, f32[4,512]{1,0:T(4,128)S(1)} %constant_dynamic-slice_fusion.13, pred[512,2048]{1,0:T(8,128)(4,1)} %broadcast_compare_fusion.16, f32[4,2048,64]{1,2,0:T(8,128)} %get-tuple-element.1165, pred[]{:T(512)S(6)} %compare.10, ...), kind=kOutput, calls=%fused_computation.106.clone.1 | convolution fusion | flops 584060928 | bytes 73678856 | tf_op jit(solution)/shard_map/while/body/eval_jaxpr/hqk,hqd->hkd/dot_general | solution.py:101
  1885.0 31.3 %fusion.769 = bf16[4,4,512,64]{2,3,1,0:T(8,128)(2,1)} fusion(bf16[4,4,512,64]{2,3,1,0:T(8,128)(2,1)} %get-tuple-element.1167, s32[]{:T(128)S(6)} %copy.87, bf16[4,2048,64]{1,2,0:T(8,128)(2,1)S(1)} %get-tuple-element.1185, f32[4,512,2048]{2,1,0:T(8,128)} %fusion.765, f32[4,512,2048]{2,1,0:T(8,128)} %copy-done.1, ...), kind=kOutput, calls=%fused_computation.109.clone.1 | convolution fusion | flops 583012352 | bytes 70795264 | tf_op jit(solution)/shard_map/while/body/eval_jaxpr/hqk,hkd->hqd/dot_general | solution.py:100
  1916.3 34.0 %fusion.767 = f32[4,2048,64]{1,2,0:T(8,128)} fusion(f32[4,512,2048]{2,1,0:T(8,128)} %fusion.765, f32[4,512,2048]{2,1,0:T(8,128)} %copy-done.1, f32[4,512]{1,0:T(4,128)S(1)} %constant_dynamic-slice_fusion.13, pred[512,2048]{1,0:T(8,128)(4,1)} %broadcast_compare_fusion.16, f32[4,2048,64]{1,2,0:T(8,128)} %get-tuple-element.1165, pred[]{:T(512)S(6)} %compare.10, ...), kind=kOutput, calls=%fused_computation.106.clone.1 | convolution fusion | flops 584060928 | bytes 73678856 | tf_op jit(solution)/shard_map/while/body/eval_jaxpr/hqk,hqd->hkd/dot_general | solution.py:101
  1977.7 31.3 %fusion.769 = bf16[4,4,512,64]{2,3,1,0:T(8,128)(2,1)} fusion(bf16[4,4,512,64]{2,3,1,0:T(8,128)(2,1)} %get-tuple-element.1167, s32[]{:T(128)S(6)} %copy.87, bf16[4,2048,64]{1,2,0:T(8,128)(2,1)S(1)} %get-tuple-element.1185, f32[4,512,2048]{2,1,0:T(8,128)} %fusion.765, f32[4,512,2048]{2,1,0:T(8,128)} %copy-done.1, ...), kind=kOutput, calls=%fused_computation.109.clone.1 | convolution fusion | flops 583012352 | bytes 70795264 | tf_op jit(solution)/shard_map/while/body/eval_jaxpr/hqk,hkd->hqd/dot_general | solution.py:100
  2009.0 34.0 %fusion.767 = f32[4,2048,64]{1,2,0:T(8,128)} fusion(f32[4,512,2048]{2,1,0:T(8,128)} %fusion.765, f32[4,512,2048]{2,1,0:T(8,128)} %copy-done.1, f32[4,512]{1,0:T(4,128)S(1)} %constant_dynamic-slice_fusion.13, pred[512,2048]{1,0:T(8,128)(4,1)} %broadcast_compare_fusion.16, f32[4,2048,64]{1,2,0:T(8,128)} %get-tuple-element.1165, pred[]{:T(512)S(6)} %compare.10, ...), kind=kOutput, calls=%fused_computation.106.clone.1 | convolution fusion | flops 584060928 | bytes 73678856 | tf_op jit(solution)/shard_map/while/body/eval_jaxpr/hqk,hqd->hkd/dot_general | solution.py:101
  2070.3 31.2 %fusion.769 = bf16[4,4,512,64]{2,3,1,0:T(8,128)(2,1)} fusion(bf16[4,4,512,64]{2,3,1,0:T(8,128)(2,1)} %get-tuple-element.1167, s32[]{:T(128)S(6)} %copy.87, bf16[4,2048,64]{1,2,0:T(8,128)(2,1)S(1)} %get-tuple-element.1185, f32[4,512,2048]{2,1,0:T(8,128)} %fusion.765, f32[4,512,2048]{2,1,0:T(8,128)} %copy-done.1, ...), kind=kOutput, calls=%fused_computation.109.clone.1 | convolution fusion | flops 583012352 | bytes 70795264 | tf_op jit(solution)/shard_map/while/body/eval_jaxpr/hqk,hkd->hqd/dot_general | solution.py:100
  2101.6 34.0 %fusion.767 = f32[4,2048,64]{1,2,0:T(8,128)} fusion(f32[4,512,2048]{2,1,0:T(8,128)} %fusion.765, f32[4,512,2048]{2,1,0:T(8,128)} %copy-done.1, f32[4,512]{1,0:T(4,128)S(1)} %constant_dynamic-slice_fusion.13, pred[512,2048]{1,0:T(8,128)(4,1)} %broadcast_compare_fusion.16, f32[4,2048,64]{1,2,0:T(8,128)} %get-tuple-element.1165, pred[]{:T(512)S(6)} %compare.10, ...), kind=kOutput, calls=%fused_computation.106.clone.1 | convolution fusion | flops 584060928 | bytes 73678856 | tf_op jit(solution)/shard_map/while/body/eval_jaxpr/hqk,hqd->hkd/dot_general | solution.py:101
  2147.7 44.6 %reduce-scatter.35.cloned.1.call-done = bf16[512,1024]{1,0:T(8,128)(2,1)} async-done(((bf16[2048,1024]{1,0:T(8,128)(2,1)}), bf16[512,1024]{1,0:T(8,128)(2,1)}) %reduce-scatter.35.cloned.1.call-update) | async-done | bytes 1048592 | tf_op jit(solution)/shard_map/reduce_scatter | solution.py:38
  2203.0 25.7 collective-permute-done.3
  2231.1 33.7 %all-gather.41.cloned.1.call-done = bf16[2048,1024]{1,0:T(8,128)(2,1)} async-done(((bf16[512,1024]{1,0:T(8,128)(2,1)}), bf16[2048,1024]{1,0:T(8,128)(2,1)}) %all-gather.41.cloned.1.call-update) | async-done | bytes 4194320 | tf_op jit(solution)/shard_map/all_gather | solution.py:34
  2286.6 44.2 %reduce-scatter.37.cloned.1.call-done = bf16[512,1024]{1,0:T(8,128)(2,1)} async-done(((bf16[2048,1024]{1,0:T(8,128)(2,1)}), bf16[512,1024]{1,0:T(8,128)(2,1)}) %reduce-scatter.37.cloned.1.call-update) | async-done | bytes 1048592 | tf_op jit(solution)/shard_map/reduce_scatter | solution.py:38
  2339.5 23.6 fusion.369
  2496.5 368.0 %while.86 = (s32[]{:T(128)}, f32[4,2048,64]{1,2,0:T(8,128)}, f32[4,2048,64]{1,2,0:T(8,128)}, bf16[4,4,512,64]{2,3,1,0:T(8,128)(2,1)}, s32[4]{0:T(128)S(1)}, /*in...) while((s32[]{:T(128)}, f32[4,2048,64]{1,2,0:T(8,128)}, ...), condition=%wide.region_63.64_spmd.clone, body=%wide.region_61.63_spmd.clone.sunk | while | flops 2796560384 | bytes 271128832 | solution.py:108
  2522.8 31.0 %fusion.784 = bf16[4,4,512,64]{2,3,1,0:T(8,128)(2,1)} fusion(bf16[4,4,512,64]{2,3,1,0:T(8,128)(2,1)} %get-tuple-element.1209, s32[]{:T(128)S(6)} %copy.99, bf16[4,2048,64]{1,2,0:T(8,128)(2,1)S(1)} %get-tuple-element.1227, f32[4,512,2048]{2,1,0:T(8,128)} %fusion.780, f32[4,512,2048]{2,1,0:T(8,128)} %copy-done.2, ...), kind=kOutput, calls=%fused_computation.151.clone.1 | convolution fusion | flops 583012352 | bytes 70795264 | tf_op jit(solution)/shard_map/while/body/eval_jaxpr/hqk,hkd->hqd/dot_general | solution.py:100
  2553.8 33.9 %fusion.782 = f32[4,2048,64]{1,2,0:T(8,128)} fusion(f32[4,512,2048]{2,1,0:T(8,128)} %fusion.780, f32[4,512,2048]{2,1,0:T(8,128)} %copy-done.2, f32[4,512]{1,0:T(4,128)S(1)} %constant_dynamic-slice_fusion.14, pred[512,2048]{1,0:T(8,128)(4,1)} %broadcast_compare_fusion.17, f32[4,2048,64]{1,2,0:T(8,128)} %get-tuple-element.1207, pred[]{:T(512)S(6)} %compare.11, ...), kind=kOutput, calls=%fused_computation.148.clone.1 | convolution fusion | flops 584060928 | bytes 73678856 | tf_op jit(solution)/shard_map/while/body/eval_jaxpr/hqk,hqd->hkd/dot_general | solution.py:101
  2614.9 31.0 %fusion.784 = bf16[4,4,512,64]{2,3,1,0:T(8,128)(2,1)} fusion(bf16[4,4,512,64]{2,3,1,0:T(8,128)(2,1)} %get-tuple-element.1209, s32[]{:T(128)S(6)} %copy.99, bf16[4,2048,64]{1,2,0:T(8,128)(2,1)S(1)} %get-tuple-element.1227, f32[4,512,2048]{2,1,0:T(8,128)} %fusion.780, f32[4,512,2048]{2,1,0:T(8,128)} %copy-done.2, ...), kind=kOutput, calls=%fused_computation.151.clone.1 | convolution fusion | flops 583012352 | bytes 70795264 | tf_op jit(solution)/shard_map/while/body/eval_jaxpr/hqk,hkd->hqd/dot_general | solution.py:100
  2645.9 34.1 %fusion.782 = f32[4,2048,64]{1,2,0:T(8,128)} fusion(f32[4,512,2048]{2,1,0:T(8,128)} %fusion.780, f32[4,512,2048]{2,1,0:T(8,128)} %copy-done.2, f32[4,512]{1,0:T(4,128)S(1)} %constant_dynamic-slice_fusion.14, pred[512,2048]{1,0:T(8,128)(4,1)} %broadcast_compare_fusion.17, f32[4,2048,64]{1,2,0:T(8,128)} %get-tuple-element.1207, pred[]{:T(512)S(6)} %compare.11, ...), kind=kOutput, calls=%fused_computation.148.clone.1 | convolution fusion | flops 584060928 | bytes 73678856 | tf_op jit(solution)/shard_map/while/body/eval_jaxpr/hqk,hqd->hkd/dot_general | solution.py:101
  2707.1 31.0 %fusion.784 = bf16[4,4,512,64]{2,3,1,0:T(8,128)(2,1)} fusion(bf16[4,4,512,64]{2,3,1,0:T(8,128)(2,1)} %get-tuple-element.1209, s32[]{:T(128)S(6)} %copy.99, bf16[4,2048,64]{1,2,0:T(8,128)(2,1)S(1)} %get-tuple-element.1227, f32[4,512,2048]{2,1,0:T(8,128)} %fusion.780, f32[4,512,2048]{2,1,0:T(8,128)} %copy-done.2, ...), kind=kOutput, calls=%fused_computation.151.clone.1 | convolution fusion | flops 583012352 | bytes 70795264 | tf_op jit(solution)/shard_map/while/body/eval_jaxpr/hqk,hkd->hqd/dot_general | solution.py:100
  2738.1 34.1 %fusion.782 = f32[4,2048,64]{1,2,0:T(8,128)} fusion(f32[4,512,2048]{2,1,0:T(8,128)} %fusion.780, f32[4,512,2048]{2,1,0:T(8,128)} %copy-done.2, f32[4,512]{1,0:T(4,128)S(1)} %constant_dynamic-slice_fusion.14, pred[512,2048]{1,0:T(8,128)(4,1)} %broadcast_compare_fusion.17, f32[4,2048,64]{1,2,0:T(8,128)} %get-tuple-element.1207, pred[]{:T(512)S(6)} %compare.11, ...), kind=kOutput, calls=%fused_computation.148.clone.1 | convolution fusion | flops 584060928 | bytes 73678856 | tf_op jit(solution)/shard_map/while/body/eval_jaxpr/hqk,hqd->hkd/dot_general | solution.py:101
  2799.3 31.0 %fusion.784 = bf16[4,4,512,64]{2,3,1,0:T(8,128)(2,1)} fusion(bf16[4,4,512,64]{2,3,1,0:T(8,128)(2,1)} %get-tuple-element.1209, s32[]{:T(128)S(6)} %copy.99, bf16[4,2048,64]{1,2,0:T(8,128)(2,1)S(1)} %get-tuple-element.1227, f32[4,512,2048]{2,1,0:T(8,128)} %fusion.780, f32[4,512,2048]{2,1,0:T(8,128)} %copy-done.2, ...), kind=kOutput, calls=%fused_computation.151.clone.1 | convolution fusion | flops 583012352 | bytes 70795264 | tf_op jit(solution)/shard_map/while/body/eval_jaxpr/hqk,hkd->hqd/dot_general | solution.py:100
  2830.3 34.1 %fusion.782 = f32[4,2048,64]{1,2,0:T(8,128)} fusion(f32[4,512,2048]{2,1,0:T(8,128)} %fusion.780, f32[4,512,2048]{2,1,0:T(8,128)} %copy-done.2, f32[4,512]{1,0:T(4,128)S(1)} %constant_dynamic-slice_fusion.14, pred[512,2048]{1,0:T(8,128)(4,1)} %broadcast_compare_fusion.17, f32[4,2048,64]{1,2,0:T(8,128)} %get-tuple-element.1207, pred[]{:T(512)S(6)} %compare.11, ...), kind=kOutput, calls=%fused_computation.148.clone.1 | convolution fusion | flops 584060928 | bytes 73678856 | tf_op jit(solution)/shard_map/while/body/eval_jaxpr/hqk,hqd->hkd/dot_general | solution.py:101
  2904.4 30.1 reduce-scatter.41.cloned.1.call-done
  2936.4 44.3 %reduce-scatter.39.cloned.1.call-done = bf16[512,1024]{1,0:T(8,128)(2,1)} async-done(((bf16[2048,1024]{1,0:T(8,128)(2,1)}), bf16[512,1024]{1,0:T(8,128)(2,1)}) %reduce-scatter.39.cloned.1.call-update) | async-done | bytes 1048592 | tf_op jit(solution)/shard_map/reduce_scatter | solution.py:38
  2986.2 33.3 %all-reduce = (f32[1,1024]{1,0:T(1,128)}, f32[1,1024]{1,0:T(1,128)}) all-reduce(f32[1,1024]{1,0:T(1,128)S(1)} %bitcast.821, f32[1,1024]{1,0:T(1,128)S(1)} %bitcast.820), channel_id=1, replica_groups=mesh['section'=2,'dp'=4,'tensor'=4] {'dp','tensor'}, use_global_device_ids=true, to_apply=%region_72.73 | all-reduce | flops 2048 | bytes 16384 | tf_op jit(solution)/shard_map/psum | solution.py:263
  (744 shorter events, 992.8 us)
Async XLA Ops:
  7.2 49.5 %all-gather.19.cloned.1.call-start = ((), (), s32[]{:S(2)}) async-start(), calls=%async_computation.17 | async-start | bytes 1966080 | tf_op jit(solution)/shard_map/all_gather | solution.py:129
  9.2 84.5 %all-gather.17.cloned.1.call-start = ((), (), s32[]{:S(2)}) async-start(), calls=%async_computation.16 | async-start | bytes 5242880 | tf_op jit(solution)/shard_map/all_gather | solution.py:24
  15.1 202.1 %reduce-scatter.17.cloned.1.call-start = ((), (), s32[]{:S(2)}) async-start(), calls=%async_computation.18 | async-start | bytes 5242880 | tf_op jit(solution)/shard_map/reduce_scatter | solution.py:28
  172.6 92.7 %all-gather.23.cloned.1.call-start = ((), (), s32[]{:S(2)}) async-start(), calls=%async_computation.20 | async-start | bytes 2621440 | tf_op jit(solution)/shard_map/all_gather | solution.py:131
  173.5 51.2 %copy-start.65 = (f32[1,1024,256]{2,1,0:T(8,128)S(1)}, f32[1,1024,256]{2,1,0:T(8,128)}, u32[]{:S(2)}) copy-start(f32[1,1024,256]{2,1,0:T(8,128)} %param.29) | copy-start | bytes 3145732
  173.5 127.0 %all-gather.21.cloned.1.call-start = ((), (), s32[]{:S(2)}) async-start(), calls=%async_computation.19 | async-start | bytes 5242880 | tf_op jit(solution)/shard_map/all_gather | solution.py:24
  224.6 124.3 %all-gather.25.cloned.1.call-start = ((), (), s32[]{:S(2)}) async-start(), calls=%async_computation.21 | async-start | bytes 2621440 | tf_op jit(solution)/shard_map/all_gather | solution.py:132
  225.5 190.9 %reduce-scatter.19.cloned.1.call-start = ((), (), s32[]{:S(2)}) async-start(), calls=%async_computation.22 | async-start | bytes 5242880 | tf_op jit(solution)/shard_map/reduce_scatter | solution.py:28
  311.3 105.1 %copy-start.23 = (bf16[512,1024]{1,0:T(8,128)(2,1)S(1)}, bf16[512,1024]{1,0:T(8,128)(2,1)}, u32[]{:S(2)}) copy-start(bf16[512,1024]{1,0:T(8,128)(2,1)} %reduce-scatter.17.cloned.1.call-done) | copy-start | bytes 3145732
  373.5 73.1 %copy-start.69 = (f32[1,1024]{1,0:T(1,128)S(1)}, f32[1,1024]{1,0:T(1,128)}, u32[]{:S(2)}) copy-start(f32[1,1024]{1,0:T(1,128)} %param.24) | copy-start | bytes 12292
  373.5 110.1 %all-gather.27.cloned.1.call-start = ((), (), s32[]{:S(2)}) async-start(), calls=%async_computation.23 | async-start | bytes 5242880 | tf_op jit(solution)/shard_map/all_gather | solution.py:24
  418.3 25.8 collective-permute-start
  448.0 158.6 %reduce-scatter.21.cloned.1.call-start = ((), (), s32[]{:S(2)}) async-start(), calls=%async_computation.24 | async-start | bytes 5242880 | tf_op jit(solution)/shard_map/reduce_scatter | solution.py:28
  561.9 86.5 %all-gather.29.cloned.1.call-start = ((), (), s32[]{:S(2)}) async-start(), calls=%async_computation.25 | async-start | bytes 5242880 | tf_op jit(solution)/shard_map/all_gather | solution.py:24
  613.8 112.4 %reduce-scatter.23.cloned.1.call-start = ((), (), s32[]{:S(2)}) async-start(), calls=%async_computation.26 | async-start | bytes 5242880 | tf_op jit(solution)/shard_map/reduce_scatter | solution.py:28
  681.5 72.7 %copy-start.12 = (bf16[2,512,1024]{2,1,0:T(8,128)(2,1)S(1)}, bf16[2,512,1024]{2,1,0:T(8,128)(2,1)}, u32[]{:S(2)}) copy-start(bf16[2,512,1024]{2,1,0:T(8,128)(2,1)} %param.21) | copy-start | bytes 6291460
  681.5 75.2 %copy-start.70 = (f32[1,1024]{1,0:T(1,128)S(1)}, f32[1,1024]{1,0:T(1,128)}, u32[]{:S(2)}) copy-start(f32[1,1024]{1,0:T(1,128)} %param.24) | copy-start | bytes 12292
  681.5 112.2 %all-gather.31.cloned.1.call-start = ((), (), s32[]{:S(2)}) async-start(), calls=%async_computation.27 | async-start | bytes 5242880 | tf_op jit(solution)/shard_map/all_gather | solution.py:24
  728.4 25.8 collective-permute-start.1
  758.1 159.1 %reduce-scatter.25.cloned.1.call-start = ((), (), s32[]{:S(2)}) async-start(), calls=%async_computation.28 | async-start | bytes 5242880 | tf_op jit(solution)/shard_map/reduce_scatter | solution.py:28
  872.5 52.0 %copy-start.28 = (bf16[2,512,1024]{2,1,0:T(8,128)(2,1)S(1)}, bf16[2,512,1024]{2,1,0:T(8,128)(2,1)}, u32[]{:S(2)}) copy-start(bf16[2,512,1024]{2,1,0:T(8,128)(2,1)} %param.23) | copy-start | bytes 6291460
  872.6 86.5 %all-gather.33.cloned.1.call-start = ((), (), s32[]{:S(2)}) async-start(), calls=%async_computation.29 | async-start | bytes 5242880 | tf_op jit(solution)/shard_map/all_gather | solution.py:24
  924.5 113.9 %all-gather.45.cloned.1.call-start = ((), (), s32[]{:S(2)}) async-start(), calls=%async_computation.46 | async-start | bytes 5242880 | tf_op jit(solution)/shard_map/all_gather | solution.py:34
  925.6 178.5 %reduce-scatter.29.cloned.1.call-start = ((), (), s32[]{:S(2)}) async-start(), calls=%async_computation.31 | async-start | bytes 5242880 | tf_op jit(solution)/shard_map/reduce_scatter | solution.py:38
  985.5 52.9 %copy-start.115 = (bf16[1,1024,1024]{2,1,0:T(8,128)(2,1)S(1)}, bf16[1,1024,1024]{2,1,0:T(8,128)(2,1)}, u32[]{:S(2)}) copy-start(bf16[1,1024,1024]{2,1,0:T(8,128)(2,1)} %all-gather.25.cloned.1.call-done) | copy-start | bytes 6291460
  1059.2 89.2 %all-gather.35.cloned.1.call-start = ((), (), s32[]{:S(2)}) async-start(), calls=%async_computation.32 | async-start | bytes 5242880 | tf_op jit(solution)/shard_map/all_gather | solution.py:34
  1113.7 464.5 %reduce-scatter.31.cloned.1.call-start = ((), (), s32[]{:S(2)}) async-start(), calls=%async_computation.33 | async-start | bytes 5242880 | tf_op jit(solution)/shard_map/reduce_scatter | solution.py:38
  1528.4 49.8 %copy-start.71 = (f32[1,1024]{1,0:T(1,128)S(1)}, f32[1,1024]{1,0:T(1,128)}, u32[]{:S(2)}) copy-start(f32[1,1024]{1,0:T(1,128)} %param.24) | copy-start | bytes 12292
  1533.5 50.8 %copy-start.17 = (f32[512,1024]{1,0:T(8,128)S(1)}, f32[512,1024]{1,0:T(8,128)}, u32[]{:S(2)}) copy-start(f32[512,1024]{1,0:T(8,128)} %copy-done.16) | copy-start | bytes 6291460
  1533.5 50.8 %copy-start.99 = (f32[512]{0:T(512)S(1)}, f32[512]{0:T(512)}, u32[]{:S(2)}) copy-start(f32[512]{0:T(512)} %copy-done.98) | copy-start | bytes 6148
  1533.6 116.5 %all-gather.37.cloned.1.call-start = ((), (), s32[]{:S(2)}) async-start(), calls=%async_computation.34 | async-start | bytes 5242880 | tf_op jit(solution)/shard_map/all_gather | solution.py:34
  1587.1 75.8 %copy-start.42 = (bf16[512,1024]{1,0:T(8,128)(2,1)}, bf16[512,1024]{1,0:T(8,128)(2,1)S(1)}, u32[]{:S(2)}) copy-start(bf16[512,1024]{1,0:T(8,128)(2,1)S(1)} %add_convert_fusion.5) | copy-start | bytes 3145732
  1587.1 26.8 collective-permute-start.2
  1616.3 99.6 %reduce-scatter.33.cloned.1.call-start = ((), (), s32[]{:S(2)}) async-start(), calls=%async_computation.35 | async-start | bytes 5242880 | tf_op jit(solution)/shard_map/reduce_scatter | solution.py:38
  1664.9 51.1 %copy-start.86 = (f32[1,1024]{1,0:T(1,128)S(1)}, f32[1,1024]{1,0:T(1,128)}, u32[]{:S(2)}) copy-start(f32[1,1024]{1,0:T(1,128)} %param.27) | copy-start | bytes 12292
  1664.9 51.1 %copy-start.93 = (f32[512]{0:T(512)S(1)}, f32[512]{0:T(512)}, u32[]{:S(2)}) copy-start(f32[512]{0:T(512)} %copy-done.92) | copy-start | bytes 6148
  1671.3 52.9 %copy-start.26 = (bf16[512,1024]{1,0:T(8,128)(2,1)S(1)}, bf16[512,1024]{1,0:T(8,128)(2,1)}, u32[]{:S(2)}) copy-start(bf16[512,1024]{1,0:T(8,128)(2,1)} %bitcast_select_fusion.1) | copy-start | bytes 3145732
  1671.3 88.9 %all-gather.39.cloned.1.call-start = ((), (), s32[]{:S(2)}) async-start(), calls=%async_computation.36 | async-start | bytes 5242880 | tf_op jit(solution)/shard_map/all_gather | solution.py:34
  1671.4 54.2 %copy-start.94 = (f32[512]{0:T(512)}, f32[512]{0:T(512)S(1)}, u32[]{:S(2)}) copy-start(f32[512]{0:T(512)S(1)} %broadcast_multiply_fusion.1) | copy-start | bytes 6148
  1725.5 466.9 %reduce-scatter.35.cloned.1.call-start = ((), (), s32[]{:S(2)}) async-start(), calls=%async_computation.37 | async-start | bytes 5242880 | tf_op jit(solution)/shard_map/reduce_scatter | solution.py:38
  2142.5 49.9 %copy-start.72 = (f32[1,1024]{1,0:T(1,128)S(1)}, f32[1,1024]{1,0:T(1,128)}, u32[]{:S(2)}) copy-start(f32[1,1024]{1,0:T(1,128)} %param.24) | copy-start | bytes 12292
  2147.6 50.8 %copy-start.21 = (f32[512,1024]{1,0:T(8,128)S(1)}, f32[512,1024]{1,0:T(8,128)}, u32[]{:S(2)}) copy-start(f32[512,1024]{1,0:T(8,128)} %copy-done.20) | copy-start | bytes 6291460
  2147.6 50.8 %copy-start.27 = (bf16[512,1024]{1,0:T(8,128)(2,1)S(1)}, bf16[512,1024]{1,0:T(8,128)(2,1)}, u32[]{:S(2)}) copy-start(bf16[512,1024]{1,0:T(8,128)(2,1)} %bitcast_select_fusion.1) | copy-start | bytes 3145732
  2147.6 50.8 %copy-start.101 = (f32[512]{0:T(512)S(1)}, f32[512]{0:T(512)}, u32[]{:S(2)}) copy-start(f32[512]{0:T(512)} %copy-done.100) | copy-start | bytes 6148
  2147.7 117.1 %all-gather.41.cloned.1.call-start = ((), (), s32[]{:S(2)}) async-start(), calls=%async_computation.38 | async-start | bytes 5242880 | tf_op jit(solution)/shard_map/all_gather | solution.py:34
  2201.7 27.0 collective-permute-start.3
  2231.0 99.7 %reduce-scatter.37.cloned.1.call-start = ((), (), s32[]{:S(2)}) async-start(), calls=%async_computation.39 | async-start | bytes 5242880 | tf_op jit(solution)/shard_map/reduce_scatter | solution.py:38
  2279.7 51.1 %copy-start.87 = (f32[1,1024]{1,0:T(1,128)S(1)}, f32[1,1024]{1,0:T(1,128)}, u32[]{:S(2)}) copy-start(f32[1,1024]{1,0:T(1,128)} %param.27) | copy-start | bytes 12292
  2279.7 51.1 %copy-start.95 = (f32[512]{0:T(512)S(1)}, f32[512]{0:T(512)}, u32[]{:S(2)}) copy-start(f32[512]{0:T(512)} %copy-done.94) | copy-start | bytes 6148
  2286.1 52.0 %copy-start.24 = (bf16[512,1024]{1,0:T(8,128)(2,1)S(1)}, bf16[512,1024]{1,0:T(8,128)(2,1)}, u32[]{:S(2)}) copy-start(bf16[512,1024]{1,0:T(8,128)(2,1)} %bitcast_select_fusion) | copy-start | bytes 3145732
  2286.1 53.4 %copy-start.116 = (bf16[1,1024,1024]{2,1,0:T(8,128)(2,1)S(1)}, bf16[1,1024,1024]{2,1,0:T(8,128)(2,1)}, u32[]{:S(2)}) copy-start(bf16[1,1024,1024]{2,1,0:T(8,128)(2,1)} %all-gather.25.cloned.1.call-done) | copy-start | bytes 6291460
  2286.1 204.8 %all-gather.43.cloned.1.call-start = ((), (), s32[]{:S(2)}) async-start(), calls=%async_computation.40 | async-start | bytes 5242880 | tf_op jit(solution)/shard_map/all_gather | solution.py:34
  2339.4 552.9 %reduce-scatter.27.cloned.1.call-start = ((), (), s32[]{:S(2)}) async-start(), calls=%async_computation.30 | async-start | bytes 5242880 | tf_op jit(solution)/shard_map/reduce_scatter | solution.py:28
  2363.1 535.4 %reduce-scatter.47.cloned.1.call-start = ((), (), s32[]{:S(2)}) async-start(), calls=%async_computation.45 | async-start | bytes 2621440 | tf_op jit(solution)/shard_map/reduce_scatter | solution.py:276
  2463.8 436.7 %reduce-scatter.45.cloned.1.call-start = ((), (), s32[]{:S(2)}) async-start(), calls=%async_computation.44 | async-start | bytes 2621440 | tf_op jit(solution)/shard_map/reduce_scatter | solution.py:273
  2490.8 411.9 %reduce-scatter.43.cloned.1.call-start = ((), (), s32[]{:S(2)}) async-start(), calls=%async_computation.43 | async-start | bytes 655360 | tf_op jit(solution)/shard_map/reduce_scatter | solution.py:270
  2876.7 57.8 %reduce-scatter.41.cloned.1.call-start = ((), (), s32[]{:S(2)}) async-start(), calls=%async_computation.42 | async-start | bytes 1966080 | tf_op jit(solution)/shard_map/reduce_scatter | solution.py:267
  2884.6 96.1 %reduce-scatter.39.cloned.1.call-start = ((), (), s32[]{:S(2)}) async-start(), calls=%async_computation.41 | async-start | bytes 5242880 | tf_op jit(solution)/shard_map/reduce_scatter | solution.py:38
  2892.3 88.4 %copy-start.73 = (f32[1,1024]{1,0:T(1,128)S(1)}, f32[1,1024]{1,0:T(1,128)}, u32[]{:S(2)}) copy-start(f32[1,1024]{1,0:T(1,128)} %param.24) | copy-start | bytes 12292
  2894.2 92.0 %copy-start.104 = (f32[1024]{0:T(1024)S(1)}, f32[1024]{0:T(1024)}, u32[]{:S(2)}) copy-start(f32[1024]{0:T(1024)} %get-tuple-element.439) | copy-start | bytes 12292
  2894.2 92.0 %copy-start.105 = (f32[1024]{0:T(1024)S(1)}, f32[1024]{0:T(1024)}, u32[]{:S(2)}) copy-start(f32[1024]{0:T(1024)} %get-tuple-element.437) | copy-start | bytes 12292
  2894.2 125.3 %copy-start.19 = (f32[512,1024]{1,0:T(8,128)S(1)}, f32[512,1024]{1,0:T(8,128)}, u32[]{:S(2)}) copy-start(f32[512,1024]{1,0:T(8,128)} %copy-done.18) | copy-start | bytes 6291460
  2894.3 125.3 %copy-start.25 = (bf16[512,1024]{1,0:T(8,128)(2,1)S(1)}, bf16[512,1024]{1,0:T(8,128)(2,1)}, u32[]{:S(2)}) copy-start(bf16[512,1024]{1,0:T(8,128)(2,1)} %bitcast_select_fusion) | copy-start | bytes 3145732
  2894.3 125.3 %copy-start.97 = (f32[512]{0:T(512)S(1)}, f32[512]{0:T(512)}, u32[]{:S(2)}) copy-start(f32[512]{0:T(512)} %copy-done.96) | copy-start | bytes 6148
  (129 other events, 1459.4 us)
Sparse Core Ops, SparseCore 0:
  10.1 46.4 all-gather.18
  58.8 34.8 all-gather.16
  172.7 44.4 reduce-scatter.16
  219.3 45.9 all-gather.22
  267.3 33.1 all-gather.20
  302.6 46.2 all-gather.24
  373.6 42.7 reduce-scatter.18
  448.1 35.4 all-gather.26
  562.1 44.4 reduce-scatter.20
  613.9 34.4 all-gather.28
  681.7 44.4 reduce-scatter.22
  758.2 35.4 all-gather.30
  872.7 44.4 reduce-scatter.24
  924.6 34.4 all-gather.32
  960.6 34.4 all-gather.44
  1059.3 44.8 reduce-scatter.28
  1113.8 34.4 all-gather.34
  1533.7 44.4 reduce-scatter.30
  1616.5 33.5 all-gather.36
  1671.4 44.5 reduce-scatter.32
  1725.6 34.5 all-gather.38
  2147.8 44.4 reduce-scatter.34
  2231.2 33.5 all-gather.40
  2286.2 44.5 reduce-scatter.36
  2339.5 34.5 all-gather.42
  2376.5 44.4 reduce-scatter.26
  2463.9 43.8 reduce-scatter.46
  2510.1 43.1 reduce-scatter.44
  2876.8 21.7 reduce-scatter.42
  2900.9 33.5 reduce-scatter.40
  2937.2 43.4 reduce-scatter.38
where the time goes:
time: 3050 us; the launch traced here: 3030 us
  matrix products  1450 us (48%)
  waiting for transfers between devices  1020 us (33%)
  other arithmetic  311 us (10%)
  local copies, waits for them, and re-layouts  109 us (4%)
  blocking collectives  58.8 us (2%)
  loops' own time  47.3 us (2%)
    dot_general x12, matrix products, one_block(): jnp.einsum('hqk,hqd->hkd', d_raw, query_block, preferred_element_type=jnp...  409 us
    dot_general x12, matrix products, one_block(): jnp.einsum('hqk,hkd->hqd', d_raw, key_rows, preferred_element_type=jnp.fl...  374 us
    reduce_scatter x6, waiting for transfers between devices, collect_grads(): lax.psum_scatter(source.astype(jnp.bfloat16), 'tensor', scatter_dimension...  257 us
    reduce_scatter x6, waiting for transfers between devices, collect_rows(): lax.psum_scatter(source.astype(jnp.bfloat16), 'tensor', scatter_dimension...  220 us
    all_gather x6, waiting for transfers between devices, spread_rows(): return lax.all_gather(source, 'tensor', axis=0, tiled=True)  211 us
    all_gather x6, waiting for transfers between devices, spread_grads(): return lax.all_gather(source, 'tensor', axis=0, tiled=True)  120 us
    dot_general x12, matrix products, one_block(): jnp.einsum('hqk,hqd->hkd', attn_probs.astype(jnp.bfloat16), d_ctx_block,...  114 us
    dot_general x12, matrix products, one_block(): jnp.einsum('hqd,hkd->hqk', d_ctx_block, value_rows, preferred_element_typ...  111 us
  transfers between devices with their start and end apart: 35, of which 29 were waited for; matrix products, arithmetic and copies ran while one was open for 22% of the time, Pallas kernels for 0%

commit v1 on v0

v1 whole, which is shorter than its diff:
```python
import functools
import math

import jax
import jax.numpy as jnp
from jax import lax
from jax.experimental import pallas as pl
from jax.experimental.pallas import tpu as pltpu
from jax.sharding import PartitionSpec as P

F32 = jnp.float32
BF = jnp.bfloat16
NT = (((1,), (1,)), ((), ()))
NN = (((1,), (0,)), ((), ()))
MASKED = -1e30
SCENES = 3


def dg(a, b, dims):
    return lax.dot_general(a, b, dims, preferred_element_type=F32)


def query_block(length):
    return 512 if length % 512 == 0 else length


def attend_kernel(bq, kc, qkv_ref, qm_ref, km_ref, ctx_ref, lse_ref, ka, vt):
    heads, length, width = qkv_ref.shape
    e = width // 3
    c = e**-0.5 * math.log2(math.e)
    for h in range(heads):
        ka[h, :, :e] = qkv_ref[h, :, e : 2 * e]
        ka[h, :, e:] = km_ref[...]
        vt[h, :e, :] = qkv_ref[h, :, 2 * e :].T
        vt[h, e:, :] = jnp.ones((16, length), BF)

    def body(i, _):
        rows = pl.ds(pl.multiple_of(i * bq, bq), bq)
        for h in range(heads):
            q = jnp.concatenate([qkv_ref[h, rows, :e], qm_ref[rows, :]], axis=1)
            parts = []
            top = None
            for k in range(length // kc):
                s = dg(ka[h, k * kc : (k + 1) * kc, :], q, NT)
                t = jnp.max(s, axis=0, keepdims=True)
                top = t if top is None else jnp.maximum(top, t)
                parts.append(s)
            top = top * c
            acc = None
            for k in range(length // kc):
                p = jnp.exp2(parts[k] * c - top).astype(BF)
                a = dg(vt[h, :, k * kc : (k + 1) * kc], p, NN)
                acc = a if acc is None else acc + a
            total = acc[e : e + 1]
            ctx_ref[h, rows, :] = (acc[:e] * (1.0 / total)).T.astype(BF)
            lse_ref[h, 0:1, rows] = top + jnp.log2(total)
        return 0

    lax.fori_loop(0, length // bq, body, 0)


def attend(qkv, qm, km):
    heads, length, width = qkv.shape
    e = width // 3
    vm = pl.BlockSpec(memory_space=pltpu.VMEM)
    bq = query_block(length)
    return pl.pallas_call(
        functools.partial(attend_kernel, bq, bq),
        out_shape=(
            jax.ShapeDtypeStruct((heads, length, e), BF),
            jax.ShapeDtypeStruct((heads, 1, length), F32),
        ),
        in_specs=[vm] * 3,
        out_specs=(vm, vm),
        scratch_shapes=[
            pltpu.VMEM((heads, length, 2 * e), BF),
            pltpu.VMEM((heads, e + 16, length), BF),
        ],
        compiler_params=pltpu.CompilerParams(vmem_limit_bytes=56 << 20),
        cost_estimate=pl.CostEstimate(
            flops=16 * heads * length * length * e,
            bytes_accessed=8 * heads * length * e,
            transcendentals=heads * length * length,
        ),
    )(qkv, qm, km)


def attend_back_kernel(
    bq, kc, qkv_ref, qm_ref, km_ref, ctx_ref, lse_ref, dctx_ref, dqkv_ref, ka, va, kt, dk, dv
):
    heads, length, width = qkv_ref.shape
    e = width // 3
    scale = e**-0.5
    c = scale * math.log2(math.e)
    lane = lax.broadcasted_iota(jnp.int32, (length, e), 1)
    for h in range(heads):
        ka[h, :, :e] = qkv_ref[h, :, e : 2 * e]
        ka[h, :, e:] = km_ref[...]
        va[h, :, :e] = qkv_ref[h, :, 2 * e :]
        va[h, :, e:] = jnp.where(lane < 3, 1.0, 0.0).astype(BF)
        kt[h] = qkv_ref[h, :, e : 2 * e].T
    dk[...] = jnp.zeros_like(dk)
    dv[...] = jnp.zeros_like(dv)
    ql = lax.broadcasted_iota(jnp.int32, (bq, e), 1)

    def body(i, _):
        rows = pl.ds(pl.multiple_of(i * bq, bq), bq)
        for h in range(heads):
            qq = qkv_ref[h, rows, :e]
            q = jnp.concatenate([qq, qm_ref[rows, :]], axis=1)
            dc = dctx_ref[h, rows, :]
            d = -jnp.sum(dc.astype(F32) * ctx_ref[h, rows, :].astype(F32), axis=1, keepdims=True)
            d1 = d.astype(BF).astype(F32)
            d2 = (d - d1).astype(BF).astype(F32)
            d3 = d - d1 - d2
            da = jnp.where(ql == 0, d1, jnp.where(ql == 1, d2, jnp.where(ql == 2, d3, 0.0)))
            dca = jnp.concatenate([dc, da.astype(BF)], axis=1)
            lse = lse_ref[h, 0:1, rows]
            dqt = None
            for k in range(length // kc):
                ks = slice(k * kc, (k + 1) * kc)
                s = dg(ka[h, ks, :], q, NT)
                p = jnp.exp2(s * c - lse)
                ds = (p * dg(va[h, ks, :], dca, NT)).astype(BF)
                dv[h, ks, :] += dg(p.astype(BF), dc, NN)
                dk[h, ks, :] += dg(ds, qq, NN)
                a = dg(kt[h, :, ks], ds, NN)
                dqt = a if dqt is None else dqt + a
            dqkv_ref[h, rows, :e] = (dqt * scale).T.astype(BF)
        return 0

    lax.fori_loop(0, length // bq, body, 0)
    for h in range(heads):
        dqkv_ref[h, :, e : 2 * e] = (dk[h] * scale).astype(BF)
        dqkv_ref[h, :, 2 * e :] = dv[h].astype(BF)


def attend_back(qkv, qm, km, ctx, lse, dctx):
    heads, length, width = qkv.shape
    e = width // 3
    vm = pl.BlockSpec(memory_space=pltpu.VMEM)
    bq = query_block(length)
    return pl.pallas_call(
        functools.partial(attend_back_kernel, bq, bq),
        out_shape=jax.ShapeDtypeStruct((heads, length, width), BF),
        in_specs=[vm] * 6,
        out_specs=vm,
        scratch_shapes=[
            pltpu.VMEM((heads, length, 2 * e), BF),
            pltpu.VMEM((heads, length, 2 * e), BF),
            pltpu.VMEM((heads, e, length), BF),
            pltpu.VMEM((heads, length, e), F32),
            pltpu.VMEM((heads, length, e), F32),
        ],
        compiler_params=pltpu.CompilerParams(vmem_limit_bytes=60 << 20),
        cost_estimate=pl.CostEstimate(
            flops=40 * heads * length * length * e,
            bytes_accessed=20 * heads * length * e,
            transcendentals=heads * length * length,
        ),
    )(qkv, qm, km, ctx, lse, dctx)


def scene_masks(segments, e):
    same = (segments[:, None] == jnp.arange(e, dtype=jnp.int32)[None]).astype(F32)
    used = jnp.arange(e)[None] < SCENES
    return (
        jnp.where(used, same * MASKED, 0.0).astype(BF),
        jnp.where(used, 1.0 - same, 0.0).astype(BF),
    )


def norm_stats(source):
    center = source - jnp.mean(source, axis=-1, keepdims=True)
    r = lax.rsqrt(jnp.mean(center * center, axis=-1, keepdims=True) + 1e-05)
    return center * r, r


def norm_back(source, gain, grad):
    n, r = norm_stats(source)
    e = grad * gain
    dh = r * (
        e - jnp.mean(e, axis=-1, keepdims=True) - n * jnp.mean(e * n, axis=-1, keepdims=True)
    )
    return dh, jnp.sum(grad * n, axis=0)


def spread(source):
    return lax.all_gather(source, "tensor", axis=0, tiled=True)


def collect(source):
    return lax.psum_scatter(
        source.astype(BF), "tensor", scatter_dimension=0, tiled=True
    ).astype(F32)


def ein(spec, a, b):
    return jnp.einsum(spec, a, b, preferred_element_type=F32)


def swap_section(value):
    return lax.ppermute(value, "section", [(0, 1), (1, 0)])


def shards(
    block_input,
    segment_ids,
    cotangent,
    norm_one_gain,
    qkv_weight,
    out_weight,
    norm_two_gain,
    up_weight,
    down_weight,
):
    section = lax.axis_index("section")
    layers = lax.axis_size("section")

    def gather_weight(w, axis):
        got = lax.all_gather(w[0].astype(BF), ("section", "dp"), axis=0, tiled=False)
        return got.reshape((layers, -1) + got.shape[1:])

    def join(w, axis):
        return jnp.concatenate([w[i] for i in range(w.shape[0])], axis=axis)

    w_qkv = gather_weight(qkv_weight, 0)
    w_out = gather_weight(out_weight, 2)
    w_up = gather_weight(up_weight, 0)
    w_down = gather_weight(down_weight, 1)
    gains_one = lax.all_gather(norm_one_gain[0], "section", axis=0, tiled=False)
    gains_two = lax.all_gather(norm_two_gain[0], "section", axis=0, tiled=False)
    segments = lax.dynamic_index_in_dim(segment_ids, section, 0, keepdims=False)
    x = lax.dynamic_index_in_dim(block_input, section, 0, keepdims=False)
    head_dim = qkv_weight.shape[3] // 3
    qm, km = scene_masks(segments, head_dim)
    kept = []
    ys = []
    for layer in range(2):
        wq = join(w_qkv[layer], 0)
        wo = join(w_out[layer], 2)
        wu = join(w_up[layer], 0)
        wd = join(w_down[layer], 1)
        g1, g2 = gains_one[layer], gains_two[layer]
        resid = x.astype(F32)
        a1 = spread((norm_stats(resid)[0] * g1).astype(BF))
        qkv = ein("sd,dhe->hse", a1, wq).astype(BF)
        ctx, lse = attend(qkv, qm, km)
        h1 = resid + collect(ein("hse,hed->sd", ctx, wo))
        a2 = spread((norm_stats(h1)[0] * g2).astype(BF))
        up = jnp.dot(a2, wu, preferred_element_type=F32)
        half = 0.5 * (1.0 + lax.erf(up * (0.5**0.5)))
        slope = (half + up * jnp.exp(-0.5 * up * up) * ((2 * math.pi) ** -0.5)).astype(BF)
        hidden = (up * half).astype(BF)
        x = (h1 + collect(jnp.dot(hidden, wd, preferred_element_type=F32))).astype(BF)
        ys.append(x)
        kept.append((wq, wo, wu, wd, g1, g2, resid, a1, qkv, ctx, lse, h1, a2, slope, hidden))
    other_y = swap_section(jnp.where(section == 0, ys[1], ys[0]))
    grad = lax.dynamic_index_in_dim(cotangent, section, 0, keepdims=False)
    dxs = [None, None]
    gain_sums = [None, None]
    sums = [None, None]

    def reduce_rows(value, axis):
        return lax.psum_scatter(value.astype(BF), "dp", scatter_dimension=axis, tiled=True)

    for layer in (1, 0):
        wq, wo, wu, wd, g1, g2, resid, a1, qkv, ctx, lse, h1, a2, slope, hidden = kept[layer]
        grad_in = grad.astype(F32)
        g_low = spread(grad)
        d_down = ein("sf,sd->fd", hidden, g_low)
        d_up = (ein("sd,fd->sf", g_low, wd) * slope.astype(F32)).astype(BF)
        g_up = ein("sd,sf->df", a2, d_up)
        dh, gain_two = norm_back(h1, g2, collect(ein("sf,df->sd", d_up, wu)))
        d_mid = dh + grad_in
        d_attn = spread(d_mid.astype(BF))
        g_out = ein("hse,sd->hed", ctx, d_attn)
        d_ctx = ein("sd,hed->hse", d_attn, wo).astype(BF)
        d_qkv = attend_back(qkv, qm, km, ctx, lse, d_ctx)
        g_qkv = ein("sd,hse->dhe", a1, d_qkv)
        dh, gain_one = norm_back(resid, g1, collect(ein("hse,dhe->sd", d_qkv, wq)))
        grad = (dh + d_mid).astype(BF)
        dxs[layer] = grad
        gain_sums[layer] = (gain_one, gain_two)
        sums[layer] = (
            reduce_rows(g_qkv, 0),
            reduce_rows(g_out, 2),
            reduce_rows(g_up, 0),
            reduce_rows(d_down, 1),
        )
    other_dx = swap_section(jnp.where(section == 0, dxs[1], dxs[0]))

    def own_layer(mine, other):
        first = jnp.where(section == 0, mine, other)
        second = jnp.where(section == 0, other, mine)
        return jnp.stack([first, second])[None]

    layer_out = own_layer(jnp.where(section == 0, ys[0], ys[1]), other_y)
    input_out = own_layer(jnp.where(section == 0, dxs[0], dxs[1]), other_dx)

    def finish(zero, one):
        send = swap_section(jnp.where(section == 0, one, zero))
        return (jnp.where(section == 0, zero, one).astype(F32) + send.astype(F32))[None]

    qkv_grad, out_grad, up_grad, down_grad = [finish(a, b) for a, b in zip(sums[0], sums[1])]
    gains = lax.psum(
        jnp.stack([jnp.stack(gain_sums[0]), jnp.stack(gain_sums[1])]), ("section", "dp", "tensor")
    )
    gains = lax.dynamic_index_in_dim(gains, section, 0, keepdims=False)
    return (
        layer_out,
        input_out,
        gains[0][None],
        qkv_grad,
        out_grad,
        gains[1][None],
        up_grad,
        down_grad,
    )


def solution(mesh):
    return jax.shard_map(
        shards,
        mesh=mesh,
        in_specs=(
            P(None, ("dp", "tensor"), None),
            P(None, "dp"),
            P(None, ("dp", "tensor"), None),
            P("section", None),
            P("section", "dp", "tensor", None),
            P("section", "tensor", None, "dp"),
            P("section", None),
            P("section", "dp", "tensor"),
            P("section", "tensor", "dp"),
        ),
        out_specs=(
            P("section", None, ("dp", "tensor"), None),
            P("section", None, ("dp", "tensor"), None),
            P("section", None),
            P("section", "dp", "tensor", None),
            P("section", "tensor", None, "dp"),
            P("section", None),
            P("section", "dp", "tensor"),
            P("section", "tensor", "dp"),
        ),
        check_vma=False,
    )
```

time: 3050 us -> 1560 us (0.51)
  matrix products: 1450 us -> 184 us
  other arithmetic: 311 us -> 74.4 us
  Pallas kernels: 0 us -> 179 us
  waiting for transfers between devices: 1020 us -> 964 us
  local copies, waits for them, and re-layouts: 109 us -> 57 us
  loops' own time: 47.3 us -> 0 us
    dot_general x114 -> x22, matrix products: 1410 us -> 171 us  [the longest x18 134 us: ein(): return jnp.einsum(spec, a, b, preferred_element_type=F32)]
    pallas_call x0 -> x4, Pallas kernels: none -> 179 us  [the longest x2 112 us: attend_back(): pl.pallas_call(functools.partial(attend_back_kernel, bq, bq), out_shape=j...]
    another operation x24 -> x5, other arithmetic: 125 us -> 4.73 us  [the longest x2 4.12 us: own_layer(): return jnp.stack([first, second])[None]]
    reduce_sum x35 -> x12, other arithmetic: 101 us -> 18.8 us  [the longest x4 11.4 us: norm_back(): return (dh, jnp.sum(grad * n, axis=0))]
    ppermute x4 -> x6, waiting for transfers between devices: 95.7 us -> 23.8 us  [swap_section(): return lax.ppermute(value, 'section', [(0, 1), (1, 0)])]
    another operation x6 -> x0, loops' own time: 47.3 us -> none  [the longest x3 23.9 us: attend(): context, logsum = lax.map(one_block, starts)]
    all_gather x15 -> x12, waiting for transfers between devices: 422 us -> 459 us  [the longest x4 235 us: gather_weight(): lax.all_gather(w[0].astype(BF), ('section', 'dp'), axis=0, tiled=False)]
  transfers between devices with their start and end apart: 35 -> 34, of which waited for: 29 -> 25; matrix products, arithmetic and copies ran while one was open for 22% -> 11% of each run, Pallas kernels for 0% -> 4%
where the time goes in v1:
time: 1560 us; the launch traced here: 1550 us
  waiting for transfers between devices  964 us (62%)
  matrix products  184 us (12%)
  Pallas kernels  179 us (11%)
  other arithmetic  74.4 us (5%)
  blocking collectives  62.5 us (4%)
  local copies, waits for them, and re-layouts  57 us (4%)
  between operations  15.8 us (1%)
    reduce_scatter x8, waiting for transfers between devices, collect(): lax.psum_scatter(source.astype(BF), 'tensor', scatter_dimension=0, tiled=...  302 us
    all_gather x4, waiting for transfers between devices, gather_weight(): lax.all_gather(w[0].astype(BF), ('section', 'dp'), axis=0, tiled=False)  235 us
    all_gather x8, waiting for transfers between devices, spread(): return lax.all_gather(source, 'tensor', axis=0, tiled=True)  224 us
    reduce_scatter x8, waiting for transfers between devices, reduce_rows(): lax.psum_scatter(value.astype(BF), 'dp', scatter_dimension=axis, tiled=True)  179 us
    dot_general x18, matrix products, ein(): return jnp.einsum(spec, a, b, preferred_element_type=F32)  134 us
    pallas_call x2, Pallas kernels, attend_back(): pl.pallas_call(functools.partial(attend_back_kernel, bq, bq), out_shape=j...  112 us
    pallas_call x2, Pallas kernels, attend(): pl.pallas_call(functools.partial(attend_kernel, bq, bq), out_shape=(jax.S...  67.4 us
    psum x1, blocking collectives, shards(): lax.psum(jnp.stack([jnp.stack(gain_sums[0]), jnp.stack(gain_sums[1])]), (...  52.9 us
  transfers between devices with their start and end apart: 34, of which 25 were waited for; matrix products, arithmetic and copies ran while one was open for 11% of the time, Pallas kernels for 4%

profile of v1, /device:TPU:0, one launch (start us, length us, event | category | flops | bytes accessed | tf_op | source)
XLA Modules:
  0.0 1548.0 jit_solution(6316937797636054230)
XLA Ops:
  11.1 5.3 all-gather.1
  20.9 32.7 %all-gather.20.cloned.1.call-done = bf16[8,4,64,256]{3,2,1,0:T(8,128)(2,1)} async-done(((bf16[1,4,64,256]{3,2,1,0:T(8,128)(2,1)}), bf16[8,4,64,256]{3,2,1,0:T(8,128)(2,1)}) %all-gather.20.cloned.1.call-update) | async-done | bytes 1048592 | tf_op jit(solution)/shard_map/all_gather | solution.py:221
  55.8 59.7 %all-gather.16.cloned.1.call-done = bf16[8,256,4,192]{1,3,2,0:T(8,128)(2,1)} async-done(((bf16[1,256,4,192]{1,3,2,0:T(8,128)(2,1)}), bf16[8,256,4,192]{1,3,2,0:T(8,128)(2,1)}) %all-gather.16.cloned.1.call-update) | async-done | bytes 3145744 | tf_op jit(solution)/shard_map/all_gather | solution.py:221
  118.7 32.1 %all-gather.18.cloned.1.call-done = bf16[2048,1024]{1,0:T(8,128)(2,1)} async-done(((bf16[512,1024]{1,0:T(8,128)(2,1)}), bf16[2048,1024]{1,0:T(8,128)(2,1)}) %all-gather.18.cloned.1.call-update) | async-done | bytes 4194320 | tf_op jit(solution)/shard_map/all_gather | solution.py:189
  150.8 7.4 fusion.25
  158.2 6.0 copy.41
  164.2 33.8 %shard_map.152 = (bf16[4,2048,64]{2,1,0:T(8,128)(2,1)}, f32[4,1,2048]{2,1,0:T(1,128)}) custom-call(bf16[4,2048,192]{2,1,0:T(8,128)(2,1)} %bitcast.243, bf16[2048,64]{1,0:T(8,128)(2,1)} %get-tuple-element.71.qm_ref, bf16[2048,64]{1,0:T(8,128)(2,1)} %get-tuple-element.70.km_ref), custom_call_target="tpu_custom_call" | custom-call | flops 17179869184 | bytes 4194304 | tf_op jit(solution)/shard_map/pallas_call | solution.py:67
  198.1 5.0 bitcast_convert_fusion.3
  207.4 4.3 all-gather.2
  211.7 36.0 %reduce-scatter.17.cloned.1.call-done = bf16[512,1024]{1,0:T(8,128)(2,1)} async-done(((bf16[2048,1024]{1,0:T(8,128)(2,1)}), bf16[512,1024]{1,0:T(8,128)(2,1)}) %reduce-scatter.17.cloned.1.call-update) | async-done | bytes 1048592 | tf_op jit(solution)/shard_map/reduce_scatter | solution.py:193
  251.5 72.4 %all-gather.24.cloned.1.call-done = bf16[8,256,1024]{2,1,0:T(8,128)(2,1)} async-done(((bf16[1,256,1024]{2,1,0:T(8,128)(2,1)}), bf16[8,256,1024]{2,1,0:T(8,128)(2,1)}) %all-gather.24.cloned.1.call-update) | async-done | bytes 4194320 | tf_op jit(solution)/shard_map/all_gather | solution.py:221
  323.9 4.0 slice_bitcast_fusion.7
  328.0 70.4 %all-gather.26.cloned.1.call-done = bf16[8,1024,256]{2,1,0:T(8,128)(2,1)} async-done(((bf16[1,1024,256]{2,1,0:T(8,128)(2,1)}), bf16[8,1024,256]{2,1,0:T(8,128)(2,1)}) %all-gather.26.cloned.1.call-update) | async-done | bytes 4194320 | tf_op jit(solution)/shard_map/all_gather | solution.py:221
  398.4 4.3 slice_bitcast_fusion.3
  402.7 30.7 %all-gather.22.cloned.1.call-done = bf16[2048,1024]{1,0:T(8,128)(2,1)} async-done(((bf16[512,1024]{1,0:T(8,128)(2,1)}), bf16[2048,1024]{1,0:T(8,128)(2,1)}) %all-gather.22.cloned.1.call-update) | async-done | bytes 4194320 | tf_op jit(solution)/shard_map/all_gather | solution.py:189
  433.4 10.1 multiply_convert_fusion.3
  445.5 6.6 convolution_convert_fusion.3
  452.2 44.6 %reduce-scatter.19.cloned.1.call-done = bf16[512,1024]{1,0:T(8,128)(2,1)} async-done(((bf16[2048,1024]{1,0:T(8,128)(2,1)}), bf16[512,1024]{1,0:T(8,128)(2,1)}) %reduce-scatter.19.cloned.1.call-update) | async-done | bytes 1048592 | tf_op jit(solution)/shard_map/reduce_scatter | solution.py:193
  500.8 34.6 %all-gather.28.cloned.1.call-done = bf16[2048,1024]{1,0:T(8,128)(2,1)} async-done(((bf16[512,1024]{1,0:T(8,128)(2,1)}), bf16[2048,1024]{1,0:T(8,128)(2,1)}) %all-gather.28.cloned.1.call-update) | async-done | bytes 4194320 | tf_op jit(solution)/shard_map/all_gather | solution.py:189
  535.4 7.5 fusion.28
  542.9 6.0 copy.43
  548.9 33.6 %shard_map.153 = (bf16[4,2048,64]{2,1,0:T(8,128)(2,1)}, f32[4,1,2048]{2,1,0:T(1,128)}) custom-call(bf16[4,2048,192]{2,1,0:T(8,128)(2,1)} %bitcast.245, bf16[2048,64]{1,0:T(8,128)(2,1)} %get-tuple-element.71.qm_ref, bf16[2048,64]{1,0:T(8,128)(2,1)} %get-tuple-element.70.km_ref), custom_call_target="tpu_custom_call" | custom-call | flops 17179869184 | bytes 4194304 | tf_op jit(solution)/shard_map/pallas_call | solution.py:67
  582.6 5.0 bitcast_convert_fusion.2
  587.8 44.4 %reduce-scatter.21.cloned.1.call-done = bf16[512,1024]{1,0:T(8,128)(2,1)} async-done(((bf16[2048,1024]{1,0:T(8,128)(2,1)}), bf16[512,1024]{1,0:T(8,128)(2,1)}) %reduce-scatter.21.cloned.1.call-update) | async-done | bytes 1048592 | tf_op jit(solution)/shard_map/reduce_scatter | solution.py:193
  638.2 32.2 %all-gather.30.cloned.1.call-done = bf16[2048,1024]{1,0:T(8,128)(2,1)} async-done(((bf16[512,1024]{1,0:T(8,128)(2,1)}), bf16[2048,1024]{1,0:T(8,128)(2,1)}) %all-gather.30.cloned.1.call-update) | async-done | bytes 4194320 | tf_op jit(solution)/shard_map/all_gather | solution.py:189
  670.5 11.2 multiply_convert_fusion.2
  681.7 24.8 %all-gather.38.cloned.1.call-done = bf16[1,2048,1024]{2,1,0:T(8,128)(2,1)} async-done(((bf16[1,512,1024]{2,1,0:T(8,128)(2,1)}), bf16[1,2048,1024]{2,1,0:T(8,128)(2,1)}) %all-gather.38.cloned.1.call-update) | async-done | bytes 4194320 | tf_op jit(solution)/shard_map/all_gather | solution.py:189
  706.5 11.2 multiply_convert_fusion.1
  719.7 7.7 convolution_convert_fusion.1
  727.7 44.4 %reduce-scatter.25.cloned.1.call-done = bf16[512,1024]{1,0:T(8,128)(2,1)} async-done(((bf16[2048,1024]{1,0:T(8,128)(2,1)}), bf16[512,1024]{1,0:T(8,128)(2,1)}) %reduce-scatter.25.cloned.1.call-update) | async-done | bytes 1048592 | tf_op jit(solution)/shard_map/reduce_scatter | solution.py:193
  777.9 34.6 %all-gather.32.cloned.1.call-done = bf16[2048,1024]{1,0:T(8,128)(2,1)} async-done(((bf16[512,1024]{1,0:T(8,128)(2,1)}), bf16[2048,1024]{1,0:T(8,128)(2,1)}) %all-gather.32.cloned.1.call-update) | async-done | bytes 4194320 | tf_op jit(solution)/shard_map/all_gather | solution.py:189
  812.5 4.7 fusion.45
  820.0 56.2 %shard_map.154 = bf16[4,2048,192]{2,1,0:T(8,128)(2,1)} custom-call(bf16[4,2048,192]{2,1,0:T(8,128)(2,1)} %bitcast.246, bf16[2048,64]{1,0:T(8,128)(2,1)} %get-tuple-element.71.qm_ref, bf16[2048,64]{1,0:T(8,128)(2,1)} %get-tuple-element.70.km_ref, bf16[4,2048,64]{2,1,0:T(8,128)(2,1)} %get-tuple-element.13.ctx_ref, f32[4,1,2048]{2,1,0:T(1,128)} %get-tuple-element.15.lse_ref, ...), custom_call_target="tpu_custom_call" | custom-call | flops 42949672960 | bytes 10485760 | tf_op jit(solution)/shard_map/pallas_call | solution.py:143
  876.2 7.8 bitcast_convert_fusion.1
  884.1 44.6 %reduce-scatter.27.cloned.1.call-done = bf16[512,1024]{1,0:T(8,128)(2,1)} async-done(((bf16[2048,1024]{1,0:T(8,128)(2,1)}), bf16[512,1024]{1,0:T(8,128)(2,1)}) %reduce-scatter.27.cloned.1.call-update) | async-done | bytes 1048592 | tf_op jit(solution)/shard_map/reduce_scatter | solution.py:193
  931.7 3.8 fusion.63
  935.6 34.6 %all-gather.34.cloned.1.call-done = bf16[2048,1024]{1,0:T(8,128)(2,1)} async-done(((bf16[512,1024]{1,0:T(8,128)(2,1)}), bf16[2048,1024]{1,0:T(8,128)(2,1)}) %all-gather.34.cloned.1.call-update) | async-done | bytes 4194320 | tf_op jit(solution)/shard_map/all_gather | solution.py:189
  970.2 11.5 multiply_convert_fusion
  983.8 7.7 convolution_convert_fusion
  991.6 44.6 %reduce-scatter.29.cloned.1.call-done = bf16[512,1024]{1,0:T(8,128)(2,1)} async-done(((bf16[2048,1024]{1,0:T(8,128)(2,1)}), bf16[512,1024]{1,0:T(8,128)(2,1)}) %reduce-scatter.29.cloned.1.call-update) | async-done | bytes 1048592 | tf_op jit(solution)/shard_map/reduce_scatter | solution.py:193
  1042.2 9.5 convolution_convert_fusion.2
  1051.7 9.4 convolution_convert_fusion.5
  1061.6 9.4 convolution_convert_fusion.6
  1071.0 9.4 fusion.85
  1080.7 9.4 convolution_convert_fusion.4
  1090.2 5.0 fusion.90
  1095.4 4.2 fusion.93
  1099.7 6.1 copy.50
  1105.7 6.2 fusion.120
  1118.8 55.8 %shard_map.155 = bf16[4,2048,192]{2,1,0:T(8,128)(2,1)} custom-call(bf16[4,2048,192]{2,1,0:T(8,128)(2,1)} %bitcast.244, bf16[2048,64]{1,0:T(8,128)(2,1)} %get-tuple-element.71.qm_ref, bf16[2048,64]{1,0:T(8,128)(2,1)} %get-tuple-element.70.km_ref, bf16[4,2048,64]{2,1,0:T(8,128)(2,1)} %get-tuple-element.12.ctx_ref, f32[4,1,2048]{2,1,0:T(1,128)} %get-tuple-element.14.lse_ref, ...), custom_call_target="tpu_custom_call" | custom-call | flops 42949672960 | bytes 10485760 | tf_op jit(solution)/shard_map/pallas_call | solution.py:143
  1174.6 6.3 copy.49
  1180.9 6.4 fusion.119
  1189.1 7.6 bitcast_convert_fusion
  1202.5 23.7 %collective-permute-done = bf16[512,1024]{1,0:T(8,128)(2,1)} collective-permute-done((bf16[512,1024]{1,0:T(8,128)(2,1)}, bf16[512,1024]{1,0:T(8,128)(2,1)}, u32[]{:S(2)}, u32[]{:S(2)}) %collective-permute-start) | collective-permute-done | bytes 1048608 | tf_op jit(solution)/shard_map/ppermute | solution.py:203
  1226.2 3.9 select_bitcast_fusion.3
  1237.1 23.9 %reduce-scatter.47.cloned.1.call-done = bf16[1024,256]{1,0:T(8,128)(2,1)} async-done(((bf16[1024,1024]{1,0:T(8,128)(2,1)}), bf16[1024,256]{1,0:T(8,128)(2,1)}) %reduce-scatter.47.cloned.1.call-update) | async-done | bytes 524304 | tf_op jit(solution)/shard_map/reduce_scatter | solution.py:265
  1261.0 45.5 %reduce-scatter.45.cloned.1.call-done = bf16[1024,256]{1,0:T(8,128)(2,1)} async-done(((bf16[1024,1024]{1,0:T(8,128)(2,1)}), bf16[1024,256]{1,0:T(8,128)(2,1)}) %reduce-scatter.45.cloned.1.call-update) | async-done | bytes 524304 | tf_op jit(solution)/shard_map/reduce_scatter | solution.py:265
  1312.3 17.3 %reduce-scatter.39.cloned.1.call-done = bf16[4,64,256]{2,1,0:T(8,128)(2,1)} async-done(((bf16[4,64,1024]{2,1,0:T(8,128)(2,1)}), bf16[4,64,256]{2,1,0:T(8,128)(2,1)}) %reduce-scatter.39.cloned.1.call-update) | async-done | bytes 131088 | tf_op jit(solution)/shard_map/reduce_scatter | solution.py:265
  1329.7 22.4 %reduce-scatter.37.cloned.1.call-done = bf16[4,64,256]{2,1,0:T(8,128)(2,1)} async-done(((bf16[4,64,1024]{2,1,0:T(8,128)(2,1)}), bf16[4,64,256]{2,1,0:T(8,128)(2,1)}) %reduce-scatter.37.cloned.1.call-update) | async-done | bytes 131088 | tf_op jit(solution)/shard_map/reduce_scatter | solution.py:265
  1355.2 32.8 %reduce-scatter.35.cloned.1.call-done = bf16[256,4,192]{0,2,1:T(8,128)(2,1)} async-done(((bf16[1024,4,192]{0,2,1:T(8,128)(2,1)}), bf16[256,4,192]{0,2,1:T(8,128)(2,1)}) %reduce-scatter.35.cloned.1.call-update) | async-done | bytes 393232 | tf_op jit(solution)/shard_map/reduce_scatter | solution.py:265
  1388.0 37.1 %reduce-scatter.33.cloned.1.call-done = bf16[256,4,192]{0,2,1:T(8,128)(2,1)} async-done(((bf16[1024,4,192]{0,2,1:T(8,128)(2,1)}), bf16[256,4,192]{0,2,1:T(8,128)(2,1)}) %reduce-scatter.33.cloned.1.call-update) | async-done | bytes 393232 | tf_op jit(solution)/shard_map/reduce_scatter | solution.py:265
  1428.4 43.0 %reduce-scatter.31.cloned.1.call-done = bf16[512,1024]{1,0:T(8,128)(2,1)} async-done(((bf16[2048,1024]{1,0:T(8,128)(2,1)}), bf16[512,1024]{1,0:T(8,128)(2,1)}) %reduce-scatter.31.cloned.1.call-update) | async-done | bytes 1048592 | tf_op jit(solution)/shard_map/reduce_scatter | solution.py:193
  1473.8 5.0 broadcast_select_fusion
  1485.4 52.9 %psum.7 = f32[2,2,1024]{2,1,0:T(2,128)S(1)} all-reduce(f32[2,2,1024]{2,1,0:T(2,128)S(1)} %pad_maximum_fusion.24), channel_id=1, replica_groups=mesh['section'=2,'dp'=4,'tensor'=4] {'section','dp','tensor'}, use_global_device_ids=true, to_apply=%region_28.29 | all-reduce | flops 4096 | bytes 32768 | tf_op jit(solution)/shard_map/psum | solution.py:306
  (337 shorter events, 101.2 us)
Async XLA Ops:
  7.2 46.4 %all-gather.20.cloned.1.call-start = ((), (), s32[]{:S(2)}) async-start(), calls=%async_computation.18 | async-start | bytes 1179648 | tf_op jit(solution)/shard_map/all_gather | solution.py:221
  9.0 106.5 %all-gather.16.cloned.1.call-start = ((), (), s32[]{:S(2)}) async-start(), calls=%async_computation.16 | async-start | bytes 3538944 | tf_op jit(solution)/shard_map/all_gather | solution.py:221
  11.0 139.7 %all-gather.18.cloned.1.call-start = ((), (), s32[]{:S(2)}) async-start(), calls=%async_computation.17 | async-start | bytes 5242880 | tf_op jit(solution)/shard_map/all_gather | solution.py:189
  19.6 228.2 %reduce-scatter.17.cloned.1.call-start = ((), (), s32[]{:S(2)}) async-start(), calls=%async_computation.19 | async-start | bytes 5242880 | tf_op jit(solution)/shard_map/reduce_scatter | solution.py:193
  55.8 142.3 %copy-start.57 = (bf16[4,64,256]{2,1,0:T(8,128)(2,1)}, bf16[4,64,256]{2,1,0:T(8,128)(2,1)S(1)}, u32[]{:S(2)}) copy-start(bf16[4,64,256]{2,1,0:T(8,128)(2,1)S(1)} %get-tuple-element.64) | copy-start | bytes 393220
  55.8 142.3 %copy-start.59 = (bf16[4,64,256]{2,1,0:T(8,128)(2,1)}, bf16[4,64,256]{2,1,0:T(8,128)(2,1)S(1)}, u32[]{:S(2)}) copy-start(bf16[4,64,256]{2,1,0:T(8,128)(2,1)S(1)} %get-tuple-element.65) | copy-start | bytes 393220
  118.7 39.5 %copy-start.45 = (bf16[256,4,192]{0,2,1:T(8,128)(2,1)}, bf16[256,4,192]{0,2,1:T(8,128)(2,1)S(1)}, u32[]{:S(2)}) copy-start(bf16[256,4,192]{0,2,1:T(8,128)(2,1)S(1)} %get-tuple-element.56) | copy-start | bytes 1179652
  118.7 39.5 %copy-start.47 = (bf16[256,4,192]{0,2,1:T(8,128)(2,1)}, bf16[256,4,192]{0,2,1:T(8,128)(2,1)S(1)}, u32[]{:S(2)}) copy-start(bf16[256,4,192]{0,2,1:T(8,128)(2,1)S(1)} %get-tuple-element.57) | copy-start | bytes 1179652
  118.7 39.5 %copy-start.49 = (bf16[256,4,192]{0,2,1:T(8,128)(2,1)}, bf16[256,4,192]{0,2,1:T(8,128)(2,1)S(1)}, u32[]{:S(2)}) copy-start(bf16[256,4,192]{0,2,1:T(8,128)(2,1)S(1)} %get-tuple-element.58) | copy-start | bytes 1179652
  203.1 120.8 %all-gather.24.cloned.1.call-start = ((), (), s32[]{:S(2)}) async-start(), calls=%async_computation.21 | async-start | bytes 4718592 | tf_op jit(solution)/shard_map/all_gather | solution.py:221
  205.2 193.2 %all-gather.26.cloned.1.call-start = ((), (), s32[]{:S(2)}) async-start(), calls=%async_computation.22 | async-start | bytes 4718592 | tf_op jit(solution)/shard_map/all_gather | solution.py:221
  207.3 226.0 %all-gather.22.cloned.1.call-start = ((), (), s32[]{:S(2)}) async-start(), calls=%async_computation.20 | async-start | bytes 5242880 | tf_op jit(solution)/shard_map/all_gather | solution.py:189
  211.7 38.2 %copy-start.69 = (f32[1,1,1024]{2,1,0:T(1,128)}, f32[1,1,1024]{2,1,0:T(1,128)S(1)}, u32[]{:S(2)}) copy-start(f32[1,1,1024]{2,1,0:T(1,128)S(1)} %get-tuple-element.75) | copy-start | bytes 12292
  251.4 245.4 %reduce-scatter.19.cloned.1.call-start = ((), (), s32[]{:S(2)}) async-start(), calls=%async_computation.23 | async-start | bytes 5242880 | tf_op jit(solution)/shard_map/reduce_scatter | solution.py:193
  328.0 105.4 %copy-start.29 = (bf16[256,1024]{1,0:T(8,128)(2,1)}, bf16[256,1024]{1,0:T(8,128)(2,1)S(1)}, u32[]{:S(2)}) copy-start(bf16[256,1024]{1,0:T(8,128)(2,1)S(1)} %get-tuple-element.46) | copy-start | bytes 1572868
  328.0 105.4 %copy-start.31 = (bf16[256,1024]{1,0:T(8,128)(2,1)}, bf16[256,1024]{1,0:T(8,128)(2,1)S(1)}, u32[]{:S(2)}) copy-start(bf16[256,1024]{1,0:T(8,128)(2,1)S(1)} %get-tuple-element.47) | copy-start | bytes 1572868
  452.1 47.2 %copy-start.75 = (f32[1,1,1024]{2,1,0:T(1,128)S(1)}, f32[1,1,1024]{2,1,0:T(1,128)}, u32[]{:S(2)}) copy-start(f32[1,1,1024]{2,1,0:T(1,128)} %get-tuple-element.72) | copy-start | bytes 12292
  452.1 83.2 %all-gather.28.cloned.1.call-start = ((), (), s32[]{:S(2)}) async-start(), calls=%async_computation.24 | async-start | bytes 5242880 | tf_op jit(solution)/shard_map/all_gather | solution.py:189
  498.9 432.8 %copy-start.2 = (bf16[512,1024]{1,0:T(8,128)(2,1)}, bf16[512,1024]{1,0:T(8,128)(2,1)S(1)}, u32[]{:S(2)}) copy-start(bf16[512,1024]{1,0:T(8,128)(2,1)S(1)} %get-tuple-element.31) | copy-start | bytes 3145732
  498.9 36.5 %copy-start.52 = (bf16[256,4,192]{0,2,1:T(8,128)(2,1)S(1)}, bf16[256,4,192]{0,2,1:T(8,128)(2,1)}, u32[]{:S(2)}) copy-start(bf16[256,4,192]{0,2,1:T(8,128)(2,1)} %get-tuple-element.52) | copy-start | bytes 1179652
  498.9 36.5 %copy-start.53 = (bf16[256,4,192]{0,2,1:T(8,128)(2,1)S(1)}, bf16[256,4,192]{0,2,1:T(8,128)(2,1)}, u32[]{:S(2)}) copy-start(bf16[256,4,192]{0,2,1:T(8,128)(2,1)} %get-tuple-element.53) | copy-start | bytes 1179652
  498.9 36.5 %copy-start.55 = (bf16[256,4,192]{0,2,1:T(8,128)(2,1)S(1)}, bf16[256,4,192]{0,2,1:T(8,128)(2,1)}, u32[]{:S(2)}) copy-start(bf16[256,4,192]{0,2,1:T(8,128)(2,1)} %get-tuple-element.54) | copy-start | bytes 1179652
  498.9 36.5 %copy-start.56 = (bf16[256,4,192]{0,2,1:T(8,128)(2,1)S(1)}, bf16[256,4,192]{0,2,1:T(8,128)(2,1)}, u32[]{:S(2)}) copy-start(bf16[256,4,192]{0,2,1:T(8,128)(2,1)} %get-tuple-element.55) | copy-start | bytes 1179652
  499.4 43.5 %copy-start.83 = (f32[512]{0:T(512)}, f32[512]{0:T(512)S(1)}, u32[]{:S(2)}) copy-start(f32[512]{0:T(512)S(1)} %add_rsqrt_fusion.1) | copy-start | bytes 6148
  500.8 131.4 %reduce-scatter.21.cloned.1.call-start = ((), (), s32[]{:S(2)}) async-start(), calls=%async_computation.25 | async-start | bytes 5242880 | tf_op jit(solution)/shard_map/reduce_scatter | solution.py:193
  587.6 82.9 %all-gather.30.cloned.1.call-start = ((), (), s32[]{:S(2)}) async-start(), calls=%async_computation.26 | async-start | bytes 5242880 | tf_op jit(solution)/shard_map/all_gather | solution.py:189
  635.8 70.6 %all-gather.38.cloned.1.call-start = ((), (), s32[]{:S(2)}) async-start(), calls=%async_computation.43 | async-start | bytes 5242880 | tf_op jit(solution)/shard_map/all_gather | solution.py:189
  638.2 134.0 %reduce-scatter.25.cloned.1.call-start = ((), (), s32[]{:S(2)}) async-start(), calls=%async_computation.28 | async-start | bytes 5242880 | tf_op jit(solution)/shard_map/reduce_scatter | solution.py:193
  727.5 85.1 %all-gather.32.cloned.1.call-start = ((), (), s32[]{:S(2)}) async-start(), calls=%async_computation.29 | async-start | bytes 5242880 | tf_op jit(solution)/shard_map/all_gather | solution.py:189
  777.9 150.8 %reduce-scatter.27.cloned.1.call-start = ((), (), s32[]{:S(2)}) async-start(), calls=%async_computation.30 | async-start | bytes 5242880 | tf_op jit(solution)/shard_map/reduce_scatter | solution.py:193
  820.0 56.2 %copy-start.54 = (bf16[256,4,192]{0,2,1:T(8,128)(2,1)S(1)}, bf16[256,4,192]{0,2,1:T(8,128)(2,1)}, u32[]{:S(2)}) copy-start(bf16[256,4,192]{0,2,1:T(8,128)(2,1)} %get-tuple-element.53) | copy-start | bytes 1179652
  884.0 44.7 %copy-start.79 = (f32[512]{0:T(512)S(1)}, f32[512]{0:T(512)}, u32[]{:S(2)}) copy-start(f32[512]{0:T(512)} %copy-done.78) | copy-start | bytes 6148
  884.0 44.7 %copy-start.84 = (f32[512]{0:T(512)S(1)}, f32[512]{0:T(512)}, u32[]{:S(2)}) copy-start(f32[512]{0:T(512)} %copy-done.83) | copy-start | bytes 6148
  884.0 47.6 %copy-start.87 = (f32[512]{0:T(512)S(1)}, f32[512]{0:T(512)}, u32[]{:S(2)}) copy-start(f32[512]{0:T(512)} %copy-done.86) | copy-start | bytes 6148
  884.1 47.6 %copy-start.89 = (f32[512]{0:T(512)S(1)}, f32[512]{0:T(512)}, u32[]{:S(2)}) copy-start(f32[512]{0:T(512)} %copy-done.88) | copy-start | bytes 6148
  884.1 86.1 %all-gather.34.cloned.1.call-start = ((), (), s32[]{:S(2)}) async-start(), calls=%async_computation.31 | async-start | bytes 5242880 | tf_op jit(solution)/shard_map/all_gather | solution.py:189
  935.5 100.7 %reduce-scatter.29.cloned.1.call-start = ((), (), s32[]{:S(2)}) async-start(), calls=%async_computation.32 | async-start | bytes 5242880 | tf_op jit(solution)/shard_map/reduce_scatter | solution.py:193
  991.5 44.7 %copy-start.7 = (bf16[2,512,1024]{2,1,0:T(8,128)(2,1)S(1)}, bf16[2,512,1024]{2,1,0:T(8,128)(2,1)}, u32[]{:S(2)}) copy-start(bf16[2,512,1024]{2,1,0:T(8,128)(2,1)} %param.9) | copy-start | bytes 6291460
  991.5 44.7 %copy-start.10 = (bf16[512,1024]{1,0:T(8,128)(2,1)S(1)}, bf16[512,1024]{1,0:T(8,128)(2,1)}, u32[]{:S(2)}) copy-start(bf16[512,1024]{1,0:T(8,128)(2,1)} %reduce-scatter.17.cloned.1.call-done) | copy-start | bytes 3145732
  991.5 44.7 %copy-start.70 = (f32[1,1,1024]{2,1,0:T(1,128)S(1)}, f32[1,1,1024]{2,1,0:T(1,128)}, u32[]{:S(2)}) copy-start(f32[1,1,1024]{2,1,0:T(1,128)} %copy-done.69) | copy-start | bytes 12292
  991.5 44.7 %copy-start.72 = (f32[512]{0:T(512)S(1)}, f32[512]{0:T(512)}, u32[]{:S(2)}) copy-start(f32[512]{0:T(512)} %copy-done.71) | copy-start | bytes 6148
  991.5 44.7 %copy-start.81 = (f32[512]{0:T(512)S(1)}, f32[512]{0:T(512)}, u32[]{:S(2)}) copy-start(f32[512]{0:T(512)} %copy-done.80) | copy-start | bytes 6148
  991.5 103.8 %all-gather.36.cloned.1.call-start = ((), (), s32[]{:S(2)}) async-start(), calls=%async_computation.33 | async-start | bytes 5242880 | tf_op jit(solution)/shard_map/all_gather | solution.py:189
  1041.9 154.7 %reduce-scatter.23.cloned.1.call-start = ((), (), s32[]{:S(2)}) async-start(), calls=%async_computation.27 | async-start | bytes 5242880 | tf_op jit(solution)/shard_map/reduce_scatter | solution.py:193
  1051.7 178.5 %reduce-scatter.43.cloned.1.call-start = ((), (), s32[]{:S(2)}) async-start(), calls=%async_computation.40 | async-start | bytes 2621440 | tf_op jit(solution)/shard_map/reduce_scatter | solution.py:265
  1061.1 169.1 %reduce-scatter.41.cloned.1.call-start = ((), (), s32[]{:S(2)}) async-start(), calls=%async_computation.39 | async-start | bytes 2621440 | tf_op jit(solution)/shard_map/reduce_scatter | solution.py:265
  1071.0 190.0 %reduce-scatter.47.cloned.1.call-start = ((), (), s32[]{:S(2)}) async-start(), calls=%async_computation.42 | async-start | bytes 2621440 | tf_op jit(solution)/shard_map/reduce_scatter | solution.py:265
  1080.5 226.1 %reduce-scatter.45.cloned.1.call-start = ((), (), s32[]{:S(2)}) async-start(), calls=%async_computation.41 | async-start | bytes 2621440 | tf_op jit(solution)/shard_map/reduce_scatter | solution.py:265
  1090.2 239.5 %reduce-scatter.39.cloned.1.call-start = ((), (), s32[]{:S(2)}) async-start(), calls=%async_computation.38 | async-start | bytes 655360 | tf_op jit(solution)/shard_map/reduce_scatter | solution.py:265
  1095.3 256.8 %reduce-scatter.37.cloned.1.call-start = ((), (), s32[]{:S(2)}) async-start(), calls=%async_computation.37 | async-start | bytes 655360 | tf_op jit(solution)/shard_map/reduce_scatter | solution.py:265
  1099.6 288.4 %reduce-scatter.35.cloned.1.call-start = ((), (), s32[]{:S(2)}) async-start(), calls=%async_computation.36 | async-start | bytes 1966080 | tf_op jit(solution)/shard_map/reduce_scatter | solution.py:265
  1113.4 311.7 %reduce-scatter.33.cloned.1.call-start = ((), (), s32[]{:S(2)}) async-start(), calls=%async_computation.35 | async-start | bytes 1966080 | tf_op jit(solution)/shard_map/reduce_scatter | solution.py:265
  1188.7 282.7 %reduce-scatter.31.cloned.1.call-start = ((), (), s32[]{:S(2)}) async-start(), calls=%async_computation.34 | async-start | bytes 5242880 | tf_op jit(solution)/shard_map/reduce_scatter | solution.py:193
  1201.0 25.2 %collective-permute-start = (bf16[512,1024]{1,0:T(8,128)(2,1)}, bf16[512,1024]{1,0:T(8,128)(2,1)}, u32[]{:S(2)}, u32[]{:S(2)}) collective-permute-start(bf16[512,1024]{1,0:T(8,128)(2,1)} %broadcast_select_fusion.2), channel_id=1, source_target_pairs={{0,16},{16,0},{1,17},{17,1},{2,18},{18,2},{3,19},{19,3},{4,20},{20... | collective-permute-start | bytes 3145736 | tf_op jit(solution)/shard_map/ppermute | solution.py:203
  1232.2 77.7 %collective-permute-start.4 = (bf16[256,1024]{1,0:T(8,128)(2,1)}, bf16[256,1024]{1,0:T(8,128)(2,1)}, u32[]{:S(2)}, u32[]{:S(2)}) collective-permute-start(bf16[256,1024]{1,0:T(8,128)(2,1)} %broadcast_select_fusion.5), channel_id=1, source_target_pairs={{0,16},{16,0},{1,17},{17,1},{2,18},{18,2},{3,19},{19,3},{4,20},{20... | collective-permute-start | bytes 1572872 | tf_op jit(solution)/shard_map/ppermute | solution.py:203
  1308.4 163.0 %copy-start.8 = (bf16[2,512,1024]{2,1,0:T(8,128)(2,1)S(1)}, bf16[2,512,1024]{2,1,0:T(8,128)(2,1)}, u32[]{:S(2)}) copy-start(bf16[2,512,1024]{2,1,0:T(8,128)(2,1)} %param.9) | copy-start | bytes 6291460
  1308.4 163.0 %copy-start.74 = (f32[1,1,1024]{2,1,0:T(1,128)S(1)}, f32[1,1,1024]{2,1,0:T(1,128)}, u32[]{:S(2)}) copy-start(f32[1,1,1024]{2,1,0:T(1,128)} %copy-done.73) | copy-start | bytes 12292
  1308.4 163.0 %copy-start.77 = (f32[512]{0:T(512)S(1)}, f32[512]{0:T(512)}, u32[]{:S(2)}) copy-start(f32[512]{0:T(512)} %copy-done.76) | copy-start | bytes 6148
  1308.4 172.1 %collective-permute-start.5 = (bf16[1024,256]{1,0:T(8,128)(2,1)}, bf16[1024,256]{1,0:T(8,128)(2,1)}, u32[]{:S(2)}, u32[]{:S(2)}) collective-permute-start(bf16[1024,256]{1,0:T(8,128)(2,1)} %broadcast_select_fusion.4), channel_id=1, source_target_pairs={{0,16},{16,0},{1,17},{17,1},{2,18},{18,2},{3,19},{19,3},{4,20},{20... | collective-permute-start | bytes 1572872 | tf_op jit(solution)/shard_map/ppermute | solution.py:203
  1353.7 129.0 %collective-permute-start.3 = (bf16[4,64,256]{2,1,0:T(8,128)(2,1)}, bf16[4,64,256]{2,1,0:T(8,128)(2,1)}, u32[]{:S(2)}, u32[]{:S(2)}) collective-permute-start(bf16[4,64,256]{2,1,0:T(8,128)(2,1)} %broadcast_select_fusion.7), channel_id=1, source_target_pairs={{0,16},{16,0},{1,17},{17,1},{2,18},{18,2},{3,19},{19,3},{4,20},{20... | collective-permute-start | bytes 393224 | tf_op jit(solution)/shard_map/ppermute | solution.py:203
  1426.9 57.4 %collective-permute-start.2 = (bf16[256,4,192]{0,2,1:T(8,128)(2,1)}, bf16[256,4,192]{0,2,1:T(8,128)(2,1)S(1)}, u32[]{:S(2)}, u32[]{:S(2)}) collective-permute-start(bf16[256,4,192]{0,2,1:T(8,128)(2,1)} %broadcast_select_fusion.6), channel_id=1, source_target_pairs={{0,16},{16,0},{1,17},{17,1},{2,18},{18,2},{3,19},{19,3},{4,20},{20... | collective-permute-start | bytes 1179656 | tf_op jit(solution)/shard_map/ppermute | solution.py:203
  1478.9 60.1 %copy-start.13 = (bf16[512,1024]{1,0:T(8,128)(2,1)S(1)}, bf16[512,1024]{1,0:T(8,128)(2,1)}, u32[]{:S(2)}) copy-start(bf16[512,1024]{1,0:T(8,128)(2,1)} %fusion.63) | copy-start | bytes 3145732
  1478.9 60.0 %copy-start.19 = (bf16[512,1024]{1,0:T(8,128)(2,1)S(1)}, bf16[512,1024]{1,0:T(8,128)(2,1)}, u32[]{:S(2)}) copy-start(bf16[512,1024]{1,0:T(8,128)(2,1)} %get-tuple-element.29) | copy-start | bytes 3145732
  1478.9 60.0 %collective-permute-start.1 = (bf16[512,1024]{1,0:T(8,128)(2,1)}, bf16[512,1024]{1,0:T(8,128)(2,1)S(1)}, u32[]{:S(2)}, u32[]{:S(2)}) collective-permute-start(bf16[512,1024]{1,0:T(8,128)(2,1)} %get-tuple-element.28), channel_id=1, source_target_pairs={{0,16},{16,0},{1,17},{17,1},{2,18},{18,2},{3,19},{19,3},{4,20},{20... | collective-permute-start | bytes 3145736 | tf_op jit(solution)/shard_map/ppermute | solution.py:203
  (70 other events, 580.4 us)
Sparse Core Ops, SparseCore 0:
  10.7 42.8 all-gather.19
  56.3 59.1 all-gather.15
  117.6 33.0 all-gather.17
  203.2 44.4 reduce-scatter.16
  250.5 73.3 all-gather.23
  326.7 71.6 all-gather.25
  400.6 32.7 all-gather.21
  452.3 44.5 reduce-scatter.18
  500.9 34.4 all-gather.27
  587.7 44.4 reduce-scatter.20
  636.0 34.4 all-gather.29
  672.0 34.4 all-gather.37
  727.6 44.5 reduce-scatter.24
  778.0 34.5 all-gather.31
  884.2 44.4 reduce-scatter.26
  935.6 34.4 all-gather.33
  991.7 44.5 reduce-scatter.28
  1042.1 34.4 all-gather.35
  1079.1 44.4 reduce-scatter.22
  1125.9 43.8 reduce-scatter.42
  1172.1 43.2 reduce-scatter.40
  1217.8 43.1 reduce-scatter.46
  1263.3 43.1 reduce-scatter.44
  1308.7 20.8 reduce-scatter.38
  1332.0 20.0 reduce-scatter.36
  1354.4 33.5 reduce-scatter.34
  1390.8 34.2 reduce-scatter.32
  1427.8 43.4 reduce-scatter.30

commit v2 on v1

v2 whole, which is shorter than its diff:
```python
import functools
import math

import jax
import jax.numpy as jnp
from jax import lax
from jax.experimental import pallas as pl
from jax.experimental.pallas import tpu as pltpu
from jax.sharding import PartitionSpec as P

F32 = jnp.float32
BF = jnp.bfloat16
NT = (((1,), (1,)), ((), ()))
NN = (((1,), (0,)), ((), ()))
TN = (((0,), (0,)), ((), ()))
MASKED = -1e30
SCENES = 3
MESH = pl.DeviceIdType.MESH
VM = pl.BlockSpec(memory_space=pltpu.VMEM)
HB = pl.BlockSpec(memory_space=pl.ANY)
DMA = pltpu.SemaphoreType.DMA
LIMIT = 58 << 20


def dg(a, b, dims):
    return lax.dot_general(a, b, dims, preferred_element_type=F32)


def chunks(rows):
    return 4 if rows % 64 == 0 else 1


def shape(dims, dtype):
    return jax.ShapeDtypeStruct(dims, dtype)


class Group:
    def __init__(self, size):
        self.size = size
        self.chips = size // 2
        self.me = lax.axis_index("tensor")
        self.chip = lax.div(self.me, 2)
        self.core = lax.rem(self.me, 2)
        self.sibling = self.chip * 2 + 1 - self.core

    def ahead(self, k):
        return lax.rem(self.chip + k, self.chips)

    def behind(self, k):
        return lax.rem(self.chip + self.chips - k, self.chips)

    def greet(self):
        barrier = pltpu.get_barrier_semaphore()
        targets = [self.sibling] + [self.ahead(k) * 2 + self.core for k in range(1, self.chips)]
        for target in targets:
            pl.semaphore_signal(
                barrier, inc=1, device_id={"tensor": target}, device_id_type=MESH
            )
        pl.semaphore_wait(barrier, self.chips)


def remote(src, dst, send, recv, target):
    return pltpu.make_async_remote_copy(
        src_ref=src,
        dst_ref=dst,
        send_sem=send,
        recv_sem=recv,
        device_id={"tensor": target},
        device_id_type=MESH,
    )


def span(j, rc):
    return pl.ds(pl.multiple_of(j * rc, rc), rc)


def comm_sems(group_size, n):
    c = group_size // 2
    far, near = DMA((max(c - 1, 1), n)), DMA((c, n))
    return [far, far, near, near]


class Gather:
    def __init__(self, g, buf, rc, sems):
        self.g, self.buf, self.rc = g, buf, rc
        self.far_send, self.far_recv, self.near_send, self.near_recv = sems

    def far(self, k, j, origin, target):
        ref = self.buf.at[origin, span(j, self.rc)]
        return remote(ref, ref, self.far_send.at[k - 1, j], self.far_recv.at[k - 1, j], target)

    def near(self, k, j, origin):
        ref = self.buf.at[origin, span(j, self.rc)]
        return remote(
            ref, ref, self.near_send.at[k, j], self.near_recv.at[k, j], self.g.sibling
        )

    def start(self, j):
        g = self.g
        for k in range(1, g.chips):
            self.far(k, j, g.me, g.ahead(k) * 2 + g.core).start()
        self.near(0, j, g.me).start()

    def relay(self, j):
        g = self.g
        for k in range(1, g.chips):
            origin = g.behind(k) * 2 + g.core
            self.far(k, j, origin, g.me).wait_recv()
            self.near(k, j, origin).start()

    def ready(self, j):
        g = self.g
        self.near(0, j, g.sibling).wait_recv()
        for k in range(1, g.chips):
            self.near(k, j, g.behind(k) * 2 + 1 - g.core).wait_recv()

    def drain(self, n):
        g = self.g

        def one(j, _):
            for k in range(1, g.chips):
                self.far(k, j, g.me, g.sibling).wait_send()
            for k in range(g.chips):
                self.near(k, j, g.me).wait_send()
            return 0

        lax.fori_loop(0, n, one, 0)


def scatter_scratch(group_size, rows, width, n):
    c = group_size // 2
    far = pltpu.VMEM((max(c - 1, 1), rows, width), BF)
    near = pltpu.VMEM((c, rows, width), BF)
    return [pltpu.VMEM((group_size, rows, width), F32), near, near, far, far] + comm_sems(
        group_size, n
    )


class Scatter:
    def __init__(self, g, rc, scratch):
        self.g, self.rc = g, rc
        self.part, self.near_out, self.near_in, self.far_out, self.far_in = scratch[:5]
        self.far_send, self.far_recv, self.near_send, self.near_recv = scratch[5:]

    def near(self, k, j):
        rows = span(j, self.rc)
        return remote(
            self.near_out.at[k, rows],
            self.near_in.at[k, rows],
            self.near_send.at[k, j],
            self.near_recv.at[k, j],
            self.g.sibling,
        )

    def far(self, k, j):
        rows = span(j, self.rc)
        return remote(
            self.far_out.at[k - 1, rows],
            self.far_in.at[k - 1, rows],
            self.far_send.at[k - 1, j],
            self.far_recv.at[k - 1, j],
            self.g.ahead(k) * 2 + self.g.core,
        )

    def first(self, j):
        g, rows = self.g, span(j, self.rc)
        for k in list(range(1, g.chips)) + [0]:
            owner = g.ahead(k) * 2 + 1 - g.core
            self.near_out[k, rows, :] = self.part[owner, rows, :].astype(BF)
            self.near(k, j).start()

    def second(self, j):
        g, rows = self.g, span(j, self.rc)
        for k in range(1, g.chips):
            owner = g.ahead(k) * 2 + g.core
            self.near(k, j).wait_recv()
            both = self.part[owner, rows, :] + self.near_in[k, rows, :].astype(F32)
            self.far_out[k - 1, rows, :] = both.astype(BF)
            self.far(k, j).start()

    def third(self, j):
        g, rows = self.g, span(j, self.rc)
        self.near(0, j).wait_recv()
        total = self.part[g.me, rows, :] + self.near_in[0, rows, :].astype(F32)
        for k in range(1, g.chips):
            self.far(k, j).wait_recv()
            total = total + self.far_in[k - 1, rows, :].astype(F32)
        return total

    def drain(self, n):
        g = self.g

        def one(j, _):
            for k in range(1, g.chips):
                self.far(k, j).wait_send()
            for k in range(g.chips):
                self.near(k, j).wait_send()
            return 0

        lax.fori_loop(0, n, one, 0)


def params(key):
    return pltpu.CompilerParams(
        vmem_limit_bytes=LIMIT, collective_id=key, has_side_effects=True
    )


def cost(flops, moved, exps=0):
    return pl.CostEstimate(flops=int(flops), bytes_accessed=int(moved), transcendentals=int(exps))


def normed(source):
    center = source - jnp.mean(source, axis=-1, keepdims=True)
    r = lax.rsqrt(jnp.mean(center * center, axis=-1, keepdims=True) + 1e-05)
    return center * r, r


def normed_back(source, gain, grad):
    n, r = normed(source)
    e = grad * gain
    dh = r * (
        e - jnp.mean(e, axis=-1, keepdims=True) - n * jnp.mean(e * n, axis=-1, keepdims=True)
    )
    return dh, jnp.sum(grad * n, axis=0, keepdims=True)


def flat(value):
    return value.reshape((value.shape[0] * value.shape[1],) + value.shape[2:])


def run(n, body):
    def one(j, carry):
        body(j)
        return carry

    lax.fori_loop(0, n, one, 0)


def qkv_kernel(
    size, layer, x_ref, gain_ref, w_ref, qkv_ref, a1_out, a1, w, w_sem, out_sem, *sems
):
    rows, width = x_ref.shape
    heads = qkv_ref.shape[0]
    parts, depth = w_ref.shape[0] // 2, w_ref.shape[2]
    n = chunks(rows)
    rc = rows // n
    g = Group(size)
    copies = [
        pltpu.make_async_copy(
            w_ref.at[layer * parts + z], w.at[:, pl.ds(z * depth, depth)], w_sem.at[z]
        )
        for z in range(parts)
    ]
    for copy in copies:
        copy.start()
    g.greet()
    gather = Gather(g, a1, rc, sems)

    def send(j):
        at = span(j, rc)
        a = normed(x_ref[at, :].astype(F32))[0] * gain_ref[layer : layer + 1, :]
        a1[g.me, at, :] = a.astype(BF)
        gather.start(j)

    run(n, send)
    for copy in copies:
        copy.wait()

    def work(j):
        at = span(j, rc)
        gather.relay(j)
        gather.ready(j)
        a = flat(a1[:, at, :])
        for h in range(heads):
            r = dg(a, w[h], NN).astype(BF)
            qkv_ref[h, :, at, :] = r.reshape(size, rc, r.shape[1])

    run(n, work)
    out = pltpu.make_async_copy(a1, a1_out, out_sem.at[0])
    out.start()
    gather.drain(n)
    out.wait()


def qkv_forward(size, layer, x, gains, w):
    rows, width = x.shape
    _, heads, depth, wide = w.shape
    n = chunks(rows)
    return pl.pallas_call(
        functools.partial(qkv_kernel, size, layer),
        out_shape=(
            shape((heads, size, rows, wide), BF),
            shape((size, rows, width), BF),
        ),
        in_specs=[VM, VM, HB],
        out_specs=(VM, HB),
        scratch_shapes=[
            pltpu.VMEM((size, rows, width), BF),
            pltpu.VMEM((heads, width, wide), BF),
            DMA((w.shape[0] // 2,)),
            DMA((1,)),
        ]
        + comm_sems(size, n),
        compiler_params=params(layer),
        cost_estimate=cost(20e9, 30e6),
    )(x, gains, w)


def attend_kernel(
    size, layer, qkv_ref, qm_ref, km_ref, x_ref, w_ref,
    h1_ref, ctx_ref, lse_ref, ka, vt, w, w_sem, *scratch
):
    heads, _, rows, wide = qkv_ref.shape
    length = size * rows
    e = wide // 3
    c = e**-0.5 * math.log2(math.e)
    parts, depth = w_ref.shape[0] // 2, w_ref.shape[2]
    n = chunks(rows)
    rc = rows // n
    bq = size * rc
    kc = bq
    g = Group(size)
    copies = [
        pltpu.make_async_copy(
            w_ref.at[layer * parts + z], w.at[:, pl.ds(z * depth, depth)], w_sem.at[z]
        )
        for z in range(parts)
    ]
    for copy in copies:
        copy.start()
    g.greet()
    scatter = Scatter(g, rc, scratch)
    for h in range(heads):
        whole = flat(qkv_ref[h])
        ka[h, :, :e] = whole[:, e : 2 * e]
        ka[h, :, e:] = flat(km_ref[...])
        vt[h, :e, :] = whole[:, 2 * e :].T
        vt[h, e:, :] = jnp.ones((16, length), BF)
    for copy in copies:
        copy.wait()

    def work(j):
        at = span(j, rc)
        qm = flat(qm_ref[:, at, :])
        found = []
        for h in range(heads):
            q = jnp.concatenate([flat(qkv_ref[h, :, at, :])[:, :e], qm], axis=1)
            held = []
            top = None
            for k in range(length // kc):
                s = dg(ka[h, k * kc : (k + 1) * kc, :], q, NT)
                t = jnp.max(s, axis=0, keepdims=True)
                top = t if top is None else jnp.maximum(top, t)
                held.append(s)
            top = top * c
            acc = None
            for k in range(length // kc):
                p = jnp.exp2(held[k] * c - top).astype(BF)
                a = dg(vt[h, :, k * kc : (k + 1) * kc], p, NN)
                acc = a if acc is None else acc + a
            total = acc[e : e + 1]
            found.append((acc[:e] * (1.0 / total)).astype(BF))
            lse_ref[j, h : h + 1, :] = top + jnp.log2(total)
        ctx = (jnp.concatenate(found, axis=0) if heads > 1 else found[0]).T
        ctx_ref[:, at, :] = ctx.reshape(size, rc, heads * e)
        for z in range(parts):
            scatter.part[:, at, z * depth : (z + 1) * depth] = dg(
                ctx, w[:, z * depth : (z + 1) * depth], NN
            ).reshape(size, rc, depth)
        scatter.first(j)
        scatter.second(j)

    run(n, work)

    def last(j):
        at = span(j, rc)
        h1_ref[at, :] = x_ref[at, :].astype(F32) + scatter.third(j)

    run(n, last)
    scatter.drain(n)


def attend(size, layer, qkv, qm, km, x, w):
    heads, _, rows, wide = qkv.shape
    e = wide // 3
    width = x.shape[1]
    n = chunks(rows)
    return pl.pallas_call(
        functools.partial(attend_kernel, size, layer),
        out_shape=(
            shape((rows, width), F32),
            shape((size, rows, heads * e), BF),
            shape((n, heads, size * rows // n), F32),
        ),
        in_specs=[VM, VM, VM, VM, HB],
        out_specs=(VM, VM, VM),
        scratch_shapes=[
            pltpu.VMEM((heads, size * rows, 2 * e), BF),
            pltpu.VMEM((heads, e + 16, size * rows), BF),
            pltpu.VMEM((heads * e, width), BF),
            DMA((w.shape[0] // 2,)),
        ]
        + scatter_scratch(size, rows, width, n),
        compiler_params=params(2 + layer),
        cost_estimate=cost(60e9, 20e6),
    )(qkv, qm, km, x, w)


def mlp_kernel(
    size, layer, h1_ref, gain_ref, wu_ref, wd_ref,
    y_ref, a2_out, hid_out, slope_out, a2, hid, slope, wu, wd, w_sem, out_sem, *scratch
):
    rows, width = h1_ref.shape
    parts, depth, hidden = wu_ref.shape[0] // 2, wu_ref.shape[1], wu_ref.shape[2]
    fb = min(256, hidden)
    n = chunks(rows)
    rc = rows // n
    g = Group(size)
    copies = []
    for z in range(parts):
        at = pl.ds(z * depth, depth)
        copies.append(pltpu.make_async_copy(wu_ref.at[layer * parts + z], wu.at[at], w_sem.at[z]))
        copies.append(
            pltpu.make_async_copy(wd_ref.at[layer * parts + z], wd.at[:, at], w_sem.at[parts + z])
        )
    for copy in copies:
        copy.start()
    g.greet()
    gather = Gather(g, a2, rc, scratch[:4])
    scatter = Scatter(g, rc, scratch[4:])

    def send(j):
        at = span(j, rc)
        a = normed(h1_ref[at, :])[0] * gain_ref[layer : layer + 1, :]
        a2[g.me, at, :] = a.astype(BF)
        gather.start(j)

    run(n, send)
    for copy in copies:
        copy.wait()

    def work(j):
        at = span(j, rc)
        gather.relay(j)
        gather.ready(j)
        a = flat(a2[:, at, :])
        for f in range(hidden // fb):
            cols = slice(f * fb, (f + 1) * fb)
            u = dg(a, wu[:, cols], NN)
            half = 0.5 + 0.5 * lax.erf(u * (0.5**0.5))
            slope[:, at, cols] = (
                (half + u * jnp.exp(-0.5 * u * u) * ((2 * math.pi) ** -0.5))
                .astype(BF)
                .reshape(size, rc, fb)
            )
            hid[:, at, cols] = (u * half).astype(BF).reshape(size, rc, fb)
        held = flat(hid[:, at, :])
        for z in range(parts):
            cols = slice(z * depth, (z + 1) * depth)
            scatter.part[:, at, cols] = dg(held, wd[:, cols], NN).reshape(size, rc, depth)
        scatter.first(j)
        scatter.second(j)

    run(n, work)
    outs = [
        pltpu.make_async_copy(a2, a2_out, out_sem.at[0]),
        pltpu.make_async_copy(hid, hid_out, out_sem.at[1]),
        pltpu.make_async_copy(slope, slope_out, out_sem.at[2]),
    ]
    for out in outs:
        out.start()

    def last(j):
        at = span(j, rc)
        y_ref[at, :] = (h1_ref[at, :] + scatter.third(j)).astype(BF)

    run(n, last)
    gather.drain(n)
    scatter.drain(n)
    for out in outs:
        out.wait()


def mlp_forward(size, layer, h1, gains, wu, wd):
    rows, width = h1.shape
    hidden = wu.shape[2]
    n = chunks(rows)
    return pl.pallas_call(
        functools.partial(mlp_kernel, size, layer),
        out_shape=(
            shape((rows, width), BF),
            shape((size, rows, width), BF),
            shape((size, rows, hidden), BF),
            shape((size, rows, hidden), BF),
        ),
        in_specs=[VM, VM, HB, HB],
        out_specs=(VM, HB, HB, HB),
        scratch_shapes=[
            pltpu.VMEM((size, rows, width), BF),
            pltpu.VMEM((size, rows, hidden), BF),
            pltpu.VMEM((size, rows, hidden), BF),
            pltpu.VMEM((width, hidden), BF),
            pltpu.VMEM((hidden, width), BF),
            DMA((wu.shape[0],)),
            DMA((3,)),
        ]
        + comm_sems(size, n)
        + scatter_scratch(size, rows, width, n),
        compiler_params=params(4 + layer),
        cost_estimate=cost(50e9, 30e6),
    )(h1, gains, wu, wd)


def mlp_back_kernel(
    size, layer, g_ref, h1_ref, gain_ref, a2_ref, hid_ref, slope_ref, wu_ref, wd_ref,
    mid_ref, gain_out, gup_ref, gdown_ref,
    grad, a2, hid, dup, wu, wd, w_sem, *scratch
):
    rows, width = h1_ref.shape
    parts, depth, hidden = wu_ref.shape[0] // 2, wu_ref.shape[1], wu_ref.shape[2]
    fb = min(256, hidden)
    n = chunks(rows)
    rc = rows // n
    g = Group(size)
    copies = []
    for z in range(parts):
        at = pl.ds(z * depth, depth)
        copies.append(pltpu.make_async_copy(wd_ref.at[layer * parts + z], wd.at[:, at], w_sem.at[z]))
        copies.append(
            pltpu.make_async_copy(wu_ref.at[layer * parts + z], wu.at[at], w_sem.at[parts + z])
        )
    copies.append(pltpu.make_async_copy(slope_ref, dup, w_sem.at[2 * parts]))
    late = [
        pltpu.make_async_copy(hid_ref, hid, w_sem.at[2 * parts + 1]),
        pltpu.make_async_copy(a2_ref, a2, w_sem.at[2 * parts + 2]),
    ]
    for copy in copies + late:
        copy.start()
    g.greet()
    gather = Gather(g, grad, rc, scratch[:4])
    scatter = Scatter(g, rc, scratch[4:])

    def send(j):
        at = span(j, rc)
        grad[g.me, at, :] = g_ref[at, :]
        gather.start(j)

    run(n, send)
    for copy in copies:
        copy.wait()

    def work(j):
        at = span(j, rc)
        gather.relay(j)
        gather.ready(j)
        held = flat(grad[:, at, :])
        for f in range(hidden // fb):
            cols = slice(f * fb, (f + 1) * fb)
            d = dg(held, wd[cols, :], NT) * flat(dup[:, at, cols]).astype(F32)
            dup[:, at, cols] = d.astype(BF).reshape(size, rc, fb)
        held = flat(dup[:, at, :])
        for z in range(parts):
            cols = slice(z * depth, (z + 1) * depth)
            scatter.part[:, at, cols] = dg(held, wu[cols, :], NT).reshape(size, rc, depth)
        scatter.first(j)
        scatter.second(j)

    run(n, work)
    for copy in late:
        copy.wait()

    def up_grad(z):
        cols = pl.ds(pl.multiple_of(z * depth, depth), depth)
        gup_ref[z] = dg(flat(a2[:, :, cols]), flat(dup[...]), TN).astype(BF)

    run(parts, up_grad)

    def down_grad(f):
        cols = pl.ds(pl.multiple_of(f * fb, fb), fb)
        r = dg(flat(hid[:, :, cols]), flat(grad[...]), TN).astype(BF)
        for z in range(parts):
            gdown_ref[z, cols, :] = r[:, z * depth : (z + 1) * depth]

    run(hidden // fb, down_grad)
    gain_out[...] = jnp.zeros_like(gain_out)

    def last(j):
        at = span(j, rc)
        dh, dgain = normed_back(h1_ref[at, :], gain_ref[layer : layer + 1, :], scatter.third(j))
        mid_ref[at, :] = g_ref[at, :].astype(F32) + dh
        gain_out[...] += dgain

    run(n, last)
    gather.drain(n)
    scatter.drain(n)


def mlp_backward(size, layer, grad, h1, gains, a2, hid, slope, wu, wd):
    rows, width = h1.shape
    depth, hidden = wu.shape[1:]
    parts = wu.shape[0] // 2
    n = chunks(rows)
    return pl.pallas_call(
        functools.partial(mlp_back_kernel, size, layer),
        out_shape=(
            shape((rows, width), F32),
            shape((1, width), F32),
            shape((parts, depth, hidden), BF),
            shape((parts, hidden, depth), BF),
        ),
        in_specs=[VM, VM, VM, HB, HB, HB, HB, HB],
        out_specs=(VM, VM, VM, VM),
        scratch_shapes=[
            pltpu.VMEM((size, rows, width), BF),
            pltpu.VMEM((size, rows, width), BF),
            pltpu.VMEM((size, rows, hidden), BF),
            pltpu.VMEM((size, rows, hidden), BF),
            pltpu.VMEM((width, hidden), BF),
            pltpu.VMEM((hidden, width), BF),
            DMA((2 * parts + 3,)),
        ]
        + comm_sems(size, n)
        + scatter_scratch(size, rows, width, n),
        compiler_params=params(6 + layer),
        cost_estimate=cost(60e9, 40e6),
    )(grad, h1, gains, a2, hid, slope, wu, wd)


def attend_back_kernel(
    size, layer, mid_ref, qkv_ref, qm_ref, km_ref, ctx_ref, lse_ref, w_ref,
    dqkv_ref, gout_ref, da, ka, va, kt, dk, dv, w, w_sem, *sems
):
    heads, _, rows, wide = qkv_ref.shape
    length = size * rows
    e = wide // 3
    scale = e**-0.5
    c = scale * math.log2(math.e)
    parts, depth = w_ref.shape[0] // 2, w_ref.shape[2]
    n = chunks(rows)
    rc = rows // n
    bq = size * rc
    kc = bq
    g = Group(size)
    copies = [
        pltpu.make_async_copy(
            w_ref.at[layer * parts + z], w.at[:, pl.ds(z * depth, depth)], w_sem.at[z]
        )
        for z in range(parts)
    ]
    for copy in copies:
        copy.start()
    g.greet()
    gather = Gather(g, da, rc, sems)

    def send(j):
        at = span(j, rc)
        da[g.me, at, :] = mid_ref[at, :].astype(BF)
        gather.start(j)

    run(n, send)
    lane = lax.broadcasted_iota(jnp.int32, (length, e), 1)
    for h in range(heads):
        whole = flat(qkv_ref[h])
        ka[h, :, :e] = whole[:, e : 2 * e]
        ka[h, :, e:] = flat(km_ref[...])
        va[h, :, :e] = whole[:, 2 * e :]
        va[h, :, e:] = jnp.where(lane < 3, 1.0, 0.0).astype(BF)
        kt[h] = whole[:, e : 2 * e].T
    dk[...] = jnp.zeros_like(dk)
    dv[...] = jnp.zeros_like(dv)
    ql = lax.broadcasted_iota(jnp.int32, (bq, e), 1)
    for copy in copies:
        copy.wait()

    def work(j):
        at = span(j, rc)
        gather.relay(j)
        gather.ready(j)
        qm = flat(qm_ref[:, at, :])
        dctx = dg(flat(da[:, at, :]), w[...], NT).astype(BF)
        ctx = flat(ctx_ref[:, at, :])
        for h in range(heads):
            qq = flat(qkv_ref[h, :, at, :])[:, :e]
            q = jnp.concatenate([qq, qm], axis=1)
            dc = dctx[:, h * e : (h + 1) * e]
            prod = dc.astype(F32) * ctx[:, h * e : (h + 1) * e].astype(F32)
            d = -jnp.sum(prod, axis=1, keepdims=True)
            d1 = d.astype(BF).astype(F32)
            d2 = (d - d1).astype(BF).astype(F32)
            d3 = d - d1 - d2
            ds_col = jnp.where(ql == 0, d1, jnp.where(ql == 1, d2, jnp.where(ql == 2, d3, 0.0)))
            dca = jnp.concatenate([dc, ds_col.astype(BF)], axis=1)
            lse = lse_ref[j, h : h + 1, :]
            dqt = None
            for k in range(length // kc):
                ks = slice(k * kc, (k + 1) * kc)
                s = dg(ka[h, ks, :], q, NT)
                p = jnp.exp2(s * c - lse)
                ds = (p * dg(va[h, ks, :], dca, NT)).astype(BF)
                dv[h, ks, :] += dg(p.astype(BF), dc, NN)
                dk[h, ks, :] += dg(ds, qq, NN)
                a = dg(kt[h, :, ks], ds, NN)
                dqt = a if dqt is None else dqt + a
            dqkv_ref[h, :, at, :e] = (dqt * scale).T.astype(BF).reshape(size, rc, e)

    run(n, work)
    for h in range(heads):
        dqkv_ref[h, :, :, e : 2 * e] = (dk[h] * scale).astype(BF).reshape(size, rows, e)
        dqkv_ref[h, :, :, 2 * e :] = dv[h].astype(BF).reshape(size, rows, e)

    def out_grad(z):
        cols = pl.ds(pl.multiple_of(z * depth, depth), depth)
        gout_ref[z] = dg(flat(ctx_ref[...]), flat(da[:, :, cols]), TN).astype(BF)

    run(parts, out_grad)
    gather.drain(n)


def attend_backward(size, layer, mid, qkv, qm, km, ctx, lse, w):
    heads, _, rows, wide = qkv.shape
    e = wide // 3
    width = mid.shape[1]
    parts, depth = w.shape[0] // 2, w.shape[2]
    length = size * rows
    n = chunks(rows)
    return pl.pallas_call(
        functools.partial(attend_back_kernel, size, layer),
        out_shape=(shape(qkv.shape, BF), shape((parts, heads * e, depth), BF)),
        in_specs=[VM] * 6 + [HB],
        out_specs=(VM, VM),
        scratch_shapes=[
            pltpu.VMEM((size, rows, width), BF),
            pltpu.VMEM((heads, length, 2 * e), BF),
            pltpu.VMEM((heads, length, 2 * e), BF),
            pltpu.VMEM((heads, e, length), BF),
            pltpu.VMEM((heads, length, e), F32),
            pltpu.VMEM((heads, length, e), F32),
            pltpu.VMEM((heads * e, width), BF),
            DMA((parts,)),
        ]
        + comm_sems(size, n),
        compiler_params=params(8 + layer),
        cost_estimate=cost(90e9, 40e6),
    )(mid, qkv, qm, km, ctx, lse, w)


def qkv_back_kernel(
    size, layer, dqkv_ref, a1_ref, x_ref, mid_ref, gain_ref, w_ref,
    dx_ref, gain_out, gqkv_ref, w, w_sem, *scratch
):
    rows, width = x_ref.shape
    heads = dqkv_ref.shape[0]
    parts, depth = w_ref.shape[0] // 2, w_ref.shape[2]
    n = chunks(rows)
    rc = rows // n
    g = Group(size)
    copies = [
        pltpu.make_async_copy(
            w_ref.at[layer * parts + z], w.at[:, pl.ds(z * depth, depth)], w_sem.at[z]
        )
        for z in range(parts)
    ]
    for copy in copies:
        copy.start()
    g.greet()
    scatter = Scatter(g, rc, scratch)
    for copy in copies:
        copy.wait()

    def work(j):
        at = span(j, rc)
        for z in range(parts):
            cols = slice(z * depth, (z + 1) * depth)
            total = None
            for h in range(heads):
                r = dg(flat(dqkv_ref[h, :, at, :]), w[h, cols, :], NT)
                total = r if total is None else total + r
            scatter.part[:, at, cols] = total.reshape(size, rc, depth)
        scatter.first(j)
        scatter.second(j)

    run(n, work)

    def qkv_grad(z):
        cols = pl.ds(pl.multiple_of(z * depth, depth), depth)
        for h in range(heads):
            gqkv_ref[z, h] = dg(flat(a1_ref[:, :, cols]), flat(dqkv_ref[h]), TN).astype(BF)

    run(parts, qkv_grad)
    gain_out[...] = jnp.zeros_like(gain_out)

    def last(j):
        at = span(j, rc)
        dh, dgain = normed_back(
            x_ref[at, :].astype(F32), gain_ref[layer : layer + 1, :], scatter.third(j)
        )
        dx_ref[at, :] = (mid_ref[at, :] + dh).astype(BF)
        gain_out[...] += dgain

    run(n, last)
    scatter.drain(n)


def qkv_backward(size, layer, dqkv, a1, x, mid, gains, w):
    rows, width = x.shape
    heads, _, _, wide = dqkv.shape
    parts, depth = w.shape[0] // 2, w.shape[2]
    n = chunks(rows)
    return pl.pallas_call(
        functools.partial(qkv_back_kernel, size, layer),
        out_shape=(
            shape((rows, width), BF),
            shape((1, width), F32),
            shape((parts, heads, depth, wide), BF),
        ),
        in_specs=[VM] * 5 + [HB],
        out_specs=(VM, VM, VM),
        scratch_shapes=[
            pltpu.VMEM((heads, width, wide), BF),
            DMA((parts,)),
        ]
        + scatter_scratch(size, rows, width, n),
        compiler_params=params(10 + layer),
        cost_estimate=cost(30e9, 30e6),
    )(dqkv, a1, x, mid, gains, w)


def scene_masks(segments, e):
    same = (segments[..., None] == jnp.arange(e, dtype=jnp.int32)).astype(F32)
    used = jnp.arange(e) < SCENES
    return (
        jnp.where(used, same * MASKED, 0.0).astype(BF),
        jnp.where(used, 1.0 - same, 0.0).astype(BF),
    )


def swap_section(value):
    return lax.ppermute(value, "section", [(0, 1), (1, 0)])


def shards(
    block_input,
    segment_ids,
    cotangent,
    norm_one_gain,
    qkv_weight,
    out_weight,
    norm_two_gain,
    up_weight,
    down_weight,
):
    section = lax.axis_index("section")
    size = lax.axis_size("tensor")

    def gather_weight(w):
        return lax.all_gather(w.astype(BF), ("section", "dp"), axis=0, tiled=False)

    w_qkv = gather_weight(jnp.swapaxes(qkv_weight[0], 0, 1))
    w_out = gather_weight(out_weight[0].reshape((-1, out_weight.shape[3])))
    w_up = gather_weight(up_weight[0])
    w_down = gather_weight(down_weight[0])
    gains_one = lax.all_gather(norm_one_gain[0], "section", axis=0, tiled=False)
    gains_two = lax.all_gather(norm_two_gain[0], "section", axis=0, tiled=False)
    segments = lax.dynamic_index_in_dim(segment_ids, section, 0, keepdims=False)
    x = lax.dynamic_index_in_dim(block_input, section, 0, keepdims=False)
    head_dim = qkv_weight.shape[3] // 3
    qm, km = scene_masks(segments.reshape((size, -1)), head_dim)
    kept = []
    ys = []
    for layer in range(2):
        qkv, a1 = qkv_forward(size, layer, x, gains_one, w_qkv)
        h1, ctx, lse = attend(size, layer, qkv, qm, km, x, w_out)
        y, a2, hid, slope = mlp_forward(size, layer, h1, gains_two, w_up, w_down)
        kept.append((x, a1, qkv, ctx, lse, h1, a2, hid, slope))
        ys.append(y)
        x = y
    other_y = swap_section(jnp.where(section == 0, ys[1], ys[0]))
    grad = lax.dynamic_index_in_dim(cotangent, section, 0, keepdims=False)
    dxs = [None, None]
    gain_sums = [None, None]
    sums = [None, None]

    def reduce_rows(value):
        return lax.psum_scatter(value, "dp", scatter_dimension=0, tiled=False)

    for layer in (1, 0):
        x, a1, qkv, ctx, lse, h1, a2, hid, slope = kept[layer]
        mid, gain_two, g_up, g_down = mlp_backward(
            size, layer, grad, h1, gains_two, a2, hid, slope, w_up, w_down
        )
        d_qkv, g_out = attend_backward(size, layer, mid, qkv, qm, km, ctx, lse, w_out)
        grad, gain_one, g_qkv = qkv_backward(size, layer, d_qkv, a1, x, mid, gains_one, w_qkv)
        dxs[layer] = grad
        gain_sums[layer] = jnp.concatenate([gain_one, gain_two], axis=0)
        sums[layer] = [reduce_rows(v) for v in (g_qkv, g_out, g_up, g_down)]
    other_dx = swap_section(jnp.where(section == 0, dxs[1], dxs[0]))

    def own_layer(mine, other):
        first = jnp.where(section == 0, mine, other)
        second = jnp.where(section == 0, other, mine)
        return jnp.stack([first, second])[None]

    layer_out = own_layer(jnp.where(section == 0, ys[0], ys[1]), other_y)
    input_out = own_layer(jnp.where(section == 0, dxs[0], dxs[1]), other_dx)

    def finish(zero, one):
        send = swap_section(jnp.where(section == 0, one, zero))
        return jnp.where(section == 0, zero, one).astype(F32) + send.astype(F32)

    qkv_grad, out_grad, up_grad, down_grad = [finish(a, b) for a, b in zip(sums[0], sums[1])]
    gains = lax.psum(jnp.stack(gain_sums), ("section", "dp", "tensor"))
    gains = lax.dynamic_index_in_dim(gains, section, 0, keepdims=False)
    return (
        layer_out,
        input_out,
        gains[0][None],
        jnp.swapaxes(qkv_grad, 0, 1)[None],
        out_grad.reshape(out_weight.shape),
        gains[1][None],
        up_grad[None],
        down_grad[None],
    )


def solution(mesh):
    return jax.shard_map(
        shards,
        mesh=mesh,
        in_specs=(
            P(None, ("dp", "tensor"), None),
            P(None, "dp"),
            P(None, ("dp", "tensor"), None),
            P("section", None),
            P("section", "dp", "tensor", None),
            P("section", "tensor", None, "dp"),
            P("section", None),
            P("section", "dp", "tensor"),
            P("section", "tensor", "dp"),
        ),
        out_specs=(
            P("section", None, ("dp", "tensor"), None),
            P("section", None, ("dp", "tensor"), None),
            P("section", None),
            P("section", "dp", "tensor", None),
            P("section", "tensor", None, "dp"),
            P("section", None),
            P("section", "dp", "tensor"),
            P("section", "tensor", "dp"),
        ),
        check_vma=False,
    )
```

time: 1560 us -> 1070 us (0.69)
  waiting for transfers between devices: 964 us -> 334 us
  Pallas kernels: 179 us -> 575 us
  matrix products: 184 us -> 0 us
  other arithmetic: 74.4 us -> 27.8 us
  local copies, waits for them, and re-layouts: 57 us -> 12.6 us
  blocking collectives: 62.5 us -> 91.5 us
    pallas_call x4 -> x12, Pallas kernels: 179 us -> 575 us  [the longest x2 138 us: attend_backward(): pl.pallas_call(functools.partial(attend_back_kernel, size, layer), out_sh...]
    all_gather x12 -> x4, waiting for transfers between devices: 459 us -> 147 us  [gather_weight(): return lax.all_gather(w.astype(BF), ('section', 'dp'), axis=0, tiled=False)]
    reduce_scatter x16 -> x8, waiting for transfers between devices: 481 us -> 175 us  [reduce_rows(): return lax.psum_scatter(value, 'dp', scatter_dimension=0, tiled=False)]
    dot_general x22 -> x0, matrix products: 171 us -> none  [the longest x18 134 us: ein(): return jnp.einsum(spec, a, b, preferred_element_type=F32)]
    psum x1, blocking collectives: 52.9 us -> 81.9 us  [shards(): gains = lax.psum(jnp.stack(gain_sums), ('section', 'dp', 'tensor'))]
    reduce_sum x12 -> x0, other arithmetic: 18.8 us -> none  [the longest x4 11.4 us: norm_back(): return (dh, jnp.sum(grad * n, axis=0))]
    convert_element_type x4 -> x0, local copies, waits for them, and re-layouts: 16.5 us -> none  [the longest x2 12.1 us: shards(): qkv = ein('sd,dhe->hse', a1, wq).astype(BF)]
    convert_element_type x13 -> x4, other arithmetic: 22.8 us -> 6.67 us  [gather_weight(): return lax.all_gather(w.astype(BF), ('section', 'dp'), axis=0, tiled=False)]
  transfers between devices with their start and end apart: 34 -> 18, of which waited for: 25 -> 9; matrix products, arithmetic and copies ran while one was open for 11% -> 3% of each run, Pallas kernels for 4% -> 11%
where the time goes in v2:
time: 1070 us; the launch traced here: 1060 us
  Pallas kernels  575 us (54%)
  waiting for transfers between devices  334 us (31%)
  blocking collectives  91.5 us (9%)
  other arithmetic  27.8 us (3%)
  between operations  15 us (1%)
  local copies, waits for them, and re-layouts  12.6 us (1%)
    reduce_scatter x8, waiting for transfers between devices, reduce_rows(): return lax.psum_scatter(value, 'dp', scatter_dimension=0, tiled=False)  175 us
    all_gather x4, waiting for transfers between devices, gather_weight(): return lax.all_gather(w.astype(BF), ('section', 'dp'), axis=0, tiled=False)  147 us
    pallas_call x2, Pallas kernels, attend_backward(): pl.pallas_call(functools.partial(attend_back_kernel, size, layer), out_sh...  138 us
    pallas_call x2, Pallas kernels, mlp_backward(): pl.pallas_call(functools.partial(mlp_back_kernel, size, layer), out_shape...  107 us
    pallas_call x2, Pallas kernels, mlp_forward(): pl.pallas_call(functools.partial(mlp_kernel, size, layer), out_shape=(sha...  102 us
    pallas_call x2, Pallas kernels, attend(): pl.pallas_call(functools.partial(attend_kernel, size, layer), out_shape=(...  98.1 us
    psum x1, blocking collectives, shards(): gains = lax.psum(jnp.stack(gain_sums), ('section', 'dp', 'tensor'))  81.9 us
    pallas_call x2, Pallas kernels, qkv_backward(): pl.pallas_call(functools.partial(qkv_back_kernel, size, layer), out_shape...  67.9 us
  transfers between devices with their start and end apart: 18, of which 9 were waited for; matrix products, arithmetic and copies ran while one was open for 3% of the time, Pallas kernels for 11%

profile of v2, /device:TPU:0, one launch (start us, length us, event | category | flops | bytes accessed | tf_op | source)
XLA Modules:
  0.0 1064.6 jit_solution(10142623812838746025)
XLA Ops:
  7.2 2.1 convert_bitcast_fusion
  9.4 1.6 convert_element_type.81
  11.1 0.0 all-gather.10.cloned.1.call-start
  11.1 0.9 convert_element_type.83
  12.0 0.0 all-gather.12.cloned.1.call-start
  12.1 2.1 convert_element_type.84
  14.3 5.3 all-gather.1
  19.5 0.6 copy.26
  20.1 1.0 dynamic-slice_bitcast_fusion.1.x_ref
  21.2 4.4 all-gather.2
  25.6 0.6 copy.25
  26.2 2.3 dynamic-slice_bitcast_fusion.g_ref
  28.5 1.2 select_convert_fusion
  29.7 43.6 %all-gather.14.cloned.1.call-done = bf16[32,256,192]{1,2,0:T(8,128)(2,1)} async-done(((bf16[4,256,192]{1,2,0:T(8,128)(2,1)}), bf16[32,256,192]{1,2,0:T(8,128)(2,1)}) %all-gather.14.cloned.1.call-update) | async-done | bytes 3145744 | tf_op jit(solution)/shard_map/all_gather | solution.py:857
  73.3 6.2 copy.19
  79.5 31.7 %shard_map.152 = (bf16[4,4,512,192]{3,2,1,0:T(8,128)(2,1)}, bf16[4,512,1024]{2,1,0:T(8,128)(2,1)}) custom-call(bf16[512,1024]{1,0:T(8,128)(2,1)} %dynamic-slice_bitcast_fusion.1.x_ref, f32[2,1024]{1,0:T(2,128)} %bitcast.73, bf16[8,4,256,192]{3,2,1,0:T(8,128)(2,1)} %bitcast.67), custom_call_target="tpu_custom_call" | custom-call | flops 20000000000 | bytes 30000000 | tf_op jit(solution)/shard_map/pallas_call | solution.py:290
  111.1 3.6 all-gather.8.cloned.1.call-done.w_ref
  114.7 48.3 %shard_map.153 = (f32[512,1024]{1,0:T(8,128)}, bf16[4,512,256]{2,1,0:T(8,128)(2,1)}, f32[4,4,512]{2,1,0:T(4,128)}) custom-call(bf16[4,4,512,192]{3,2,1,0:T(8,128)(2,1)} %get-tuple-element.44.qkv_ref, bf16[4,512,64]{2,1,0:T(8,128)(2,1)} %get-tuple-element.103.qm_ref, bf16[4,512,64]{2,1,0:T(8,128)(2,1)} %get-tuple-element.102.km_ref, ...), custom_call_target="tpu_custom_call" | custom-call | flops 60000002048 | bytes 20000000 | tf_op jit(solution)/shard_map/pallas_call | solution.py:389
  163.0 26.5 %all-gather.10.cloned.1.call-done.wu_ref = bf16[8,256,1024]{2,1,0:T(8,128)(2,1)} async-done(((bf16[1,256,1024]{2,1,0:T(8,128)(2,1)}), bf16[8,256,1024]{2,1,0:T(8,128)(2,1)}) %all-gather.10.cloned.1.call-update) | async-done | bytes 4194320 | tf_op jit(solution)/shard_map/all_gather | solution.py:857
  189.6 73.7 %all-gather.12.cloned.1.call-done.wd_ref = bf16[8,1024,256]{2,1,0:T(8,128)(2,1)} async-done(((bf16[1,1024,256]{2,1,0:T(8,128)(2,1)}), bf16[8,1024,256]{2,1,0:T(8,128)(2,1)}) %all-gather.12.cloned.1.call-update) | async-done | bytes 4194320 | tf_op jit(solution)/shard_map/all_gather | solution.py:857
  263.2 51.3 %shard_map.154 = (bf16[512,1024]{1,0:T(8,128)(2,1)}, bf16[4,512,1024]{2,1,0:T(8,128)(2,1)}, bf16[4,512,1024]{2,1,0:T(8,128)(2,1)}, bf16[4,512,1024]{2,1,0:T(8,128)(2,1)}) custom-call(f32[512,1024]{1,0:T(8,128)} %get-tuple-element.45.h1_ref, f32[2,1024]{1,0:T(2,128)} %bitcast.77, bf16[8,256,1024]{2,1,0:T(8,128)(2,1)} %all-gather.10.cloned.1.call-done.wu_ref, ...), custom_call_target="tpu_custom_call" | custom-call | flops 49999998976 | bytes 30000000 | tf_op jit(solution)/shard_map/pallas_call | solution.py:489
  314.5 30.3 %shard_map.155 = (bf16[4,4,512,192]{3,2,1,0:T(8,128)(2,1)}, bf16[4,512,1024]{2,1,0:T(8,128)(2,1)}) custom-call(bf16[512,1024]{1,0:T(8,128)(2,1)} %get-tuple-element.46.x_ref, f32[2,1024]{1,0:T(2,128)} %bitcast.74, bf16[8,4,256,192]{3,2,1,0:T(8,128)(2,1)} %bitcast.68), custom_call_target="tpu_custom_call" | custom-call | flops 20000000000 | bytes 30000000 | tf_op jit(solution)/shard_map/pallas_call | solution.py:290
  344.8 49.8 %shard_map.156 = (f32[512,1024]{1,0:T(8,128)}, bf16[4,512,256]{2,1,0:T(8,128)(2,1)}, f32[4,4,512]{2,1,0:T(4,128)}) custom-call(bf16[4,4,512,192]{3,2,1,0:T(8,128)(2,1)} %get-tuple-element.47.qkv_ref, bf16[4,512,64]{2,1,0:T(8,128)(2,1)} %get-tuple-element.103.qm_ref, bf16[4,512,64]{2,1,0:T(8,128)(2,1)} %get-tuple-element.102.km_ref, ...), custom_call_target="tpu_custom_call" | custom-call | flops 60000002048 | bytes 20000000 | tf_op jit(solution)/shard_map/pallas_call | solution.py:389
  394.7 50.9 %shard_map.157 = (bf16[512,1024]{1,0:T(8,128)(2,1)}, bf16[4,512,1024]{2,1,0:T(8,128)(2,1)}, bf16[4,512,1024]{2,1,0:T(8,128)(2,1)}, bf16[4,512,1024]{2,1,0:T(8,128)(2,1)}) custom-call(f32[512,1024]{1,0:T(8,128)} %get-tuple-element.48.h1_ref, f32[2,1024]{1,0:T(2,128)} %bitcast.78, bf16[8,256,1024]{2,1,0:T(8,128)(2,1)} %all-gather.10.cloned.1.call-done.wu_ref, ...), custom_call_target="tpu_custom_call" | custom-call | flops 49999998976 | bytes 30000000 | tf_op jit(solution)/shard_map/pallas_call | solution.py:489
  445.6 53.2 %shard_map.158 = (f32[512,1024]{1,0:T(8,128)}, f32[1,1024]{1,0:T(1,128)}, bf16[4,256,1024]{2,1,0:T(8,128)(2,1)}, bf16[4,1024,256]{2,1,0:T(8,128)(2,1)}) custom-call(bf16[512,1024]{1,0:T(8,128)(2,1)} %dynamic-slice_bitcast_fusion.g_ref, f32[512,1024]{1,0:T(8,128)} %get-tuple-element.48.h1_ref, f32[2,1024]{1,0:T(2,128)} %bitcast.79, ...), custom_call_target="tpu_custom_call" | custom-call | flops 60000002048 | bytes 40000000 | tf_op jit(solution)/shard_map/pallas_call | solution.py:604
  498.8 69.2 %shard_map.159 = (bf16[4,4,512,192]{3,2,1,0:T(8,128)(2,1)}, bf16[4,256,256]{2,1,0:T(8,128)(2,1)}) custom-call(f32[512,1024]{1,0:T(8,128)} %get-tuple-element.53.mid_ref, bf16[4,4,512,192]{3,2,1,0:T(8,128)(2,1)} %get-tuple-element.47.qkv_ref, bf16[4,512,64]{2,1,0:T(8,128)(2,1)} %get-tuple-element.103.qm_ref, bf16[4,512,64]{2,1,0:T(8,128)(2,1)} %get-tuple-element.102.km_ref, ...), custom_call_target="tpu_custom_call" | custom-call | flops 89999998976 | bytes 40000000 | tf_op jit(solution)/shard_map/pallas_call | solution.py:727
  568.0 33.4 %shard_map.160 = (bf16[512,1024]{1,0:T(8,128)(2,1)}, f32[1,1024]{1,0:T(1,128)}, bf16[4,4,256,192]{3,2,1,0:T(8,128)(2,1)}) custom-call(bf16[4,4,512,192]{3,2,1,0:T(8,128)(2,1)} %get-tuple-element.56.dqkv_ref, bf16[4,512,1024]{2,1,0:T(8,128)(2,1)} %get-tuple-element.57.a1_ref, bf16[512,1024]{1,0:T(8,128)(2,1)} %get-tuple-element.46.x_ref, ...), custom_call_target="tpu_custom_call" | custom-call | flops 30000001024 | bytes 30000000 | tf_op jit(solution)/shard_map/pallas_call | solution.py:810
  601.4 53.8 %shard_map.161 = (f32[512,1024]{1,0:T(8,128)}, f32[1,1024]{1,0:T(1,128)}, bf16[4,256,1024]{2,1,0:T(8,128)(2,1)}, bf16[4,1024,256]{2,1,0:T(8,128)(2,1)}) custom-call(bf16[512,1024]{1,0:T(8,128)(2,1)} %get-tuple-element.58.g_ref, f32[512,1024]{1,0:T(8,128)} %get-tuple-element.45.h1_ref, f32[2,1024]{1,0:T(2,128)} %bitcast.80, ...), custom_call_target="tpu_custom_call" | custom-call | flops 60000002048 | bytes 40000000 | tf_op jit(solution)/shard_map/pallas_call | solution.py:604
  655.2 69.0 %shard_map.162 = (bf16[4,4,512,192]{3,2,1,0:T(8,128)(2,1)}, bf16[4,256,256]{2,1,0:T(8,128)(2,1)}) custom-call(f32[512,1024]{1,0:T(8,128)} %get-tuple-element.62.mid_ref, bf16[4,4,512,192]{3,2,1,0:T(8,128)(2,1)} %get-tuple-element.44.qkv_ref, bf16[4,512,64]{2,1,0:T(8,128)(2,1)} %get-tuple-element.103.qm_ref, bf16[4,512,64]{2,1,0:T(8,128)(2,1)} %get-tuple-element.102.km_ref, ...), custom_call_target="tpu_custom_call" | custom-call | flops 89999998976 | bytes 40000000 | tf_op jit(solution)/shard_map/pallas_call | solution.py:727
  724.3 0.5 reduce-scatter.15.cloned.1.call-update
  724.9 34.5 %shard_map.163 = (bf16[512,1024]{1,0:T(8,128)(2,1)}, f32[1,1024]{1,0:T(1,128)}, bf16[4,4,256,192]{3,2,1,0:T(8,128)(2,1)}) custom-call(bf16[4,4,512,192]{3,2,1,0:T(8,128)(2,1)} %get-tuple-element.65.dqkv_ref, bf16[4,512,1024]{2,1,0:T(8,128)(2,1)} %get-tuple-element.66.a1_ref, bf16[512,1024]{1,0:T(8,128)(2,1)} %dynamic-slice_bitcast_fusion.1.x_ref, ...), custom_call_target="tpu_custom_call" | custom-call | flops 30000001024 | bytes 30000000 | tf_op jit(solution)/shard_map/pallas_call | solution.py:810
  759.5 0.7 reduce-scatter.11.cloned.1.call-update
  760.2 0.7 reduce-scatter.21.cloned.1.call-update
  761.0 0.5 reduce-scatter.23.cloned.1.call-update
  761.6 0.7 reduce-scatter.17.cloned.1.call-update
  762.3 0.5 reduce-scatter.19.cloned.1.call-update
  762.9 1.1 broadcast_select_fusion
  764.0 1.9 collective-permute-start.1
  765.8 1.1 broadcast_select_fusion.2
  766.9 0.2 collective-permute-start
  767.2 81.9 %psum.7 = f32[2,2,1024]{2,1,0:T(2,128)S(1)} all-reduce(f32[2,2,1024]{2,1,0:T(2,128)S(1)} %pad_maximum_fusion), channel_id=1, replica_groups=mesh['section'=2,'dp'=4,'tensor'=4] {'section','dp','tensor'}, use_global_device_ids=true, to_apply=%region_0.1 | all-reduce | flops 4096 | bytes 32768 | tf_op jit(solution)/shard_map/psum | solution.py:912
  849.1 0.6 dynamic-slice_bitcast_fusion.2
  849.8 0.9 select_bitcast_fusion.7
  850.7 2.4 collective-permute-start.3
  853.1 1.7 select_bitcast_fusion.1
  854.8 1.5 maximum_bitcast_fusion.1
  856.3 1.4 select_bitcast_fusion.3
  857.7 1.5 maximum_bitcast_fusion
  859.2 0.8 convert_add_fusion.3
  860.0 1.2 select_bitcast_fusion.6
  861.2 0.1 collective-permute-start.2
  861.3 41.6 %reduce-scatter.21.cloned.1.call-done = bf16[1,1024,256]{2,1,0:T(8,128)(2,1)} async-done(((bf16[4,1024,256]{2,1,0:T(8,128)(2,1)}), bf16[1,1024,256]{2,1,0:T(8,128)(2,1)}) %reduce-scatter.21.cloned.1.call-update) | async-done | bytes 524304 | tf_op jit(solution)/shard_map/reduce_scatter | solution.py:885
  902.9 45.5 %reduce-scatter.23.cloned.1.call-done = bf16[1,1024,256]{2,1,0:T(8,128)(2,1)} async-done(((bf16[4,1024,256]{2,1,0:T(8,128)(2,1)}), bf16[1,1024,256]{2,1,0:T(8,128)(2,1)}) %reduce-scatter.23.cloned.1.call-update) | async-done | bytes 524304 | tf_op jit(solution)/shard_map/reduce_scatter | solution.py:885
  948.3 1.9 select_bitcast_fusion.4
  950.2 1.5 collective-permute-start.5
  951.7 42.1 %reduce-scatter.17.cloned.1.call-done = bf16[1,256,1024]{2,1,0:T(8,128)(2,1)} async-done(((bf16[4,256,1024]{2,1,0:T(8,128)(2,1)}), bf16[1,256,1024]{2,1,0:T(8,128)(2,1)}) %reduce-scatter.17.cloned.1.call-update) | async-done | bytes 524304 | tf_op jit(solution)/shard_map/reduce_scatter | solution.py:885
  993.8 45.5 %reduce-scatter.19.cloned.1.call-done = bf16[1,256,1024]{2,1,0:T(8,128)(2,1)} async-done(((bf16[4,256,1024]{2,1,0:T(8,128)(2,1)}), bf16[1,256,1024]{2,1,0:T(8,128)(2,1)}) %reduce-scatter.19.cloned.1.call-update) | async-done | bytes 524304 | tf_op jit(solution)/shard_map/reduce_scatter | solution.py:885
  1039.3 1.9 select_bitcast_fusion.5
  1041.2 1.5 collective-permute-start.4
  1042.7 0.2 fusion.2
  1042.9 1.2 copy.20
  1044.1 2.4 fusion
  1046.5 8.5 collective-permute-done.4
  1055.0 2.3 fusion.1
  (69 shorter events, 0.7 us)
Async XLA Ops:
  7.2 13.0 %copy-start = (bf16[2,512,1024]{2,1,0:T(8,128)(2,1)S(1)}, bf16[2,512,1024]{2,1,0:T(8,128)(2,1)}, u32[]{:S(2)}) copy-start(bf16[2,512,1024]{2,1,0:T(8,128)(2,1)} %param.9) | copy-start | bytes 6291460
  7.2 3.9 copy-start.9
  7.2 66.1 %all-gather.14.cloned.1.call-start = ((), (), s32[]{:S(2)}) async-start(), calls=%async_computation.19 | async-start | bytes 3538944 | tf_op jit(solution)/shard_map/all_gather | solution.py:857
  9.4 105.3 %all-gather.8.cloned.1.call-start = ((), (), s32[]{:S(2)}) async-start(), calls=%async_computation.8 | async-start | bytes 1179648 | tf_op jit(solution)/shard_map/all_gather | solution.py:857
  11.1 3.2 copy-start.12
  11.1 178.5 %all-gather.10.cloned.1.call-start = ((), (), s32[]{:S(2)}) async-start(), calls=%async_computation.9 | async-start | bytes 4718592 | tf_op jit(solution)/shard_map/all_gather | solution.py:857
  12.0 9.2 copy-start.14
  12.0 9.2 copy-start.13
  12.0 251.2 %all-gather.12.cloned.1.call-start = ((), (), s32[]{:S(2)}) async-start(), calls=%async_computation.10 | async-start | bytes 4718592 | tf_op jit(solution)/shard_map/all_gather | solution.py:857
  14.2 835.6 %reduce-scatter.13.cloned.1.call-start = ((), (), s32[]{:S(2)}) async-start(), calls=%async_computation.13 | async-start | bytes 655360 | tf_op jit(solution)/shard_map/reduce_scatter | solution.py:885
  724.3 125.5 %reduce-scatter.15.cloned.1.call-start = ((), (), s32[]{:S(2)}) async-start(), calls=%async_computation.14 | async-start | bytes 655360 | tf_op jit(solution)/shard_map/reduce_scatter | solution.py:885
  724.9 135.1 %reduce-scatter.9.cloned.1.call-start = ((), (), s32[]{:S(2)}) async-start(), calls=%async_computation.11 | async-start | bytes 2621440 | tf_op jit(solution)/shard_map/reduce_scatter | solution.py:885
  759.4 100.6 %reduce-scatter.11.cloned.1.call-start = ((), (), s32[]{:S(2)}) async-start(), calls=%async_computation.12 | async-start | bytes 2621440 | tf_op jit(solution)/shard_map/reduce_scatter | solution.py:885
  760.2 142.7 %reduce-scatter.21.cloned.1.call-start = ((), (), s32[]{:S(2)}) async-start(), calls=%async_computation.17 | async-start | bytes 2621440 | tf_op jit(solution)/shard_map/reduce_scatter | solution.py:885
  760.9 187.4 %reduce-scatter.23.cloned.1.call-start = ((), (), s32[]{:S(2)}) async-start(), calls=%async_computation.18 | async-start | bytes 2621440 | tf_op jit(solution)/shard_map/reduce_scatter | solution.py:885
  761.5 232.3 %reduce-scatter.17.cloned.1.call-start = ((), (), s32[]{:S(2)}) async-start(), calls=%async_computation.15 | async-start | bytes 2621440 | tf_op jit(solution)/shard_map/reduce_scatter | solution.py:885
  761.6 1.3 copy-start.4
  762.2 277.1 %reduce-scatter.19.cloned.1.call-start = ((), (), s32[]{:S(2)}) async-start(), calls=%async_computation.16 | async-start | bytes 2621440 | tf_op jit(solution)/shard_map/reduce_scatter | solution.py:885
  762.8 3.0 copy-start.2
  762.8 3.0 copy-start.3
  764.0 3.2 copy-start.17
  764.0 3.2 copy-start.18
  764.0 3.2 copy-start.15
  764.0 3.2 copy-start.16
  764.0 89.1 %collective-permute-start.1 = (bf16[512,1024]{1,0:T(8,128)(2,1)}, bf16[512,1024]{1,0:T(8,128)(2,1)}, u32[]{:S(2)}, u32[]{:S(2)}) collective-permute-start(bf16[512,1024]{1,0:T(8,128)(2,1)} %broadcast_select_fusion), channel_id=1, source_target_pairs={{0,16},{16,0},{1,17},{17,1},{2,18},{18,2},{3,19},{19,3},{4,20},{20... | collective-permute-start | bytes 3145736 | tf_op jit(solution)/shard_map/ppermute | solution.py:839
  766.9 89.4 %collective-permute-start = (bf16[512,1024]{1,0:T(8,128)(2,1)}, bf16[512,1024]{1,0:T(8,128)(2,1)}, u32[]{:S(2)}, u32[]{:S(2)}) collective-permute-start(bf16[512,1024]{1,0:T(8,128)(2,1)} %broadcast_select_fusion.2), channel_id=1, source_target_pairs={{0,16},{16,0},{1,17},{17,1},{2,18},{18,2},{3,19},{19,3},{4,20},{20... | collective-permute-start | bytes 3145736 | tf_op jit(solution)/shard_map/ppermute | solution.py:839
  850.7 8.6 collective-permute-start.3
  857.7 1.5 copy-start.10
  857.7 1.5 copy-start.11
  860.0 182.7 %copy-start.5 = (bf16[1,4,256,192]{3,2,1,0:T(8,128)(2,1)S(1)}, bf16[1,4,256,192]{3,2,1,0:T(8,128)(2,1)}, u32[]{:S(2)}) copy-start(bf16[1,4,256,192]{3,2,1,0:T(8,128)(2,1)} %reduce-scatter.9.cloned.1.call-done) | copy-start | bytes 1179652
  860.0 182.7 %copy-start.6 = (bf16[1,4,256,192]{3,2,1,0:T(8,128)(2,1)S(1)}, bf16[1,4,256,192]{3,2,1,0:T(8,128)(2,1)}, u32[]{:S(2)}) copy-start(bf16[1,4,256,192]{3,2,1,0:T(8,128)(2,1)} %reduce-scatter.11.cloned.1.call-done) | copy-start | bytes 1179652
  861.2 181.5 %collective-permute-start.2 = (bf16[4,256,192]{2,1,0:T(8,128)(2,1)S(1)}, bf16[4,256,192]{2,1,0:T(8,128)(2,1)S(1)}, u32[]{:S(2)}, u32[]{:S(2)}) collective-permute-start(bf16[4,256,192]{2,1,0:T(8,128)(2,1)S(1)} %select_bitcast_fusion.6), channel_id=1, source_target_pairs={{0,16},{16,0},{1,17},{17,1},{2,18},{18,2},{3,19},{19,3},{4,20},{20... | collective-permute-start | bytes 1179656 | tf_op jit(solution)/shard_map/ppermute | solution.py:839
  950.2 93.9 %collective-permute-start.5 = (bf16[1024,256]{1,0:T(8,128)(2,1)}, bf16[1024,256]{1,0:T(8,128)(2,1)}, u32[]{:S(2)}, u32[]{:S(2)}) collective-permute-start(bf16[1024,256]{1,0:T(8,128)(2,1)} %select_bitcast_fusion.4), channel_id=1, source_target_pairs={{0,16},{16,0},{1,17},{17,1},{2,18},{18,2},{3,19},{19,3},{4,20},{20... | collective-permute-start | bytes 1572872 | tf_op jit(solution)/shard_map/ppermute | solution.py:839
  1041.2 13.8 %collective-permute-start.4 = (bf16[256,1024]{1,0:T(8,128)(2,1)}, bf16[256,1024]{1,0:T(8,128)(2,1)}, u32[]{:S(2)}, u32[]{:S(2)}) collective-permute-start(bf16[256,1024]{1,0:T(8,128)(2,1)} %select_bitcast_fusion.5), channel_id=1, source_target_pairs={{0,16},{16,0},{1,17},{17,1},{2,18},{18,2},{3,19},{19,3},{4,20},{20... | collective-permute-start | bytes 1572872 | tf_op jit(solution)/shard_map/ppermute | solution.py:839
  1042.9 14.4 %copy-start.1 = (bf16[2,512,1024]{2,1,0:T(8,128)(2,1)S(1)}, bf16[2,512,1024]{2,1,0:T(8,128)(2,1)}, u32[]{:S(2)}) copy-start(bf16[2,512,1024]{2,1,0:T(8,128)(2,1)} %param.9) | copy-start | bytes 6291460
  1044.1 10.9 %copy-start.7 = (bf16[1,256,1024]{2,1,0:T(8,128)(2,1)S(1)}, bf16[1,256,1024]{2,1,0:T(8,128)(2,1)}, u32[]{:S(2)}) copy-start(bf16[1,256,1024]{2,1,0:T(8,128)(2,1)} %reduce-scatter.17.cloned.1.call-done) | copy-start | bytes 1572868
  1044.1 10.9 %copy-start.8 = (bf16[1,256,1024]{2,1,0:T(8,128)(2,1)S(1)}, bf16[1,256,1024]{2,1,0:T(8,128)(2,1)}, u32[]{:S(2)}) copy-start(bf16[1,256,1024]{2,1,0:T(8,128)(2,1)} %reduce-scatter.19.cloned.1.call-done) | copy-start | bytes 1572868
Sparse Core Ops, SparseCore 0:
  10.1 63.1 all-gather.13
  76.0 38.6 all-gather.7
  117.4 72.1 all-gather.9
  191.5 71.6 all-gather.11
  724.4 19.9 reduce-scatter.12
  746.5 19.9 reduce-scatter.14
  768.7 42.0 reduce-scatter.8
  813.3 44.0 reduce-scatter.10
  859.7 43.1 reduce-scatter.20
  905.1 43.1 reduce-scatter.22
  950.6 43.1 reduce-scatter.16
  996.1 43.1 reduce-scatter.18

commit v3 on v2

--- a/solution.py
+++ b/solution.py
@@ -49,14 +49,17 @@
     def behind(self, k):
         return lax.rem(self.chip + self.chips - k, self.chips)
 
-    def greet(self):
+    def greet(self, replicas=0):
         barrier = pltpu.get_barrier_semaphore()
         targets = [self.sibling] + [self.ahead(k) * 2 + self.core for k in range(1, self.chips)]
+        targets = [{"tensor": target} for target in targets]
+        if replicas:
+            d = lax.axis_index("dp")
+            targets += [{"dp": lax.rem(d + k, replicas)} for k in range(1, replicas)]
+            targets += [{"section": 1 - lax.axis_index("section")}]
         for target in targets:
-            pl.semaphore_signal(
-                barrier, inc=1, device_id={"tensor": target}, device_id_type=MESH
-            )
-        pl.semaphore_wait(barrier, self.chips)
+            pl.semaphore_signal(barrier, inc=1, device_id=target, device_id_type=MESH)
+        pl.semaphore_wait(barrier, len(targets))
 
 
 def remote(src, dst, send, recv, target):
@@ -200,6 +203,123 @@
         lax.fori_loop(0, n, one, 0)
 
 
+class Spread:
+    def __init__(self, src, dst, by_columns, sems):
+        self.src, self.dst, self.by_columns = src, dst, by_columns
+        self.own_sem, self.far_send, self.far_recv, self.side_send, self.side_recv = sems
+        self.replicas = far = self.side_send.shape[0]
+        self.s = lax.axis_index("section")
+        self.d = lax.axis_index("dp")
+        self.stages = [
+            sorted({k, far - k}) for k in range(1, far // 2 + 1)
+        ]
+
+    def place(self, half, z):
+        rows, cols = self.src.shape
+        if self.by_columns:
+            return self.dst.at[
+                pl.ds(pl.multiple_of(half * rows, rows), rows),
+                pl.ds(pl.multiple_of(z * cols, cols), cols),
+            ]
+        return self.dst.at[pl.ds(pl.multiple_of((2 * z + half) * rows, rows), rows)]
+
+    def origin(self, k):
+        return lax.rem(self.d + self.replicas - k, self.replicas)
+
+    def own(self):
+        return pltpu.make_async_copy(self.src, self.place(self.s, self.d), self.own_sem.at[0])
+
+    def far(self, k, origin):
+        return pltpu.make_async_remote_copy(
+            src_ref=self.src,
+            dst_ref=self.place(self.s, origin),
+            send_sem=self.far_send.at[k - 1],
+            recv_sem=self.far_recv.at[k - 1],
+            device_id={"dp": lax.rem(self.d + k, self.replicas)},
+            device_id_type=MESH,
+        )
+
+    def side(self, k, half):
+        place = self.place(half, self.origin(k))
+        return pltpu.make_async_remote_copy(
+            src_ref=self.src if k == 0 else place,
+            dst_ref=place,
+            send_sem=self.side_send.at[k],
+            recv_sem=self.side_recv.at[k],
+            device_id={"section": 1 - self.s},
+            device_id_type=MESH,
+        )
+
+    def start(self):
+        for k in self.stages[0]:
+            self.far(k, self.d).start()
+        self.side(0, self.s).start()
+        self.own().start()
+
+    def step(self, i):
+        for k in self.stages[i]:
+            self.far(k, self.origin(k)).wait_recv()
+            self.side(k, self.s).start()
+        if i + 1 < len(self.stages):
+            for k in self.stages[i + 1]:
+                self.far(k, self.d).start()
+
+    def finish(self):
+        self.own().wait()
+        for k in range(self.replicas):
+            self.side(k, 1 - self.s).wait_recv()
+        for k in range(1, self.replicas):
+            self.far(k, self.d).wait_send()
+        for k in range(self.replicas):
+            self.side(k, self.s).wait_send()
+
+
+def rider_sems(replicas):
+    far, side = DMA((replicas - 1,)), DMA((replicas,))
+    return [DMA((1,)), far, far, side, side]
+
+
+class Riders:
+    def __init__(self, srcs, dsts, columns, sems):
+        self.all = [
+            Spread(src, dst, by, sems[5 * i : 5 * i + 5])
+            for i, (src, dst, by) in enumerate(zip(srcs, dsts, columns))
+        ]
+        self.replicas = self.all[0].replicas if self.all else 0
+
+    def start(self):
+        for one in self.all:
+            one.start()
+
+    def step(self, j, n):
+        if not self.all:
+            return
+        stages = len(self.all[0].stages)
+        for i in range(stages):
+
+            @pl.when(j == n * (i + 1) // stages - 1)
+            def _(i=i):
+                for one in self.all:
+                    one.step(i)
+
+    def finish(self):
+        for one in self.all:
+            one.finish()
+
+
+def riding(riders, replicas):
+    halves = [half for half, _ in riders]
+    columns = tuple(by for _, by in riders)
+    outs = []
+    for half, by in riders:
+        rows, cols = half.shape
+        outs.append(
+            shape((2 * rows, replicas * cols) if by else (2 * replicas * rows, cols), BF)
+        )
+    sems = rider_sems(replicas) * len(riders)
+    return halves, columns, outs, sems
+
+
 def params(key):
     return pltpu.CompilerParams(
         vmem_limit_bytes=LIMIT, collective_id=key, has_side_effects=True
@@ -237,25 +357,32 @@
     lax.fori_loop(0, n, one, 0)
 
 
-def qkv_kernel(
-    size, layer, x_ref, gain_ref, w_ref, qkv_ref, a1_out, a1, w, w_sem, out_sem, *sems
-):
+def qkv_kernel(size, layer, columns, fresh, *refs):
+    m = len(columns)
+    x_ref, gain_ref, w_ref = refs[:3]
+    halves, refs = refs[3 : 3 + m], refs[3 + m :]
+    qkv_ref, a1_out = refs[:2]
+    wholes, refs = refs[2 : 2 + m], refs[2 + m :]
+    if fresh:
+        w_out, refs = refs[0], refs[1:]
+    a1, w, w_sem, out_sem = refs[:4]
+    sems, refs = refs[4:8], refs[8:]
+    if fresh:
+        spread_w, refs = Spread(w_ref, w, False, refs[:5]), refs[5:]
+    riders = Riders(halves, wholes, columns, refs)
     rows, width = x_ref.shape
-    heads = qkv_ref.shape[0]
-    parts, depth = w_ref.shape[0] // 2, w_ref.shape[2]
     n = chunks(rows)
     rc = rows // n
     g = Group(size)
-    copies = [
-        pltpu.make_async_copy(
-            w_ref.at[layer * parts + z], w.at[:, pl.ds(z * depth, depth)], w_sem.at[z]
-        )
-        for z in range(parts)
-    ]
-    for copy in copies:
+    if not fresh:
+        copy = pltpu.make_async_copy(w_ref, w, w_sem.at[0])
         copy.start()
-    g.greet()
+    else:
+        riders.all.insert(0, spread_w)
+        riders.replicas = spread_w.replicas
+    g.greet(riders.replicas)
     gather = Gather(g, a1, rc, sems)
+    riders.start()
 
     def send(j):
         at = span(j, rc)
@@ -264,88 +391,116 @@
         gather.start(j)
 
     run(n, send)
-    for copy in copies:
+
+    def multiply(j):
+        at = span(j, rc)
+        gather.ready(j)
+        r = dg(flat(a1[:, at, :]), w[...], NN).astype(BF)
+        qkv_ref[:, at, :] = r.reshape(size, rc, r.shape[1])
+
+    if fresh:
+
+        def relay(j):
+            gather.relay(j)
+            riders.step(j, n)
+
+        run(n, relay)
+        riders.finish()
+        outs = [
+            pltpu.make_async_copy(w, w_out, w_sem.at[0]),
+            pltpu.make_async_copy(a1, a1_out, out_sem.at[0]),
+        ]
+        outs[0].start()
+        run(n, multiply)
+        outs[1].start()
+    else:
         copy.wait()
 
-    def work(j):
-        at = span(j, rc)
-        gather.relay(j)
-        gather.ready(j)
-        a = flat(a1[:, at, :])
-        for h in range(heads):
-            r = dg(a, w[h], NN).astype(BF)
-            qkv_ref[h, :, at, :] = r.reshape(size, rc, r.shape[1])
-
-    run(n, work)
-    out = pltpu.make_async_copy(a1, a1_out, out_sem.at[0])
-    out.start()
+        def work(j):
+            gather.relay(j)
+            multiply(j)
+            riders.step(j, n)
+
+        run(n, work)
+        outs = [pltpu.make_async_copy(a1, a1_out, out_sem.at[0])]
+        outs[0].start()
+        riders.finish()
     gather.drain(n)
-    out.wait()
-
-
-def qkv_forward(size, layer, x, gains, w):
+    for out in outs:
+        out.wait()
+
+
+def qkv_forward(size, replicas, layer, x, gains, w, riders, fresh):
     rows, width = x.shape
-    _, heads, depth, wide = w.shape
+    wide = w.shape[1]
     n = chunks(rows)
+    halves, columns, outs, sems = riding(riders, replicas)
+    extra = [shape((width, wide), BF)] if fresh else []
     return pl.pallas_call(
-        functools.partial(qkv_kernel, size, layer),
-        out_shape=(
-            shape((heads, size, rows, wide), BF),
+        functools.partial(qkv_kernel, size, layer, columns, fresh),
+        out_shape=[
+            shape((size, rows, wide), BF),
             shape((size, rows, width), BF),
-        ),
-        in_specs=[VM, VM, HB],
-        out_specs=(VM, HB),
+        ]
+        + outs
+        + extra,
+        in_specs=[VM, VM, HB] + [HB] * len(riders),
+        out_specs=[VM, HB] + [HB] * (len(outs) + len(extra)),
         scratch_shapes=[
             pltpu.VMEM((size, rows, width), BF),
-            pltpu.VMEM((heads, width, wide), BF),
-            DMA((w.shape[0] // 2,)),
+            pltpu.VMEM((width, wide), BF),
+            DMA((1,)),
             DMA((1,)),
         ]
-        + comm_sems(size, n),
+        + comm_sems(size, n)
+        + (rider_sems(replicas) if fresh else [])
+        + sems,
         compiler_params=params(layer),
         cost_estimate=cost(20e9, 30e6),
-    )(x, gains, w)
-
-
-def attend_kernel(
-    size, layer, qkv_ref, qm_ref, km_ref, x_ref, w_ref,
-    h1_ref, ctx_ref, lse_ref, ka, vt, w, w_sem, *scratch
-):
-    heads, _, rows, wide = qkv_ref.shape
+    )(x, gains, w, *halves)
+
+
+def attend_kernel(size, layer, columns, *refs):
+    m = len(columns)
+    qkv_ref, qm_ref, km_ref, x_ref, w_ref = refs[:5]
+    halves, refs = refs[5 : 5 + m], refs[5 + m :]
+    h1_ref, ctx_ref, lse_ref = refs[:3]
+    wholes, refs = refs[3 : 3 + m], refs[3 + m :]
+    ka, vt, w, w_sem = refs[:4]
+    scratch, refs = refs[4:13], refs[13:]
+    riders = Riders(halves, wholes, columns, refs)
+    _, rows, wide = qkv_ref.shape
     length = size * rows
-    e = wide // 3
+    e = qm_ref.shape[2]
+    heads = wide // (3 * e)
     c = e**-0.5 * math.log2(math.e)
-    parts, depth = w_ref.shape[0] // 2, w_ref.shape[2]
     n = chunks(rows)
     rc = rows // n
     bq = size * rc
     kc = bq
     g = Group(size)
-    copies = [
-        pltpu.make_async_copy(
-            w_ref.at[layer * parts + z], w.at[:, pl.ds(z * depth, depth)], w_sem.at[z]
-        )
-        for z in range(parts)
-    ]
-    for copy in copies:
-        copy.start()
-    g.greet()
+    copy = pltpu.make_async_copy(w_ref, w, w_sem.at[0])
+    copy.start()
+    g.greet(riders.replicas)
+    riders.start()
     scatter = Scatter(g, rc, scratch)
+    whole = flat(qkv_ref[...])
     for h in range(heads):
-        whole = flat(qkv_ref[h])
-        ka[h, :, :e] = whole[:, e : 2 * e]
+        o = 3 * e * h
+        ka[h, :, :e] = whole[:, o + e : o + 2 * e]
         ka[h, :, e:] = flat(km_ref[...])
-        vt[h, :e, :] = whole[:, 2 * e :].T
+        vt[h, :e, :] = whole[:, o + 2 * e : o + 3 * e].T
         vt[h, e:, :] = jnp.ones((16, length), BF)
-    for copy in copies:
-        copy.wait()
+    copy.wait()
 
     def work(j):
         at = span(j, rc)
         qm = flat(qm_ref[:, at, :])
         found = []
+        held_qkv = flat(qkv_ref[:, at, :])
         for h in range(heads):
-            q = jnp.concatenate([flat(qkv_ref[h, :, at, :])[:, :e], qm], axis=1)
+            o = 3 * e * h
+            q = jnp.concatenate([held_qkv[:, o : o + e], qm], axis=1)
             held = []
             top = None
             for k in range(length // kc):
@@ -364,12 +519,11 @@
             lse_ref[j, h : h + 1, :] = top + jnp.log2(total)
         ctx = (jnp.concatenate(found, axis=0) if heads > 1 else found[0]).T
         ctx_ref[:, at, :] = ctx.reshape(size, rc, heads * e)
-        for z in range(parts):
-            scatter.part[:, at, z * depth : (z + 1) * depth] = dg(
-                ctx, w[:, z * depth : (z + 1) * depth], NN
-            ).reshape(size, rc, depth)
+        width = x_ref.shape[1]
+        scatter.part[:, at, :] = dg(ctx, w[...], NN).reshape(size, rc, width)
         scatter.first(j)
         scatter.second(j)
+        riders.step(j, n)
 
     run(n, work)
 
@@ -379,54 +533,61 @@
 
     run(n, last)
     scatter.drain(n)
-
-
-def attend(size, layer, qkv, qm, km, x, w):
-    heads, _, rows, wide = qkv.shape
-    e = wide // 3
+    riders.finish()
+
+
+def attend(size, replicas, layer, qkv, qm, km, x, w, riders):
+    _, rows, wide = qkv.shape
+    e = qm.shape[2]
+    heads = wide // (3 * e)
     width = x.shape[1]
     n = chunks(rows)
+    halves, columns, outs, sems = riding(riders, replicas)
     return pl.pallas_call(
-        functools.partial(attend_kernel, size, layer),
-        out_shape=(
+        functools.partial(attend_kernel, size, layer, columns),
+        out_shape=[
             shape((rows, width), F32),
             shape((size, rows, heads * e), BF),
             shape((n, heads, size * rows // n), F32),
-        ),
-        in_specs=[VM, VM, VM, VM, HB],
-        out_specs=(VM, VM, VM),
+        ]
+        + outs,
+        in_specs=[VM, VM, VM, VM, HB] + [HB] * len(riders),
+        out_specs=[VM, VM, VM] + [HB] * len(outs),
         scratch_shapes=[
             pltpu.VMEM((heads, size * rows, 2 * e), BF),
             pltpu.VMEM((heads, e + 16, size * rows), BF),
             pltpu.VMEM((heads * e, width), BF),
-            DMA((w.shape[0] // 2,)),
+            DMA((1,)),
         ]
-        + scatter_scratch(size, rows, width, n),
+        + scatter_scratch(size, rows, width, n)
+        + sems,
         compiler_params=params(2 + layer),
         cost_estimate=cost(60e9, 20e6),
-    )(qkv, qm, km, x, w)
-
-
-def mlp_kernel(
-    size, layer, h1_ref, gain_ref, wu_ref, wd_ref,
-    y_ref, a2_out, hid_out, slope_out, a2, hid, slope, wu, wd, w_sem, out_sem, *scratch
-):
+    )(qkv, qm, km, x, w, *halves)
+
+
+def mlp_kernel(size, layer, columns, *refs):
+    m = len(columns)
+    h1_ref, gain_ref, wu_ref, wd_ref = refs[:4]
+    halves, refs = refs[4 : 4 + m], refs[4 + m :]
+    y_ref, a2_out, hid_out, slope_out = refs[:4]
+    wholes, refs = refs[4 : 4 + m], refs[4 + m :]
+    a2, hid, slope, wu, wd, w_sem, out_sem = refs[:7]
+    scratch, refs = refs[7:20], refs[20:]
+    riders = Riders(halves, wholes, columns, refs)
     rows, width = h1_ref.shape
-    parts, depth, hidden = wu_ref.shape[0] // 2, wu_ref.shape[1], wu_ref.shape[2]
+    hidden = wu_ref.shape[1]
     fb = min(256, hidden)
     n = chunks(rows)
     rc = rows // n
     g = Group(size)
-    copies = []
-    for z in range(parts):
-        at = pl.ds(z * depth, depth)
-        copies.append(pltpu.make_async_copy(wu_ref.at[layer * parts + z], wu.at[at], w_sem.at[z]))
-        copies.append(
-            pltpu.make_async_copy(wd_ref.at[layer * parts + z], wd.at[:, at], w_sem.at[parts + z])
-        )
+    copies = [
+        pltpu.make_async_copy(wu_ref, wu, w_sem.at[0]),
+        pltpu.make_async_copy(wd_ref, wd, w_sem.at[1]),
+    ]
     for copy in copies:
         copy.start()
-    g.greet()
+    g.greet(riders.replicas)
     gather = Gather(g, a2, rc, scratch[:4])
     scatter = Scatter(g, rc, scratch[4:])
 
@@ -437,6 +598,7 @@
         gather.start(j)
 
     run(n, send)
+    riders.start()
     for copy in copies:
         copy.wait()
 
@@ -456,11 +618,12 @@
             )
             hid[:, at, cols] = (u * half).astype(BF).reshape(size, rc, fb)
         held = flat(hid[:, at, :])
-        for z in range(parts):
-            cols = slice(z * depth, (z + 1) * depth)
-            scatter.part[:, at, cols] = dg(held, wd[:, cols], NN).reshape(size, rc, depth)
+        for f in range(width // 256):
+            cols = slice(f * 256, (f + 1) * 256)
+            scatter.part[:, at, cols] = dg(held, wd[:, cols], NN).reshape(size, rc, 256)
         scatter.first(j)
         scatter.second(j)
+        riders.step(j, n)
 
     run(n, work)
     outs = [
@@ -476,64 +639,66 @@
         y_ref[at, :] = (h1_ref[at, :] + scatter.third(j)).astype(BF)
 
     run(n, last)
+    riders.finish()
     gather.drain(n)
     scatter.drain(n)
     for out in outs:
         out.wait()
 
 
-def mlp_forward(size, layer, h1, gains, wu, wd):
+def mlp_forward(size, replicas, layer, h1, gains, wu, wd, riders):
     rows, width = h1.shape
-    hidden = wu.shape[2]
+    hidden = wu.shape[1]
     n = chunks(rows)
+    halves, columns, outs, sems = riding(riders, replicas)
     return pl.pallas_call(
-        functools.partial(mlp_kernel, size, layer),
-        out_shape=(
+        functools.partial(mlp_kernel, size, layer, columns),
+        out_shape=[
             shape((rows, width), BF),
             shape((size, rows, width), BF),
             shape((size, rows, hidden), BF),
             shape((size, rows, hidden), BF),
-        ),
-        in_specs=[VM, VM, HB, HB],
-        out_specs=(VM, HB, HB, HB),
+        ]
+        + outs,
+        in_specs=[VM, VM, HB, HB] + [HB] * len(riders),
+        out_specs=[VM, HB, HB, HB] + [HB] * len(outs),
         scratch_shapes=[
             pltpu.VMEM((size, rows, width), BF),
             pltpu.VMEM((size, rows, hidden), BF),
             pltpu.VMEM((size, rows, hidden), BF),
             pltpu.VMEM((width, hidden), BF),
             pltpu.VMEM((hidden, width), BF),
-            DMA((wu.shape[0],)),
+            DMA((2,)),
             DMA((3,)),
         ]
         + comm_sems(size, n)
-        + scatter_scratch(size, rows, width, n),
+        + scatter_scratch(size, rows, width, n)
+        + sems,
         compiler_params=params(4 + layer),
         cost_estimate=cost(50e9, 30e6),
-    )(h1, gains, wu, wd)
+    )(h1, gains, wu, wd, *halves)
 
 
 def mlp_back_kernel(
-    size, layer, g_ref, h1_ref, gain_ref, a2_ref, hid_ref, slope_ref, wu_ref, wd_ref,
+    size, layer, parts, g_ref, h1_ref, gain_ref, a2_ref, hid_ref, slope_ref, wu_ref, wd_ref,
     mid_ref, gain_out, gup_ref, gdown_ref,
     grad, a2, hid, dup, wu, wd, w_sem, *scratch
 ):
     rows, width = h1_ref.shape
-    parts, depth, hidden = wu_ref.shape[0] // 2, wu_ref.shape[1], wu_ref.shape[2]
+    hidden = wu_ref.shape[1]
+    depth = width // parts
     fb = min(256, hidden)
     n = chunks(rows)
     rc = rows // n
     g = Group(size)
-    copies = []
-    for z in range(parts):
-        at = pl.ds(z * depth, depth)
-        copies.append(pltpu.make_async_copy(wd_ref.at[layer * parts + z], wd.at[:, at], w_sem.at[z]))
-        copies.append(
-            pltpu.make_async_copy(wu_ref.at[layer * parts + z], wu.at[at], w_sem.at[parts + z])
-        )
-    copies.append(pltpu.make_async_copy(slope_ref, dup, w_sem.at[2 * parts]))
+    copies = [
+        pltpu.make_async_copy(wd_ref, wd, w_sem.at[0]),
+        pltpu.make_async_copy(slope_ref, dup, w_sem.at[1]),
+        pltpu.make_async_copy(wu_ref, wu, w_sem.at[2]),
+    ]
     late = [
-        pltpu.make_async_copy(hid_ref, hid, w_sem.at[2 * parts + 1]),
-        pltpu.make_async_copy(a2_ref, a2, w_sem.at[2 * parts + 2]),
+        pltpu.make_async_copy(hid_ref, hid, w_sem.at[3]),
+        pltpu.make_async_copy(a2_ref, a2, w_sem.at[4]),
     ]
     for copy in copies + late:
         copy.start()
@@ -596,13 +761,13 @@
     scatter.drain(n)
 
 
-def mlp_backward(size, layer, grad, h1, gains, a2, hid, slope, wu, wd):
+def mlp_backward(size, replicas, layer, grad, h1, gains, a2, hid, slope, wu, wd):
     rows, width = h1.shape
-    depth, hidden = wu.shape[1:]
-    parts = wu.shape[0] // 2
+    hidden = wu.shape[1]
+    parts, depth = replicas, width // replicas
     n = chunks(rows)
     return pl.pallas_call(
-        functools.partial(mlp_back_kernel, size, layer),
+        functools.partial(mlp_back_kernel, size, layer, parts),
         out_shape=(
             shape((rows, width), F32),
             shape((1, width), F32),
@@ -618,7 +783,7 @@
             pltpu.VMEM((size, rows, hidden), BF),
             pltpu.VMEM((width, hidden), BF),
             pltpu.VMEM((hidden, width), BF),
-            DMA((2 * parts + 3,)),
+            DMA((5,)),
         ]
         + comm_sems(size, n)
         + scatter_scratch(size, rows, width, n),
@@ -628,26 +793,22 @@
 
 
 def attend_back_kernel(
-    size, layer, mid_ref, qkv_ref, qm_ref, km_ref, ctx_ref, lse_ref, w_ref,
+    size, layer, parts, mid_ref, qkv_ref, qm_ref, km_ref, ctx_ref, lse_ref, w_ref,
     dqkv_ref, gout_ref, da, ka, va, kt, dk, dv, w, w_sem, *sems
 ):
-    heads, _, rows, wide = qkv_ref.shape
+    _, rows, wide = qkv_ref.shape
     length = size * rows
-    e = wide // 3
+    e = qm_ref.shape[2]
+    heads = wide // (3 * e)
     scale = e**-0.5
     c = scale * math.log2(math.e)
-    parts, depth = w_ref.shape[0] // 2, w_ref.shape[2]
+    depth = w_ref.shape[1] // parts
     n = chunks(rows)
     rc = rows // n
     bq = size * rc
     kc = bq
     g = Group(size)
-    copies = [
-        pltpu.make_async_copy(
-            w_ref.at[layer * parts + z], w.at[:, pl.ds(z * depth, depth)], w_sem.at[z]
-        )
-        for z in range(parts)
-    ]
+    copies = [pltpu.make_async_copy(w_ref, w, w_sem.at[0])]
     for copy in copies:
         copy.start()
     g.greet()
@@ -660,13 +821,14 @@
 
     run(n, send)
     lane = lax.broadcasted_iota(jnp.int32, (length, e), 1)
+    whole = flat(qkv_ref[...])
     for h in range(heads):
-        whole = flat(qkv_ref[h])
-        ka[h, :, :e] = whole[:, e : 2 * e]
+        o = 3 * e * h
+        ka[h, :, :e] = whole[:, o + e : o + 2 * e]
         ka[h, :, e:] = flat(km_ref[...])
-        va[h, :, :e] = whole[:, 2 * e :]
+        va[h, :, :e] = whole[:, o + 2 * e : o + 3 * e]
         va[h, :, e:] = jnp.where(lane < 3, 1.0, 0.0).astype(BF)
-        kt[h] = whole[:, e : 2 * e].T
+        kt[h] = whole[:, o + e : o + 2 * e].T
     dk[...] = jnp.zeros_like(dk)
     dv[...] = jnp.zeros_like(dv)
     ql = lax.broadcasted_iota(jnp.int32, (bq, e), 1)
@@ -680,8 +842,10 @@
         qm = flat(qm_ref[:, at, :])
         dctx = dg(flat(da[:, at, :]), w[...], NT).astype(BF)
         ctx = flat(ctx_ref[:, at, :])
+        held_qkv = flat(qkv_ref[:, at, :])
         for h in range(heads):
-            qq = flat(qkv_ref[h, :, at, :])[:, :e]
+            o = 3 * e * h
+            qq = held_qkv[:, o : o + e]
             q = jnp.concatenate([qq, qm], axis=1)
             dc = dctx[:, h * e : (h + 1) * e]
             prod = dc.astype(F32) * ctx[:, h * e : (h + 1) * e].astype(F32)
@@ -702,12 +866,13 @@
                 dk[h, ks, :] += dg(ds, qq, NN)
                 a = dg(kt[h, :, ks], ds, NN)
                 dqt = a if dqt is None else dqt + a
-            dqkv_ref[h, :, at, :e] = (dqt * scale).T.astype(BF).reshape(size, rc, e)
+            dqkv_ref[:, at, o : o + e] = (dqt * scale).T.astype(BF).reshape(size, rc, e)
 
     run(n, work)
     for h in range(heads):
-        dqkv_ref[h, :, :, e : 2 * e] = (dk[h] * scale).astype(BF).reshape(size, rows, e)
-        dqkv_ref[h, :, :, 2 * e :] = dv[h].astype(BF).reshape(size, rows, e)
+        o = 3 * e * h
+        dqkv_ref[:, :, o + e : o + 2 * e] = (dk[h] * scale).astype(BF).reshape(size, rows, e)
+        dqkv_ref[:, :, o + 2 * e : o + 3 * e] = dv[h].astype(BF).reshape(size, rows, e)
 
     def out_grad(z):
         cols = pl.ds(pl.multiple_of(z * depth, depth), depth)
@@ -717,15 +882,16 @@
     gather.drain(n)
 
 
-def attend_backward(size, layer, mid, qkv, qm, km, ctx, lse, w):
-    heads, _, rows, wide = qkv.shape
-    e = wide // 3
+def attend_backward(size, replicas, layer, mid, qkv, qm, km, ctx, lse, w):
+    _, rows, wide = qkv.shape
+    e = qm.shape[2]
+    heads = wide // (3 * e)
     width = mid.shape[1]
-    parts, depth = w.shape[0] // 2, w.shape[2]
+    parts, depth = replicas, width // replicas
     length = size * rows
     n = chunks(rows)
     return pl.pallas_call(
-        functools.partial(attend_back_kernel, size, layer),
+        functools.partial(attend_back_kernel, size, layer, parts),
         out_shape=(shape(qkv.shape, BF), shape((parts, heads * e, depth), BF)),
         in_specs=[VM] * 6 + [HB],
         out_specs=(VM, VM),
@@ -737,7 +903,7 @@
             pltpu.VMEM((heads, length, e), F32),
             pltpu.VMEM((heads, length, e), F32),
             pltpu.VMEM((heads * e, width), BF),
-            DMA((parts,)),
+            DMA((1,)),
         ]
         + comm_sems(size, n),
         compiler_params=params(8 + layer),
@@ -746,21 +912,15 @@
 
 
 def qkv_back_kernel(
-    size, layer, dqkv_ref, a1_ref, x_ref, mid_ref, gain_ref, w_ref,
+    size, layer, parts, dqkv_ref, a1_ref, x_ref, mid_ref, gain_ref, w_ref,
     dx_ref, gain_out, gqkv_ref, w, w_sem, *scratch
 ):
     rows, width = x_ref.shape
-    heads = dqkv_ref.shape[0]
-    parts, depth = w_ref.shape[0] // 2, w_ref.shape[2]
+    depth = width // parts
     n = chunks(rows)
     rc = rows // n
     g = Group(size)
-    copies = [
-        pltpu.make_async_copy(
-            w_ref.at[layer * parts + z], w.at[:, pl.ds(z * depth, depth)], w_sem.at[z]
-        )
-        for z in range(parts)
-    ]
+    copies = [pltpu.make_async_copy(w_ref, w, w_sem.at[0])]
     for copy in copies:
         copy.start()
     g.greet()
@@ -770,13 +930,10 @@
 
     def work(j):
         at = span(j, rc)
+        held = flat(dqkv_ref[:, at, :])
         for z in range(parts):
             cols = slice(z * depth, (z + 1) * depth)
-            total = None
-            for h in range(heads):
-                r = dg(flat(dqkv_ref[h, :, at, :]), w[h, cols, :], NT)
-                total = r if total is None else total + r
-            scatter.part[:, at, cols] = total.reshape(size, rc, depth)
+            scatter.part[:, at, cols] = dg(held, w[cols, :], NT).reshape(size, rc, depth)
         scatter.first(j)
         scatter.second(j)
 
@@ -784,8 +941,7 @@
 
     def qkv_grad(z):
         cols = pl.ds(pl.multiple_of(z * depth, depth), depth)
-        for h in range(heads):
-            gqkv_ref[z, h] = dg(flat(a1_ref[:, :, cols]), flat(dqkv_ref[h]), TN).astype(BF)
+        gqkv_ref[z] = dg(flat(a1_ref[:, :, cols]), flat(dqkv_ref[...]), TN).astype(BF)
 
     run(parts, qkv_grad)
     gain_out[...] = jnp.zeros_like(gain_out)
@@ -802,28 +958,207 @@
     scatter.drain(n)
 
 
-def qkv_backward(size, layer, dqkv, a1, x, mid, gains, w):
+def qkv_backward(size, replicas, layer, dqkv, a1, x, mid, gains, w):
     rows, width = x.shape
-    heads, _, _, wide = dqkv.shape
-    parts, depth = w.shape[0] // 2, w.shape[2]
+    wide = w.shape[1]
+    parts, depth = replicas, width // replicas
     n = chunks(rows)
     return pl.pallas_call(
-        functools.partial(qkv_back_kernel, size, layer),
+        functools.partial(qkv_back_kernel, size, layer, parts),
         out_shape=(
             shape((rows, width), BF),
             shape((1, width), F32),
-            shape((parts, heads, depth, wide), BF),
+            shape((parts, depth, wide), BF),
         ),
         in_specs=[VM] * 5 + [HB],
         out_specs=(VM, VM, VM),
         scratch_shapes=[
-            pltpu.VMEM((heads, width, wide), BF),
-            DMA((parts,)),
+            pltpu.VMEM((width, wide), BF),
+            DMA((1,)),
         ]
         + scatter_scratch(size, rows, width, n),
-        compiler_params=params(10 + layer),
+        compiler_params=params(11),
         cost_estimate=cost(30e9, 30e6),
     )(dqkv, a1, x, mid, gains, w)
+
+
+def far_copy(src, dst, send, recv, target):
+    return pltpu.make_async_remote_copy(
+        src_ref=src, dst_ref=dst, send_sem=send, recv_sem=recv, device_id=target,
+        device_id_type=MESH,
+    )
+
+
+def last_kernel(
+    size, parts, dqkv_ref, a1_ref, x_ref, mid_ref, gain_ref, w_ref, two_ref, above_ref,
+    dx_ref, gain_out, gqkv_ref,
+    w, own, away, came, over, back, gsum, gcame, w_sem,
+    z_send, z_recv, y_send, y_recv, g_send, g_recv, *scratch
+):
+    rows, width = x_ref.shape
+    depth = width // parts
+    half = depth // 2
+    n = chunks(rows)
+    rc = rows // n
+    g = Group(size)
+    section = lax.axis_index("section")
+    d = lax.axis_index("dp")
+    copy = pltpu.make_async_copy(w_ref, w, w_sem.at[0])
+    copy.start()
+    g.greet(parts)
+    scatter = Scatter(g, rc, scratch)
+
+    def block(z):
+        cols = pl.ds(pl.multiple_of(z * depth, depth), depth)
+        return dg(flat(a1_ref[:, :, cols]), flat(dqkv_ref[...]), TN)
+
+    def z_copy(k, i):
+        part = pl.ds(pl.multiple_of(i * half, half), half)
+        return far_copy(
+            away.at[k - 1, part], came.at[k - 1, part], z_send.at[k - 1, i], z_recv.at[k - 1, i],
+            {"dp": lax.rem(d + k, parts)},
+        )
+
+    def y_copy(i):
+        part = pl.ds(pl.multiple_of(i * half, half), half)
+        return far_copy(
+            over.at[part], back.at[part], y_send.at[i], y_recv.at[i], {"section": 1 - section}
+        )
+
+    def send(i):
+        k = i + 1
+        away[i] = block(lax.rem(d + k, parts)).astype(BF)
+        z_copy(k, 0).start()
+        z_copy(k, 1).start()
+
+    run(parts - 1, send)
+    copy.wait()
+
+    def work(j):
+        at = span(j, rc)
+        held = flat(dqkv_ref[:, at, :])
+        for z in range(parts):
+            cols = slice(z * depth, (z + 1) * depth)
+            scatter.part[:, at, cols] = dg(held, w[cols, :], NT).reshape(size, rc, depth)
+        scatter.first(j)
+        scatter.second(j)
+
+    run(n, work)
+    own[...] = block(d)
+    gsum[0] = jnp.zeros_like(gsum[0])
+
+    def last(j):
+        at = span(j, rc)
+        dh, dgain = normed_back(x_ref[at, :].astype(F32), gain_ref[0:1, :], scatter.third(j))
+        dx_ref[at, :] = (mid_ref[at, :] + dh).astype(BF)
+        gsum[0, 0:1, :] += dgain
+
+    run(n, last)
+    gsum[0, 1:2, :] = two_ref[...]
+    gsum[0, 2:4, :] = above_ref[...]
+
+    targets = [
+        [{"tensor": g.sibling}],
+        [{"tensor": g.ahead(k) * 2 + g.core} for k in range(1, g.chips)],
+        [{"dp": lax.rem(d + k, parts)} for k in range(1, parts)],
+        [{"section": 1 - section}],
+    ]
+    slot = 0
+    sent = []
+
+    def exchange(stage):
+        nonlocal slot
+        copies = []
+        for target in targets[stage]:
+            copies.append(
+                far_copy(gsum.at[stage], gcame.at[slot], g_send.at[slot], g_recv.at[slot], target)
+            )
+            copies[-1].start()
+            slot += 1
+        total = gsum[stage]
+        for i, copy in enumerate(copies):
+            copy.wait_recv()
+            total = total + gcame[slot - len(copies) + i]
+        gsum[stage + 1] = total
+        sent.extend(copies)
+
+    exchange(0)
+    exchange(1)
+
+    def collect(i):
+        part = pl.ds(pl.multiple_of(i * half, half), half)
+        total = own[part, :]
+        for k in range(1, parts):
+            z_copy(k, i).wait_recv()
+            total = total + came[k - 1, part, :].astype(F32)
+        own[part, :] = total
+        over[part, :] = total.astype(BF)
+
+        @pl.when(section == 1)
+        def _():
+            y_copy(i).start()
+
+    run(2, collect)
+    exchange(2)
+    exchange(3)
+    gain_out[...] = gsum[4]
+
+    @pl.when(section == 0)
+    def _():
+        y_copy(0).wait_recv()
+        y_copy(1).wait_recv()
+
+    gqkv_ref[...] = own[...] + back[...].astype(F32)
+
+    @pl.when(section == 1)
+    def _():
+        y_copy(0).wait_send()
+        y_copy(1).wait_send()
+
+    for copy in sent:
+        copy.wait_send()
+    for k in range(1, parts):
+        z_copy(k, 0).wait_send()
+        z_copy(k, 1).wait_send()
+    scatter.drain(n)
+
+
+def last_backward(size, replicas, dqkv, a1, x, mid, gains, w, two, above):
+    rows, width = x.shape
+    wide = w.shape[1]
+    depth = width // replicas
+    n = chunks(rows)
+    slots = 1 + (size // 2 - 1) + (replicas - 1) + 1
+    return pl.pallas_call(
+        functools.partial(last_kernel, size, replicas),
+        out_shape=(
+            shape((rows, width), BF),
+            shape((8, width), F32),
+            shape((depth, wide), F32),
+        ),
+        in_specs=[VM] * 5 + [HB, VM, VM],
+        out_specs=(VM, VM, VM),
+        scratch_shapes=[
+            pltpu.VMEM((width, wide), BF),
+            pltpu.VMEM((depth, wide), F32),
+            pltpu.VMEM((replicas - 1, depth, wide), BF),
+            pltpu.VMEM((replicas - 1, depth, wide), BF),
+            pltpu.VMEM((depth, wide), BF),
+            pltpu.VMEM((depth, wide), BF),
+            pltpu.VMEM((5, 8, width), F32),
+            pltpu.VMEM((slots, 8, width), F32),
+            DMA((1,)),
+            DMA((replicas - 1, 2)),
+            DMA((replicas - 1, 2)),
+            DMA((2,)),
+            DMA((2,)),
+            DMA((slots,)),
+            DMA((slots,)),
+        ]
+        + scatter_scratch(size, rows, width, n),
+        compiler_params=params(10),
+        cost_estimate=cost(40e9, 30e6),
+    )(dqkv, a1, x, mid, gains, w, two, above)
 
 
 def scene_masks(segments, e):
@@ -852,48 +1187,84 @@
 ):
     section = lax.axis_index("section")
     size = lax.axis_size("tensor")
-
-    def gather_weight(w):
-        return lax.all_gather(w.astype(BF), ("section", "dp"), axis=0, tiled=False)
-
-    w_qkv = gather_weight(jnp.swapaxes(qkv_weight[0], 0, 1))
-    w_out = gather_weight(out_weight[0].reshape((-1, out_weight.shape[3])))
-    w_up = gather_weight(up_weight[0])
-    w_down = gather_weight(down_weight[0])
-    gains_one = lax.all_gather(norm_one_gain[0], "section", axis=0, tiled=False)
-    gains_two = lax.all_gather(norm_two_gain[0], "section", axis=0, tiled=False)
+    replicas = lax.axis_size("dp")
+
+    mine = [
+        qkv_weight[0].reshape((qkv_weight.shape[1], -1)),
+        out_weight[0].reshape((-1, out_weight.shape[3])),
+        up_weight[0],
+        down_weight[0],
+    ]
+    def halves(w):
+        w = w.astype(BF).reshape((2, -1, w.shape[1]))
+        keep = jnp.where(section == 0, w[0], w[1])
+        other = swap_section(jnp.where(section == 0, w[1], w[0]))
+        return [jnp.where(section == layer, keep, other) for layer in range(2)]
+
+    h_qkv, h_out, h_up, h_down = [halves(w) for w in mine]
+    gains_mine = jnp.concatenate([norm_one_gain, norm_two_gain], axis=0)
+    gains_other = swap_section(gains_mine)
+    gains = [jnp.where(section == layer, gains_mine, gains_other) for layer in range(2)]
+    gains_one = jnp.stack([gains[0][0], gains[1][0]])
+    gains_two = jnp.stack([gains[0][1], gains[1][1]])
     segments = lax.dynamic_index_in_dim(segment_ids, section, 0, keepdims=False)
     x = lax.dynamic_index_in_dim(block_input, section, 0, keepdims=False)
     head_dim = qkv_weight.shape[3] // 3
     qm, km = scene_masks(segments.reshape((size, -1)), head_dim)
-    kept = []
-    ys = []
-    for layer in range(2):
-        qkv, a1 = qkv_forward(size, layer, x, gains_one, w_qkv)
-        h1, ctx, lse = attend(size, layer, qkv, qm, km, x, w_out)
-        y, a2, hid, slope = mlp_forward(size, layer, h1, gains_two, w_up, w_down)
-        kept.append((x, a1, qkv, ctx, lse, h1, a2, hid, slope))
-        ys.append(y)
-        x = y
+    qkv, a1, w_out_0, w_qkv_0 = qkv_forward(
+        size, replicas, 0, x, gains_one, h_qkv[0], [(h_out[0], True)], True
+    )
+    h1, ctx, lse, w_up_0, w_down_0 = attend(
+        size, replicas, 0, qkv, qm, km, x, w_out_0, [(h_up[0], False), (h_down[0], True)]
+    )
+    y0, a2, hid, slope, w_qkv_1, w_out_1 = mlp_forward(
+        size, replicas, 0, h1, gains_two, w_up_0, w_down_0, [(h_qkv[1], False), (h_out[1], True)]
+    )
+    kept = [(x, a1, qkv, ctx, lse, h1, a2, hid, slope)]
+    qkv, a1, w_up_1 = qkv_forward(
+        size, replicas, 1, y0, gains_one, w_qkv_1, [(h_up[1], False)], False
+    )
+    h1, ctx, lse, w_down_1 = attend(
+        size, replicas, 1, qkv, qm, km, y0, w_out_1, [(h_down[1], True)]
+    )
+    y1, a2, hid, slope = mlp_forward(size, replicas, 1, h1, gains_two, w_up_1, w_down_1, [])
+    kept.append((y0, a1, qkv, ctx, lse, h1, a2, hid, slope))
+    ys = [y0, y1]
+    weights = [
+        (w_qkv_0, w_out_0, w_up_0, w_down_0),
+        (w_qkv_1, w_out_1, w_up_1, w_down_1),
+    ]
     other_y = swap_section(jnp.where(section == 0, ys[1], ys[0]))
     grad = lax.dynamic_index_in_dim(cotangent, section, 0, keepdims=False)
     dxs = [None, None]
-    gain_sums = [None, None]
-    sums = [None, None]
 
     def reduce_rows(value):
         return lax.psum_scatter(value, "dp", scatter_dimension=0, tiled=False)
 
     for layer in (1, 0):
         x, a1, qkv, ctx, lse, h1, a2, hid, slope = kept[layer]
+        w_qkv, w_out, w_up, w_down = weights[layer]
         mid, gain_two, g_up, g_down = mlp_backward(
-            size, layer, grad, h1, gains_two, a2, hid, slope, w_up, w_down
+            size, replicas, layer, grad, h1, gains_two, a2, hid, slope, w_up, w_down
         )
-        d_qkv, g_out = attend_backward(size, layer, mid, qkv, qm, km, ctx, lse, w_out)
-        grad, gain_one, g_qkv = qkv_backward(size, layer, d_qkv, a1, x, mid, gains_one, w_qkv)
+        if layer == 0:
+            mid, sums = lax.optimization_barrier((mid, sums))
+        d_qkv, g_out = attend_backward(size, replicas, layer, mid, qkv, qm, km, ctx, lse, w_out)
+        up, down = reduce_rows(g_up), reduce_rows(g_down)
+        if layer == 1:
+            grad, gain_one, g_qkv = qkv_backward(
+                size, replicas, layer, d_qkv, a1, x, mid, gains_one, w_qkv
+            )
+            gains_above = jnp.concatenate([gain_one, gain_two], axis=0)
+            grad, up, down = lax.optimization_barrier((grad, up, down))
+            sums = [reduce_rows(g_qkv), reduce_rows(g_out), up, down]
+        else:
+            d_qkv, g_out, up, down = lax.optimization_barrier((d_qkv, g_out, up, down))
+            grad, gains, qkv_grad = last_backward(
+                size, replicas, d_qkv, a1, x, mid, gains_one, w_qkv, gain_two, gains_above
+            )
+            lower = [None, reduce_rows(g_out), up, down]
         dxs[layer] = grad
-        gain_sums[layer] = jnp.concatenate([gain_one, gain_two], axis=0)
-        sums[layer] = [reduce_rows(v) for v in (g_qkv, g_out, g_up, g_down)]
     other_dx = swap_section(jnp.where(section == 0, dxs[1], dxs[0]))
 
     def own_layer(mine, other):
@@ -908,16 +1279,18 @@
         send = swap_section(jnp.where(section == 0, one, zero))
         return jnp.where(section == 0, zero, one).astype(F32) + send.astype(F32)
 
-    qkv_grad, out_grad, up_grad, down_grad = [finish(a, b) for a, b in zip(sums[0], sums[1])]
-    gains = lax.psum(jnp.stack(gain_sums), ("section", "dp", "tensor"))
-    gains = lax.dynamic_index_in_dim(gains, section, 0, keepdims=False)
+    qkv_grad = jnp.where(
+        section == 0, qkv_grad, sums[0].astype(F32) + swap_section(sums[0]).astype(F32)
+    )
+    out_grad, up_grad, down_grad = [finish(a, b) for a, b in zip(lower[1:], sums[1:])]
+    gains = lax.dynamic_slice_in_dim(gains, 2 * section, 2, 0)
     return (
         layer_out,
         input_out,
-        gains[0][None],
-        jnp.swapaxes(qkv_grad, 0, 1)[None],
+        gains[0:1],
+        qkv_grad.reshape(qkv_weight.shape),
         out_grad.reshape(out_weight.shape),
-        gains[1][None],
+        gains[1:2],
         up_grad[None],
         down_grad[None],
     )

time: 1070 us -> 753 us (0.70)
  waiting for transfers between devices: 334 us -> 37.8 us
  blocking collectives: 91.5 us -> 0 us
  Pallas kernels: 575 us -> 634 us
    reduce_scatter x8 -> x7, waiting for transfers between devices: 175 us -> 0.08 us  [reduce_rows(): return lax.psum_scatter(value, 'dp', scatter_dimension=0, tiled=False)]
    all_gather x4 -> x0, waiting for transfers between devices: 147 us -> none  [gather_weight(): return lax.all_gather(w.astype(BF), ('section', 'dp'), axis=0, tiled=False)]
    psum x1 -> x0, blocking collectives: 81.9 us -> none  [shards(): gains = lax.psum(jnp.stack(gain_sums), ('section', 'dp', 'tensor'))]
    pallas_call x12, Pallas kernels: 575 us -> 634 us  [the longest x2 137 us: attend_backward(): pl.pallas_call(functools.partial(attend_back_kernel, size, layer, parts),...]
    ppermute x6 -> x11, waiting for transfers between devices: 8.5 us -> 36.9 us  [swap_section(): return lax.ppermute(value, 'section', [(0, 1), (1, 0)])]
  transfers between devices with their start and end apart: 18 -> 18, of which waited for: 9 -> 2; matrix products, arithmetic and copies ran while one was open for 3% -> 5% of each run, Pallas kernels for 11% -> 44%
where the time goes in v3:
time: 753 us; the launch traced here: 743 us
  Pallas kernels  634 us (84%)
  waiting for transfers between devices  37.8 us (5%)
  other arithmetic  32.5 us (4%)
  between operations  15 us (2%)
  starting transfers between devices  14.5 us (2%)
  local copies, waits for them, and re-layouts  9.29 us (1%)
    pallas_call x2, Pallas kernels, attend_backward(): pl.pallas_call(functools.partial(attend_back_kernel, size, layer, parts),...  137 us
    pallas_call x2, Pallas kernels, attend(): pl.pallas_call(functools.partial(attend_kernel, size, layer, columns), ou...  113 us
    pallas_call x2, Pallas kernels, mlp_backward(): pl.pallas_call(functools.partial(mlp_back_kernel, size, layer, parts), ou...  107 us
    pallas_call x2, Pallas kernels, mlp_forward(): pl.pallas_call(functools.partial(mlp_kernel, size, layer, columns), out_s...  101 us
    pallas_call x2, Pallas kernels, qkv_forward(): pl.pallas_call(functools.partial(qkv_kernel, size, layer, columns, fresh)...  82.6 us
    pallas_call x1, Pallas kernels, last_backward(): pl.pallas_call(functools.partial(last_kernel, size, replicas), out_shape=...  59 us
    ppermute x11, waiting for transfers between devices, swap_section(): return lax.ppermute(value, 'section', [(0, 1), (1, 0)])  36.9 us
    pallas_call x1, Pallas kernels, qkv_backward(): pl.pallas_call(functools.partial(qkv_back_kernel, size, layer, parts), ou...  33.4 us
  transfers between devices with their start and end apart: 18, of which 2 were waited for; matrix products, arithmetic and copies ran while one was open for 5% of the time, Pallas kernels for 44%

profile of v3, /device:TPU:0, one launch (start us, length us, event | category | flops | bytes accessed | tf_op | source)
XLA Modules:
  0.0 743.2 jit_solution(12923584096590627923)
XLA Ops:
  7.2 0.9 pad_maximum_fusion
  8.1 3.0 collective-permute-start
  11.2 1.2 convert_element_type.49
  12.4 0.8 copy.20
  13.3 2.1 collective-permute-start.2
  15.3 1.3 convert_element_type.55
  16.6 0.7 select_bitcast_fusion.4
  17.4 1.3 convert_element_type.54
  18.7 0.7 select_bitcast_fusion.5
  19.4 2.0 collective-permute-start.3
  21.4 0.5 iota_compare_fusion.1
  21.9 1.0 dynamic-slice_bitcast_fusion.1.refs_0_.refs_3_.x_ref
  23.0 1.9 select_convert_fusion
  24.9 2.3 dynamic-slice_bitcast_fusion.g_ref
  27.2 0.1 copy.21
  27.4 0.6 pad_maximum_fusion.1.refs_1_.gain_ref
  28.0 0.6 pad_maximum_fusion.2.refs_1_.gain_ref
  28.7 0.7 bitcast_select_fusion.6
  29.3 1.7 broadcast_select_fusion.8
  31.0 40.2 %shard_map.152 = (bf16[4,512,768]{2,1,0:T(8,128)(2,1)}, bf16[4,512,1024]{2,1,0:T(8,128)(2,1)}, bf16[256,1024]{1,0:T(8,128)(2,1)}, bf16[1024,768]{1,0:T(8,128)(2,1)}) custom-call(bf16[512,1024]{1,0:T(8,128)(2,1)} %dynamic-slice_bitcast_fusion.1.refs_0_.refs_3_.x_ref, f32[2,1024]{1,0:T(2,128)} %pad_maximum_fusion.1.refs_1_.gain_ref, ...), custom_call_target="tpu_custom_call" | custom-call | flops 20000000000 | bytes 30000000 | tf_op jit(solution)/shard_map/pallas_call | solution.py:439
  71.3 1.8 bitcast_select_fusion
  73.1 1.8 bitcast_select_fusion.2
  74.9 62.7 %shard_map.153 = (f32[512,1024]{1,0:T(8,128)}, bf16[4,512,256]{2,1,0:T(8,128)(2,1)}, f32[4,4,512]{2,1,0:T(4,128)}, bf16[1024,1024]{1,0:T(8,128)(2,1)}, bf16[1024,1024]{1,0:T(8,128)(2,1)}) custom-call(bf16[4,512,768]{2,1,0:T(8,128)(2,1)} %get-tuple-element.64.refs_0_.qkv_ref, bf16[4,512,64]{2,1,0:T(8,128)(2,1)} %get-tuple-element.149.refs_1_.qm_ref, ...), custom_call_target="tpu_custom_call" | custom-call | flops 60000002048 | bytes 20000000 | tf_op jit(solution)/shard_map/pallas_call | solution.py:546
  137.6 50.7 %shard_map.154 = (bf16[512,1024]{1,0:T(8,128)(2,1)}, bf16[4,512,1024]{2,1,0:T(8,128)(2,1)}, bf16[4,512,1024]{2,1,0:T(8,128)(2,1)}, bf16[4,512,1024]{2,1,0:T(8,12...) custom-call(f32[512,1024]{1,0:T(8,128)} %get-tuple-element.66.refs_0_.h1_ref, ...), custom_call_target="tpu_custom_call" | custom-call | flops 49999998976 | bytes 30000000 | tf_op jit(solution)/shard_map/pallas_call | solution.py:654
  188.3 42.3 %shard_map.155 = (bf16[4,512,768]{2,1,0:T(8,128)(2,1)}, bf16[4,512,1024]{2,1,0:T(8,128)(2,1)}, bf16[1024,1024]{1,0:T(8,128)(2,1)}) custom-call(bf16[512,1024]{1,0:T(8,128)(2,1)} %get-tuple-element.69.refs_0_.refs_3_.x_ref, f32[2,1024]{1,0:T(2,128)} %pad_maximum_fusion.1.refs_1_.gain_ref, bf16[1024,768]{1,0:T(8,128)(2,1)} %get-tuple-element.70.refs_2_.w_ref, ...), custom_call_target="tpu_custom_call" | custom-call | flops 20000000000 | bytes 30000000 | tf_op jit(solution)/shard_map/pallas_call | solution.py:439
  230.7 50.7 %shard_map.156 = (f32[512,1024]{1,0:T(8,128)}, bf16[4,512,256]{2,1,0:T(8,128)(2,1)}, f32[4,4,512]{2,1,0:T(4,128)}, bf16[1024,1024]{1,0:T(8,128)(2,1)}) custom-call(bf16[4,512,768]{2,1,0:T(8,128)(2,1)} %get-tuple-element.71.refs_0_.qkv_ref, bf16[4,512,64]{2,1,0:T(8,128)(2,1)} %get-tuple-element.149.refs_1_.qm_ref, ...), custom_call_target="tpu_custom_call" | custom-call | flops 60000002048 | bytes 20000000 | tf_op jit(solution)/shard_map/pallas_call | solution.py:546
  281.4 50.2 %shard_map.157 = (bf16[512,1024]{1,0:T(8,128)(2,1)}, bf16[4,512,1024]{2,1,0:T(8,128)(2,1)}, bf16[4,512,1024]{2,1,0:T(8,128)(2,1)}, bf16[4,512,1024]{2,1,0:T(8,128)(2,1)}) custom-call(f32[512,1024]{1,0:T(8,128)} %get-tuple-element.73.refs_0_.h1_ref, f32[2,1024]{1,0:T(2,128)} %pad_maximum_fusion.2.refs_1_.gain_ref, ...), custom_call_target="tpu_custom_call" | custom-call | flops 49999998976 | bytes 30000000 | tf_op jit(solution)/shard_map/pallas_call | solution.py:654
  331.6 53.3 %shard_map.158 = (f32[512,1024]{1,0:T(8,128)}, f32[1,1024]{1,0:T(1,128)}, bf16[4,256,1024]{2,1,0:T(8,128)(2,1)}, bf16[4,1024,256]{2,1,0:T(8,128)(2,1)}) custom-call(bf16[512,1024]{1,0:T(8,128)(2,1)} %dynamic-slice_bitcast_fusion.g_ref, f32[512,1024]{1,0:T(8,128)} %get-tuple-element.73.refs_0_.h1_ref, f32[2,1024]{1,0:T(2,128)} %pad_maximum_fusion.2.refs_1_.gain_ref, ...), custom_call_target="tpu_custom_call" | custom-call | flops 60000002048 | bytes 40000000 | tf_op jit(solution)/shard_map/pallas_call | solution.py:769
  385.0 0.7 reduce-scatter.10.cloned.1.call-update
  385.7 68.6 %shard_map.159 = (bf16[4,512,768]{2,1,0:T(8,128)(2,1)}, bf16[4,256,256]{2,1,0:T(8,128)(2,1)}) custom-call(f32[512,1024]{1,0:T(8,128)} %get-tuple-element.80.mid_ref, bf16[4,512,768]{2,1,0:T(8,128)(2,1)} %get-tuple-element.71.refs_0_.qkv_ref, bf16[4,512,64]{2,1,0:T(8,128)(2,1)} %get-tuple-element.149.refs_1_.qm_ref, ...), custom_call_target="tpu_custom_call" | custom-call | flops 89999998976 | bytes 40000000 | tf_op jit(solution)/shard_map/pallas_call | solution.py:893
  454.4 33.4 %shard_map.160 = (bf16[512,1024]{1,0:T(8,128)(2,1)}, f32[1,1024]{1,0:T(1,128)}, bf16[4,256,768]{2,1,0:T(8,128)(2,1)}) custom-call(bf16[4,512,768]{2,1,0:T(8,128)(2,1)} %get-tuple-element.83.dqkv_ref, bf16[4,512,1024]{2,1,0:T(8,128)(2,1)} %get-tuple-element.84.a1_ref, bf16[512,1024]{1,0:T(8,128)(2,1)} %get-tuple-element.69.refs_0_.refs_3_.x_ref, ...), custom_call_target="tpu_custom_call" | custom-call | flops 30000001024 | bytes 30000000 | tf_op jit(solution)/shard_map/pallas_call | solution.py:966
  487.9 0.0 reduce-scatter.16.cloned.1.call-start
  488.0 54.0 %shard_map.161 = (f32[512,1024]{1,0:T(8,128)}, f32[1,1024]{1,0:T(1,128)}, bf16[4,256,1024]{2,1,0:T(8,128)(2,1)}, bf16[4,1024,256]{2,1,0:T(8,128)(2,1)}) custom-call(bf16[512,1024]{1,0:T(8,128)(2,1)} %get-tuple-element.88.g_ref, f32[512,1024]{1,0:T(8,128)} %get-tuple-element.66.refs_0_.h1_ref, f32[2,1024]{1,0:T(2,128)} %pad_maximum_fusion.2.refs_1_.gain_ref, ...), custom_call_target="tpu_custom_call" | custom-call | flops 60000002048 | bytes 40000000 | tf_op jit(solution)/shard_map/pallas_call | solution.py:769
  542.1 0.0 reduce-scatter.18.cloned.1.call-start
  542.1 1.1 copy-done.3
  543.2 0.3 copy-done.4
  543.6 0.1 broadcast_select_fusion.2
  543.7 0.6 collective-permute-start.5
  544.3 0.6 pad_maximum_fusion.3.above_ref
  544.9 24.0 %collective-permute-done.5 = bf16[512,1024]{1,0:T(8,128)(2,1)} collective-permute-done((bf16[512,1024]{1,0:T(8,128)(2,1)S(1)}, bf16[512,1024]{1,0:T(8,128)(2,1)}, u32[]{:S(2)}, u32[]{:S(2)}) %collective-permute-start.5) | collective-permute-done | bytes 1048608 | tf_op jit(solution)/shard_map/ppermute | solution.py:1174
  569.0 1.4 select_bitcast_fusion.3
  570.4 1.5 maximum_bitcast_fusion
  571.9 0.5 collective-permute-start.7
  572.5 68.8 %shard_map.162 = (bf16[4,512,768]{2,1,0:T(8,128)(2,1)}, bf16[4,256,256]{2,1,0:T(8,128)(2,1)}) custom-call(f32[512,1024]{1,0:T(8,128)} %get-tuple-element.97.mid_ref, bf16[4,512,768]{2,1,0:T(8,128)(2,1)} %get-tuple-element.64.refs_0_.qkv_ref, bf16[4,512,64]{2,1,0:T(8,128)(2,1)} %get-tuple-element.149.refs_1_.qm_ref, ...), custom_call_target="tpu_custom_call" | custom-call | flops 89999998976 | bytes 40000000 | tf_op jit(solution)/shard_map/pallas_call | solution.py:893
  641.4 0.8 broadcast_select_fusion.4
  642.3 2.6 collective-permute-start.10
  644.8 0.9 broadcast_select_fusion.5
  645.7 1.0 collective-permute-start.9
  646.8 59.0 %shard_map.163 = (bf16[512,1024]{1,0:T(8,128)(2,1)}, f32[8,1024]{1,0:T(8,128)}, f32[256,768]{1,0:T(8,128)}) custom-call(bf16[4,512,768]{2,1,0:T(8,128)(2,1)} %get-tuple-element.104.dqkv_ref, bf16[4,512,1024]{2,1,0:T(8,128)(2,1)} %get-tuple-element.105.a1_ref, bf16[512,1024]{1,0:T(8,128)(2,1)} %dynamic-slice_bitcast_fusion.1.refs_0_.refs_3_.x_ref, ...), custom_call_target="tpu_custom_call" | custom-call | flops 40000000000 | bytes 30000000 | tf_op jit(solution)/shard_map/pallas_call | solution.py:1132
  705.8 1.1 broadcast_select_fusion
  706.9 2.2 collective-permute-start.6
  709.1 0.7 copy-done.14
  709.9 1.1 add_select_fusion
  711.0 1.1 copy.23
  712.2 1.4 constant_dynamic-slice_fusion.1
  713.6 2.2 add_bitcast_fusion
  715.8 2.4 add_bitcast_fusion.1
  718.2 0.9 bitcast_select_fusion.4
  719.1 0.1 collective-permute-start.8
  719.2 12.9 %collective-permute-done.6 = bf16[512,1024]{1,0:T(8,128)(2,1)} collective-permute-done((bf16[512,1024]{1,0:T(8,128)(2,1)}, bf16[512,1024]{1,0:T(8,128)(2,1)}, u32[]{:S(2)}, u32[]{:S(2)}) %collective-permute-start.6) | collective-permute-done | bytes 1048608 | tf_op jit(solution)/shard_map/ppermute | solution.py:1174
  732.1 1.4 select_bitcast_fusion.1
  733.5 1.5 maximum_bitcast_fusion.1
  735.0 0.8 convert_add_fusion
  735.8 0.1 copy-done.1
  (74 shorter events, 0.7 us)
Async XLA Ops:
  7.2 14.8 %copy-start = (bf16[2,512,1024]{2,1,0:T(8,128)(2,1)S(1)}, bf16[2,512,1024]{2,1,0:T(8,128)(2,1)}, u32[]{:S(2)}) copy-start(bf16[2,512,1024]{2,1,0:T(8,128)(2,1)} %param.9) | copy-start | bytes 6291460
  7.2 6.1 copy-start.15
  7.2 480.8 %reduce-scatter.8.cloned.1.call-start = ((), (), s32[]{:S(2)}) async-start(), calls=%async_computation.7 | async-start | bytes 2621440 | tf_op jit(solution)/shard_map/reduce_scatter | solution.py:1242
  8.1 19.2 %collective-permute-start = (f32[2,1024]{1,0:T(2,128)S(1)}, f32[2,1024]{1,0:T(2,128)S(1)}, u32[]{:S(2)}, u32[]{:S(2)}) collective-permute-start(f32[2,1024]{1,0:T(2,128)S(1)} %pad_maximum_fusion), channel_id=1, source_target_pairs={{0,16},{16,0},{1,17},{17,1},{2,18},{18,2},{3,19},{19,3},{4,20},{20... | collective-permute-start | bytes 24584 | tf_op jit(solution)/shard_map/ppermute | solution.py:1174
  13.2 16.1 %collective-permute-start.1 = (bf16[128,768]{1,0:T(8,128)(2,1)}, bf16[128,768]{1,0:T(8,128)(2,1)}, u32[]{:S(2)}, u32[]{:S(2)}) collective-permute-start(bf16[128,768]{1,0:T(8,128)(2,1)} %copy.20), channel_id=1, source_target_pairs={{0,16},{16,0},{1,17},{17,1},{2,18},{18,2},{3,19},{19,3},{4,20},{20... | collective-permute-start | bytes 589832 | tf_op jit(solution)/shard_map/ppermute | solution.py:1174
  13.3 15.4 %collective-permute-start.2 = (bf16[128,256]{1,0:T(8,128)(2,1)S(1)}, bf16[128,256]{1,0:T(8,128)(2,1)S(1)}, u32[]{:S(2)}, u32[]{:S(2)}) collective-permute-start(bf16[128,256]{1,0:T(8,128)(2,1)S(1)} %bitcast.65), channel_id=1, source_target_pairs={{0,16},{16,0},{1,17},{17,1},{2,18},{18,2},{3,19},{19,3},{4,20},{20... | collective-permute-start | bytes 196616 | tf_op jit(solution)/shard_map/ppermute | solution.py:1174
  17.4 53.9 %collective-permute-start.4 = (bf16[512,256]{1,0:T(8,128)(2,1)}, bf16[512,256]{1,0:T(8,128)(2,1)}, u32[]{:S(2)}, u32[]{:S(2)}) collective-permute-start(bf16[512,256]{1,0:T(8,128)(2,1)} %select_bitcast_fusion.4), channel_id=1, source_target_pairs={{0,16},{16,0},{1,17},{17,1},{2,18},{18,2},{3,19},{19,3},{4,20},{20... | collective-permute-start | bytes 786440 | tf_op jit(solution)/shard_map/ppermute | solution.py:1174
  19.4 53.7 %collective-permute-start.3 = (bf16[128,1024]{1,0:T(8,128)(2,1)}, bf16[128,1024]{1,0:T(8,128)(2,1)}, u32[]{:S(2)}, u32[]{:S(2)}) collective-permute-start(bf16[128,1024]{1,0:T(8,128)(2,1)} %select_bitcast_fusion.5), channel_id=1, source_target_pairs={{0,16},{16,0},{1,17},{17,1},{2,18},{18,2},{3,19},{19,3},{4,20},{20... | collective-permute-start | bytes 786440 | tf_op jit(solution)/shard_map/ppermute | solution.py:1174
  21.9 1.0 copy-start.18
  23.0 4.4 copy-start.16
  23.0 4.4 copy-start.17
  384.9 103.1 %reduce-scatter.10.cloned.1.call-start = ((), (), s32[]{:S(2)}) async-start(), calls=%async_computation.8 | async-start | bytes 2621440 | tf_op jit(solution)/shard_map/reduce_scatter | solution.py:1242
  385.7 186.2 %reduce-scatter.14.cloned.1.call-start = ((), (), s32[]{:S(2)}) async-start(), calls=%async_computation.10 | async-start | bytes 655360 | tf_op jit(solution)/shard_map/reduce_scatter | solution.py:1242
  454.4 117.5 %reduce-scatter.12.cloned.1.call-start = ((), (), s32[]{:S(2)}) async-start(), calls=%async_computation.9 | async-start | bytes 1966080 | tf_op jit(solution)/shard_map/reduce_scatter | solution.py:1242
  487.9 153.5 %reduce-scatter.16.cloned.1.call-start = ((), (), s32[]{:S(2)}) async-start(), calls=%async_computation.11 | async-start | bytes 2621440 | tf_op jit(solution)/shard_map/reduce_scatter | solution.py:1242
  542.0 1.2 copy-start.3
  542.0 1.5 copy-start.4
  542.1 2.3 copy-start.19
  542.1 2.2 copy-start.20
  542.1 99.3 %reduce-scatter.18.cloned.1.call-start = ((), (), s32[]{:S(2)}) async-start(), calls=%async_computation.12 | async-start | bytes 2621440 | tf_op jit(solution)/shard_map/reduce_scatter | solution.py:1242
  543.7 25.3 %collective-permute-start.5 = (bf16[512,1024]{1,0:T(8,128)(2,1)S(1)}, bf16[512,1024]{1,0:T(8,128)(2,1)}, u32[]{:S(2)}, u32[]{:S(2)}) collective-permute-start(bf16[512,1024]{1,0:T(8,128)(2,1)S(1)} %broadcast_select_fusion.2), channel_id=1, source_target_pairs={{0,16},{16,0},{1,17},{17,1},{2,18},{18,2},{3,19},{19,3},{4,20},{20... | collective-permute-start | bytes 3145736 | tf_op jit(solution)/shard_map/ppermute | solution.py:1174
  571.9 137.2 %collective-permute-start.7 = (bf16[256,768]{1,0:T(8,128)(2,1)}, bf16[256,768]{1,0:T(8,128)(2,1)S(1)}, u32[]{:S(2)}, u32[]{:S(2)}) collective-permute-start(bf16[256,768]{1,0:T(8,128)(2,1)} %bitcast.62), channel_id=1, source_target_pairs={{0,16},{16,0},{1,17},{17,1},{2,18},{18,2},{3,19},{19,3},{4,20},{20... | collective-permute-start | bytes 1179656 | tf_op jit(solution)/shard_map/ppermute | solution.py:1174
  572.5 145.7 %reduce-scatter.20.cloned.1.call-start = ((), (), s32[]{:S(2)}) async-start(), calls=%async_computation.13 | async-start | bytes 655360 | tf_op jit(solution)/shard_map/reduce_scatter | solution.py:1242
  572.5 68.9 %copy-start.7 = (bf16[1,1024,256]{2,1,0:T(8,128)(2,1)S(1)}, bf16[1,1024,256]{2,1,0:T(8,128)(2,1)}, u32[]{:S(2)}) copy-start(bf16[1,1024,256]{2,1,0:T(8,128)(2,1)} %reduce-scatter.10.cloned.1.call-done) | copy-start | bytes 1572868
  572.5 72.3 %copy-start.6 = (bf16[1,256,1024]{2,1,0:T(8,128)(2,1)S(1)}, bf16[1,256,1024]{2,1,0:T(8,128)(2,1)}, u32[]{:S(2)}) copy-start(bf16[1,256,1024]{2,1,0:T(8,128)(2,1)} %reduce-scatter.8.cloned.1.call-done) | copy-start | bytes 1572868
  642.3 71.3 %collective-permute-start.10 = (bf16[1024,256]{1,0:T(8,128)(2,1)}, bf16[1024,256]{1,0:T(8,128)(2,1)}, u32[]{:S(2)}, u32[]{:S(2)}) collective-permute-start(bf16[1024,256]{1,0:T(8,128)(2,1)} %broadcast_select_fusion.4), channel_id=1, source_target_pairs={{0,16},{16,0},{1,17},{17,1},{2,18},{18,2},{3,19},{19,3},{4,20},{20... | collective-permute-start | bytes 1572872 | tf_op jit(solution)/shard_map/ppermute | solution.py:1174
  645.7 70.1 %collective-permute-start.9 = (bf16[256,1024]{1,0:T(8,128)(2,1)}, bf16[256,1024]{1,0:T(8,128)(2,1)}, u32[]{:S(2)}, u32[]{:S(2)}) collective-permute-start(bf16[256,1024]{1,0:T(8,128)(2,1)} %broadcast_select_fusion.5), channel_id=1, source_target_pairs={{0,16},{16,0},{1,17},{17,1},{2,18},{18,2},{3,19},{19,3},{4,20},{20... | collective-permute-start | bytes 1572872 | tf_op jit(solution)/shard_map/ppermute | solution.py:1174
  646.8 59.1 %copy-start.2 = (bf16[512,1024]{1,0:T(8,128)(2,1)S(1)}, bf16[512,1024]{1,0:T(8,128)(2,1)}, u32[]{:S(2)}) copy-start(bf16[512,1024]{1,0:T(8,128)(2,1)} %get-tuple-element.88.g_ref) | copy-start | bytes 3145732
  705.8 4.1 copy-start.10
  705.8 4.1 copy-start.13
  706.9 6.7 copy-start.9
  706.9 25.1 %collective-permute-start.6 = (bf16[512,1024]{1,0:T(8,128)(2,1)}, bf16[512,1024]{1,0:T(8,128)(2,1)}, u32[]{:S(2)}, u32[]{:S(2)}) collective-permute-start(bf16[512,1024]{1,0:T(8,128)(2,1)} %broadcast_select_fusion), channel_id=1, source_target_pairs={{0,16},{16,0},{1,17},{17,1},{2,18},{18,2},{3,19},{19,3},{4,20},{20... | collective-permute-start | bytes 3145736 | tf_op jit(solution)/shard_map/ppermute | solution.py:1174
  709.1 0.7 copy-start.14
  712.2 3.7 copy-start.8
  713.6 4.6 copy-start.11
  715.8 16.2 %copy-start.5 = (bf16[512,1024]{1,0:T(8,128)(2,1)S(1)}, bf16[512,1024]{1,0:T(8,128)(2,1)}, u32[]{:S(2)}) copy-start(bf16[512,1024]{1,0:T(8,128)(2,1)} %get-tuple-element.110) | copy-start | bytes 3145732
  719.1 15.9 %collective-permute-start.8 = (bf16[256,256]{1,0:T(8,128)(2,1)S(1)}, bf16[256,256]{1,0:T(8,128)(2,1)S(1)}, u32[]{:S(2)}, u32[]{:S(2)}) collective-permute-start(bf16[256,256]{1,0:T(8,128)(2,1)S(1)} %bitcast_select_fusion.4), channel_id=1, source_target_pairs={{0,16},{16,0},{1,17},{17,1},{2,18},{18,2},{3,19},{19,3},{4,20},{20... | collective-permute-start | bytes 393224 | tf_op jit(solution)/shard_map/ppermute | solution.py:1174
  733.5 2.4 copy-start.1
  733.5 1.5 copy-start.12
Sparse Core Ops, SparseCore 0:
  385.1 41.9 reduce-scatter.7
  429.5 43.2 reduce-scatter.9
  475.0 20.8 reduce-scatter.13
  498.1 33.5 reduce-scatter.11
  542.2 41.6 reduce-scatter.15
  586.1 43.1 reduce-scatter.17
  646.9 29.4 reduce-scatter.19

commit v4 on v3

--- a/solution.py
+++ b/solution.py
@@ -49,13 +49,14 @@
     def behind(self, k):
         return lax.rem(self.chip + self.chips - k, self.chips)
 
-    def greet(self, replicas=0):
+    def greet(self, replicas=0, side=False):
         barrier = pltpu.get_barrier_semaphore()
         targets = [self.sibling] + [self.ahead(k) * 2 + self.core for k in range(1, self.chips)]
         targets = [{"tensor": target} for target in targets]
         if replicas:
             d = lax.axis_index("dp")
             targets += [{"dp": lax.rem(d + k, replicas)} for k in range(1, replicas)]
+        if replicas or side:
             targets += [{"section": 1 - lax.axis_index("section")}]
         for target in targets:
             pl.semaphore_signal(barrier, inc=1, device_id=target, device_id_type=MESH)
@@ -201,6 +202,133 @@
             return 0
 
         lax.fori_loop(0, n, one, 0)
+
+
+def far_copy(src, dst, send, recv, target):
+    return pltpu.make_async_remote_copy(
+        src_ref=src,
+        dst_ref=dst,
+        send_sem=send,
+        recv_sem=recv,
+        device_id=target,
+        device_id_type=MESH,
+    )
+
+
+class Swap:
+    def __init__(self, src, stage, sems):
+        self.src, self.stage, self.sems = src, stage, sems
+        self.s = lax.axis_index("section")
+
+    def copies(self, layer):
+        local = pltpu.make_async_copy(self.src.at[self.s], self.stage.at[self.s], self.sems.at[0])
+        side = far_copy(
+            self.src.at[1 - self.s],
+            self.stage.at[layer],
+            self.sems.at[1],
+            self.sems.at[2],
+            {"section": 1 - self.s},
+        )
+        return local, side
+
+    def start(self):
+        for copy in self.copies(self.s):
+            copy.start()
+
+    def arrive(self):
+        local, side = self.copies(1 - self.s)
+        local.wait()
+        side.wait_recv()
+
+    def finish(self):
+        self.copies(self.s)[1].wait_send()
+
+
+def reduce_scratch(replicas, rows, cols):
+    many = pltpu.VMEM((replicas - 1, rows, cols), BF)
+    one = pltpu.VMEM((rows, cols), BF)
+    far, side = DMA((replicas - 1, 2)), DMA((2,))
+    return [pltpu.VMEM((rows, cols), F32), many, many, one, one, far, far, side, side]
+
+
+class Reduce:
+    def __init__(self, layer, scratch):
+        self.layer = layer
+        self.own, self.away, self.came, self.over, self.back = scratch[:5]
+        self.z_send, self.z_recv, self.y_send, self.y_recv = scratch[5:]
+        self.replicas = self.away.shape[0] + 1
+        self.half = self.own.shape[0] // 2
+        self.d = lax.axis_index("dp")
+        self.s = lax.axis_index("section")
+
+    def target(self, k):
+        return lax.rem(self.d + k, self.replicas)
+
+    def part(self, i):
+        return pl.ds(pl.multiple_of(i * self.half, self.half), self.half)
+
+    def z_copy(self, k, i):
+        part = self.part(i)
+        return far_copy(
+            self.away.at[k - 1, part],
+            self.came.at[k - 1, part],
+            self.z_send.at[k - 1, i],
+            self.z_recv.at[k - 1, i],
+            {"dp": self.target(k)},
+        )
+
+    def y_copy(self, i):
+        part = self.part(i)
+        return far_copy(
+            self.over.at[part],
+            self.back.at[part],
+            self.y_send.at[i],
+            self.y_recv.at[i],
+            {"section": 1 - self.s},
+        )
+
+    def send(self, block):
+        def one(i):
+            k = i + 1
+            self.away[i] = block(self.target(k)).astype(BF)
+            self.z_copy(k, 0).start()
+            self.z_copy(k, 1).start()
+
+        run(self.replicas - 1, one)
+        self.own[...] = block(self.d)
+
+    def collect(self):
+        def one(i):
+            part = self.part(i)
+            total = self.own[part, :]
+            for k in range(1, self.replicas):
+                self.z_copy(k, i).wait_recv()
+                total = total + self.came[k - 1, part, :].astype(F32)
+            self.own[part, :] = total
+            self.over[part, :] = total.astype(BF)
+
+            @pl.when(self.s != self.layer)
+            def _():
+                self.y_copy(i).start()
+
+        run(2, one)
+
+    def finish(self, out):
+        @pl.when(self.s == self.layer)
+        def _():
+            self.y_copy(0).wait_recv()
+            self.y_copy(1).wait_recv()
+            out[...] = self.own[...] + self.back[...].astype(F32)
+
+        @pl.when(self.s != self.layer)
+        def _():
+            self.y_copy(0).wait_send()
+            self.y_copy(1).wait_send()
+            out[...] = self.own[...]
+
+        for k in range(1, self.replicas):
+            self.z_copy(k, 0).wait_send()
+            self.z_copy(k, 1).wait_send()
 
 
 class Spread:
@@ -282,8 +410,8 @@
 class Riders:
     def __init__(self, srcs, dsts, columns, sems):
         self.all = [
-            Spread(src, dst, by, sems[5 * i : 5 * i + 5])
-            for i, (src, dst, by) in enumerate(zip(srcs, dsts, columns))
+            Spread(src.at[layer], dst, by, sems[5 * i : 5 * i + 5])
+            for i, (src, dst, (layer, by)) in enumerate(zip(srcs, dsts, columns))
         ]
         self.replicas = self.all[0].replicas if self.all else 0
 
@@ -308,11 +436,11 @@
 
 
 def riding(riders, replicas):
-    halves = [half for half, _ in riders]
-    columns = tuple(by for _, by in riders)
+    halves = [stage for stage, _, _ in riders]
+    columns = tuple((layer, by) for _, layer, by in riders)
     outs = []
-    for half, by in riders:
-        rows, cols = half.shape
+    for stage, _, by in riders:
+        _, rows, cols = stage.shape
         outs.append(
             shape((2 * rows, replicas * cols) if by else (2 * replicas * rows, cols), BF)
         )
@@ -357,95 +485,180 @@
     lax.fori_loop(0, n, one, 0)
 
 
-def qkv_kernel(size, layer, columns, fresh, *refs):
+def first_kernel(
+    size, replicas, x_ref, gain_ref, wq_ref, wo_ref, wu_ref, wd_ref,
+    qkv_ref, gains_out, a1_out, wq_out, wo_out, q_stage, o_stage, u_stage, d_stage,
+    a1, w, gains, own_sem, q_sem, o_sem, u_sem, d_sem, gain_sem, *sems
+):
+    rows, width = x_ref.shape
+    n = chunks(rows)
+    rc = rows // n
+    g = Group(size)
+    section = lax.axis_index("section")
+    gather = Gather(g, a1, rc, sems[:4])
+    swaps = [
+        Swap(wq_ref, q_stage, q_sem),
+        Swap(wo_ref, o_stage, o_sem),
+        Swap(wu_ref, u_stage, u_sem),
+        Swap(wd_ref, d_stage, d_sem),
+    ]
+    spreads = [
+        Spread(q_stage.at[0], w, False, sems[4:9]),
+        Spread(o_stage.at[0], wo_out, True, sems[9:14]),
+    ]
+    riders = Riders([], [], (), [])
+    riders.all = spreads
+    riders.replicas = replicas
+    g.greet(replicas)
+
+    def gain_copy(layer):
+        return far_copy(
+            gain_ref, gains.at[layer], gain_sem.at[0], gain_sem.at[1], {"section": 1 - section}
+        )
+
+    gain_copy(section).start()
+    swaps[0].start()
+    swaps[1].start()
+    gains[section] = gain_ref[...]
+    gain_copy(1 - section).wait_recv()
+    gains_out[...] = gains[...]
+
+    def send(j):
+        at = span(j, rc)
+        a = normed(x_ref[at, :].astype(F32))[0] * gains[0, 0:1, :]
+        a1[g.me, at, :] = a.astype(BF)
+        gather.start(j)
+
+    run(n, send)
+    swaps[0].arrive()
+    swaps[1].arrive()
+    riders.start()
+    swaps[2].start()
+    swaps[3].start()
+
+    def relay(j):
+        gather.relay(j)
+        riders.step(j, n)
+
+    run(n, relay)
+    riders.finish()
+    outs = [
+        pltpu.make_async_copy(w, wq_out, own_sem.at[0]),
+        pltpu.make_async_copy(a1, a1_out, own_sem.at[1]),
+    ]
+    outs[0].start()
+
+    def multiply(j):
+        at = span(j, rc)
+        gather.ready(j)
+        r = dg(flat(a1[:, at, :]), w[...], NN).astype(BF)
+        qkv_ref[:, at, :] = r.reshape(size, rc, r.shape[1])
+
+    run(n, multiply)
+    outs[1].start()
+    swaps[2].arrive()
+    swaps[3].arrive()
+    for swap in swaps:
+        swap.finish()
+    gain_copy(section).wait_send()
+    gather.drain(n)
+    for out in outs:
+        out.wait()
+
+
+def first_forward(size, replicas, x, gains, ws):
+    rows, width = x.shape
+    wide = ws[0].shape[2]
+    deep = 2 * ws[1].shape[1]
+    n = chunks(rows)
+    return pl.pallas_call(
+        functools.partial(first_kernel, size, replicas),
+        out_shape=[
+            shape((size, rows, wide), BF),
+            shape((2,) + gains.shape, F32),
+            shape((size, rows, width), BF),
+            shape((width, wide), BF),
+            shape((deep, width), BF),
+        ]
+        + [shape(w.shape, BF) for w in ws],
+        in_specs=[VM, VM] + [HB] * 4,
+        out_specs=[VM, VM] + [HB] * 7,
+        scratch_shapes=[
+            pltpu.VMEM((size, rows, width), BF),
+            pltpu.VMEM((width, wide), BF),
+            pltpu.VMEM((2,) + gains.shape, F32),
+            DMA((2,)),
+            DMA((3,)),
+            DMA((3,)),
+            DMA((3,)),
+            DMA((3,)),
+            DMA((2,)),
+        ]
+        + comm_sems(size, n)
+        + rider_sems(replicas) * 2,
+        compiler_params=params(0),
+        cost_estimate=cost(30e9, 30e6),
+    )(x, gains, *ws)
+
+
+def qkv_kernel(size, layer, columns, *refs):
     m = len(columns)
     x_ref, gain_ref, w_ref = refs[:3]
     halves, refs = refs[3 : 3 + m], refs[3 + m :]
     qkv_ref, a1_out = refs[:2]
     wholes, refs = refs[2 : 2 + m], refs[2 + m :]
-    if fresh:
-        w_out, refs = refs[0], refs[1:]
     a1, w, w_sem, out_sem = refs[:4]
     sems, refs = refs[4:8], refs[8:]
-    if fresh:
-        spread_w, refs = Spread(w_ref, w, False, refs[:5]), refs[5:]
     riders = Riders(halves, wholes, columns, refs)
     rows, width = x_ref.shape
     n = chunks(rows)
     rc = rows // n
     g = Group(size)
-    if not fresh:
-        copy = pltpu.make_async_copy(w_ref, w, w_sem.at[0])
-        copy.start()
-    else:
-        riders.all.insert(0, spread_w)
-        riders.replicas = spread_w.replicas
+    copy = pltpu.make_async_copy(w_ref, w, w_sem.at[0])
+    copy.start()
     g.greet(riders.replicas)
     gather = Gather(g, a1, rc, sems)
     riders.start()
 
     def send(j):
         at = span(j, rc)
-        a = normed(x_ref[at, :].astype(F32))[0] * gain_ref[layer : layer + 1, :]
+        a = normed(x_ref[at, :].astype(F32))[0] * gain_ref[layer, 0:1, :]
         a1[g.me, at, :] = a.astype(BF)
         gather.start(j)
 
     run(n, send)
-
-    def multiply(j):
-        at = span(j, rc)
+    copy.wait()
+
+    def work(j):
+        at = span(j, rc)
+        gather.relay(j)
         gather.ready(j)
         r = dg(flat(a1[:, at, :]), w[...], NN).astype(BF)
         qkv_ref[:, at, :] = r.reshape(size, rc, r.shape[1])
-
-    if fresh:
-
-        def relay(j):
-            gather.relay(j)
-            riders.step(j, n)
-
-        run(n, relay)
-        riders.finish()
-        outs = [
-            pltpu.make_async_copy(w, w_out, w_sem.at[0]),
-            pltpu.make_async_copy(a1, a1_out, out_sem.at[0]),
-        ]
-        outs[0].start()
-        run(n, multiply)
-        outs[1].start()
-    else:
-        copy.wait()
-
-        def work(j):
-            gather.relay(j)
-            multiply(j)
-            riders.step(j, n)
-
-        run(n, work)
-        outs = [pltpu.make_async_copy(a1, a1_out, out_sem.at[0])]
-        outs[0].start()
-        riders.finish()
+        riders.step(j, n)
+
+    run(n, work)
+    out = pltpu.make_async_copy(a1, a1_out, out_sem.at[0])
+    out.start()
+    riders.finish()
     gather.drain(n)
-    for out in outs:
-        out.wait()
-
-
-def qkv_forward(size, replicas, layer, x, gains, w, riders, fresh):
+    out.wait()
+
+
+def qkv_forward(size, replicas, layer, x, gains, w, riders):
     rows, width = x.shape
     wide = w.shape[1]
     n = chunks(rows)
     halves, columns, outs, sems = riding(riders, replicas)
-    extra = [shape((width, wide), BF)] if fresh else []
     return pl.pallas_call(
-        functools.partial(qkv_kernel, size, layer, columns, fresh),
+        functools.partial(qkv_kernel, size, layer, columns),
         out_shape=[
             shape((size, rows, wide), BF),
             shape((size, rows, width), BF),
         ]
-        + outs
-        + extra,
+        + outs,
         in_specs=[VM, VM, HB] + [HB] * len(riders),
-        out_specs=[VM, HB] + [HB] * (len(outs) + len(extra)),
+        out_specs=[VM, HB] + [HB] * len(outs),
         scratch_shapes=[
             pltpu.VMEM((size, rows, width), BF),
             pltpu.VMEM((width, wide), BF),
@@ -453,7 +666,6 @@
             DMA((1,)),
         ]
         + comm_sems(size, n)
-        + (rider_sems(replicas) if fresh else [])
         + sems,
         compiler_params=params(layer),
         cost_estimate=cost(20e9, 30e6),
@@ -593,7 +805,7 @@
 
     def send(j):
         at = span(j, rc)
-        a = normed(h1_ref[at, :])[0] * gain_ref[layer : layer + 1, :]
+        a = normed(h1_ref[at, :])[0] * gain_ref[layer, 1:2, :]
         a2[g.me, at, :] = a.astype(BF)
         gather.start(j)
 
@@ -679,11 +891,17 @@
     )(h1, gains, wu, wd, *halves)
 
 
-def mlp_back_kernel(
-    size, layer, parts, g_ref, h1_ref, gain_ref, a2_ref, hid_ref, slope_ref, wu_ref, wd_ref,
-    mid_ref, gain_out, gup_ref, gdown_ref,
-    grad, a2, hid, dup, wu, wd, w_sem, *scratch
-):
+def mlp_back_kernel(size, layer, parts, *refs):
+    g_ref, h1_ref, gain_ref, a2_ref, hid_ref, slope_ref, wu_ref, wd_ref = refs[:8]
+    refs = refs[8:]
+    if layer == 1:
+        ys, refs = refs[:2], refs[2:]
+    mid_ref, gain_out, gup_ref, gdown_ref = refs[:4]
+    refs = refs[4:]
+    if layer == 1:
+        y_out, refs = refs[0], refs[1:]
+    grad, a2, hid, dup, wu, wd, w_sem = refs[:7]
+    scratch, refs = refs[7:20], refs[20:]
     rows, width = h1_ref.shape
     hidden = wu_ref.shape[1]
     depth = width // parts
@@ -702,7 +920,26 @@
     ]
     for copy in copies + late:
         copy.start()
-    g.greet()
+    g.greet(side=layer == 1)
+    section = lax.axis_index("section")
+    if layer == 1:
+        y_sem = refs[0]
+
+        def y_copies(own, other, at):
+            return (
+                pltpu.make_async_copy(own, y_out.at[section], y_sem.at[0]),
+                far_copy(
+                    other, y_out.at[at], y_sem.at[1], y_sem.at[2], {"section": 1 - section}
+                ),
+            )
+
+        for i in range(2):
+
+            @pl.when(section == i)
+            def _(i=i):
+                for copy in y_copies(ys[i], ys[1 - i], section):
+                    copy.start()
+
     gather = Gather(g, grad, rc, scratch[:4])
     scatter = Scatter(g, rc, scratch[4:])
 
@@ -752,30 +989,36 @@
 
     def last(j):
         at = span(j, rc)
-        dh, dgain = normed_back(h1_ref[at, :], gain_ref[layer : layer + 1, :], scatter.third(j))
+        dh, dgain = normed_back(h1_ref[at, :], gain_ref[layer, 1:2, :], scatter.third(j))
         mid_ref[at, :] = g_ref[at, :].astype(F32) + dh
         gain_out[...] += dgain
 
     run(n, last)
+    if layer == 1:
+        local, side = y_copies(ys[0], ys[1], 1 - section)
+        local.wait()
+        side.wait_recv()
+        y_copies(ys[0], ys[1], section)[1].wait_send()
     gather.drain(n)
     scatter.drain(n)
 
 
-def mlp_backward(size, replicas, layer, grad, h1, gains, a2, hid, slope, wu, wd):
+def mlp_backward(size, replicas, layer, grad, h1, gains, a2, hid, slope, wu, wd, ys):
     rows, width = h1.shape
     hidden = wu.shape[1]
     parts, depth = replicas, width // replicas
     n = chunks(rows)
     return pl.pallas_call(
         functools.partial(mlp_back_kernel, size, layer, parts),
-        out_shape=(
+        out_shape=[
             shape((rows, width), F32),
             shape((1, width), F32),
             shape((parts, depth, hidden), BF),
             shape((parts, hidden, depth), BF),
-        ),
-        in_specs=[VM, VM, VM, HB, HB, HB, HB, HB],
-        out_specs=(VM, VM, VM, VM),
+        ]
+        + [shape((2, rows, width), BF)] * (len(ys) // 2),
+        in_specs=[VM, VM, VM] + [HB] * (5 + len(ys)),
+        out_specs=[VM, VM, VM, VM] + [HB] * (len(ys) // 2),
         scratch_shapes=[
             pltpu.VMEM((size, rows, width), BF),
             pltpu.VMEM((size, rows, width), BF),
@@ -786,16 +1029,19 @@
             DMA((5,)),
         ]
         + comm_sems(size, n)
-        + scatter_scratch(size, rows, width, n),
+        + scatter_scratch(size, rows, width, n)
+        + [DMA((3,))] * (len(ys) // 2),
         compiler_params=params(6 + layer),
         cost_estimate=cost(60e9, 40e6),
-    )(grad, h1, gains, a2, hid, slope, wu, wd)
+    )(grad, h1, gains, a2, hid, slope, wu, wd, *ys)
 
 
 def attend_back_kernel(
     size, layer, parts, mid_ref, qkv_ref, qm_ref, km_ref, ctx_ref, lse_ref, w_ref,
     dqkv_ref, gout_ref, da, ka, va, kt, dk, dv, w, w_sem, *sems
 ):
+    reduce = Reduce(layer, sems[4:])
+    sems = sems[:4]
     _, rows, wide = qkv_ref.shape
     length = size * rows
     e = qm_ref.shape[2]
@@ -811,7 +1057,7 @@
     copies = [pltpu.make_async_copy(w_ref, w, w_sem.at[0])]
     for copy in copies:
         copy.start()
-    g.greet()
+    g.greet(parts)
     gather = Gather(g, da, rc, sems)
 
     def send(j):
@@ -835,10 +1081,26 @@
     for copy in copies:
         copy.wait()
 
+    def out_grad(z):
+        cols = pl.ds(pl.multiple_of(z * depth, depth), depth)
+        return dg(flat(ctx_ref[...]), flat(da[:, :, cols]), TN)
+
     def work(j):
         at = span(j, rc)
-        gather.relay(j)
-        gather.ready(j)
+
+        @pl.when(j == 0)
+        def _():
+            gather.relay(0)
+            gather.ready(0)
+
+        @pl.when(j == min(1, n - 1))
+        def _():
+            for i in range(1, n):
+                gather.relay(i)
+            for i in range(1, n):
+                gather.ready(i)
+            reduce.send(out_grad)
+
         qm = flat(qm_ref[:, at, :])
         dctx = dg(flat(da[:, at, :]), w[...], NT).astype(BF)
         ctx = flat(ctx_ref[:, at, :])
@@ -874,11 +1136,8 @@
         dqkv_ref[:, :, o + e : o + 2 * e] = (dk[h] * scale).astype(BF).reshape(size, rows, e)
         dqkv_ref[:, :, o + 2 * e : o + 3 * e] = dv[h].astype(BF).reshape(size, rows, e)
 
-    def out_grad(z):
-        cols = pl.ds(pl.multiple_of(z * depth, depth), depth)
-        gout_ref[z] = dg(flat(ctx_ref[...]), flat(da[:, :, cols]), TN).astype(BF)
-
-    run(parts, out_grad)
+    reduce.collect()
+    reduce.finish(gout_ref)
     gather.drain(n)
 
 
@@ -892,7 +1151,7 @@
     n = chunks(rows)
     return pl.pallas_call(
         functools.partial(attend_back_kernel, size, layer, parts),
-        out_shape=(shape(qkv.shape, BF), shape((parts, heads * e, depth), BF)),
+        out_shape=(shape(qkv.shape, BF), shape((heads * e, depth), F32)),
         in_specs=[VM] * 6 + [HB],
         out_specs=(VM, VM),
         scratch_shapes=[
@@ -905,7 +1164,8 @@
             pltpu.VMEM((heads * e, width), BF),
             DMA((1,)),
         ]
-        + comm_sems(size, n),
+        + comm_sems(size, n)
+        + reduce_scratch(parts, heads * e, depth),
         compiler_params=params(8 + layer),
         cost_estimate=cost(90e9, 40e6),
     )(mid, qkv, qm, km, ctx, lse, w)
@@ -949,7 +1209,7 @@
     def last(j):
         at = span(j, rc)
         dh, dgain = normed_back(
-            x_ref[at, :].astype(F32), gain_ref[layer : layer + 1, :], scatter.third(j)
+            x_ref[at, :].astype(F32), gain_ref[layer, 0:1, :], scatter.third(j)
         )
         dx_ref[at, :] = (mid_ref[at, :] + dh).astype(BF)
         gain_out[...] += dgain
@@ -982,22 +1242,13 @@
     )(dqkv, a1, x, mid, gains, w)
 
 
-def far_copy(src, dst, send, recv, target):
-    return pltpu.make_async_remote_copy(
-        src_ref=src, dst_ref=dst, send_sem=send, recv_sem=recv, device_id=target,
-        device_id_type=MESH,
-    )
-
-
 def last_kernel(
-    size, parts, dqkv_ref, a1_ref, x_ref, mid_ref, gain_ref, w_ref, two_ref, above_ref,
-    dx_ref, gain_out, gqkv_ref,
-    w, own, away, came, over, back, gsum, gcame, w_sem,
-    z_send, z_recv, y_send, y_recv, g_send, g_recv, *scratch
+    size, parts, dqkv_ref, a1_ref, x_ref, mid_ref, gain_ref, w_ref, two_ref, above_ref, dx1_ref,
+    gain_out, gqkv_ref, dx_out,
+    w, dx, gsum, gcame, w_sem, x_sem, x_send, x_recv, g_send, g_recv, *scratch
 ):
     rows, width = x_ref.shape
     depth = width // parts
-    half = depth // 2
     n = chunks(rows)
     rc = rows // n
     g = Group(size)
@@ -1005,33 +1256,41 @@
     d = lax.axis_index("dp")
     copy = pltpu.make_async_copy(w_ref, w, w_sem.at[0])
     copy.start()
+    reduce = Reduce(0, scratch[:9])
+    scatter = Scatter(g, rc, scratch[9:])
     g.greet(parts)
-    scatter = Scatter(g, rc, scratch)
+
+    def upper():
+        return far_copy(
+            dx1_ref, dx_out.at[0], x_send.at[n], x_recv.at[n], {"section": 1 - section}
+        )
+
+    def keep_upper():
+        return pltpu.make_async_copy(dx1_ref, dx_out.at[1], x_sem.at[0])
+
+    def lower(j):
+        at = span(j, rc)
+        return far_copy(
+            dx.at[at], dx_out.at[1, at], x_send.at[j], x_recv.at[j], {"section": 1 - section}
+        )
+
+    def keep_lower(j):
+        at = span(j, rc)
+        return pltpu.make_async_copy(dx.at[at], dx_out.at[0, at], x_sem.at[j])
+
+    @pl.when(section == 0)
+    def _():
+        upper().start()
+
+    @pl.when(section == 1)
+    def _():
+        keep_upper().start()
 
     def block(z):
         cols = pl.ds(pl.multiple_of(z * depth, depth), depth)
         return dg(flat(a1_ref[:, :, cols]), flat(dqkv_ref[...]), TN)
 
-    def z_copy(k, i):
-        part = pl.ds(pl.multiple_of(i * half, half), half)
-        return far_copy(
-            away.at[k - 1, part], came.at[k - 1, part], z_send.at[k - 1, i], z_recv.at[k - 1, i],
-            {"dp": lax.rem(d + k, parts)},
-        )
-
-    def y_copy(i):
-        part = pl.ds(pl.multiple_of(i * half, half), half)
-        return far_copy(
-            over.at[part], back.at[part], y_send.at[i], y_recv.at[i], {"section": 1 - section}
-        )
-
-    def send(i):
-        k = i + 1
-        away[i] = block(lax.rem(d + k, parts)).astype(BF)
-        z_copy(k, 0).start()
-        z_copy(k, 1).start()
-
-    run(parts - 1, send)
+    reduce.send(block)
     copy.wait()
 
     def work(j):
@@ -1044,13 +1303,21 @@
         scatter.second(j)
 
     run(n, work)
-    own[...] = block(d)
     gsum[0] = jnp.zeros_like(gsum[0])
 
     def last(j):
         at = span(j, rc)
-        dh, dgain = normed_back(x_ref[at, :].astype(F32), gain_ref[0:1, :], scatter.third(j))
-        dx_ref[at, :] = (mid_ref[at, :] + dh).astype(BF)
+        dh, dgain = normed_back(x_ref[at, :].astype(F32), gain_ref[0, 0:1, :], scatter.third(j))
+        dx[at, :] = (mid_ref[at, :] + dh).astype(BF)
+
+        @pl.when(section == 0)
+        def _():
+            keep_lower(j).start()
+
+        @pl.when(section == 1)
+        def _():
+            lower(j).start()
+
         gsum[0, 0:1, :] += dgain
 
     run(n, last)
@@ -1082,48 +1349,32 @@
         gsum[stage + 1] = total
         sent.extend(copies)
 
-    exchange(0)
-    exchange(1)
-
-    def collect(i):
-        part = pl.ds(pl.multiple_of(i * half, half), half)
-        total = own[part, :]
-        for k in range(1, parts):
-            z_copy(k, i).wait_recv()
-            total = total + came[k - 1, part, :].astype(F32)
-        own[part, :] = total
-        over[part, :] = total.astype(BF)
-
-        @pl.when(section == 1)
-        def _():
-            y_copy(i).start()
-
-    run(2, collect)
-    exchange(2)
-    exchange(3)
+    for stage in range(4):
+        exchange(stage)
     gain_out[...] = gsum[4]
+    reduce.collect()
 
     @pl.when(section == 0)
     def _():
-        y_copy(0).wait_recv()
-        y_copy(1).wait_recv()
-
-    gqkv_ref[...] = own[...] + back[...].astype(F32)
+        for j in range(n):
+            lower(j).wait_recv()
+            keep_lower(j).wait()
+        upper().wait_send()
 
     @pl.when(section == 1)
     def _():
-        y_copy(0).wait_send()
-        y_copy(1).wait_send()
-
+        keep_upper().wait()
+        upper().wait_recv()
+        for j in range(n):
+            lower(j).wait_send()
+
+    reduce.finish(gqkv_ref)
     for copy in sent:
         copy.wait_send()
-    for k in range(1, parts):
-        z_copy(k, 0).wait_send()
-        z_copy(k, 1).wait_send()
     scatter.drain(n)
 
 
-def last_backward(size, replicas, dqkv, a1, x, mid, gains, w, two, above):
+def last_backward(size, replicas, dqkv, a1, x, mid, gains, w, two, above, dx1):
     rows, width = x.shape
     wide = w.shape[1]
     depth = width // replicas
@@ -1132,33 +1383,29 @@
     return pl.pallas_call(
         functools.partial(last_kernel, size, replicas),
         out_shape=(
-            shape((rows, width), BF),
             shape((8, width), F32),
             shape((depth, wide), F32),
+            shape((2, rows, width), BF),
         ),
-        in_specs=[VM] * 5 + [HB, VM, VM],
-        out_specs=(VM, VM, VM),
+        in_specs=[VM] * 5 + [HB, VM, VM, HB],
+        out_specs=(VM, VM, HB),
         scratch_shapes=[
             pltpu.VMEM((width, wide), BF),
-            pltpu.VMEM((depth, wide), F32),
-            pltpu.VMEM((replicas - 1, depth, wide), BF),
-            pltpu.VMEM((replicas - 1, depth, wide), BF),
-            pltpu.VMEM((depth, wide), BF),
-            pltpu.VMEM((depth, wide), BF),
+            pltpu.VMEM((rows, width), BF),
             pltpu.VMEM((5, 8, width), F32),
             pltpu.VMEM((slots, 8, width), F32),
             DMA((1,)),
-            DMA((replicas - 1, 2)),
-            DMA((replicas - 1, 2)),
-            DMA((2,)),
-            DMA((2,)),
+            DMA((n,)),
+            DMA((n + 1,)),
+            DMA((n + 1,)),
             DMA((slots,)),
             DMA((slots,)),
         ]
+        + reduce_scratch(replicas, depth, wide)
         + scatter_scratch(size, rows, width, n),
         compiler_params=params(10),
         cost_estimate=cost(40e9, 30e6),
-    )(dqkv, a1, x, mid, gains, w, two, above)
+    )(dqkv, a1, x, mid, gains, w, two, above, dx1)
 
 
 def scene_masks(segments, e):
@@ -1195,98 +1442,78 @@
         up_weight[0],
         down_weight[0],
     ]
-    def halves(w):
-        w = w.astype(BF).reshape((2, -1, w.shape[1]))
-        keep = jnp.where(section == 0, w[0], w[1])
-        other = swap_section(jnp.where(section == 0, w[1], w[0]))
-        return [jnp.where(section == layer, keep, other) for layer in range(2)]
-
-    h_qkv, h_out, h_up, h_down = [halves(w) for w in mine]
-    gains_mine = jnp.concatenate([norm_one_gain, norm_two_gain], axis=0)
-    gains_other = swap_section(gains_mine)
-    gains = [jnp.where(section == layer, gains_mine, gains_other) for layer in range(2)]
-    gains_one = jnp.stack([gains[0][0], gains[1][0]])
-    gains_two = jnp.stack([gains[0][1], gains[1][1]])
+    mine = [w.astype(BF).reshape((2, -1, w.shape[1])) for w in mine]
+    gains = jnp.concatenate(
+        [norm_one_gain, norm_two_gain, jnp.zeros((6, norm_one_gain.shape[1]), F32)], axis=0
+    )
     segments = lax.dynamic_index_in_dim(segment_ids, section, 0, keepdims=False)
     x = lax.dynamic_index_in_dim(block_input, section, 0, keepdims=False)
     head_dim = qkv_weight.shape[3] // 3
     qm, km = scene_masks(segments.reshape((size, -1)), head_dim)
-    qkv, a1, w_out_0, w_qkv_0 = qkv_forward(
-        size, replicas, 0, x, gains_one, h_qkv[0], [(h_out[0], True)], True
+    qkv, gains, a1, w_qkv_0, w_out_0, h_qkv, h_out, h_up, h_down = first_forward(
+        size, replicas, x, gains, mine
     )
     h1, ctx, lse, w_up_0, w_down_0 = attend(
-        size, replicas, 0, qkv, qm, km, x, w_out_0, [(h_up[0], False), (h_down[0], True)]
+        size, replicas, 0, qkv, qm, km, x, w_out_0, [(h_up, 0, False), (h_down, 0, True)]
     )
     y0, a2, hid, slope, w_qkv_1, w_out_1 = mlp_forward(
-        size, replicas, 0, h1, gains_two, w_up_0, w_down_0, [(h_qkv[1], False), (h_out[1], True)]
+        size, replicas, 0, h1, gains, w_up_0, w_down_0, [(h_qkv, 1, False), (h_out, 1, True)]
     )
     kept = [(x, a1, qkv, ctx, lse, h1, a2, hid, slope)]
     qkv, a1, w_up_1 = qkv_forward(
-        size, replicas, 1, y0, gains_one, w_qkv_1, [(h_up[1], False)], False
+        size, replicas, 1, y0, gains, w_qkv_1, [(h_up, 1, False)]
     )
     h1, ctx, lse, w_down_1 = attend(
-        size, replicas, 1, qkv, qm, km, y0, w_out_1, [(h_down[1], True)]
-    )
-    y1, a2, hid, slope = mlp_forward(size, replicas, 1, h1, gains_two, w_up_1, w_down_1, [])
+        size, replicas, 1, qkv, qm, km, y0, w_out_1, [(h_down, 1, True)]
+    )
+    y1, a2, hid, slope = mlp_forward(size, replicas, 1, h1, gains, w_up_1, w_down_1, [])
     kept.append((y0, a1, qkv, ctx, lse, h1, a2, hid, slope))
-    ys = [y0, y1]
     weights = [
         (w_qkv_0, w_out_0, w_up_0, w_down_0),
         (w_qkv_1, w_out_1, w_up_1, w_down_1),
     ]
-    other_y = swap_section(jnp.where(section == 0, ys[1], ys[0]))
     grad = lax.dynamic_index_in_dim(cotangent, section, 0, keepdims=False)
-    dxs = [None, None]
 
     def reduce_rows(value):
         return lax.psum_scatter(value, "dp", scatter_dimension=0, tiled=False)
 
-    for layer in (1, 0):
-        x, a1, qkv, ctx, lse, h1, a2, hid, slope = kept[layer]
-        w_qkv, w_out, w_up, w_down = weights[layer]
-        mid, gain_two, g_up, g_down = mlp_backward(
-            size, replicas, layer, grad, h1, gains_two, a2, hid, slope, w_up, w_down
-        )
-        if layer == 0:
-            mid, sums = lax.optimization_barrier((mid, sums))
-        d_qkv, g_out = attend_backward(size, replicas, layer, mid, qkv, qm, km, ctx, lse, w_out)
-        up, down = reduce_rows(g_up), reduce_rows(g_down)
-        if layer == 1:
-            grad, gain_one, g_qkv = qkv_backward(
-                size, replicas, layer, d_qkv, a1, x, mid, gains_one, w_qkv
-            )
-            gains_above = jnp.concatenate([gain_one, gain_two], axis=0)
-            grad, up, down = lax.optimization_barrier((grad, up, down))
-            sums = [reduce_rows(g_qkv), reduce_rows(g_out), up, down]
-        else:
-            d_qkv, g_out, up, down = lax.optimization_barrier((d_qkv, g_out, up, down))
-            grad, gains, qkv_grad = last_backward(
-                size, replicas, d_qkv, a1, x, mid, gains_one, w_qkv, gain_two, gains_above
-            )
-            lower = [None, reduce_rows(g_out), up, down]
-        dxs[layer] = grad
-    other_dx = swap_section(jnp.where(section == 0, dxs[1], dxs[0]))
-
-    def own_layer(mine, other):
-        first = jnp.where(section == 0, mine, other)
-        second = jnp.where(section == 0, other, mine)
-        return jnp.stack([first, second])[None]
-
-    layer_out = own_layer(jnp.where(section == 0, ys[0], ys[1]), other_y)
-    input_out = own_layer(jnp.where(section == 0, dxs[0], dxs[1]), other_dx)
+    x, a1, qkv, ctx, lse, h1, a2, hid, slope = kept[1]
+    w_qkv, w_out, w_up, w_down = weights[1]
+    mid, gain_two, g_up, g_down, layer_out = mlp_backward(
+        size, replicas, 1, grad, h1, gains, a2, hid, slope, w_up, w_down, [y0, y1]
+    )
+    d_qkv, out_1 = attend_backward(size, replicas, 1, mid, qkv, qm, km, ctx, lse, w_out)
+    up_1, down_1 = reduce_rows(g_up), reduce_rows(g_down)
+    dx1, gain_one, g_qkv = qkv_backward(size, replicas, 1, d_qkv, a1, x, mid, gains, w_qkv)
+    gains_above = jnp.concatenate([gain_one, gain_two], axis=0)
+    dx1, up_1, down_1 = lax.optimization_barrier((dx1, up_1, down_1))
+    qkv_1 = reduce_rows(g_qkv)
+
+    x, a1, qkv, ctx, lse, h1, a2, hid, slope = kept[0]
+    w_qkv, w_out, w_up, w_down = weights[0]
+    mid, gain_two, g_up, g_down = mlp_backward(
+        size, replicas, 0, dx1, h1, gains, a2, hid, slope, w_up, w_down, []
+    )
+    mid, qkv_1 = lax.optimization_barrier((mid, qkv_1))
+    d_qkv, out_0 = attend_backward(size, replicas, 0, mid, qkv, qm, km, ctx, lse, w_out)
+    up_0, down_0 = reduce_rows(g_up), reduce_rows(g_down)
+    d_qkv, up_0, down_0 = lax.optimization_barrier((d_qkv, up_0, down_0))
+    gains, qkv_0, input_out = last_backward(
+        size, replicas, d_qkv, a1, x, mid, gains, w_qkv, gain_two, gains_above, dx1
+    )
 
     def finish(zero, one):
         send = swap_section(jnp.where(section == 0, one, zero))
         return jnp.where(section == 0, zero, one).astype(F32) + send.astype(F32)
 
-    qkv_grad = jnp.where(
-        section == 0, qkv_grad, sums[0].astype(F32) + swap_section(sums[0]).astype(F32)
-    )
-    out_grad, up_grad, down_grad = [finish(a, b) for a, b in zip(lower[1:], sums[1:])]
+    other_qkv_1 = swap_section(qkv_1)
+    qkv_grad = jnp.where(section == 0, qkv_0, qkv_1.astype(F32) + other_qkv_1.astype(F32))
+    out_grad = jnp.where(section == 0, out_0, out_1)
+    up_grad, down_grad = finish(up_0, up_1), finish(down_0, down_1)
     gains = lax.dynamic_slice_in_dim(gains, 2 * section, 2, 0)
     return (
-        layer_out,
-        input_out,
+        layer_out[None],
+        input_out[None],
         gains[0:1],
         qkv_grad.reshape(qkv_weight.shape),
         out_grad.reshape(out_weight.shape),

time: 753 us -> 731 us (0.971)
  Pallas kernels: 634 us -> 655 us
  other arithmetic: 32.5 us -> 14.8 us
  waiting for transfers between devices: 37.8 us -> 21 us
  starting transfers between devices: 14.5 us -> 6.23 us
    ppermute x11 -> x3, waiting for transfers between devices: 36.9 us -> 0.01 us  [swap_section(): return lax.ppermute(value, 'section', [(0, 1), (1, 0)])]
    reduce_scatter x7 -> x5, waiting for transfers between devices: 0.08 us -> 20.2 us  [reduce_rows(): return lax.psum_scatter(value, 'dp', scatter_dimension=0, tiled=False)]
    pallas_call x2, Pallas kernels: 82.6 us -> 101 us  [the longest x1 58.6 us: first_forward(): pl.pallas_call(functools.partial(first_kernel, size, replicas), out_shape...]
    ppermute x11 -> x3, starting transfers between devices: 14.2 us -> 6.03 us  [swap_section(): return lax.ppermute(value, 'section', [(0, 1), (1, 0)])]
  transfers between devices with their start and end apart: 18 -> 8, of which waited for: 2 -> 1; matrix products, arithmetic and copies ran while one was open for 5% -> 1% of each run, Pallas kernels for 44% -> 40%
where the time goes in v4:
time: 731 us; the launch traced here: 722 us
  Pallas kernels  655 us (90%)
  waiting for transfers between devices  21 us (3%)
  other arithmetic  14.8 us (2%)
  between operations  14.3 us (2%)
  local copies, waits for them, and re-layouts  11.2 us (2%)
    pallas_call x2, Pallas kernels, attend_backward(): pl.pallas_call(functools.partial(attend_back_kernel, size, layer, parts),...  144 us
    pallas_call x2, Pallas kernels, attend(): pl.pallas_call(functools.partial(attend_kernel, size, layer, columns), ou...  108 us
    pallas_call x2, Pallas kernels, mlp_backward(): pl.pallas_call(functools.partial(mlp_back_kernel, size, layer, parts), ou...  106 us
    pallas_call x2, Pallas kernels, mlp_forward(): pl.pallas_call(functools.partial(mlp_kernel, size, layer, columns), out_s...  104 us
    pallas_call x1, Pallas kernels, first_forward(): pl.pallas_call(functools.partial(first_kernel, size, replicas), out_shape...  58.6 us
    pallas_call x1, Pallas kernels, last_backward(): pl.pallas_call(functools.partial(last_kernel, size, replicas), out_shape=...  57.6 us
    pallas_call x1, Pallas kernels, qkv_forward(): pl.pallas_call(functools.partial(qkv_kernel, size, layer, columns), out_s...  42.1 us
    pallas_call x1, Pallas kernels, qkv_backward(): pl.pallas_call(functools.partial(qkv_back_kernel, size, layer, parts), ou...  34.4 us
  transfers between devices with their start and end apart: 8, of which 1 were waited for; matrix products, arithmetic and copies ran while one was open for 1% of the time, Pallas kernels for 40%

profile of v4, /device:TPU:0, one launch (start us, length us, event | category | flops | bytes accessed | tf_op | source)
XLA Modules:
  0.0 722.3 jit_solution(10827715076066073349)
XLA Ops:
  7.2 0.0 copy-start
  7.2 0.0 copy-start.8
  7.2 0.0 reduce-scatter.6.cloned.1.call-start
  7.3 0.0 copy-start.9
  7.3 1.3 convert_element_type.55
  8.6 0.1 convert_element_type.56
  8.7 0.0 copy-start.11
  8.7 1.1 copy.19.wq_ref
  9.8 0.0 copy-done.8
  9.8 0.9 convert_element_type.59
  10.7 0.8 convert_element_type.61
  11.5 0.7 convert_element_type.57
  12.2 0.0 copy-start.15
  12.2 0.0 copy-start.16
  12.2 3.0 dynamic-slice_bitcast_fusion
  15.3 0.1 pad.4.clone
  15.4 1.2 select_convert_fusion
  16.6 0.0 copy-done.16
  16.6 0.7 maximum_maximum_fusion.gain_ref
  17.3 58.6 %shard_map.152 = (bf16[4,512,768]{2,1,0:T(8,128)(2,1)}, f32[2,8,1024]{2,1,0:T(8,128)}, bf16[4,512,1024]{2,1,0:T(8,128)(2,1)}, bf16[1024,768]{1,0:T(8,128)(2,1)},...) custom-call(bf16[512,1024]{1,0:T(8,128)(2,1)} %get-tuple-element.136, ...), custom_call_target="tpu_custom_call" | custom-call | flops 30000001024 | bytes 30000000 | tf_op jit(solution)/shard_map/pallas_call | solution.py:574
  75.9 59.3 %shard_map.153 = (f32[512,1024]{1,0:T(8,128)}, bf16[4,512,256]{2,1,0:T(8,128)(2,1)}, f32[4,4,512]{2,1,0:T(4,128)}, bf16[1024,1024]{1,0:T(8,128)(2,1)}, bf16[1024,1024]{1,0:T(8,128)(2,1)}) custom-call(bf16[4,512,768]{2,1,0:T(8,128)(2,1)} %get-tuple-element.66.refs_0_.qkv_ref, bf16[4,512,64]{2,1,0:T(8,128)(2,1)} %get-tuple-element.135.refs_1_.qm_ref, ...), custom_call_target="tpu_custom_call" | custom-call | flops 60000002048 | bytes 20000000 | tf_op jit(solution)/shard_map/pallas_call | solution.py:758
  135.2 53.2 %shard_map.154 = (bf16[512,1024]{1,0:T(8,128)(2,1)}, bf16[4,512,1024]{2,1,0:T(8,128)(2,1)}, bf16[4,512,1024]{2,1,0:T(8,128)(2,1)}, bf16[4,512,1024]{2,1,0:T(8,12...) custom-call(f32[512,1024]{1,0:T(8,128)} %get-tuple-element.70.refs_0_.refs_1_, ...), custom_call_target="tpu_custom_call" | custom-call | flops 49999998976 | bytes 30000000 | tf_op jit(solution)/shard_map/pallas_call | solution.py:866
  188.4 42.1 %shard_map.155 = (bf16[4,512,768]{2,1,0:T(8,128)(2,1)}, bf16[4,512,1024]{2,1,0:T(8,128)(2,1)}, bf16[1024,1024]{1,0:T(8,128)(2,1)}) custom-call(bf16[512,1024]{1,0:T(8,128)(2,1)} %get-tuple-element.76.refs_0_.refs_3_.refs_8_.x_ref, f32[2,8,1024]{2,1,0:T(8,128)} %get-tuple-element.71.refs_1_.refs_2_.gain_ref, ...), custom_call_target="tpu_custom_call" | custom-call | flops 20000000000 | bytes 30000000 | tf_op jit(solution)/shard_map/pallas_call | solution.py:653
  230.5 49.1 %shard_map.156 = (f32[512,1024]{1,0:T(8,128)}, bf16[4,512,256]{2,1,0:T(8,128)(2,1)}, f32[4,4,512]{2,1,0:T(4,128)}, bf16[1024,1024]{1,0:T(8,128)(2,1)}) custom-call(bf16[4,512,768]{2,1,0:T(8,128)(2,1)} %get-tuple-element.78.refs_0_.qkv_ref, bf16[4,512,64]{2,1,0:T(8,128)(2,1)} %get-tuple-element.135.refs_1_.qm_ref, ...), custom_call_target="tpu_custom_call" | custom-call | flops 60000002048 | bytes 20000000 | tf_op jit(solution)/shard_map/pallas_call | solution.py:758
  279.6 51.0 %shard_map.157 = (bf16[512,1024]{1,0:T(8,128)(2,1)}, bf16[4,512,1024]{2,1,0:T(8,128)(2,1)}, bf16[4,512,1024]{2,1,0:T(8,128)(2,1)}, bf16[4,512,1024]{2,1,0:T(8,128)(2,1)}) custom-call(f32[512,1024]{1,0:T(8,128)} %get-tuple-element.80.refs_0_.refs_1_, f32[2,8,1024]{2,1,0:T(8,128)} %get-tuple-element.71.refs_1_.refs_2_.gain_ref, ...), custom_call_target="tpu_custom_call" | custom-call | flops 49999998976 | bytes 30000000 | tf_op jit(solution)/shard_map/pallas_call | solution.py:866
  330.6 52.6 %shard_map.158 = (f32[512,1024]{1,0:T(8,128)}, f32[1,1024]{1,0:T(1,128)}, bf16[4,256,1024]{2,1,0:T(8,128)(2,1)}, bf16[4,1024,256]{2,1,0:T(8,128)(2,1)}, bf16[2,512,1024]{2,1,0:T(8,128)(2,1)}) custom-call(bf16[512,1024]{1,0:T(8,128)(2,1)} %get-tuple-element.137.refs_0_, f32[512,1024]{1,0:T(8,128)} %get-tuple-element.80.refs_0_.refs_1_, ...), custom_call_target="tpu_custom_call" | custom-call | flops 60000002048 | bytes 40000000 | tf_op jit(solution)/shard_map/pallas_call | solution.py:1011
  383.2 0.0 reduce-scatter.6.cloned.1.call-update
  383.2 0.0 reduce-scatter.8.cloned.1.call-start
  383.2 0.7 reduce-scatter.8.cloned.1.call-update
  384.0 0.0 reduce-scatter.10.cloned.1.call-start
  384.0 72.0 %shard_map.159 = (bf16[4,512,768]{2,1,0:T(8,128)(2,1)}, f32[256,256]{1,0:T(8,128)}) custom-call(f32[512,1024]{1,0:T(8,128)} %get-tuple-element.88.mid_ref, bf16[4,512,768]{2,1,0:T(8,128)(2,1)} %get-tuple-element.78.refs_0_.qkv_ref, bf16[4,512,64]{2,1,0:T(8,128)(2,1)} %get-tuple-element.135.refs_1_.qm_ref, ...), custom_call_target="tpu_custom_call" | custom-call | flops 89999998976 | bytes 40000000 | tf_op jit(solution)/shard_map/pallas_call | solution.py:1152
  456.0 34.4 %shard_map.160 = (bf16[512,1024]{1,0:T(8,128)(2,1)}, f32[1,1024]{1,0:T(1,128)}, bf16[4,256,768]{2,1,0:T(8,128)(2,1)}) custom-call(bf16[4,512,768]{2,1,0:T(8,128)(2,1)} %get-tuple-element.91.dqkv_ref, bf16[4,512,1024]{2,1,0:T(8,128)(2,1)} %get-tuple-element.92.a1_ref, bf16[512,1024]{1,0:T(8,128)(2,1)} %get-tuple-element.76.refs_0_.refs_3_.refs_8_.x_ref, ...), custom_call_target="tpu_custom_call" | custom-call | flops 30000001024 | bytes 30000000 | tf_op jit(solution)/shard_map/pallas_call | solution.py:1226
  490.4 0.0 reduce-scatter.10.cloned.1.call-update
  490.5 0.0 reduce-scatter.14.cloned.1.call-start
  490.5 0.0 reduce-scatter.6.cloned.1.call-done
  490.5 0.0 reduce-scatter.8.cloned.1.call-done
  490.6 53.0 %shard_map.161 = (f32[512,1024]{1,0:T(8,128)}, f32[1,1024]{1,0:T(1,128)}, bf16[4,256,1024]{2,1,0:T(8,128)(2,1)}, bf16[4,1024,256]{2,1,0:T(8,128)(2,1)}) custom-call(bf16[512,1024]{1,0:T(8,128)(2,1)} %get-tuple-element.96.refs_0_.dx1_ref, f32[512,1024]{1,0:T(8,128)} %get-tuple-element.70.refs_0_.refs_1_, ...), custom_call_target="tpu_custom_call" | custom-call | flops 60000002048 | bytes 40000000 | tf_op jit(solution)/shard_map/pallas_call | solution.py:1011
  543.6 0.0 reduce-scatter.14.cloned.1.call-update
  543.6 0.0 reduce-scatter.12.cloned.1.call-start
  543.7 0.6 copy-done.13
  544.2 0.0 copy-done.14
  544.3 0.6 pad_maximum_fusion.above_ref
  544.9 2.5 collective-permute-start
  547.4 0.0 reduce-scatter.12.cloned.1.call-update
  547.4 71.9 %shard_map.162 = (bf16[4,512,768]{2,1,0:T(8,128)(2,1)}, f32[256,256]{1,0:T(8,128)}) custom-call(f32[512,1024]{1,0:T(8,128)} %get-tuple-element.102.mid_ref, bf16[4,512,768]{2,1,0:T(8,128)(2,1)} %get-tuple-element.66.refs_0_.qkv_ref, bf16[4,512,64]{2,1,0:T(8,128)(2,1)} %get-tuple-element.135.refs_1_.qm_ref, ...), custom_call_target="tpu_custom_call" | custom-call | flops 89999998976 | bytes 40000000 | tf_op jit(solution)/shard_map/pallas_call | solution.py:1152
  619.4 1.7 broadcast_select_fusion.2
  621.1 20.2 %reduce-scatter.12.cloned.1.call-done = bf16[1,256,1024]{2,1,0:T(8,128)(2,1)} async-done(((bf16[4,256,1024]{2,1,0:T(8,128)(2,1)}), bf16[1,256,1024]{2,1,0:T(8,128)(2,1)}) %reduce-scatter.12.cloned.1.call-update) | async-done | bytes 524304 | tf_op jit(solution)/shard_map/reduce_scatter | solution.py:1478
  641.3 0.9 broadcast_select_fusion
  642.2 2.4 collective-permute-start.2
  644.6 0.1 broadcast_select_fusion.1
  644.7 1.1 collective-permute-start.1
  645.8 57.6 %shard_map.163 = (f32[8,1024]{1,0:T(8,128)}, f32[256,768]{1,0:T(8,128)}, bf16[2,512,1024]{2,1,0:T(8,128)(2,1)}) custom-call(bf16[4,512,768]{2,1,0:T(8,128)(2,1)} %get-tuple-element.108.dqkv_ref, bf16[4,512,1024]{2,1,0:T(8,128)(2,1)} %get-tuple-element.109.a1_ref, bf16[512,1024]{1,0:T(8,128)(2,1)} %get-tuple-element.136.x_ref.refs_3_, ...), custom_call_target="tpu_custom_call" | custom-call | flops 40000000000 | bytes 30000000 | tf_op jit(solution)/shard_map/pallas_call | solution.py:1383
  703.4 0.0 collective-permute-done
  703.4 1.3 add_select_fusion
  704.7 1.1 copy.20
  705.9 1.4 constant_dynamic-slice_fusion.1
  707.3 0.0 collective-permute-done.2
  707.3 2.3 add_bitcast_fusion
  709.6 0.0 collective-permute-done.1
  709.6 0.0 copy-done.7
  709.6 2.3 add_bitcast_fusion.1
  711.9 1.3 copy.23
  713.2 1.0 copy-done.3
  714.3 1.3 copy.24
  (28 shorter events, 0.1 us)
Async XLA Ops:
  7.2 5.0 copy-start
  7.2 2.6 copy-start.8
  7.2 483.3 %reduce-scatter.6.cloned.1.call-start = ((), (), s32[]{:S(2)}) async-start(), calls=%async_computation.5 | async-start | bytes 2621440 | tf_op jit(solution)/shard_map/reduce_scatter | solution.py:1478
  7.3 3.4 copy-start.9
  8.7 2.8 copy-start.11
  12.2 4.4 copy-start.15
  12.2 4.4 copy-start.16
  383.2 107.4 %reduce-scatter.8.cloned.1.call-start = ((), (), s32[]{:S(2)}) async-start(), calls=%async_computation.6 | async-start | bytes 2621440 | tf_op jit(solution)/shard_map/reduce_scatter | solution.py:1478
  384.0 160.9 %reduce-scatter.10.cloned.1.call-start = ((), (), s32[]{:S(2)}) async-start(), calls=%async_computation.7 | async-start | bytes 1966080 | tf_op jit(solution)/shard_map/reduce_scatter | solution.py:1478
  490.5 130.7 %reduce-scatter.14.cloned.1.call-start = ((), (), s32[]{:S(2)}) async-start(), calls=%async_computation.9 | async-start | bytes 2621440 | tf_op jit(solution)/shard_map/reduce_scatter | solution.py:1478
  543.6 0.7 copy-start.13
  543.6 0.7 copy-start.14
  543.6 97.7 %reduce-scatter.12.cloned.1.call-start = ((), (), s32[]{:S(2)}) async-start(), calls=%async_computation.8 | async-start | bytes 2621440 | tf_op jit(solution)/shard_map/reduce_scatter | solution.py:1478
  544.9 158.5 %collective-permute-start = (bf16[256,768]{1,0:T(8,128)(2,1)}, bf16[256,768]{1,0:T(8,128)(2,1)S(1)}, u32[]{:S(2)}, u32[]{:S(2)}) collective-permute-start(bf16[256,768]{1,0:T(8,128)(2,1)} %bitcast.37), channel_id=1, source_target_pairs={{0,16},{16,0},{1,17},{17,1},{2,18},{18,2},{3,19},{19,3},{4,20},{20... | collective-permute-start | bytes 1179656 | tf_op jit(solution)/shard_map/ppermute | solution.py:1421
  547.4 72.0 %copy-start.12 = (f32[256,256]{1,0:T(8,128)S(1)}, f32[256,256]{1,0:T(8,128)}, u32[]{:S(2)}) copy-start(f32[256,256]{1,0:T(8,128)} %get-tuple-element.119) | copy-start | bytes 786436
  547.4 93.9 %copy-start.5 = (bf16[1,1024,256]{2,1,0:T(8,128)(2,1)S(1)}, bf16[1,1024,256]{2,1,0:T(8,128)(2,1)}, u32[]{:S(2)}) copy-start(bf16[1,1024,256]{2,1,0:T(8,128)(2,1)} %reduce-scatter.8.cloned.1.call-done) | copy-start | bytes 1572868
  619.4 25.2 %copy-start.4 = (bf16[1,256,1024]{2,1,0:T(8,128)(2,1)S(1)}, bf16[1,256,1024]{2,1,0:T(8,128)(2,1)}, u32[]{:S(2)}) copy-start(bf16[1,256,1024]{2,1,0:T(8,128)(2,1)} %reduce-scatter.6.cloned.1.call-done) | copy-start | bytes 1572868
  642.2 65.1 %collective-permute-start.2 = (bf16[1024,256]{1,0:T(8,128)(2,1)}, bf16[1024,256]{1,0:T(8,128)(2,1)}, u32[]{:S(2)}, u32[]{:S(2)}) collective-permute-start(bf16[1024,256]{1,0:T(8,128)(2,1)} %broadcast_select_fusion), channel_id=1, source_target_pairs={{0,16},{16,0},{1,17},{17,1},{2,18},{18,2},{3,19},{19,3},{4,20},{20... | collective-permute-start | bytes 1572872 | tf_op jit(solution)/shard_map/ppermute | solution.py:1421
  644.7 65.0 %collective-permute-start.1 = (bf16[256,1024]{1,0:T(8,128)(2,1)S(1)}, bf16[256,1024]{1,0:T(8,128)(2,1)}, u32[]{:S(2)}, u32[]{:S(2)}) collective-permute-start(bf16[256,1024]{1,0:T(8,128)(2,1)S(1)} %broadcast_select_fusion.1), channel_id=1, source_target_pairs={{0,16},{16,0},{1,17},{17,1},{2,18},{18,2},{3,19},{19,3},{4,20},{20... | collective-permute-start | bytes 1572872 | tf_op jit(solution)/shard_map/ppermute | solution.py:1421
  645.8 57.6 %copy-start.10 = (bf16[1,256,768]{2,1,0:T(8,128)(2,1)S(1)}, bf16[1,256,768]{2,1,0:T(8,128)(2,1)}, u32[]{:S(2)}) copy-start(bf16[1,256,768]{2,1,0:T(8,128)(2,1)} %reduce-scatter.10.cloned.1.call-done) | copy-start | bytes 1179652
  703.4 3.9 copy-start.6
  704.7 4.9 copy-start.7
  707.3 4.6 copy-start.2
  711.9 2.3 copy-start.3
  711.9 3.7 copy-start.1
Sparse Core Ops, SparseCore 0:
  383.3 51.5 reduce-scatter.5
  437.3 43.7 reduce-scatter.7
  490.6 35.1 reduce-scatter.9
  543.7 50.0 reduce-scatter.13
  596.1 45.1 reduce-scatter.11

commit v5 on v4

--- a/solution.py
+++ b/solution.py
@@ -329,6 +329,108 @@
         for k in range(1, self.replicas):
             self.z_copy(k, 0).wait_send()
             self.z_copy(k, 1).wait_send()
+
+
+class HalfSwap:
+    def __init__(self, src, came, sems):
+        self.src, self.came, self.sems = src, came, sems
+        self.s = lax.axis_index("section")
+        self.rows = came.shape[1]
+
+    def copy(self):
+        at = pl.ds(pl.multiple_of((1 - self.s) * self.rows, self.rows), self.rows)
+        return far_copy(
+            self.src.at[:, at],
+            self.came,
+            self.sems.at[0],
+            self.sems.at[1],
+            {"section": 1 - self.s},
+        )
+
+
+def half_scratch(replicas, rows, cols):
+    rows = rows // 2
+    all_, far = pltpu.VMEM((replicas, rows, cols), BF), pltpu.VMEM((replicas - 1, rows, cols), BF)
+    one = pltpu.VMEM((rows, cols), BF)
+    z = DMA((replicas - 1,))
+    return [all_, all_, far, far, pltpu.VMEM((rows, cols), F32), one, one, DMA((3,)), z, z, DMA((2,))]
+
+
+HALF = 11
+
+
+class HalfReduce:
+    def __init__(self, layer, scratch):
+        self.layer = layer
+        self.mine, self.other, self.away, self.came, self.own, self.over, self.back = scratch[:7]
+        self.in_sem, self.z_send, self.z_recv, self.y_sem = scratch[7:]
+        self.replicas, self.rows = self.mine.shape[:2]
+        self.s = lax.axis_index("section")
+        self.d = lax.axis_index("dp")
+
+    def half(self, s):
+        return pl.ds(pl.multiple_of(s * self.rows, self.rows), self.rows)
+
+    def loads(self, src, other):
+        loads = [pltpu.make_async_copy(src.at[:, self.half(self.s)], self.mine, self.in_sem.at[0])]
+        if other is not None:
+            loads.append(pltpu.make_async_copy(other, self.other, self.in_sem.at[1]))
+        return loads
+
+    def z_copy(self, k):
+        return far_copy(
+            self.away.at[k - 1],
+            self.came.at[k - 1],
+            self.z_send.at[k - 1],
+            self.z_recv.at[k - 1],
+            {"dp": lax.rem(self.d + k, self.replicas)},
+        )
+
+    def y_copy(self):
+        return far_copy(
+            self.over, self.back, self.y_sem.at[0], self.y_sem.at[1], {"section": 1 - self.s}
+        )
+
+    def middle(self):
+        def both(z):
+            return self.mine[z].astype(F32) + self.other[z].astype(F32)
+
+        for k in range(1, self.replicas):
+            self.away[k - 1] = both(lax.rem(self.d + k, self.replicas)).astype(BF)
+            self.z_copy(k).start()
+        self.own[...] = both(self.d)
+
+    def late(self):
+        total = self.own[...]
+        for k in range(1, self.replicas):
+            self.z_copy(k).wait_recv()
+            total = total + self.came[k - 1].astype(F32)
+        self.own[...] = total
+        self.over[...] = total.astype(BF)
+
+        @pl.when(self.s != self.layer)
+        def _():
+            self.y_copy().start()
+
+    def finish(self, out, above=None):
+        @pl.when(self.s == self.layer)
+        def _():
+            self.y_copy().wait_recv()
+            out[self.half(self.s), :] = self.own[...]
+            out[self.half(1 - self.s), :] = self.back[...].astype(F32)
+
+        @pl.when(self.s != self.layer)
+        def _():
+            if above is None:
+                out[...] = jnp.zeros_like(out)
+            else:
+                copy = pltpu.make_async_copy(above, out, self.in_sem.at[2])
+                copy.start()
+                copy.wait()
+            self.y_copy().wait_send()
+
+        for k in range(1, self.replicas):
+            self.z_copy(k).wait_send()
 
 
 class Spread:
@@ -894,14 +996,12 @@
 def mlp_back_kernel(size, layer, parts, *refs):
     g_ref, h1_ref, gain_ref, a2_ref, hid_ref, slope_ref, wu_ref, wd_ref = refs[:8]
     refs = refs[8:]
-    if layer == 1:
-        ys, refs = refs[:2], refs[2:]
-    mid_ref, gain_out, gup_ref, gdown_ref = refs[:4]
-    refs = refs[4:]
-    if layer == 1:
-        y_out, refs = refs[0], refs[1:]
+    extra, refs = refs[:2], refs[2:]
+    mid_ref, gain_out, gup_ref, gdown_out, down_came, extra_out = refs[:6]
+    gdown_ref, refs = refs[6], refs[7:]
     grad, a2, hid, dup, wu, wd, w_sem = refs[:7]
     scratch, refs = refs[7:20], refs[20:]
+    down_sem, out_sem, refs = refs[0], refs[1], refs[2:]
     rows, width = h1_ref.shape
     hidden = wu_ref.shape[1]
     depth = width // parts
@@ -920,10 +1020,12 @@
     ]
     for copy in copies + late:
         copy.start()
-    g.greet(side=layer == 1)
+    g.greet(parts if layer == 0 else 0, side=True)
+    down_swap = HalfSwap(gdown_ref, down_came, down_sem)
     section = lax.axis_index("section")
     if layer == 1:
         y_sem = refs[0]
+        ys, y_out = extra, extra_out
 
         def y_copies(own, other, at):
             return (
@@ -940,6 +1042,12 @@
                 for copy in y_copies(ys[i], ys[1 - i], section):
                     copy.start()
 
+    else:
+        above = HalfReduce(1, refs)
+        loads = above.loads(*extra)
+        for load in loads:
+            load.start()
+
     gather = Gather(g, grad, rc, scratch[:4])
     scatter = Scatter(g, rc, scratch[4:])
 
@@ -951,6 +1059,10 @@
     run(n, send)
     for copy in copies:
         copy.wait()
+    if layer == 0:
+        for load in loads:
+            load.wait()
+        above.middle()
 
     def work(j):
         at = span(j, rc)
@@ -976,8 +1088,6 @@
         cols = pl.ds(pl.multiple_of(z * depth, depth), depth)
         gup_ref[z] = dg(flat(a2[:, :, cols]), flat(dup[...]), TN).astype(BF)
 
-    run(parts, up_grad)
-
     def down_grad(f):
         cols = pl.ds(pl.multiple_of(f * fb, fb), fb)
         r = dg(flat(hid[:, :, cols]), flat(grad[...]), TN).astype(BF)
@@ -985,6 +1095,12 @@
             gdown_ref[z, cols, :] = r[:, z * depth : (z + 1) * depth]
 
     run(hidden // fb, down_grad)
+    down_swap.copy().start()
+    down_out = pltpu.make_async_copy(gdown_ref, gdown_out, out_sem.at[0])
+    down_out.start()
+    run(parts, up_grad)
+    if layer == 0:
+        above.late()
     gain_out[...] = jnp.zeros_like(gain_out)
 
     def last(j):
@@ -999,11 +1115,16 @@
         local.wait()
         side.wait_recv()
         y_copies(ys[0], ys[1], section)[1].wait_send()
+    else:
+        above.finish(extra_out)
+    down_swap.copy().wait_recv()
+    down_swap.copy().wait_send()
+    down_out.wait()
     gather.drain(n)
     scatter.drain(n)
 
 
-def mlp_backward(size, replicas, layer, grad, h1, gains, a2, hid, slope, wu, wd, ys):
+def mlp_backward(size, replicas, layer, grad, h1, gains, a2, hid, slope, wu, wd, extra):
     rows, width = h1.shape
     hidden = wu.shape[1]
     parts, depth = replicas, width // replicas
@@ -1015,11 +1136,17 @@
             shape((1, width), F32),
             shape((parts, depth, hidden), BF),
             shape((parts, hidden, depth), BF),
-        ]
-        + [shape((2, rows, width), BF)] * (len(ys) // 2),
-        in_specs=[VM, VM, VM] + [HB] * (5 + len(ys)),
-        out_specs=[VM, VM, VM, VM] + [HB] * (len(ys) // 2),
+            shape((parts, hidden // 2, depth), BF),
+            (
+                shape((2, rows, width), BF)
+                if layer == 1
+                else shape((extra[0].shape[1], extra[0].shape[2]), F32)
+            ),
+        ],
+        in_specs=[VM, VM, VM] + [HB] * 7,
+        out_specs=[VM, VM, VM, HB, HB, HB if layer == 1 else VM],
         scratch_shapes=[
+            pltpu.VMEM((parts, hidden, depth), BF),
             pltpu.VMEM((size, rows, width), BF),
             pltpu.VMEM((size, rows, width), BF),
             pltpu.VMEM((size, rows, hidden), BF),
@@ -1030,18 +1157,27 @@
         ]
         + comm_sems(size, n)
         + scatter_scratch(size, rows, width, n)
-        + [DMA((3,))] * (len(ys) // 2),
+        + [DMA((2,)), DMA((1,))]
+        + ([DMA((3,))] if layer == 1 else half_scratch(parts, *extra[0].shape[1:])),
         compiler_params=params(6 + layer),
         cost_estimate=cost(60e9, 40e6),
-    )(grad, h1, gains, a2, hid, slope, wu, wd, *ys)
-
-
-def attend_back_kernel(
-    size, layer, parts, mid_ref, qkv_ref, qm_ref, km_ref, ctx_ref, lse_ref, w_ref,
-    dqkv_ref, gout_ref, da, ka, va, kt, dk, dv, w, w_sem, *sems
-):
-    reduce = Reduce(layer, sems[4:])
-    sems = sems[:4]
+    )(grad, h1, gains, a2, hid, slope, wu, wd, *extra)
+
+
+def attend_back_kernel(size, layer, parts, *refs):
+    mid_ref, qkv_ref, qm_ref, km_ref, ctx_ref, lse_ref, w_ref, gdown_ref, down_came, gup_ref = refs[:10]
+    refs = refs[10:]
+    if layer == 0:
+        aboves, refs = refs[:2], refs[2:]
+    else:
+        aboves = (None, None)
+    dqkv_ref, gout_ref, down_out, up_out = refs[:4]
+    da, ka, va, kt, dk, dv, w, w_sem = refs[4:12]
+    sems, refs = refs[12:16], refs[16:]
+    reduce = Reduce(layer, refs[:9])
+    down = HalfReduce(layer, refs[9 : 9 + HALF])
+    up = HalfReduce(layer, refs[9 + HALF : 9 + 2 * HALF])
+    up_swap = HalfSwap(gup_ref, up.other, refs[9 + 2 * HALF])
     _, rows, wide = qkv_ref.shape
     length = size * rows
     e = qm_ref.shape[2]
@@ -1059,6 +1195,10 @@
         copy.start()
     g.greet(parts)
     gather = Gather(g, da, rc, sems)
+    up_swap.copy().start()
+    loads = down.loads(gdown_ref, down_came) + up.loads(gup_ref, None)
+    for load in loads:
+        load.start()
 
     def send(j):
         at = span(j, rc)
@@ -1078,8 +1218,9 @@
     dk[...] = jnp.zeros_like(dk)
     dv[...] = jnp.zeros_like(dv)
     ql = lax.broadcasted_iota(jnp.int32, (bq, e), 1)
-    for copy in copies:
+    for copy in copies + loads:
         copy.wait()
+    down.middle()
 
     def out_grad(z):
         cols = pl.ds(pl.multiple_of(z * depth, depth), depth)
@@ -1100,6 +1241,15 @@
             for i in range(1, n):
                 gather.ready(i)
             reduce.send(out_grad)
+
+        @pl.when(j == n // 2)
+        def _():
+            up_swap.copy().wait_recv()
+            up.middle()
+
+        @pl.when(j == n - 1)
+        def _():
+            down.late()
 
         qm = flat(qm_ref[:, at, :])
         dctx = dg(flat(da[:, at, :]), w[...], NT).astype(BF)
@@ -1137,11 +1287,15 @@
         dqkv_ref[:, :, o + 2 * e : o + 3 * e] = dv[h].astype(BF).reshape(size, rows, e)
 
     reduce.collect()
+    up.late()
+    down.finish(down_out, aboves[0])
     reduce.finish(gout_ref)
+    up.finish(up_out, aboves[1])
+    up_swap.copy().wait_send()
     gather.drain(n)
 
 
-def attend_backward(size, replicas, layer, mid, qkv, qm, km, ctx, lse, w):
+def attend_backward(size, replicas, layer, mid, qkv, qm, km, ctx, lse, w, grads, aboves):
     _, rows, wide = qkv.shape
     e = qm.shape[2]
     heads = wide // (3 * e)
@@ -1151,9 +1305,14 @@
     n = chunks(rows)
     return pl.pallas_call(
         functools.partial(attend_back_kernel, size, layer, parts),
-        out_shape=(shape(qkv.shape, BF), shape((heads * e, depth), F32)),
-        in_specs=[VM] * 6 + [HB],
-        out_specs=(VM, VM),
+        out_shape=(
+            shape(qkv.shape, BF),
+            shape((heads * e, depth), F32),
+            shape(grads[0].shape[1:], F32),
+            shape(grads[2].shape[1:], F32),
+        ),
+        in_specs=[VM] * 6 + [HB] * (4 + len(aboves)),
+        out_specs=(VM, VM, VM, VM),
         scratch_shapes=[
             pltpu.VMEM((size, rows, width), BF),
             pltpu.VMEM((heads, length, 2 * e), BF),
@@ -1165,15 +1324,18 @@
             DMA((1,)),
         ]
         + comm_sems(size, n)
-        + reduce_scratch(parts, heads * e, depth),
+        + reduce_scratch(parts, heads * e, depth)
+        + half_scratch(parts, *grads[0].shape[1:])
+        + half_scratch(parts, *grads[2].shape[1:])
+        + [DMA((2,))],
         compiler_params=params(8 + layer),
         cost_estimate=cost(90e9, 40e6),
-    )(mid, qkv, qm, km, ctx, lse, w)
+    )(mid, qkv, qm, km, ctx, lse, w, *grads, *aboves)
 
 
 def qkv_back_kernel(
     size, layer, parts, dqkv_ref, a1_ref, x_ref, mid_ref, gain_ref, w_ref,
-    dx_ref, gain_out, gqkv_ref, w, w_sem, *scratch
+    dx_ref, gain_out, gqkv_out, came, gqkv_ref, w, w_sem, swap_sem, *scratch
 ):
     rows, width = x_ref.shape
     depth = width // parts
@@ -1183,8 +1345,17 @@
     copies = [pltpu.make_async_copy(w_ref, w, w_sem.at[0])]
     for copy in copies:
         copy.start()
-    g.greet()
+    g.greet(side=True)
+    swap = HalfSwap(gqkv_ref, came, swap_sem)
     scatter = Scatter(g, rc, scratch)
+    def qkv_grad(z):
+        cols = pl.ds(pl.multiple_of(z * depth, depth), depth)
+        gqkv_ref[z] = dg(flat(a1_ref[:, :, cols]), flat(dqkv_ref[...]), TN).astype(BF)
+
+    run(parts, qkv_grad)
+    swap.copy().start()
+    out = pltpu.make_async_copy(gqkv_ref, gqkv_out, w_sem.at[1])
+    out.start()
     for copy in copies:
         copy.wait()
 
@@ -1198,12 +1369,6 @@
         scatter.second(j)
 
     run(n, work)
-
-    def qkv_grad(z):
-        cols = pl.ds(pl.multiple_of(z * depth, depth), depth)
-        gqkv_ref[z] = dg(flat(a1_ref[:, :, cols]), flat(dqkv_ref[...]), TN).astype(BF)
-
-    run(parts, qkv_grad)
     gain_out[...] = jnp.zeros_like(gain_out)
 
     def last(j):
@@ -1215,6 +1380,9 @@
         gain_out[...] += dgain
 
     run(n, last)
+    swap.copy().wait_recv()
+    swap.copy().wait_send()
+    out.wait()
     scatter.drain(n)
 
 
@@ -1229,12 +1397,15 @@
             shape((rows, width), BF),
             shape((1, width), F32),
             shape((parts, depth, wide), BF),
+            shape((parts, depth // 2, wide), BF),
         ),
         in_specs=[VM] * 5 + [HB],
-        out_specs=(VM, VM, VM),
+        out_specs=(VM, VM, HB, HB),
         scratch_shapes=[
+            pltpu.VMEM((parts, depth, wide), BF),
             pltpu.VMEM((width, wide), BF),
-            DMA((1,)),
+            DMA((2,)),
+            DMA((2,)),
         ]
         + scatter_scratch(size, rows, width, n),
         compiler_params=params(11),
@@ -1244,8 +1415,8 @@
 
 def last_kernel(
     size, parts, dqkv_ref, a1_ref, x_ref, mid_ref, gain_ref, w_ref, two_ref, above_ref, dx1_ref,
-    gain_out, gqkv_ref, dx_out,
-    w, dx, gsum, gcame, w_sem, x_sem, x_send, x_recv, g_send, g_recv, *scratch
+    qkv_above, gain_out, gqkv_out, dx_out,
+    gqkv, swap_sem, w, dx, gsum, gcame, w_sem, x_sem, x_send, x_recv, g_send, g_recv, *scratch
 ):
     rows, width = x_ref.shape
     depth = width // parts
@@ -1256,8 +1427,9 @@
     d = lax.axis_index("dp")
     copy = pltpu.make_async_copy(w_ref, w, w_sem.at[0])
     copy.start()
-    reduce = Reduce(0, scratch[:9])
-    scatter = Scatter(g, rc, scratch[9:])
+    reduce = HalfReduce(0, scratch[:HALF])
+    swap = HalfSwap(gqkv, reduce.other, swap_sem)
+    scatter = Scatter(g, rc, scratch[HALF:])
     g.greet(parts)
 
     def upper():
@@ -1278,19 +1450,19 @@
         at = span(j, rc)
         return pltpu.make_async_copy(dx.at[at], dx_out.at[0, at], x_sem.at[j])
 
-    @pl.when(section == 0)
-    def _():
-        upper().start()
+    def qkv_grad(z):
+        cols = pl.ds(pl.multiple_of(z * depth, depth), depth)
+        gqkv[z] = dg(flat(a1_ref[:, :, cols]), flat(dqkv_ref[...]), TN).astype(BF)
+
+    run(parts, qkv_grad)
+    swap.copy().start()
+    load = reduce.loads(gqkv, None)[0]
+    load.start()
 
     @pl.when(section == 1)
     def _():
         keep_upper().start()
 
-    def block(z):
-        cols = pl.ds(pl.multiple_of(z * depth, depth), depth)
-        return dg(flat(a1_ref[:, :, cols]), flat(dqkv_ref[...]), TN)
-
-    reduce.send(block)
     copy.wait()
 
     def work(j):
@@ -1303,6 +1475,14 @@
         scatter.second(j)
 
     run(n, work)
+    load.wait()
+    swap.copy().wait_recv()
+    reduce.middle()
+
+    @pl.when(section == 0)
+    def _():
+        upper().start()
+
     gsum[0] = jnp.zeros_like(gsum[0])
 
     def last(j):
@@ -1352,7 +1532,7 @@
     for stage in range(4):
         exchange(stage)
     gain_out[...] = gsum[4]
-    reduce.collect()
+    reduce.late()
 
     @pl.when(section == 0)
     def _():
@@ -1368,13 +1548,14 @@
         for j in range(n):
             lower(j).wait_send()
 
-    reduce.finish(gqkv_ref)
+    reduce.finish(gqkv_out, qkv_above)
+    swap.copy().wait_send()
     for copy in sent:
         copy.wait_send()
     scatter.drain(n)
 
 
-def last_backward(size, replicas, dqkv, a1, x, mid, gains, w, two, above, dx1):
+def last_backward(size, replicas, dqkv, a1, x, mid, gains, w, two, above, dx1, qkv_above):
     rows, width = x.shape
     wide = w.shape[1]
     depth = width // replicas
@@ -1387,9 +1568,11 @@
             shape((depth, wide), F32),
             shape((2, rows, width), BF),
         ),
-        in_specs=[VM] * 5 + [HB, VM, VM, HB],
+        in_specs=[VM] * 5 + [HB, VM, VM, HB, HB],
         out_specs=(VM, VM, HB),
         scratch_shapes=[
+            pltpu.VMEM((replicas, depth, wide), BF),
+            DMA((2,)),
             pltpu.VMEM((width, wide), BF),
             pltpu.VMEM((rows, width), BF),
             pltpu.VMEM((5, 8, width), F32),
@@ -1401,11 +1584,11 @@
             DMA((slots,)),
             DMA((slots,)),
         ]
-        + reduce_scratch(replicas, depth, wide)
+        + half_scratch(replicas, depth, wide)
         + scatter_scratch(size, rows, width, n),
         compiler_params=params(10),
         cost_estimate=cost(40e9, 30e6),
-    )(dqkv, a1, x, mid, gains, w, two, above, dx1)
+    )(dqkv, a1, x, mid, gains, w, two, above, dx1, qkv_above)
 
 
 def scene_masks(segments, e):
@@ -1415,10 +1598,6 @@
         jnp.where(used, same * MASKED, 0.0).astype(BF),
         jnp.where(used, 1.0 - same, 0.0).astype(BF),
     )
-
-
-def swap_section(value):
-    return lax.ppermute(value, "section", [(0, 1), (1, 0)])
 
 
 def shards(
@@ -1456,13 +1635,12 @@
     h1, ctx, lse, w_up_0, w_down_0 = attend(
         size, replicas, 0, qkv, qm, km, x, w_out_0, [(h_up, 0, False), (h_down, 0, True)]
     )
-    y0, a2, hid, slope, w_qkv_1, w_out_1 = mlp_forward(
-        size, replicas, 0, h1, gains, w_up_0, w_down_0, [(h_qkv, 1, False), (h_out, 1, True)]
+    y0, a2, hid, slope, w_qkv_1, w_out_1, w_up_1 = mlp_forward(
+        size, replicas, 0, h1, gains, w_up_0, w_down_0,
+        [(h_qkv, 1, False), (h_out, 1, True), (h_up, 1, False)],
     )
     kept = [(x, a1, qkv, ctx, lse, h1, a2, hid, slope)]
-    qkv, a1, w_up_1 = qkv_forward(
-        size, replicas, 1, y0, gains, w_qkv_1, [(h_up, 1, False)]
-    )
+    qkv, a1 = qkv_forward(size, replicas, 1, y0, gains, w_qkv_1, [])
     h1, ctx, lse, w_down_1 = attend(
         size, replicas, 1, qkv, qm, km, y0, w_out_1, [(h_down, 1, True)]
     )
@@ -1474,42 +1652,32 @@
     ]
     grad = lax.dynamic_index_in_dim(cotangent, section, 0, keepdims=False)
 
-    def reduce_rows(value):
-        return lax.psum_scatter(value, "dp", scatter_dimension=0, tiled=False)
-
     x, a1, qkv, ctx, lse, h1, a2, hid, slope = kept[1]
     w_qkv, w_out, w_up, w_down = weights[1]
-    mid, gain_two, g_up, g_down, layer_out = mlp_backward(
+    mid, gain_two, g_up, g_down, came, layer_out = mlp_backward(
         size, replicas, 1, grad, h1, gains, a2, hid, slope, w_up, w_down, [y0, y1]
     )
-    d_qkv, out_1 = attend_backward(size, replicas, 1, mid, qkv, qm, km, ctx, lse, w_out)
-    up_1, down_1 = reduce_rows(g_up), reduce_rows(g_down)
-    dx1, gain_one, g_qkv = qkv_backward(size, replicas, 1, d_qkv, a1, x, mid, gains, w_qkv)
+    d_qkv, out_1, down_1, up_1 = attend_backward(
+        size, replicas, 1, mid, qkv, qm, km, ctx, lse, w_out, [g_down, came, g_up], []
+    )
+    dx1, gain_one, g_qkv, came = qkv_backward(
+        size, replicas, 1, d_qkv, a1, x, mid, gains, w_qkv
+    )
     gains_above = jnp.concatenate([gain_one, gain_two], axis=0)
-    dx1, up_1, down_1 = lax.optimization_barrier((dx1, up_1, down_1))
-    qkv_1 = reduce_rows(g_qkv)
 
     x, a1, qkv, ctx, lse, h1, a2, hid, slope = kept[0]
     w_qkv, w_out, w_up, w_down = weights[0]
-    mid, gain_two, g_up, g_down = mlp_backward(
-        size, replicas, 0, dx1, h1, gains, a2, hid, slope, w_up, w_down, []
-    )
-    mid, qkv_1 = lax.optimization_barrier((mid, qkv_1))
-    d_qkv, out_0 = attend_backward(size, replicas, 0, mid, qkv, qm, km, ctx, lse, w_out)
-    up_0, down_0 = reduce_rows(g_up), reduce_rows(g_down)
-    d_qkv, up_0, down_0 = lax.optimization_barrier((d_qkv, up_0, down_0))
-    gains, qkv_0, input_out = last_backward(
-        size, replicas, d_qkv, a1, x, mid, gains, w_qkv, gain_two, gains_above, dx1
-    )
-
-    def finish(zero, one):
-        send = swap_section(jnp.where(section == 0, one, zero))
-        return jnp.where(section == 0, zero, one).astype(F32) + send.astype(F32)
-
-    other_qkv_1 = swap_section(qkv_1)
-    qkv_grad = jnp.where(section == 0, qkv_0, qkv_1.astype(F32) + other_qkv_1.astype(F32))
+    mid, gain_two, g_up, g_down, came, qkv_1 = mlp_backward(
+        size, replicas, 0, dx1, h1, gains, a2, hid, slope, w_up, w_down, [g_qkv, came]
+    )
+    d_qkv, out_0, down_grad, up_grad = attend_backward(
+        size, replicas, 0, mid, qkv, qm, km, ctx, lse, w_out,
+        [g_down, came, g_up], [down_1, up_1],
+    )
+    gains, qkv_grad, input_out = last_backward(
+        size, replicas, d_qkv, a1, x, mid, gains, w_qkv, gain_two, gains_above, dx1, qkv_1
+    )
     out_grad = jnp.where(section == 0, out_0, out_1)
-    up_grad, down_grad = finish(up_0, up_1), finish(down_0, down_1)
     gains = lax.dynamic_slice_in_dim(gains, 2 * section, 2, 0)
     return (
         layer_out[None],

time: 731 us -> 736 us (level)
  Pallas kernels: 655 us -> 704 us
  waiting for transfers between devices: 21 us -> 0 us
  between operations: 14.3 us -> 1.1 us
  other arithmetic: 14.8 us -> 6.66 us
    pallas_call x2, Pallas kernels: 106 us -> 133 us  [mlp_backward(): pl.pallas_call(functools.partial(mlp_back_kernel, size, layer, parts), ou...]
    reduce_scatter x5 -> x0, waiting for transfers between devices: 20.2 us -> none  [reduce_rows(): return lax.psum_scatter(value, 'dp', scatter_dimension=0, tiled=False)]
    pallas_call x2, Pallas kernels: 144 us -> 160 us  [attend_backward(): pl.pallas_call(functools.partial(attend_back_kernel, size, layer, parts),...]
    pallas_call x1, Pallas kernels: 42.1 us -> 30.1 us  [qkv_forward(): pl.pallas_call(functools.partial(qkv_kernel, size, layer, columns), out_s...]
    pallas_call x2, Pallas kernels: 104 us -> 114 us  [mlp_forward(): pl.pallas_call(functools.partial(mlp_kernel, size, layer, columns), out_s...]
  transfers between devices with their start and end apart: 8 -> 0, of which waited for: 1 -> 0; matrix products, arithmetic and copies ran while one was open for 1% -> 0% of each run, Pallas kernels for 40% -> 0%
where the time goes in v5:
time: 736 us; the launch traced here: 727 us
  Pallas kernels  704 us (96%)
  local copies, waits for them, and re-layouts  14.4 us (2%)
    pallas_call x2, Pallas kernels, attend_backward(): pl.pallas_call(functools.partial(attend_back_kernel, size, layer, parts),...  160 us
    pallas_call x2, Pallas kernels, mlp_backward(): pl.pallas_call(functools.partial(mlp_back_kernel, size, layer, parts), ou...  133 us
    pallas_call x2, Pallas kernels, mlp_forward(): pl.pallas_call(functools.partial(mlp_kernel, size, layer, columns), out_s...  114 us
    pallas_call x2, Pallas kernels, attend(): pl.pallas_call(functools.partial(attend_kernel, size, layer, columns), ou...  109 us
    pallas_call x1, Pallas kernels, last_backward(): pl.pallas_call(functools.partial(last_kernel, size, replicas), out_shape=...  60.4 us
    pallas_call x1, Pallas kernels, first_forward(): pl.pallas_call(functools.partial(first_kernel, size, replicas), out_shape...  58.5 us
    pallas_call x1, Pallas kernels, qkv_backward(): pl.pallas_call(functools.partial(qkv_back_kernel, size, layer, parts), ou...  40 us
    pallas_call x1, Pallas kernels, qkv_forward(): pl.pallas_call(functools.partial(qkv_kernel, size, layer, columns), out_s...  30.1 us

profile of v5, /device:TPU:0, one launch (start us, length us, event | category | flops | bytes accessed | tf_op | source)
XLA Modules:
  0.0 726.5 jit_solution(617200055415178066)
XLA Ops:
  0.6 0.0 copy-start
  0.7 0.0 copy-start.8
  0.7 3.1 dynamic-slice_bitcast_fusion
  3.8 0.0 copy-start.4
  3.8 0.0 copy-done.8
  3.8 0.0 copy-start.5
  3.8 0.1 convert_element_type.38
  3.9 0.0 copy-start.9
  3.9 0.0 copy-start.13
  4.0 0.0 copy-start.14
  4.0 1.0 copy.19.wq_ref
  5.0 0.0 copy-done.4
  5.0 0.9 convert_element_type.41
  5.9 0.0 copy-done.5
  5.9 0.8 convert_element_type.43
  6.7 0.0 copy-done.9
  6.7 0.7 convert_element_type.39
  7.4 0.1 pad.4.clone
  7.5 0.0 copy-done.13
  7.5 0.0 copy-done.14
  7.5 0.7 maximum_maximum_fusion.gain_ref
  8.2 58.5 %shard_map.152 = (bf16[4,512,768]{2,1,0:T(8,128)(2,1)}, f32[2,8,1024]{2,1,0:T(8,128)}, bf16[4,512,1024]{2,1,0:T(8,128)(2,1)}, bf16[1024,768]{1,0:T(8,128)(2,1)},...) custom-call(bf16[512,1024]{1,0:T(8,128)(2,1)} %get-tuple-element.136, ...), custom_call_target="tpu_custom_call" | custom-call | flops 30000001024 | bytes 30000000 | tf_op jit(solution)/shard_map/pallas_call | solution.py:676
  66.7 0.0 copy-done
  66.8 1.3 select_convert_fusion
  68.0 59.3 %shard_map.153 = (f32[512,1024]{1,0:T(8,128)}, bf16[4,512,256]{2,1,0:T(8,128)(2,1)}, f32[4,4,512]{2,1,0:T(4,128)}, bf16[1024,1024]{1,0:T(8,128)(2,1)}, bf16[1024,1024]{1,0:T(8,128)(2,1)}) custom-call(bf16[4,512,768]{2,1,0:T(8,128)(2,1)} %get-tuple-element.66.refs_0_.refs_1_, bf16[4,512,64]{2,1,0:T(8,128)(2,1)} %get-tuple-element.135.refs_1_.refs_2_, ...), custom_call_target="tpu_custom_call" | custom-call | flops 60000002048 | bytes 20000000 | tf_op jit(solution)/shard_map/pallas_call | solution.py:860
  127.3 62.7 %shard_map.154 = (bf16[512,1024]{1,0:T(8,128)(2,1)}, bf16[4,512,1024]{2,1,0:T(8,128)(2,1)}, bf16[4,512,1024]{2,1,0:T(8,128)(2,1)}, bf16[4,512,1024]{2,1,0:T(8,12...) custom-call(f32[512,1024]{1,0:T(8,128)} %get-tuple-element.70.refs_0_.refs_1_, ...), custom_call_target="tpu_custom_call" | custom-call | flops 49999998976 | bytes 30000000 | tf_op jit(solution)/shard_map/pallas_call | solution.py:968
  190.0 30.1 %shard_map.155 = (bf16[4,512,768]{2,1,0:T(8,128)(2,1)}, bf16[4,512,1024]{2,1,0:T(8,128)(2,1)}) custom-call(bf16[512,1024]{1,0:T(8,128)(2,1)} %get-tuple-element.76.refs_0_.refs_3_.refs_8_.x_ref, f32[2,8,1024]{2,1,0:T(8,128)} %get-tuple-element.71.refs_1_.refs_2_.gain_ref, bf16[1024,768]{1,0:T(8,128)(2,1)} %get-tuple-element.77.refs_2_.w_ref), custom_call_target="tpu_custom_call" | custom-call | flops 20000000000 | bytes 30000000 | tf_op jit(solution)/shard_map/pallas_call | solution.py:755
  220.2 49.7 %shard_map.156 = (f32[512,1024]{1,0:T(8,128)}, bf16[4,512,256]{2,1,0:T(8,128)(2,1)}, f32[4,4,512]{2,1,0:T(4,128)}, bf16[1024,1024]{1,0:T(8,128)(2,1)}) custom-call(bf16[4,512,768]{2,1,0:T(8,128)(2,1)} %get-tuple-element.78.refs_0_.refs_1_, bf16[4,512,64]{2,1,0:T(8,128)(2,1)} %get-tuple-element.135.refs_1_.refs_2_, ...), custom_call_target="tpu_custom_call" | custom-call | flops 60000002048 | bytes 20000000 | tf_op jit(solution)/shard_map/pallas_call | solution.py:860
  269.9 51.3 %shard_map.157 = (bf16[512,1024]{1,0:T(8,128)(2,1)}, bf16[4,512,1024]{2,1,0:T(8,128)(2,1)}, bf16[4,512,1024]{2,1,0:T(8,128)(2,1)}, bf16[4,512,1024]{2,1,0:T(8,128)(2,1)}) custom-call(f32[512,1024]{1,0:T(8,128)} %get-tuple-element.80.refs_0_.refs_1_, f32[2,8,1024]{2,1,0:T(8,128)} %get-tuple-element.71.refs_1_.refs_2_.gain_ref, ...), custom_call_target="tpu_custom_call" | custom-call | flops 49999998976 | bytes 30000000 | tf_op jit(solution)/shard_map/pallas_call | solution.py:968
  321.2 64.8 %shard_map.158 = (f32[512,1024]{1,0:T(8,128)}, f32[1,1024]{1,0:T(1,128)}, bf16[4,256,1024]{2,1,0:T(8,128)(2,1)}, bf16[4,1024,256]{2,1,0:T(8,128)(2,1)}, bf16[4,5...) custom-call(bf16[512,1024]{1,0:T(8,128)(2,1)} %get-tuple-element.137.refs_0_, ...), custom_call_target="tpu_custom_call" | custom-call | flops 60000002048 | bytes 40000000 | tf_op jit(solution)/shard_map/pallas_call | solution.py:1132
  386.0 77.9 %shard_map.159 = (bf16[4,512,768]{2,1,0:T(8,128)(2,1)}, f32[256,256]{1,0:T(8,128)}, f32[1024,256]{1,0:T(8,128)}, f32[256,1024]{1,0:T(8,128)}) custom-call(f32[512,1024]{1,0:T(8,128)} %get-tuple-element.88.refs_0_.mid_ref, bf16[4,512,768]{2,1,0:T(8,128)(2,1)} %get-tuple-element.78.refs_0_.refs_1_, bf16[4,512,64]{2,1,0:T(8,128)(2,1)} %get-tuple-element.135.refs_1_.refs_2_, ...), custom_call_target="tpu_custom_call" | custom-call | flops 89999998976 | bytes 40000000 | tf_op jit(solution)/shard_map/pallas_call | solution.py:1306
  464.0 40.0 %shard_map.160 = (bf16[512,1024]{1,0:T(8,128)(2,1)}, f32[1,1024]{1,0:T(1,128)}, bf16[4,256,768]{2,1,0:T(8,128)(2,1)}, bf16[4,128,768]{2,1,0:T(8,128)(2,1)}) custom-call(bf16[4,512,768]{2,1,0:T(8,128)(2,1)} %get-tuple-element.94.dqkv_ref, bf16[4,512,1024]{2,1,0:T(8,128)(2,1)} %get-tuple-element.95.a1_ref, ...), custom_call_target="tpu_custom_call" | custom-call | flops 30000001024 | bytes 30000000 | tf_op jit(solution)/shard_map/pallas_call | solution.py:1394
  504.0 67.7 %shard_map.161 = (f32[512,1024]{1,0:T(8,128)}, f32[1,1024]{1,0:T(1,128)}, bf16[4,256,1024]{2,1,0:T(8,128)(2,1)}, bf16[4,1024,256]{2,1,0:T(8,128)(2,1)}, bf16[4,5...) custom-call(bf16[512,1024]{1,0:T(8,128)(2,1)} %get-tuple-element.96.refs_0_.dx1_ref, ...), custom_call_target="tpu_custom_call" | custom-call | flops 60000002048 | bytes 40000000 | tf_op jit(solution)/shard_map/pallas_call | solution.py:1132
  571.7 0.0 copy-start.10
  571.7 0.0 copy-start.11
  571.7 0.0 copy-start.12
  571.7 81.8 %shard_map.162 = (bf16[4,512,768]{2,1,0:T(8,128)(2,1)}, f32[256,256]{1,0:T(8,128)}, f32[1024,256]{1,0:T(8,128)}, f32[256,1024]{1,0:T(8,128)}) custom-call(f32[512,1024]{1,0:T(8,128)} %get-tuple-element.102.refs_0_.mid_ref, bf16[4,512,768]{2,1,0:T(8,128)(2,1)} %get-tuple-element.66.refs_0_.refs_1_, bf16[4,512,64]{2,1,0:T(8,128)(2,1)} %get-tuple-element.135.refs_1_.refs_2_, ...), custom_call_target="tpu_custom_call" | custom-call | flops 89999998976 | bytes 40000000 | tf_op jit(solution)/shard_map/pallas_call | solution.py:1306
  653.6 0.0 copy-done.10
  653.6 1.7 broadcast_select_fusion
  655.3 0.0 copy-done.11
  655.3 0.0 copy-done.12
  655.3 0.6 pad_maximum_fusion.above_ref
  655.9 0.0 copy-start.2
  655.9 60.4 %shard_map.163 = (f32[8,1024]{1,0:T(8,128)}, f32[256,768]{1,0:T(8,128)}, bf16[2,512,1024]{2,1,0:T(8,128)(2,1)}) custom-call(bf16[4,512,768]{2,1,0:T(8,128)(2,1)} %get-tuple-element.110.dqkv_ref, bf16[4,512,1024]{2,1,0:T(8,128)(2,1)} %get-tuple-element.111.a1_ref, bf16[512,1024]{1,0:T(8,128)(2,1)} %get-tuple-element.136.x_ref.refs_3_, ...), custom_call_target="tpu_custom_call" | custom-call | flops 40000000000 | bytes 30000000 | tf_op jit(solution)/shard_map/pallas_call | solution.py:1564
  716.3 2.3 copy.20
  718.6 1.4 constant_dynamic-slice_fusion.1
  720.0 0.0 copy-done.2
  720.0 0.0 copy-start.3
  720.0 1.3 copy.25
  721.4 1.0 copy-done.3
  722.4 0.0 copy-start.7
  722.4 0.0 copy-start.6
  722.4 0.0 copy-start.1
  722.4 1.3 copy.26
  723.7 0.6 copy-done.7
  724.4 1.0 copy.27
  725.3 0.0 copy-done.6
  725.3 1.0 copy.28
  726.3 0.0 copy-done.1
  (5 shorter events, 0.1 us)
Async XLA Ops:
  0.6 66.1 %copy-start = (s32[2,2048]{1,0:T(2,128)S(1)}, s32[2,2048]{1,0:T(2,128)}, u32[]{:S(2)}) copy-start(s32[2,2048]{1,0:T(2,128)} %param.10) | copy-start | bytes 49156
  0.7 3.1 copy-start.8
  3.8 1.2 copy-start.4
  3.8 2.1 copy-start.5
  3.9 2.8 copy-start.9
  3.9 3.5 copy-start.13
  4.0 3.5 copy-start.14
  571.7 81.9 %copy-start.10 = (f32[256,256]{1,0:T(8,128)S(1)}, f32[256,256]{1,0:T(8,128)}, u32[]{:S(2)}) copy-start(f32[256,256]{1,0:T(8,128)} %get-tuple-element.121) | copy-start | bytes 786436
  571.7 83.6 %copy-start.11 = (f32[1,1024]{1,0:T(1,128)S(1)}, f32[1,1024]{1,0:T(1,128)}, u32[]{:S(2)}) copy-start(f32[1,1024]{1,0:T(1,128)} %get-tuple-element.115) | copy-start | bytes 12292
  571.7 83.6 %copy-start.12 = (f32[1,1024]{1,0:T(1,128)S(1)}, f32[1,1024]{1,0:T(1,128)}, u32[]{:S(2)}) copy-start(f32[1,1024]{1,0:T(1,128)} %get-tuple-element.114) | copy-start | bytes 12292
  655.9 64.2 %copy-start.2 = (bf16[2,512,1024]{2,1,0:T(8,128)(2,1)S(1)}, bf16[2,512,1024]{2,1,0:T(8,128)(2,1)}, u32[]{:S(2)}) copy-start(bf16[2,512,1024]{2,1,0:T(8,128)(2,1)} %get-tuple-element.87) | copy-start | bytes 6291460
  720.0 2.3 copy-start.3
  722.4 2.0 copy-start.7
  722.4 2.9 copy-start.6
  722.4 3.9 copy-start.1

commit v6 on v5

--- a/solution.py
+++ b/solution.py
@@ -504,6 +504,84 @@
             self.side(k, self.s).wait_send()
 
 
+class ZGather:
+    def __init__(self, src, got, sems):
+        self.src, self.got = src, got
+        self.own_sem, self.send, self.recv = sems
+        self.replicas = got.shape[0]
+        self.d = lax.axis_index("dp")
+
+    def own(self):
+        return pltpu.make_async_copy(self.src, self.got.at[self.d], self.own_sem.at[0])
+
+    def far(self, k, origin):
+        return far_copy(
+            self.src,
+            self.got.at[origin],
+            self.send.at[k - 1],
+            self.recv.at[k - 1],
+            {"dp": lax.rem(self.d + k, self.replicas)},
+        )
+
+    def start(self):
+        for k in range(1, self.replicas):
+            self.far(k, self.d).start()
+        self.own().start()
+
+    def step(self, i):
+        pass
+
+    def finish(self):
+        self.own().wait()
+        for k in range(1, self.replicas):
+            self.far(k, lax.rem(self.d + self.replicas - k, self.replicas)).wait_recv()
+        for k in range(1, self.replicas):
+            self.far(k, self.d).wait_send()
+
+
+class YJoin:
+    def __init__(self, got, dst, by_columns, sems):
+        self.got, self.dst, self.by_columns = got, dst, by_columns
+        self.own_sem, self.send, self.recv = sems
+        self.replicas, self.rows, self.cols = got.shape
+        self.s = lax.axis_index("section")
+
+    def place(self, half, z):
+        rows, cols = self.rows, self.cols
+        if self.by_columns:
+            return self.dst.at[
+                pl.ds(pl.multiple_of(half * rows, rows), rows), pl.ds(z * cols, cols)
+            ]
+        return self.dst.at[pl.ds(pl.multiple_of((2 * z + half) * rows, rows), rows)]
+
+    def own(self, z):
+        return pltpu.make_async_copy(self.got.at[z], self.place(self.s, z), self.own_sem.at[z])
+
+    def side(self, z, half):
+        return far_copy(
+            self.got.at[z],
+            self.place(half, z),
+            self.send.at[z],
+            self.recv.at[z],
+            {"section": 1 - self.s},
+        )
+
+    def start(self):
+        for z in range(self.replicas):
+            self.side(z, self.s).start()
+            self.own(z).start()
+
+    def step(self, i):
+        pass
+
+    def finish(self):
+        for z in range(self.replicas):
+            self.own(z).wait()
+            self.side(z, 1 - self.s).wait_recv()
+        for z in range(self.replicas):
+            self.side(z, self.s).wait_send()
+
+
 def rider_sems(replicas):
     far, side = DMA((replicas - 1,)), DMA((replicas,))
     return [DMA((1,)), far, far, side, side]
@@ -511,10 +589,16 @@
 
 class Riders:
     def __init__(self, srcs, dsts, columns, sems):
-        self.all = [
-            Spread(src.at[layer], dst, by, sems[5 * i : 5 * i + 5])
-            for i, (src, dst, (layer, by)) in enumerate(zip(srcs, dsts, columns))
-        ]
+        self.all = []
+        for src, dst, (kind, layer, by) in zip(srcs, dsts, columns):
+            count = 5 if kind == "spread" else 3
+            own, sems = sems[:count], sems[count:]
+            if kind == "spread":
+                self.all.append(Spread(src.at[layer], dst, by, own))
+            elif kind == "z":
+                self.all.append(ZGather(src.at[layer], dst, own))
+            else:
+                self.all.append(YJoin(src, dst, by, own))
         self.replicas = self.all[0].replicas if self.all else 0
 
     def start(self):
@@ -524,7 +608,7 @@
     def step(self, j, n):
         if not self.all:
             return
-        stages = len(self.all[0].stages)
+        stages = self.replicas // 2
         for i in range(stages):
 
             @pl.when(j == n * (i + 1) // stages - 1)
@@ -538,16 +622,24 @@
 
 
 def riding(riders, replicas):
-    halves = [stage for stage, _, _ in riders]
-    columns = tuple((layer, by) for _, layer, by in riders)
-    outs = []
-    for stage, _, by in riders:
-        _, rows, cols = stage.shape
-        outs.append(
-            shape((2 * rows, replicas * cols) if by else (2 * replicas * rows, cols), BF)
-        )
-    sems = rider_sems(replicas) * len(riders)
-    return halves, columns, outs, sems
+    arrays = [array for array, _, _, _ in riders]
+    columns = tuple(rider[1:] for rider in riders)
+    outs, sems = [], []
+    for array, kind, _, by in riders:
+        rows, cols = array.shape[1:]
+        if kind == "z":
+            outs.append(shape((replicas, rows, cols), BF))
+        else:
+            outs.append(
+                shape((2 * rows, replicas * cols) if by else (2 * replicas * rows, cols), BF)
+            )
+        far, side = DMA((replicas - 1,)), DMA((replicas,))
+        sems += {
+            "spread": rider_sems(replicas),
+            "z": [DMA((1,)), far, far],
+            "y": [side, side, side],
+        }[kind]
+    return arrays, columns, outs, sems
 
 
 def params(key):
@@ -589,7 +681,7 @@
 
 def first_kernel(
     size, replicas, x_ref, gain_ref, wq_ref, wo_ref, wu_ref, wd_ref,
-    qkv_ref, gains_out, a1_out, wq_out, wo_out, q_stage, o_stage, u_stage, d_stage,
+    qkv_ref, gains_out, a1_out, wq_out, wo_out, q_stage, o_stage, u_stage, d_stage, u_got,
     a1, w, gains, own_sem, q_sem, o_sem, u_sem, d_sem, gain_sem, *sems
 ):
     rows, width = x_ref.shape
@@ -638,8 +730,16 @@
     swaps[2].start()
     swaps[3].start()
 
+    u_gather = ZGather(u_stage.at[0], u_got, sems[14:17])
+
     def relay(j):
         gather.relay(j)
+
+        @pl.when(j == n - 1)
+        def _():
+            swaps[2].arrive()
+            u_gather.start()
+
         riders.step(j, n)
 
     run(n, relay)
@@ -658,8 +758,8 @@
 
     run(n, multiply)
     outs[1].start()
-    swaps[2].arrive()
     swaps[3].arrive()
+    u_gather.finish()
     for swap in swaps:
         swap.finish()
     gain_copy(section).wait_send()
@@ -682,9 +782,10 @@
             shape((width, wide), BF),
             shape((deep, width), BF),
         ]
-        + [shape(w.shape, BF) for w in ws],
+        + [shape(w.shape, BF) for w in ws]
+        + [shape((replicas,) + ws[2].shape[1:], BF)],
         in_specs=[VM, VM] + [HB] * 4,
-        out_specs=[VM, VM] + [HB] * 7,
+        out_specs=[VM, VM] + [HB] * 8,
         scratch_shapes=[
             pltpu.VMEM((size, rows, width), BF),
             pltpu.VMEM((width, wide), BF),
@@ -697,7 +798,8 @@
             DMA((2,)),
         ]
         + comm_sems(size, n)
-        + rider_sems(replicas) * 2,
+        + rider_sems(replicas) * 2
+        + [DMA((1,)), DMA((replicas - 1,)), DMA((replicas - 1,))],
         compiler_params=params(0),
         cost_estimate=cost(30e9, 30e6),
     )(x, gains, *ws)
@@ -1064,10 +1166,28 @@
             load.wait()
         above.middle()
 
+    for copy in late:
+        copy.wait()
+
+    def down_grad(f):
+        cols = pl.ds(pl.multiple_of(f * fb, fb), fb)
+        r = dg(flat(hid[:, :, cols]), flat(grad[...]), TN).astype(BF)
+        for z in range(parts):
+            gdown_ref[z, cols, :] = r[:, z * depth : (z + 1) * depth]
+
+    down_out = pltpu.make_async_copy(gdown_ref, gdown_out, out_sem.at[0])
+
     def work(j):
         at = span(j, rc)
         gather.relay(j)
         gather.ready(j)
+
+        @pl.when(j == n - 1)
+        def _():
+            run(hidden // fb, down_grad)
+            down_swap.copy().start()
+            down_out.start()
+
         held = flat(grad[:, at, :])
         for f in range(hidden // fb):
             cols = slice(f * fb, (f + 1) * fb)
@@ -1081,23 +1201,11 @@
         scatter.second(j)
 
     run(n, work)
-    for copy in late:
-        copy.wait()
 
     def up_grad(z):
         cols = pl.ds(pl.multiple_of(z * depth, depth), depth)
         gup_ref[z] = dg(flat(a2[:, :, cols]), flat(dup[...]), TN).astype(BF)
 
-    def down_grad(f):
-        cols = pl.ds(pl.multiple_of(f * fb, fb), fb)
-        r = dg(flat(hid[:, :, cols]), flat(grad[...]), TN).astype(BF)
-        for z in range(parts):
-            gdown_ref[z, cols, :] = r[:, z * depth : (z + 1) * depth]
-
-    run(hidden // fb, down_grad)
-    down_swap.copy().start()
-    down_out = pltpu.make_async_copy(gdown_ref, gdown_out, out_sem.at[0])
-    down_out.start()
     run(parts, up_grad)
     if layer == 0:
         above.late()
@@ -1242,15 +1350,6 @@
                 gather.ready(i)
             reduce.send(out_grad)
 
-        @pl.when(j == n // 2)
-        def _():
-            up_swap.copy().wait_recv()
-            up.middle()
-
-        @pl.when(j == n - 1)
-        def _():
-            down.late()
-
         qm = flat(qm_ref[:, at, :])
         dctx = dg(flat(da[:, at, :]), w[...], NT).astype(BF)
         ctx = flat(ctx_ref[:, at, :])
@@ -1278,16 +1377,29 @@
                 dk[h, ks, :] += dg(ds, qq, NN)
                 a = dg(kt[h, :, ks], ds, NN)
                 dqt = a if dqt is None else dqt + a
+            if h == heads // 2:
+
+                @pl.when(j == min(1, n - 1))
+                def _():
+                    up_swap.copy().wait_recv()
+                    up.middle()
+
+            if h == heads - 1:
+
+                @pl.when(j == n // 2)
+                def _():
+                    down.late()
+
             dqkv_ref[:, at, o : o + e] = (dqt * scale).T.astype(BF).reshape(size, rc, e)
 
     run(n, work)
+    reduce.collect()
+    up.late()
     for h in range(heads):
         o = 3 * e * h
         dqkv_ref[:, :, o + e : o + 2 * e] = (dk[h] * scale).astype(BF).reshape(size, rows, e)
         dqkv_ref[:, :, o + 2 * e : o + 3 * e] = dv[h].astype(BF).reshape(size, rows, e)
 
-    reduce.collect()
-    up.late()
     down.finish(down_out, aboves[0])
     reduce.finish(gout_ref)
     up.finish(up_out, aboves[1])
@@ -1352,10 +1464,6 @@
         cols = pl.ds(pl.multiple_of(z * depth, depth), depth)
         gqkv_ref[z] = dg(flat(a1_ref[:, :, cols]), flat(dqkv_ref[...]), TN).astype(BF)
 
-    run(parts, qkv_grad)
-    swap.copy().start()
-    out = pltpu.make_async_copy(gqkv_ref, gqkv_out, w_sem.at[1])
-    out.start()
     for copy in copies:
         copy.wait()
 
@@ -1369,6 +1477,10 @@
         scatter.second(j)
 
     run(n, work)
+    run(parts, qkv_grad)
+    swap.copy().start()
+    out = pltpu.make_async_copy(gqkv_ref, gqkv_out, w_sem.at[1])
+    out.start()
     gain_out[...] = jnp.zeros_like(gain_out)
 
     def last(j):
@@ -1475,14 +1587,6 @@
         scatter.second(j)
 
     run(n, work)
-    load.wait()
-    swap.copy().wait_recv()
-    reduce.middle()
-
-    @pl.when(section == 0)
-    def _():
-        upper().start()
-
     gsum[0] = jnp.zeros_like(gsum[0])
 
     def last(j):
@@ -1500,7 +1604,20 @@
 
         gsum[0, 0:1, :] += dgain
 
-    run(n, last)
+    def rest(j):
+        @pl.when(j == n // 2)
+        def _():
+            load.wait()
+            swap.copy().wait_recv()
+            reduce.middle()
+
+            @pl.when(section == 0)
+            def _():
+                upper().start()
+
+        last(j)
+
+    run(n, rest)
     gsum[0, 1:2, :] = two_ref[...]
     gsum[0, 2:4, :] = above_ref[...]
 
@@ -1629,20 +1746,33 @@
     x = lax.dynamic_index_in_dim(block_input, section, 0, keepdims=False)
     head_dim = qkv_weight.shape[3] // 3
     qm, km = scene_masks(segments.reshape((size, -1)), head_dim)
-    qkv, gains, a1, w_qkv_0, w_out_0, h_qkv, h_out, h_up, h_down = first_forward(
+    qkv, gains, a1, w_qkv_0, w_out_0, h_qkv, h_out, h_up, h_down, got_up = first_forward(
         size, replicas, x, gains, mine
     )
-    h1, ctx, lse, w_up_0, w_down_0 = attend(
-        size, replicas, 0, qkv, qm, km, x, w_out_0, [(h_up, 0, False), (h_down, 0, True)]
-    )
-    y0, a2, hid, slope, w_qkv_1, w_out_1, w_up_1 = mlp_forward(
+    h1, ctx, lse, w_up_0, w_down_0, got_qkv, got_out = attend(
+        size, replicas, 0, qkv, qm, km, x, w_out_0,
+        [
+            (got_up, "y", 0, False),
+            (h_down, "spread", 0, True),
+            (h_qkv, "z", 1, False),
+            (h_out, "z", 1, True),
+        ],
+    )
+    y0, a2, hid, slope, w_qkv_1, w_out_1, got_up, got_down = mlp_forward(
         size, replicas, 0, h1, gains, w_up_0, w_down_0,
-        [(h_qkv, 1, False), (h_out, 1, True), (h_up, 1, False)],
+        [
+            (got_qkv, "y", 1, False),
+            (got_out, "y", 1, True),
+            (h_up, "z", 1, False),
+            (h_down, "z", 1, True),
+        ],
     )
     kept = [(x, a1, qkv, ctx, lse, h1, a2, hid, slope)]
-    qkv, a1 = qkv_forward(size, replicas, 1, y0, gains, w_qkv_1, [])
+    qkv, a1, w_up_1 = qkv_forward(
+        size, replicas, 1, y0, gains, w_qkv_1, [(got_up, "y", 1, False)]
+    )
     h1, ctx, lse, w_down_1 = attend(
-        size, replicas, 1, qkv, qm, km, y0, w_out_1, [(h_down, 1, True)]
+        size, replicas, 1, qkv, qm, km, y0, w_out_1, [(got_down, "y", 1, True)]
     )
     y1, a2, hid, slope = mlp_forward(size, replicas, 1, h1, gains, w_up_1, w_down_1, [])
     kept.append((y0, a1, qkv, ctx, lse, h1, a2, hid, slope))

time: 736 us -> 739 us (level)
    pallas_call x2, Pallas kernels: 114 us -> 106 us  [mlp_forward(): pl.pallas_call(functools.partial(mlp_kernel, size, layer, columns), out_s...]
    pallas_call x1, Pallas kernels: 30.1 us -> 37.7 us  [qkv_forward(): pl.pallas_call(functools.partial(qkv_kernel, size, layer, columns), out_s...]
where the time goes in v6:
time: 739 us; the launch traced here: 730 us
  Pallas kernels  708 us (96%)
  local copies, waits for them, and re-layouts  14.4 us (2%)
    pallas_call x2, Pallas kernels, attend_backward(): pl.pallas_call(functools.partial(attend_back_kernel, size, layer, parts),...  166 us
    pallas_call x2, Pallas kernels, mlp_backward(): pl.pallas_call(functools.partial(mlp_back_kernel, size, layer, parts), ou...  125 us
    pallas_call x2, Pallas kernels, attend(): pl.pallas_call(functools.partial(attend_kernel, size, layer, columns), ou...  109 us
    pallas_call x2, Pallas kernels, mlp_forward(): pl.pallas_call(functools.partial(mlp_kernel, size, layer, columns), out_s...  106 us
    pallas_call x1, Pallas kernels, first_forward(): pl.pallas_call(functools.partial(first_kernel, size, replicas), out_shape...  63.4 us
    pallas_call x1, Pallas kernels, last_backward(): pl.pallas_call(functools.partial(last_kernel, size, replicas), out_shape=...  59.1 us
    pallas_call x1, Pallas kernels, qkv_backward(): pl.pallas_call(functools.partial(qkv_back_kernel, size, layer, parts), ou...  41.4 us
    pallas_call x1, Pallas kernels, qkv_forward(): pl.pallas_call(functools.partial(qkv_kernel, size, layer, columns), out_s...  37.7 us

profile of v6, /device:TPU:0, one launch (start us, length us, event | category | flops | bytes accessed | tf_op | source)
XLA Modules:
  0.0 730.1 jit_solution(13954414250665230061)
XLA Ops:
  0.6 0.0 copy-start
  0.7 0.0 copy-start.8
  0.7 3.1 dynamic-slice_bitcast_fusion
  3.8 0.0 copy-start.4
  3.8 0.0 copy-done.8
  3.8 0.0 copy-start.5
  3.8 0.1 convert_element_type.38
  3.9 0.0 copy-start.9
  3.9 0.0 copy-start.13
  4.0 0.0 copy-start.14
  4.0 1.0 copy.19.wq_ref
  5.0 0.0 copy-done.4
  5.0 0.9 convert_element_type.41
  5.9 0.0 copy-done.5
  5.9 0.8 convert_element_type.43
  6.7 0.0 copy-done.9
  6.7 0.7 convert_element_type.39
  7.4 0.1 pad.4.clone
  7.5 0.0 copy-done.13
  7.5 0.0 copy-done.14
  7.5 0.7 maximum_maximum_fusion.gain_ref
  8.2 63.4 %shard_map.152 = (bf16[4,512,768]{2,1,0:T(8,128)(2,1)}, f32[2,8,1024]{2,1,0:T(8,128)}, bf16[4,512,1024]{2,1,0:T(8,128)(2,1)}, bf16[1024,768]{1,0:T(8,128)(2,1)},...) custom-call(bf16[512,1024]{1,0:T(8,128)(2,1)} %get-tuple-element.146, ...), custom_call_target="tpu_custom_call" | custom-call | flops 30000001024 | bytes 30000000 | tf_op jit(solution)/shard_map/pallas_call | solution.py:776
  71.5 0.0 copy-done
  71.6 1.3 select_convert_fusion
  72.9 60.5 %shard_map.153 = (f32[512,1024]{1,0:T(8,128)}, bf16[4,512,256]{2,1,0:T(8,128)(2,1)}, f32[4,4,512]{2,1,0:T(4,128)}, bf16[1024,1024]{1,0:T(8,128)(2,1)}, bf16[1024...) custom-call(bf16[4,512,768]{2,1,0:T(8,128)(2,1)} %get-tuple-element.71.refs_0_.refs_1_, ...), custom_call_target="tpu_custom_call" | custom-call | flops 60000002048 | bytes 20000000 | tf_op jit(solution)/shard_map/pallas_call | solution.py:962
  133.4 55.6 %shard_map.154 = (bf16[512,1024]{1,0:T(8,128)(2,1)}, bf16[4,512,1024]{2,1,0:T(8,128)(2,1)}, bf16[4,512,1024]{2,1,0:T(8,128)(2,1)}, bf16[4,512,1024]{2,1,0:T(8,12...) custom-call(f32[512,1024]{1,0:T(8,128)} %get-tuple-element.77.refs_0, ...), custom_call_target="tpu_custom_call" | custom-call | flops 49999998976 | bytes 30000000 | tf_op jit(solution)/shard_map/pallas_call | solution.py:1070
  189.0 37.7 %shard_map.155 = (bf16[4,512,768]{2,1,0:T(8,128)(2,1)}, bf16[4,512,1024]{2,1,0:T(8,128)(2,1)}, bf16[1024,1024]{1,0:T(8,128)(2,1)}) custom-call(bf16[512,1024]{1,0:T(8,128)(2,1)} %get-tuple-element.84.refs_0_.refs_3_.refs_8_.x_ref, f32[2,8,1024]{2,1,0:T(8,128)} %get-tuple-element.78.refs_1_.refs_2_.gain_ref, ...), custom_call_target="tpu_custom_call" | custom-call | flops 20000000000 | bytes 30000000 | tf_op jit(solution)/shard_map/pallas_call | solution.py:857
  226.8 48.9 %shard_map.156 = (f32[512,1024]{1,0:T(8,128)}, bf16[4,512,256]{2,1,0:T(8,128)(2,1)}, f32[4,4,512]{2,1,0:T(4,128)}, bf16[1024,1024]{1,0:T(8,128)(2,1)}) custom-call(bf16[4,512,768]{2,1,0:T(8,128)(2,1)} %get-tuple-element.87.refs_0_.refs_1_, bf16[4,512,64]{2,1,0:T(8,128)(2,1)} %get-tuple-element.145.refs_1_.refs_2_, ...), custom_call_target="tpu_custom_call" | custom-call | flops 60000002048 | bytes 20000000 | tf_op jit(solution)/shard_map/pallas_call | solution.py:962
  275.7 50.2 %shard_map.157 = (bf16[512,1024]{1,0:T(8,128)(2,1)}, bf16[4,512,1024]{2,1,0:T(8,128)(2,1)}, bf16[4,512,1024]{2,1,0:T(8,128)(2,1)}, bf16[4,512,1024]{2,1,0:T(8,128)(2,1)}) custom-call(f32[512,1024]{1,0:T(8,128)} %get-tuple-element.90.refs_0_.refs_1_, f32[2,8,1024]{2,1,0:T(8,128)} %get-tuple-element.78.refs_1_.refs_2_.gain_ref, ...), custom_call_target="tpu_custom_call" | custom-call | flops 49999998976 | bytes 30000000 | tf_op jit(solution)/shard_map/pallas_call | solution.py:1070
  325.8 60.8 %shard_map.158 = (f32[512,1024]{1,0:T(8,128)}, f32[1,1024]{1,0:T(1,128)}, bf16[4,256,1024]{2,1,0:T(8,128)(2,1)}, bf16[4,1024,256]{2,1,0:T(8,128)(2,1)}, bf16[4,5...) custom-call(bf16[512,1024]{1,0:T(8,128)(2,1)} %get-tuple-element.147.refs_0_, ...), custom_call_target="tpu_custom_call" | custom-call | flops 60000002048 | bytes 40000000 | tf_op jit(solution)/shard_map/pallas_call | solution.py:1240
  386.6 81.2 %shard_map.159 = (bf16[4,512,768]{2,1,0:T(8,128)(2,1)}, f32[256,256]{1,0:T(8,128)}, f32[1024,256]{1,0:T(8,128)}, f32[256,1024]{1,0:T(8,128)}) custom-call(f32[512,1024]{1,0:T(8,128)} %get-tuple-element.98.refs_0_.mid_ref, bf16[4,512,768]{2,1,0:T(8,128)(2,1)} %get-tuple-element.87.refs_0_.refs_1_, bf16[4,512,64]{2,1,0:T(8,128)(2,1)} %get-tuple-element.145.refs_1_.refs_2_, ...), custom_call_target="tpu_custom_call" | custom-call | flops 89999998976 | bytes 40000000 | tf_op jit(solution)/shard_map/pallas_call | solution.py:1418
  467.9 41.4 %shard_map.160 = (bf16[512,1024]{1,0:T(8,128)(2,1)}, f32[1,1024]{1,0:T(1,128)}, bf16[4,256,768]{2,1,0:T(8,128)(2,1)}, bf16[4,128,768]{2,1,0:T(8,128)(2,1)}) custom-call(bf16[4,512,768]{2,1,0:T(8,128)(2,1)} %get-tuple-element.104.dqkv_ref, bf16[4,512,1024]{2,1,0:T(8,128)(2,1)} %get-tuple-element.105.a1_ref, ...), custom_call_target="tpu_custom_call" | custom-call | flops 30000001024 | bytes 30000000 | tf_op jit(solution)/shard_map/pallas_call | solution.py:1506
  509.2 64.6 %shard_map.161 = (f32[512,1024]{1,0:T(8,128)}, f32[1,1024]{1,0:T(1,128)}, bf16[4,256,1024]{2,1,0:T(8,128)(2,1)}, bf16[4,1024,256]{2,1,0:T(8,128)(2,1)}, bf16[4,5...) custom-call(bf16[512,1024]{1,0:T(8,128)(2,1)} %get-tuple-element.106.refs_0_.dx1_ref, ...), custom_call_target="tpu_custom_call" | custom-call | flops 60000002048 | bytes 40000000 | tf_op jit(solution)/shard_map/pallas_call | solution.py:1240
  573.9 0.0 copy-start.10
  573.9 0.0 copy-start.11
  573.9 0.0 copy-start.12
  573.9 84.5 %shard_map.162 = (bf16[4,512,768]{2,1,0:T(8,128)(2,1)}, f32[256,256]{1,0:T(8,128)}, f32[1024,256]{1,0:T(8,128)}, f32[256,1024]{1,0:T(8,128)}) custom-call(f32[512,1024]{1,0:T(8,128)} %get-tuple-element.112.refs_0_.mid_ref, bf16[4,512,768]{2,1,0:T(8,128)(2,1)} %get-tuple-element.71.refs_0_.refs_1_, bf16[4,512,64]{2,1,0:T(8,128)(2,1)} %get-tuple-element.145.refs_1_.refs_2_, ...), custom_call_target="tpu_custom_call" | custom-call | flops 89999998976 | bytes 40000000 | tf_op jit(solution)/shard_map/pallas_call | solution.py:1418
  658.5 0.0 copy-done.10
  658.5 1.7 broadcast_select_fusion
  660.2 0.0 copy-done.11
  660.2 0.0 copy-done.12
  660.2 0.6 pad_maximum_fusion.above_ref
  660.8 0.0 copy-start.2
  660.8 59.1 %shard_map.163 = (f32[8,1024]{1,0:T(8,128)}, f32[256,768]{1,0:T(8,128)}, bf16[2,512,1024]{2,1,0:T(8,128)(2,1)}) custom-call(bf16[4,512,768]{2,1,0:T(8,128)(2,1)} %get-tuple-element.120.dqkv_ref, bf16[4,512,1024]{2,1,0:T(8,128)(2,1)} %get-tuple-element.121.a1_ref, bf16[512,1024]{1,0:T(8,128)(2,1)} %get-tuple-element.146.x_ref.refs_3_, ...), custom_call_target="tpu_custom_call" | custom-call | flops 40000000000 | bytes 30000000 | tf_op jit(solution)/shard_map/pallas_call | solution.py:1681
  719.9 2.3 copy.20
  722.2 1.4 constant_dynamic-slice_fusion.1
  723.6 0.0 copy-done.2
  723.6 0.0 copy-start.3
  723.6 1.3 copy.25
  725.0 1.0 copy-done.3
  726.0 0.0 copy-start.7
  726.0 0.0 copy-start.6
  726.0 0.0 copy-start.1
  726.0 1.3 copy.26
  727.3 0.6 copy-done.7
  727.9 1.0 copy.27
  728.9 0.0 copy-done.6
  728.9 1.0 copy.28
  729.9 0.0 copy-done.1
  (5 shorter events, 0.1 us)
Async XLA Ops:
  0.6 70.9 %copy-start = (s32[2,2048]{1,0:T(2,128)S(1)}, s32[2,2048]{1,0:T(2,128)}, u32[]{:S(2)}) copy-start(s32[2,2048]{1,0:T(2,128)} %param.10) | copy-start | bytes 49156
  0.7 3.1 copy-start.8
  3.8 1.2 copy-start.4
  3.8 2.1 copy-start.5
  3.9 2.8 copy-start.9
  3.9 3.5 copy-start.13
  4.0 3.5 copy-start.14
  573.9 84.6 %copy-start.10 = (f32[256,256]{1,0:T(8,128)S(1)}, f32[256,256]{1,0:T(8,128)}, u32[]{:S(2)}) copy-start(f32[256,256]{1,0:T(8,128)} %get-tuple-element.131) | copy-start | bytes 786436
  573.9 86.3 %copy-start.11 = (f32[1,1024]{1,0:T(1,128)S(1)}, f32[1,1024]{1,0:T(1,128)}, u32[]{:S(2)}) copy-start(f32[1,1024]{1,0:T(1,128)} %get-tuple-element.125) | copy-start | bytes 12292
  573.9 86.3 %copy-start.12 = (f32[1,1024]{1,0:T(1,128)S(1)}, f32[1,1024]{1,0:T(1,128)}, u32[]{:S(2)}) copy-start(f32[1,1024]{1,0:T(1,128)} %get-tuple-element.124) | copy-start | bytes 12292
  660.8 62.9 %copy-start.2 = (bf16[2,512,1024]{2,1,0:T(8,128)(2,1)S(1)}, bf16[2,512,1024]{2,1,0:T(8,128)(2,1)}, u32[]{:S(2)}) copy-start(bf16[2,512,1024]{2,1,0:T(8,128)(2,1)} %get-tuple-element.97) | copy-start | bytes 6291460
  723.6 2.3 copy-start.3
  726.0 2.0 copy-start.7
  726.0 2.9 copy-start.6
  726.0 3.9 copy-start.1

commit v7 on v6

--- a/solution.py
+++ b/solution.py
@@ -681,7 +681,7 @@
 
 def first_kernel(
     size, replicas, x_ref, gain_ref, wq_ref, wo_ref, wu_ref, wd_ref,
-    qkv_ref, gains_out, a1_out, wq_out, wo_out, q_stage, o_stage, u_stage, d_stage, u_got,
+    qkv_ref, gains_out, a1_out, wq_out, wo_out, q_stage, o_stage, u_stage, d_stage,
     a1, w, gains, own_sem, q_sem, o_sem, u_sem, d_sem, gain_sem, *sems
 ):
     rows, width = x_ref.shape
@@ -730,16 +730,8 @@
     swaps[2].start()
     swaps[3].start()
 
-    u_gather = ZGather(u_stage.at[0], u_got, sems[14:17])
-
     def relay(j):
         gather.relay(j)
-
-        @pl.when(j == n - 1)
-        def _():
-            swaps[2].arrive()
-            u_gather.start()
-
         riders.step(j, n)
 
     run(n, relay)
@@ -758,8 +750,8 @@
 
     run(n, multiply)
     outs[1].start()
+    swaps[2].arrive()
     swaps[3].arrive()
-    u_gather.finish()
     for swap in swaps:
         swap.finish()
     gain_copy(section).wait_send()
@@ -782,10 +774,9 @@
             shape((width, wide), BF),
             shape((deep, width), BF),
         ]
-        + [shape(w.shape, BF) for w in ws]
-        + [shape((replicas,) + ws[2].shape[1:], BF)],
+        + [shape(w.shape, BF) for w in ws],
         in_specs=[VM, VM] + [HB] * 4,
-        out_specs=[VM, VM] + [HB] * 8,
+        out_specs=[VM, VM] + [HB] * 7,
         scratch_shapes=[
             pltpu.VMEM((size, rows, width), BF),
             pltpu.VMEM((width, wide), BF),
@@ -798,8 +789,7 @@
             DMA((2,)),
         ]
         + comm_sems(size, n)
-        + rider_sems(replicas) * 2
-        + [DMA((1,)), DMA((replicas - 1,)), DMA((replicas - 1,))],
+        + rider_sems(replicas) * 2,
         compiler_params=params(0),
         cost_estimate=cost(30e9, 30e6),
     )(x, gains, *ws)
@@ -879,11 +869,19 @@
 def attend_kernel(size, layer, columns, *refs):
     m = len(columns)
     qkv_ref, qm_ref, km_ref, x_ref, w_ref = refs[:5]
-    halves, refs = refs[5 : 5 + m], refs[5 + m :]
+    refs = refs[5:]
+    if layer == 1:
+        cot_ref, refs = refs[0], refs[1:]
+    halves, refs = refs[:m], refs[m:]
     h1_ref, ctx_ref, lse_ref = refs[:3]
-    wholes, refs = refs[3 : 3 + m], refs[3 + m :]
+    refs = refs[3:]
+    if layer == 1:
+        cot_out, refs = refs[0], refs[1:]
+    wholes, refs = refs[:m], refs[m:]
     ka, vt, w, w_sem = refs[:4]
     scratch, refs = refs[4:13], refs[13:]
+    if layer == 1:
+        cot_sems, cot_sem, refs = refs[:4], refs[4], refs[5:]
     riders = Riders(halves, wholes, columns, refs)
     _, rows, wide = qkv_ref.shape
     length = size * rows
@@ -899,6 +897,12 @@
     copy.start()
     g.greet(riders.replicas)
     riders.start()
+    if layer == 1:
+        cot = Gather(g, cot_out, rows, cot_sems)
+        own = pltpu.make_async_copy(cot_ref, cot_out.at[g.me], cot_sem.at[0])
+        own.start()
+        own.wait()
+        cot.start(0)
     scatter = Scatter(g, rc, scratch)
     whole = flat(qkv_ref[...])
     for h in range(heads):
@@ -940,6 +944,11 @@
         scatter.first(j)
         scatter.second(j)
         riders.step(j, n)
+        if layer == 1:
+
+            @pl.when(j == n - 1)
+            def _():
+                cot.relay(0)
 
     run(n, work)
 
@@ -949,10 +958,13 @@
 
     run(n, last)
     scatter.drain(n)
+    if layer == 1:
+        cot.ready(0)
+        cot.drain(1)
     riders.finish()
 
 
-def attend(size, replicas, layer, qkv, qm, km, x, w, riders):
+def attend(size, replicas, layer, qkv, qm, km, x, w, riders, cot=()):
     _, rows, wide = qkv.shape
     e = qm.shape[2]
     heads = wide // (3 * e)
@@ -966,9 +978,10 @@
             shape((size, rows, heads * e), BF),
             shape((n, heads, size * rows // n), F32),
         ]
+        + [shape((size, rows, width), BF) for _ in cot]
         + outs,
-        in_specs=[VM, VM, VM, VM, HB] + [HB] * len(riders),
-        out_specs=[VM, VM, VM] + [HB] * len(outs),
+        in_specs=[VM, VM, VM, VM, HB] + [HB] * (len(cot) + len(riders)),
+        out_specs=[VM, VM, VM] + [HB] * (len(cot) + len(outs)),
         scratch_shapes=[
             pltpu.VMEM((heads, size * rows, 2 * e), BF),
             pltpu.VMEM((heads, e + 16, size * rows), BF),
@@ -976,10 +989,11 @@
             DMA((1,)),
         ]
         + scatter_scratch(size, rows, width, n)
+        + (comm_sems(size, 1) + [DMA((1,))]) * len(cot)
         + sems,
         compiler_params=params(2 + layer),
         cost_estimate=cost(60e9, 20e6),
-    )(qkv, qm, km, x, w, *halves)
+    )(qkv, qm, km, x, w, *cot, *halves)
 
 
 def mlp_kernel(size, layer, columns, *refs):
@@ -1098,12 +1112,14 @@
 def mlp_back_kernel(size, layer, parts, *refs):
     g_ref, h1_ref, gain_ref, a2_ref, hid_ref, slope_ref, wu_ref, wd_ref = refs[:8]
     refs = refs[8:]
-    extra, refs = refs[:2], refs[2:]
-    mid_ref, gain_out, gup_ref, gdown_out, down_came, extra_out = refs[:6]
-    gdown_ref, refs = refs[6], refs[7:]
+    if layer == 1:
+        ys, whole_ref, refs = refs[:2], refs[2], refs[3:]
+    mid_ref, gain_out, gup_ref, gdown_ref = refs[:4]
+    refs = refs[4:]
+    if layer == 1:
+        y_out, refs = refs[0], refs[1:]
     grad, a2, hid, dup, wu, wd, w_sem = refs[:7]
     scratch, refs = refs[7:20], refs[20:]
-    down_sem, out_sem, refs = refs[0], refs[1], refs[2:]
     rows, width = h1_ref.shape
     hidden = wu_ref.shape[1]
     depth = width // parts
@@ -1122,12 +1138,10 @@
     ]
     for copy in copies + late:
         copy.start()
-    g.greet(parts if layer == 0 else 0, side=True)
-    down_swap = HalfSwap(gdown_ref, down_came, down_sem)
+    g.greet(side=layer == 1)
     section = lax.axis_index("section")
     if layer == 1:
         y_sem = refs[0]
-        ys, y_out = extra, extra_out
 
         def y_copies(own, other, at):
             return (
@@ -1144,12 +1158,6 @@
                 for copy in y_copies(ys[i], ys[1 - i], section):
                     copy.start()
 
-    else:
-        above = HalfReduce(1, refs)
-        loads = above.loads(*extra)
-        for load in loads:
-            load.start()
-
     gather = Gather(g, grad, rc, scratch[:4])
     scatter = Scatter(g, rc, scratch[4:])
 
@@ -1158,36 +1166,20 @@
         grad[g.me, at, :] = g_ref[at, :]
         gather.start(j)
 
-    run(n, send)
+    if layer == 1:
+        whole = pltpu.make_async_copy(whole_ref, grad, w_sem.at[5])
+        whole.start()
+        copies.append(whole)
+    else:
+        run(n, send)
     for copy in copies:
         copy.wait()
-    if layer == 0:
-        for load in loads:
-            load.wait()
-        above.middle()
-
-    for copy in late:
-        copy.wait()
-
-    def down_grad(f):
-        cols = pl.ds(pl.multiple_of(f * fb, fb), fb)
-        r = dg(flat(hid[:, :, cols]), flat(grad[...]), TN).astype(BF)
-        for z in range(parts):
-            gdown_ref[z, cols, :] = r[:, z * depth : (z + 1) * depth]
-
-    down_out = pltpu.make_async_copy(gdown_ref, gdown_out, out_sem.at[0])
 
     def work(j):
         at = span(j, rc)
-        gather.relay(j)
-        gather.ready(j)
-
-        @pl.when(j == n - 1)
-        def _():
-            run(hidden // fb, down_grad)
-            down_swap.copy().start()
-            down_out.start()
-
+        if layer == 0:
+            gather.relay(j)
+            gather.ready(j)
         held = flat(grad[:, at, :])
         for f in range(hidden // fb):
             cols = slice(f * fb, (f + 1) * fb)
@@ -1201,14 +1193,22 @@
         scatter.second(j)
 
     run(n, work)
+    for copy in late:
+        copy.wait()
 
     def up_grad(z):
         cols = pl.ds(pl.multiple_of(z * depth, depth), depth)
         gup_ref[z] = dg(flat(a2[:, :, cols]), flat(dup[...]), TN).astype(BF)
 
     run(parts, up_grad)
-    if layer == 0:
-        above.late()
+
+    def down_grad(f):
+        cols = pl.ds(pl.multiple_of(f * fb, fb), fb)
+        r = dg(flat(hid[:, :, cols]), flat(grad[...]), TN).astype(BF)
+        for z in range(parts):
+            gdown_ref[z, cols, :] = r[:, z * depth : (z + 1) * depth]
+
+    run(hidden // fb, down_grad)
     gain_out[...] = jnp.zeros_like(gain_out)
 
     def last(j):
@@ -1223,12 +1223,8 @@
         local.wait()
         side.wait_recv()
         y_copies(ys[0], ys[1], section)[1].wait_send()
-    else:
-        above.finish(extra_out)
-    down_swap.copy().wait_recv()
-    down_swap.copy().wait_send()
-    down_out.wait()
-    gather.drain(n)
+    if layer == 0:
+        gather.drain(n)
     scatter.drain(n)
 
 
@@ -1244,48 +1240,41 @@
             shape((1, width), F32),
             shape((parts, depth, hidden), BF),
             shape((parts, hidden, depth), BF),
-            shape((parts, hidden // 2, depth), BF),
-            (
-                shape((2, rows, width), BF)
-                if layer == 1
-                else shape((extra[0].shape[1], extra[0].shape[2]), F32)
-            ),
-        ],
-        in_specs=[VM, VM, VM] + [HB] * 7,
-        out_specs=[VM, VM, VM, HB, HB, HB if layer == 1 else VM],
+        ]
+        + [shape((2, rows, width), BF)] * (len(extra) // 3),
+        in_specs=[VM, VM, VM] + [HB] * (5 + len(extra)),
+        out_specs=[VM, VM, VM, VM] + [HB] * (len(extra) // 3),
         scratch_shapes=[
-            pltpu.VMEM((parts, hidden, depth), BF),
             pltpu.VMEM((size, rows, width), BF),
             pltpu.VMEM((size, rows, width), BF),
             pltpu.VMEM((size, rows, hidden), BF),
             pltpu.VMEM((size, rows, hidden), BF),
             pltpu.VMEM((width, hidden), BF),
             pltpu.VMEM((hidden, width), BF),
-            DMA((5,)),
+            DMA((6,)),
         ]
         + comm_sems(size, n)
         + scatter_scratch(size, rows, width, n)
-        + [DMA((2,)), DMA((1,))]
-        + ([DMA((3,))] if layer == 1 else half_scratch(parts, *extra[0].shape[1:])),
+        + [DMA((3,))] * (len(extra) // 3),
         compiler_params=params(6 + layer),
         cost_estimate=cost(60e9, 40e6),
     )(grad, h1, gains, a2, hid, slope, wu, wd, *extra)
 
 
 def attend_back_kernel(size, layer, parts, *refs):
-    mid_ref, qkv_ref, qm_ref, km_ref, ctx_ref, lse_ref, w_ref, gdown_ref, down_came, gup_ref = refs[:10]
-    refs = refs[10:]
+    mid_ref, qkv_ref, qm_ref, km_ref, ctx_ref, lse_ref, w_ref = refs[:7]
+    refs = refs[7:]
     if layer == 0:
-        aboves, refs = refs[:2], refs[2:]
-    else:
-        aboves = (None, None)
-    dqkv_ref, gout_ref, down_out, up_out = refs[:4]
-    da, ka, va, kt, dk, dv, w, w_sem = refs[4:12]
-    sems, refs = refs[12:16], refs[16:]
+        gdown_ref, refs = refs[0], refs[1:]
+    dqkv_ref, gout_ref, refs = refs[0], refs[1], refs[2:]
+    if layer == 0:
+        down_out, refs = refs[0], refs[1:]
+    da, ka, va, kt, dk, dv, w, w_sem = refs[:8]
+    sems, refs = refs[8:12], refs[12:]
     reduce = Reduce(layer, refs[:9])
-    down = HalfReduce(layer, refs[9 : 9 + HALF])
-    up = HalfReduce(layer, refs[9 + HALF : 9 + 2 * HALF])
-    up_swap = HalfSwap(gup_ref, up.other, refs[9 + 2 * HALF])
+    if layer == 0:
+        down = HalfReduce(layer, refs[9 : 9 + HALF])
+        down_swap = HalfSwap(gdown_ref, down.other, refs[9 + HALF])
     _, rows, wide = qkv_ref.shape
     length = size * rows
     e = qm_ref.shape[2]
@@ -1303,10 +1292,12 @@
         copy.start()
     g.greet(parts)
     gather = Gather(g, da, rc, sems)
-    up_swap.copy().start()
-    loads = down.loads(gdown_ref, down_came) + up.loads(gup_ref, None)
-    for load in loads:
-        load.start()
+    loads = []
+    if layer == 0:
+        down_swap.copy().start()
+        loads = down.loads(gdown_ref, None)
+        for load in loads:
+            load.start()
 
     def send(j):
         at = span(j, rc)
@@ -1328,7 +1319,6 @@
     ql = lax.broadcasted_iota(jnp.int32, (bq, e), 1)
     for copy in copies + loads:
         copy.wait()
-    down.middle()
 
     def out_grad(z):
         cols = pl.ds(pl.multiple_of(z * depth, depth), depth)
@@ -1377,37 +1367,36 @@
                 dk[h, ks, :] += dg(ds, qq, NN)
                 a = dg(kt[h, :, ks], ds, NN)
                 dqt = a if dqt is None else dqt + a
-            if h == heads // 2:
+            if layer == 0 and h == heads // 2:
 
                 @pl.when(j == min(1, n - 1))
                 def _():
-                    up_swap.copy().wait_recv()
-                    up.middle()
-
-            if h == heads - 1:
-
-                @pl.when(j == n // 2)
+                    down_swap.copy().wait_recv()
+                    down.middle()
+
+            if layer == 0 and h == heads - 1:
+
+                @pl.when(j == n - 1)
                 def _():
                     down.late()
 
             dqkv_ref[:, at, o : o + e] = (dqt * scale).T.astype(BF).reshape(size, rc, e)
 
     run(n, work)
-    reduce.collect()
-    up.late()
     for h in range(heads):
         o = 3 * e * h
         dqkv_ref[:, :, o + e : o + 2 * e] = (dk[h] * scale).astype(BF).reshape(size, rows, e)
         dqkv_ref[:, :, o + 2 * e : o + 3 * e] = dv[h].astype(BF).reshape(size, rows, e)
 
-    down.finish(down_out, aboves[0])
+    reduce.collect()
     reduce.finish(gout_ref)
-    up.finish(up_out, aboves[1])
-    up_swap.copy().wait_send()
+    if layer == 0:
+        down.finish(down_out)
+        down_swap.copy().wait_send()
     gather.drain(n)
 
 
-def attend_backward(size, replicas, layer, mid, qkv, qm, km, ctx, lse, w, grads, aboves):
+def attend_backward(size, replicas, layer, mid, qkv, qm, km, ctx, lse, w, grads):
     _, rows, wide = qkv.shape
     e = qm.shape[2]
     heads = wide // (3 * e)
@@ -1417,14 +1406,10 @@
     n = chunks(rows)
     return pl.pallas_call(
         functools.partial(attend_back_kernel, size, layer, parts),
-        out_shape=(
-            shape(qkv.shape, BF),
-            shape((heads * e, depth), F32),
-            shape(grads[0].shape[1:], F32),
-            shape(grads[2].shape[1:], F32),
-        ),
-        in_specs=[VM] * 6 + [HB] * (4 + len(aboves)),
-        out_specs=(VM, VM, VM, VM),
+        out_shape=[shape(qkv.shape, BF), shape((heads * e, depth), F32)]
+        + [shape(grad.shape[1:], F32) for grad in grads],
+        in_specs=[VM] * 6 + [HB] * (1 + len(grads)),
+        out_specs=[VM, VM] + [VM] * len(grads),
         scratch_shapes=[
             pltpu.VMEM((size, rows, width), BF),
             pltpu.VMEM((heads, length, 2 * e), BF),
@@ -1437,17 +1422,15 @@
         ]
         + comm_sems(size, n)
         + reduce_scratch(parts, heads * e, depth)
-        + half_scratch(parts, *grads[0].shape[1:])
-        + half_scratch(parts, *grads[2].shape[1:])
-        + [DMA((2,))],
+        + sum([half_scratch(parts, *grad.shape[1:]) + [DMA((2,))] for grad in grads], []),
         compiler_params=params(8 + layer),
         cost_estimate=cost(90e9, 40e6),
-    )(mid, qkv, qm, km, ctx, lse, w, *grads, *aboves)
+    )(mid, qkv, qm, km, ctx, lse, w, *grads)
 
 
 def qkv_back_kernel(
     size, layer, parts, dqkv_ref, a1_ref, x_ref, mid_ref, gain_ref, w_ref,
-    dx_ref, gain_out, gqkv_out, came, gqkv_ref, w, w_sem, swap_sem, *scratch
+    dx_ref, gain_out, gqkv_ref, w, w_sem, *scratch
 ):
     rows, width = x_ref.shape
     depth = width // parts
@@ -1457,13 +1440,8 @@
     copies = [pltpu.make_async_copy(w_ref, w, w_sem.at[0])]
     for copy in copies:
         copy.start()
-    g.greet(side=True)
-    swap = HalfSwap(gqkv_ref, came, swap_sem)
+    g.greet()
     scatter = Scatter(g, rc, scratch)
-    def qkv_grad(z):
-        cols = pl.ds(pl.multiple_of(z * depth, depth), depth)
-        gqkv_ref[z] = dg(flat(a1_ref[:, :, cols]), flat(dqkv_ref[...]), TN).astype(BF)
-
     for copy in copies:
         copy.wait()
 
@@ -1477,10 +1455,12 @@
         scatter.second(j)
 
     run(n, work)
+
+    def qkv_grad(z):
+        cols = pl.ds(pl.multiple_of(z * depth, depth), depth)
+        gqkv_ref[z] = dg(flat(a1_ref[:, :, cols]), flat(dqkv_ref[...]), TN).astype(BF)
+
     run(parts, qkv_grad)
-    swap.copy().start()
-    out = pltpu.make_async_copy(gqkv_ref, gqkv_out, w_sem.at[1])
-    out.start()
     gain_out[...] = jnp.zeros_like(gain_out)
 
     def last(j):
@@ -1492,9 +1472,6 @@
         gain_out[...] += dgain
 
     run(n, last)
-    swap.copy().wait_recv()
-    swap.copy().wait_send()
-    out.wait()
     scatter.drain(n)
 
 
@@ -1509,15 +1486,12 @@
             shape((rows, width), BF),
             shape((1, width), F32),
             shape((parts, depth, wide), BF),
-            shape((parts, depth // 2, wide), BF),
         ),
         in_specs=[VM] * 5 + [HB],
-        out_specs=(VM, VM, HB, HB),
+        out_specs=(VM, VM, VM),
         scratch_shapes=[
-            pltpu.VMEM((parts, depth, wide), BF),
             pltpu.VMEM((width, wide), BF),
-            DMA((2,)),
-            DMA((2,)),
+            DMA((1,)),
         ]
         + scatter_scratch(size, rows, width, n),
         compiler_params=params(11),
@@ -1527,7 +1501,7 @@
 
 def last_kernel(
     size, parts, dqkv_ref, a1_ref, x_ref, mid_ref, gain_ref, w_ref, two_ref, above_ref, dx1_ref,
-    qkv_above, gain_out, gqkv_out, dx_out,
+    gain_out, gqkv_out, dx_out,
     gqkv, swap_sem, w, dx, gsum, gcame, w_sem, x_sem, x_send, x_recv, g_send, g_recv, *scratch
 ):
     rows, width = x_ref.shape
@@ -1646,10 +1620,12 @@
         gsum[stage + 1] = total
         sent.extend(copies)
 
-    for stage in range(4):
-        exchange(stage)
+    exchange(0)
+    exchange(1)
+    reduce.late()
+    exchange(2)
+    exchange(3)
     gain_out[...] = gsum[4]
-    reduce.late()
 
     @pl.when(section == 0)
     def _():
@@ -1665,14 +1641,14 @@
         for j in range(n):
             lower(j).wait_send()
 
-    reduce.finish(gqkv_out, qkv_above)
+    reduce.finish(gqkv_out)
     swap.copy().wait_send()
     for copy in sent:
         copy.wait_send()
     scatter.drain(n)
 
 
-def last_backward(size, replicas, dqkv, a1, x, mid, gains, w, two, above, dx1, qkv_above):
+def last_backward(size, replicas, dqkv, a1, x, mid, gains, w, two, above, dx1):
     rows, width = x.shape
     wide = w.shape[1]
     depth = width // replicas
@@ -1685,7 +1661,7 @@
             shape((depth, wide), F32),
             shape((2, rows, width), BF),
         ),
-        in_specs=[VM] * 5 + [HB, VM, VM, HB, HB],
+        in_specs=[VM] * 5 + [HB, VM, VM, HB],
         out_specs=(VM, VM, HB),
         scratch_shapes=[
             pltpu.VMEM((replicas, depth, wide), BF),
@@ -1705,7 +1681,7 @@
         + scatter_scratch(size, rows, width, n),
         compiler_params=params(10),
         cost_estimate=cost(40e9, 30e6),
-    )(dqkv, a1, x, mid, gains, w, two, above, dx1, qkv_above)
+    )(dqkv, a1, x, mid, gains, w, two, above, dx1)
 
 
 def scene_masks(segments, e):
@@ -1715,6 +1691,10 @@
         jnp.where(used, same * MASKED, 0.0).astype(BF),
         jnp.where(used, 1.0 - same, 0.0).astype(BF),
     )
+
+
+def swap_section(value):
+    return lax.ppermute(value, "section", [(0, 1), (1, 0)])
 
 
 def shards(
@@ -1746,33 +1726,25 @@
     x = lax.dynamic_index_in_dim(block_input, section, 0, keepdims=False)
     head_dim = qkv_weight.shape[3] // 3
     qm, km = scene_masks(segments.reshape((size, -1)), head_dim)
-    qkv, gains, a1, w_qkv_0, w_out_0, h_qkv, h_out, h_up, h_down, got_up = first_forward(
+    qkv, gains, a1, w_qkv_0, w_out_0, h_qkv, h_out, h_up, h_down = first_forward(
         size, replicas, x, gains, mine
     )
-    h1, ctx, lse, w_up_0, w_down_0, got_qkv, got_out = attend(
+    h1, ctx, lse, w_up_0, w_down_0 = attend(
         size, replicas, 0, qkv, qm, km, x, w_out_0,
-        [
-            (got_up, "y", 0, False),
-            (h_down, "spread", 0, True),
-            (h_qkv, "z", 1, False),
-            (h_out, "z", 1, True),
-        ],
+        [(h_up, "spread", 0, False), (h_down, "spread", 0, True)],
     )
-    y0, a2, hid, slope, w_qkv_1, w_out_1, got_up, got_down = mlp_forward(
+    y0, a2, hid, slope, w_qkv_1, w_out_1, got_up = mlp_forward(
         size, replicas, 0, h1, gains, w_up_0, w_down_0,
-        [
-            (got_qkv, "y", 1, False),
-            (got_out, "y", 1, True),
-            (h_up, "z", 1, False),
-            (h_down, "z", 1, True),
-        ],
+        [(h_qkv, "spread", 1, False), (h_out, "spread", 1, True), (h_up, "z", 1, False)],
     )
     kept = [(x, a1, qkv, ctx, lse, h1, a2, hid, slope)]
-    qkv, a1, w_up_1 = qkv_forward(
-        size, replicas, 1, y0, gains, w_qkv_1, [(got_up, "y", 1, False)]
+    qkv, a1, got_down = qkv_forward(
+        size, replicas, 1, y0, gains, w_qkv_1, [(h_down, "z", 1, True)]
     )
-    h1, ctx, lse, w_down_1 = attend(
-        size, replicas, 1, qkv, qm, km, y0, w_out_1, [(got_down, "y", 1, True)]
+    grad = lax.dynamic_index_in_dim(cotangent, section, 0, keepdims=False)
+    h1, ctx, lse, grad_all, w_up_1, w_down_1 = attend(
+        size, replicas, 1, qkv, qm, km, y0, w_out_1,
+        [(got_up, "y", 1, False), (got_down, "y", 1, True)], [grad],
     )
     y1, a2, hid, slope = mlp_forward(size, replicas, 1, h1, gains, w_up_1, w_down_1, [])
     kept.append((y0, a1, qkv, ctx, lse, h1, a2, hid, slope))
@@ -1780,34 +1752,46 @@
         (w_qkv_0, w_out_0, w_up_0, w_down_0),
         (w_qkv_1, w_out_1, w_up_1, w_down_1),
     ]
-    grad = lax.dynamic_index_in_dim(cotangent, section, 0, keepdims=False)
+    def reduce_rows(value):
+        return lax.psum_scatter(value, "dp", scatter_dimension=0, tiled=False)
 
     x, a1, qkv, ctx, lse, h1, a2, hid, slope = kept[1]
     w_qkv, w_out, w_up, w_down = weights[1]
-    mid, gain_two, g_up, g_down, came, layer_out = mlp_backward(
-        size, replicas, 1, grad, h1, gains, a2, hid, slope, w_up, w_down, [y0, y1]
+    mid, gain_two, g_up, g_down, layer_out = mlp_backward(
+        size, replicas, 1, grad, h1, gains, a2, hid, slope, w_up, w_down, [y0, y1, grad_all]
     )
-    d_qkv, out_1, down_1, up_1 = attend_backward(
-        size, replicas, 1, mid, qkv, qm, km, ctx, lse, w_out, [g_down, came, g_up], []
-    )
-    dx1, gain_one, g_qkv, came = qkv_backward(
-        size, replicas, 1, d_qkv, a1, x, mid, gains, w_qkv
-    )
+    d_qkv, out_1 = attend_backward(size, replicas, 1, mid, qkv, qm, km, ctx, lse, w_out, [])
+    up_1, down_1 = reduce_rows(g_up), reduce_rows(g_down)
+    dx1, gain_one, g_qkv = qkv_backward(size, replicas, 1, d_qkv, a1, x, mid, gains, w_qkv)
     gains_above = jnp.concatenate([gain_one, gain_two], axis=0)
+    dx1, up_1, down_1 = lax.optimization_barrier((dx1, up_1, down_1))
+    qkv_1 = reduce_rows(g_qkv)
 
     x, a1, qkv, ctx, lse, h1, a2, hid, slope = kept[0]
     w_qkv, w_out, w_up, w_down = weights[0]
-    mid, gain_two, g_up, g_down, came, qkv_1 = mlp_backward(
-        size, replicas, 0, dx1, h1, gains, a2, hid, slope, w_up, w_down, [g_qkv, came]
+    mid, gain_two, g_up, g_down = mlp_backward(
+        size, replicas, 0, dx1, h1, gains, a2, hid, slope, w_up, w_down, []
     )
-    d_qkv, out_0, down_grad, up_grad = attend_backward(
-        size, replicas, 0, mid, qkv, qm, km, ctx, lse, w_out,
-        [g_down, came, g_up], [down_1, up_1],
+    mid, qkv_1 = lax.optimization_barrier((mid, qkv_1))
+    d_qkv, out_0, down_0 = attend_backward(
+        size, replicas, 0, mid, qkv, qm, km, ctx, lse, w_out, [g_down]
     )
-    gains, qkv_grad, input_out = last_backward(
-        size, replicas, d_qkv, a1, x, mid, gains, w_qkv, gain_two, gains_above, dx1, qkv_1
+    up_0 = reduce_rows(g_up)
+    d_qkv, up_0 = lax.optimization_barrier((d_qkv, up_0))
+    gains, qkv_0, input_out = last_backward(
+        size, replicas, d_qkv, a1, x, mid, gains, w_qkv, gain_two, gains_above, dx1
     )
+
+    def finish(zero, one):
+        send = swap_section(jnp.where(section == 0, one, zero))
+        return jnp.where(section == 0, zero, one).astype(F32) + send.astype(F32)
+
+    other_qkv_1 = swap_section(qkv_1)
+    qkv_grad = jnp.where(section == 0, qkv_0, qkv_1.astype(F32) + other_qkv_1.astype(F32))
     out_grad = jnp.where(section == 0, out_0, out_1)
+    up_grad = finish(up_0, up_1)
+    other_down_1 = swap_section(down_1)
+    down_grad = jnp.where(section == 0, down_0, down_1.astype(F32) + other_down_1.astype(F32))
     gains = lax.dynamic_slice_in_dim(gains, 2 * section, 2, 0)
     return (
         layer_out[None],

time: 739 us -> 811 us (1.097)
  Pallas kernels: 708 us -> 758 us
  between operations: 1.1 us -> 14.3 us
  other arithmetic: 6.66 us -> 15.5 us
    pallas_call x2, Pallas kernels: 109 us -> 209 us  [attend(): pl.pallas_call(functools.partial(attend_kernel, size, layer, columns), ou...]
    pallas_call x2, Pallas kernels: 125 us -> 93.5 us  [mlp_backward(): pl.pallas_call(functools.partial(mlp_back_kernel, size, layer, parts), ou...]
    pallas_call x2, Pallas kernels: 166 us -> 155 us  [attend_backward(): pl.pallas_call(functools.partial(attend_back_kernel, size, layer, parts),...]
  transfers between devices with their start and end apart: 0 -> 7, of which waited for: 0 -> 0; matrix products, arithmetic and copies ran while one was open for 0% -> 1% of each run, Pallas kernels for 0% -> 38%
where the time goes in v7:
time: 811 us; the launch traced here: 802 us
  Pallas kernels  758 us (93%)
  other arithmetic  15.5 us (2%)
  between operations  14.3 us (2%)
  local copies, waits for them, and re-layouts  10.6 us (1%)
    pallas_call x2, Pallas kernels, attend(): pl.pallas_call(functools.partial(attend_kernel, size, layer, columns), ou...  209 us
    pallas_call x2, Pallas kernels, attend_backward(): pl.pallas_call(functools.partial(attend_back_kernel, size, layer, parts),...  155 us
    pallas_call x2, Pallas kernels, mlp_forward(): pl.pallas_call(functools.partial(mlp_kernel, size, layer, columns), out_s...  111 us
    pallas_call x2, Pallas kernels, mlp_backward(): pl.pallas_call(functools.partial(mlp_back_kernel, size, layer, parts), ou...  93.5 us
    pallas_call x1, Pallas kernels, last_backward(): pl.pallas_call(functools.partial(last_kernel, size, replicas), out_shape=...  63.7 us
    pallas_call x1, Pallas kernels, first_forward(): pl.pallas_call(functools.partial(first_kernel, size, replicas), out_shape...  58.5 us
    pallas_call x1, Pallas kernels, qkv_backward(): pl.pallas_call(functools.partial(qkv_back_kernel, size, layer, parts), ou...  35.4 us
    pallas_call x1, Pallas kernels, qkv_forward(): pl.pallas_call(functools.partial(qkv_kernel, size, layer, columns), out_s...  31.2 us
  transfers between devices with their start and end apart: 7, of which 0 were waited for; matrix products, arithmetic and copies ran while one was open for 1% of the time, Pallas kernels for 38%

profile of v7, /device:TPU:0, one launch (start us, length us, event | category | flops | bytes accessed | tf_op | source)
XLA Modules:
  0.0 802.3 jit_solution(4684679408579421993)
XLA Ops:
  7.2 0.0 copy-start
  7.2 0.0 copy-start.5
  7.2 0.0 reduce-scatter.5.cloned.1.call-start
  7.3 0.0 copy-start.6
  7.3 1.3 convert_element_type.55
  8.6 0.1 convert_element_type.56
  8.7 0.0 copy-start.9
  8.7 1.1 copy.19.wq_ref
  9.8 0.0 copy-done.5
  9.8 0.9 convert_element_type.59
  10.6 0.0 copy-done.6
  10.6 0.8 convert_element_type.61
  11.5 0.0 copy-done.9
  11.5 0.7 convert_element_type.57
  12.2 0.0 copy-done
  12.2 0.0 copy-start.12
  12.2 0.0 copy-start.13
  12.2 3.0 dynamic-slice_bitcast_fusion
  15.3 0.1 pad.4.clone
  15.3 1.2 select_convert_fusion
  16.6 0.0 copy-done.12
  16.6 0.0 copy-done.13
  16.6 0.7 maximum_maximum_fusion.gain_ref
  17.2 58.5 %shard_map.152 = (bf16[4,512,768]{2,1,0:T(8,128)(2,1)}, f32[2,8,1024]{2,1,0:T(8,128)}, bf16[4,512,1024]{2,1,0:T(8,128)(2,1)}, bf16[1024,768]{1,0:T(8,128)(2,1)},...) custom-call(bf16[512,1024]{1,0:T(8,128)(2,1)} %get-tuple-element.142, ...), custom_call_target="tpu_custom_call" | custom-call | flops 30000001024 | bytes 30000000 | tf_op jit(solution)/shard_map/pallas_call | solution.py:768
  75.8 59.3 %shard_map.153 = (f32[512,1024]{1,0:T(8,128)}, bf16[4,512,256]{2,1,0:T(8,128)(2,1)}, f32[4,4,512]{2,1,0:T(4,128)}, bf16[1024,1024]{1,0:T(8,128)(2,1)}, bf16[1024,1024]{1,0:T(8,128)(2,1)}) custom-call(bf16[4,512,768]{2,1,0:T(8,128)(2,1)} %get-tuple-element.69.refs_0_.refs_1_, bf16[4,512,64]{2,1,0:T(8,128)(2,1)} %get-tuple-element.141.refs_1_.refs_2_, ...), custom_call_target="tpu_custom_call" | custom-call | flops 60000002048 | bytes 20000000 | tf_op jit(solution)/shard_map/pallas_call | solution.py:974
  135.1 59.5 %shard_map.154 = (bf16[512,1024]{1,0:T(8,128)(2,1)}, bf16[4,512,1024]{2,1,0:T(8,128)(2,1)}, bf16[4,512,1024]{2,1,0:T(8,128)(2,1)}, bf16[4,512,1024]{2,1,0:T(8,12...) custom-call(f32[512,1024]{1,0:T(8,128)} %get-tuple-element.73.refs_0_.refs_1_, ...), custom_call_target="tpu_custom_call" | custom-call | flops 49999998976 | bytes 30000000 | tf_op jit(solution)/shard_map/pallas_call | solution.py:1084
  194.6 31.2 %shard_map.155 = (bf16[4,512,768]{2,1,0:T(8,128)(2,1)}, bf16[4,512,1024]{2,1,0:T(8,128)(2,1)}, bf16[4,512,256]{2,1,0:T(8,128)(2,1)}) custom-call(bf16[512,1024]{1,0:T(8,128)(2,1)} %get-tuple-element.79.refs_0_.refs_3_.refs_8_.x_ref, f32[2,8,1024]{2,1,0:T(8,128)} %get-tuple-element.74.refs_1_.refs_2_.gain_ref, ...), custom_call_target="tpu_custom_call" | custom-call | flops 20000000000 | bytes 30000000 | tf_op jit(solution)/shard_map/pallas_call | solution.py:847
  225.8 149.6 %shard_map.156 = (f32[512,1024]{1,0:T(8,128)}, bf16[4,512,256]{2,1,0:T(8,128)(2,1)}, f32[4,4,512]{2,1,0:T(4,128)}, bf16[4,512,1024]{2,1,0:T(8,128)(2,1)}, bf16[1...) custom-call(bf16[4,512,768]{2,1,0:T(8,128)(2,1)} %get-tuple-element.81.refs_0_.refs_1_, ...), custom_call_target="tpu_custom_call" | custom-call | flops 60000002048 | bytes 20000000 | tf_op jit(solution)/shard_map/pallas_call | solution.py:974
  375.4 51.8 %shard_map.157 = (bf16[512,1024]{1,0:T(8,128)(2,1)}, bf16[4,512,1024]{2,1,0:T(8,128)(2,1)}, bf16[4,512,1024]{2,1,0:T(8,128)(2,1)}, bf16[4,512,1024]{2,1,0:T(8,128)(2,1)}) custom-call(f32[512,1024]{1,0:T(8,128)} %get-tuple-element.85.refs_0_.refs_1_, f32[2,8,1024]{2,1,0:T(8,128)} %get-tuple-element.74.refs_1_.refs_2_.gain_ref, ...), custom_call_target="tpu_custom_call" | custom-call | flops 49999998976 | bytes 30000000 | tf_op jit(solution)/shard_map/pallas_call | solution.py:1084
  427.2 40.9 %shard_map.158 = (f32[512,1024]{1,0:T(8,128)}, f32[1,1024]{1,0:T(1,128)}, bf16[4,256,1024]{2,1,0:T(8,128)(2,1)}, bf16[4,1024,256]{2,1,0:T(8,128)(2,1)}, bf16[2,512,1024]{2,1,0:T(8,128)(2,1)}) custom-call(bf16[512,1024]{1,0:T(8,128)(2,1)} %get-tuple-element.143.refs_5_.refs_0_, f32[512,1024]{1,0:T(8,128)} %get-tuple-element.85.refs_0_.refs_1_, ...), custom_call_target="tpu_custom_call" | custom-call | flops 60000002048 | bytes 40000000 | tf_op jit(solution)/shard_map/pallas_call | solution.py:1236
  468.1 0.0 reduce-scatter.5.cloned.1.call-update
  468.1 0.0 reduce-scatter.7.cloned.1.call-start
  468.2 0.7 reduce-scatter.7.cloned.1.call-update
  468.9 0.0 reduce-scatter.9.cloned.1.call-start
  468.9 73.1 %shard_map.159 = (bf16[4,512,768]{2,1,0:T(8,128)(2,1)}, f32[256,256]{1,0:T(8,128)}) custom-call(f32[512,1024]{1,0:T(8,128)} %get-tuple-element.94.refs_0_.mid_ref, bf16[4,512,768]{2,1,0:T(8,128)(2,1)} %get-tuple-element.81.refs_0_.refs_1_, bf16[4,512,64]{2,1,0:T(8,128)(2,1)} %get-tuple-element.141.refs_1_.refs_2_, ...), custom_call_target="tpu_custom_call" | custom-call | flops 89999998976 | bytes 40000000 | tf_op jit(solution)/shard_map/pallas_call | solution.py:1407
  542.0 35.4 %shard_map.160 = (bf16[512,1024]{1,0:T(8,128)(2,1)}, f32[1,1024]{1,0:T(1,128)}, bf16[4,256,768]{2,1,0:T(8,128)(2,1)}) custom-call(bf16[4,512,768]{2,1,0:T(8,128)(2,1)} %get-tuple-element.97.dqkv_ref, bf16[4,512,1024]{2,1,0:T(8,128)(2,1)} %get-tuple-element.98.a1_ref, bf16[512,1024]{1,0:T(8,128)(2,1)} %get-tuple-element.79.refs_0_.refs_3_.refs_8_.x_ref, ...), custom_call_target="tpu_custom_call" | custom-call | flops 30000001024 | bytes 30000000 | tf_op jit(solution)/shard_map/pallas_call | solution.py:1483
  577.4 0.0 reduce-scatter.9.cloned.1.call-update
  577.4 0.0 reduce-scatter.11.cloned.1.call-start
  577.5 1.3 pad_maximum_fusion.above_ref
  578.8 52.6 %shard_map.161 = (f32[512,1024]{1,0:T(8,128)}, f32[1,1024]{1,0:T(1,128)}, bf16[4,256,1024]{2,1,0:T(8,128)(2,1)}, bf16[4,1024,256]{2,1,0:T(8,128)(2,1)}) custom-call(bf16[512,1024]{1,0:T(8,128)(2,1)} %get-tuple-element.102.refs_0_.dx1_ref, f32[512,1024]{1,0:T(8,128)} %get-tuple-element.73.refs_0_.refs_1_, ...), custom_call_target="tpu_custom_call" | custom-call | flops 60000002048 | bytes 40000000 | tf_op jit(solution)/shard_map/pallas_call | solution.py:1236
  631.4 0.0 reduce-scatter.9.cloned.1.call-done
  631.4 0.0 copy-start.8
  631.5 0.0 copy-done.7
  631.5 2.4 collective-permute-start.2
  633.8 0.0 reduce-scatter.11.cloned.1.call-update
  633.9 0.9 collective-permute-start
  634.8 82.1 %shard_map.162 = (bf16[4,512,768]{2,1,0:T(8,128)(2,1)}, f32[256,256]{1,0:T(8,128)}, f32[1024,256]{1,0:T(8,128)}) custom-call(f32[512,1024]{1,0:T(8,128)} %get-tuple-element.108.refs_0_.mid_ref, bf16[4,512,768]{2,1,0:T(8,128)(2,1)} %get-tuple-element.69.refs_0_.refs_1_, bf16[4,512,64]{2,1,0:T(8,128)(2,1)} %get-tuple-element.141.refs_1_.refs_2_, ...), custom_call_target="tpu_custom_call" | custom-call | flops 89999998976 | bytes 40000000 | tf_op jit(solution)/shard_map/pallas_call | solution.py:1407
  716.9 1.7 broadcast_select_fusion.1
  718.6 0.0 collective-permute-done.2
  718.6 2.3 select_bitcast_fusion
  721.0 0.0 copy-done.4
  721.0 0.9 broadcast_select_fusion
  721.8 0.0 collective-permute-start.1
  721.8 63.7 %shard_map.163 = (f32[8,1024]{1,0:T(8,128)}, f32[256,768]{1,0:T(8,128)}, bf16[2,512,1024]{2,1,0:T(8,128)(2,1)}) custom-call(bf16[4,512,768]{2,1,0:T(8,128)(2,1)} %get-tuple-element.114.dqkv_ref, bf16[4,512,1024]{2,1,0:T(8,128)(2,1)} %get-tuple-element.115.a1_ref, bf16[512,1024]{1,0:T(8,128)(2,1)} %get-tuple-element.142.x_ref.refs_3_, ...), custom_call_target="tpu_custom_call" | custom-call | flops 40000000000 | bytes 30000000 | tf_op jit(solution)/shard_map/pallas_call | solution.py:1657
  785.5 0.0 collective-permute-done
  785.5 1.2 add_select_fusion
  786.8 1.1 copy.20
  788.0 1.4 constant_dynamic-slice_fusion.1
  789.4 0.0 collective-permute-done.1
  789.4 2.4 add_bitcast_fusion
  791.8 1.3 copy.23
  793.2 1.0 copy-done.3
  794.2 1.3 copy.24
  795.5 0.0 copy-done.1
  (18 shorter events, 0.1 us)
Async XLA Ops:
  7.2 5.0 copy-start
  7.2 2.6 copy-start.5
  7.2 571.6 %reduce-scatter.5.cloned.1.call-start = ((), (), s32[]{:S(2)}) async-start(), calls=%async_computation.4 | async-start | bytes 2621440 | tf_op jit(solution)/shard_map/reduce_scatter | solution.py:1756
  7.3 3.4 copy-start.6
  8.7 2.8 copy-start.9
  12.2 4.4 copy-start.12
  12.2 4.4 copy-start.13
  468.1 110.7 %reduce-scatter.7.cloned.1.call-start = ((), (), s32[]{:S(2)}) async-start(), calls=%async_computation.5 | async-start | bytes 2621440 | tf_op jit(solution)/shard_map/reduce_scatter | solution.py:1756
  468.9 162.6 %reduce-scatter.9.cloned.1.call-start = ((), (), s32[]{:S(2)}) async-start(), calls=%async_computation.6 | async-start | bytes 1966080 | tf_op jit(solution)/shard_map/reduce_scatter | solution.py:1756
  542.0 35.5 %copy-start.11 = (f32[1,1024]{1,0:T(1,128)S(1)}, f32[1,1024]{1,0:T(1,128)}, u32[]{:S(2)}) copy-start(f32[1,1024]{1,0:T(1,128)} %get-tuple-element.119) | copy-start | bytes 12292
  577.4 143.5 %reduce-scatter.11.cloned.1.call-start = ((), (), s32[]{:S(2)}) async-start(), calls=%async_computation.7 | async-start | bytes 2621440 | tf_op jit(solution)/shard_map/reduce_scatter | solution.py:1756
  578.8 52.7 %copy-start.7 = (bf16[1,1024,256]{2,1,0:T(8,128)(2,1)S(1)}, bf16[1,1024,256]{2,1,0:T(8,128)(2,1)}, u32[]{:S(2)}) copy-start(bf16[1,1024,256]{2,1,0:T(8,128)(2,1)} %reduce-scatter.7.cloned.1.call-done) | copy-start | bytes 1572868
  631.4 2.4 copy-start.8
  631.5 87.2 %collective-permute-start.2 = (bf16[1024,256]{1,0:T(8,128)(2,1)S(1)}, bf16[1024,256]{1,0:T(8,128)(2,1)S(1)}, u32[]{:S(2)}, u32[]{:S(2)}) collective-permute-start(bf16[1024,256]{1,0:T(8,128)(2,1)S(1)} %bitcast.32), channel_id=1, source_target_pairs={{0,16},{16,0},{1,17},{17,1},{2,18},{18,2},{3,19},{19,3},{4,20},{20... | collective-permute-start | bytes 1572872 | tf_op jit(solution)/shard_map/ppermute | solution.py:1697
  633.9 151.7 %collective-permute-start = (bf16[256,768]{1,0:T(8,128)(2,1)S(1)}, bf16[256,768]{1,0:T(8,128)(2,1)S(1)}, u32[]{:S(2)}, u32[]{:S(2)}) collective-permute-start(bf16[256,768]{1,0:T(8,128)(2,1)S(1)} %bitcast.34), channel_id=1, source_target_pairs={{0,16},{16,0},{1,17},{17,1},{2,18},{18,2},{3,19},{19,3},{4,20},{20... | collective-permute-start | bytes 1179656 | tf_op jit(solution)/shard_map/ppermute | solution.py:1697
  634.8 82.1 %copy-start.10 = (f32[256,256]{1,0:T(8,128)S(1)}, f32[256,256]{1,0:T(8,128)}, u32[]{:S(2)}) copy-start(f32[256,256]{1,0:T(8,128)} %get-tuple-element.125) | copy-start | bytes 786436
  716.9 4.1 copy-start.4
  721.8 67.6 %collective-permute-start.1 = (bf16[256,1024]{1,0:T(8,128)(2,1)}, bf16[256,1024]{1,0:T(8,128)(2,1)}, u32[]{:S(2)}, u32[]{:S(2)}) collective-permute-start(bf16[256,1024]{1,0:T(8,128)(2,1)} %broadcast_select_fusion), channel_id=1, source_target_pairs={{0,16},{16,0},{1,17},{17,1},{2,18},{18,2},{3,19},{19,3},{4,20},{20... | collective-permute-start | bytes 1572872 | tf_op jit(solution)/shard_map/ppermute | solution.py:1697
  786.8 5.0 copy-start.2
  791.8 2.3 copy-start.3
  791.8 3.7 copy-start.1
Sparse Core Ops, SparseCore 0:
  468.2 47.5 reduce-scatter.4
  518.2 45.8 reduce-scatter.6
  577.5 35.4 reduce-scatter.8
  634.0 49.3 reduce-scatter.10

commit v8 on v7

--- a/solution.py
+++ b/solution.py
@@ -89,21 +89,23 @@
         self.g, self.buf, self.rc = g, buf, rc
         self.far_send, self.far_recv, self.near_send, self.near_recv = sems
 
-    def far(self, k, j, origin, target):
+    def far(self, k, j, origin, target, src=None):
         ref = self.buf.at[origin, span(j, self.rc)]
-        return remote(ref, ref, self.far_send.at[k - 1, j], self.far_recv.at[k - 1, j], target)
-
-    def near(self, k, j, origin):
+        src = ref if src is None else src
+        return remote(src, ref, self.far_send.at[k - 1, j], self.far_recv.at[k - 1, j], target)
+
+    def near(self, k, j, origin, src=None):
         ref = self.buf.at[origin, span(j, self.rc)]
+        src = ref if src is None else src
         return remote(
-            ref, ref, self.near_send.at[k, j], self.near_recv.at[k, j], self.g.sibling
+            src, ref, self.near_send.at[k, j], self.near_recv.at[k, j], self.g.sibling
         )
 
-    def start(self, j):
+    def start(self, j, src=None):
         g = self.g
         for k in range(1, g.chips):
-            self.far(k, j, g.me, g.ahead(k) * 2 + g.core).start()
-        self.near(0, j, g.me).start()
+            self.far(k, j, g.me, g.ahead(k) * 2 + g.core, src).start()
+        self.near(0, j, g.me, src).start()
 
     def relay(self, j):
         g = self.g
@@ -541,8 +543,8 @@
 
 class YJoin:
     def __init__(self, got, dst, by_columns, sems):
-        self.got, self.dst, self.by_columns = got, dst, by_columns
-        self.own_sem, self.send, self.recv = sems
+        self.src, self.dst, self.by_columns = got, dst, by_columns
+        self.own_sem, self.send, self.recv, self.got, self.in_sem = sems
         self.replicas, self.rows, self.cols = got.shape
         self.s = lax.axis_index("section")
 
@@ -567,6 +569,9 @@
         )
 
     def start(self):
+        load = pltpu.make_async_copy(self.src, self.got, self.in_sem.at[0])
+        load.start()
+        load.wait()
         for z in range(self.replicas):
             self.side(z, self.s).start()
             self.own(z).start()
@@ -591,7 +596,7 @@
     def __init__(self, srcs, dsts, columns, sems):
         self.all = []
         for src, dst, (kind, layer, by) in zip(srcs, dsts, columns):
-            count = 5 if kind == "spread" else 3
+            count = 3 if kind == "z" else 5
             own, sems = sems[:count], sems[count:]
             if kind == "spread":
                 self.all.append(Spread(src.at[layer], dst, by, own))
@@ -637,7 +642,7 @@
         sems += {
             "spread": rider_sems(replicas),
             "z": [DMA((1,)), far, far],
-            "y": [side, side, side],
+            "y": [side, side, side, pltpu.VMEM(array.shape, BF), DMA((1,))],
         }[kind]
     return arrays, columns, outs, sems
 
@@ -775,7 +780,7 @@
             shape((deep, width), BF),
         ]
         + [shape(w.shape, BF) for w in ws],
-        in_specs=[VM, VM] + [HB] * 4,
+        in_specs=[VM] * 6,
         out_specs=[VM, VM] + [HB] * 7,
         scratch_shapes=[
             pltpu.VMEM((size, rows, width), BF),
@@ -901,8 +906,7 @@
         cot = Gather(g, cot_out, rows, cot_sems)
         own = pltpu.make_async_copy(cot_ref, cot_out.at[g.me], cot_sem.at[0])
         own.start()
-        own.wait()
-        cot.start(0)
+        cot.start(0, cot_ref)
     scatter = Scatter(g, rc, scratch)
     whole = flat(qkv_ref[...])
     for h in range(heads):
@@ -961,6 +965,7 @@
     if layer == 1:
         cot.ready(0)
         cot.drain(1)
+        own.wait()
     riders.finish()
 
 
@@ -980,7 +985,7 @@
         ]
         + [shape((size, rows, width), BF) for _ in cot]
         + outs,
-        in_specs=[VM, VM, VM, VM, HB] + [HB] * (len(cot) + len(riders)),
+        in_specs=[VM, VM, VM, VM, HB] + [VM] * len(cot) + [HB] * len(riders),
         out_specs=[VM, VM, VM] + [HB] * (len(cot) + len(outs)),
         scratch_shapes=[
             pltpu.VMEM((heads, size * rows, 2 * e), BF),
@@ -1141,11 +1146,14 @@
     g.greet(side=layer == 1)
     section = lax.axis_index("section")
     if layer == 1:
-        y_sem = refs[0]
+        y_sem, y_own = refs
+
+        def y_load(own):
+            return pltpu.make_async_copy(own, y_own, y_sem.at[3])
 
         def y_copies(own, other, at):
             return (
-                pltpu.make_async_copy(own, y_out.at[section], y_sem.at[0]),
+                pltpu.make_async_copy(y_own, y_out.at[section], y_sem.at[0]),
                 far_copy(
                     other, y_out.at[at], y_sem.at[1], y_sem.at[2], {"section": 1 - section}
                 ),
@@ -1155,8 +1163,8 @@
 
             @pl.when(section == i)
             def _(i=i):
-                for copy in y_copies(ys[i], ys[1 - i], section):
-                    copy.start()
+                y_load(ys[i]).start()
+                y_copies(ys[i], ys[1 - i], section)[1].start()
 
     gather = Gather(g, grad, rc, scratch[:4])
     scatter = Scatter(g, rc, scratch[4:])
@@ -1174,6 +1182,9 @@
         run(n, send)
     for copy in copies:
         copy.wait()
+    if layer == 1:
+        y_load(ys[0]).wait()
+        y_copies(ys[0], ys[1], section)[0].start()
 
     def work(j):
         at = span(j, rc)
@@ -1255,7 +1266,7 @@
         ]
         + comm_sems(size, n)
         + scatter_scratch(size, rows, width, n)
-        + [DMA((3,))] * (len(extra) // 3),
+        + [DMA((4,)), pltpu.VMEM((rows, width), BF)] * (len(extra) // 3),
         compiler_params=params(6 + layer),
         cost_estimate=cost(60e9, 40e6),
     )(grad, h1, gains, a2, hid, slope, wu, wd, *extra)
@@ -1661,7 +1672,7 @@
             shape((depth, wide), F32),
             shape((2, rows, width), BF),
         ),
-        in_specs=[VM] * 5 + [HB, VM, VM, HB],
+        in_specs=[VM] * 5 + [HB, VM, VM, VM],
         out_specs=(VM, VM, HB),
         scratch_shapes=[
             pltpu.VMEM((replicas, depth, wide), BF),

time: 811 us -> 726 us (0.90)
  Pallas kernels: 758 us -> 672 us
    pallas_call x2, Pallas kernels: 209 us -> 118 us  [attend(): pl.pallas_call(functools.partial(attend_kernel, size, layer, columns), ou...]
  transfers between devices with their start and end apart: 7 -> 7, of which waited for: 0 -> 0; matrix products, arithmetic and copies ran while one was open for 1% -> 1% of each run, Pallas kernels for 38% -> 43%
where the time goes in v8:
time: 726 us; the launch traced here: 717 us
  Pallas kernels  672 us (93%)
  other arithmetic  15.5 us (2%)
  between operations  14.3 us (2%)
  local copies, waits for them, and re-layouts  10.6 us (1%)
    pallas_call x2, Pallas kernels, attend_backward(): pl.pallas_call(functools.partial(attend_back_kernel, size, layer, parts),...  156 us
    pallas_call x2, Pallas kernels, attend(): pl.pallas_call(functools.partial(attend_kernel, size, layer, columns), ou...  118 us
    pallas_call x2, Pallas kernels, mlp_forward(): pl.pallas_call(functools.partial(mlp_kernel, size, layer, columns), out_s...  117 us
    pallas_call x2, Pallas kernels, mlp_backward(): pl.pallas_call(functools.partial(mlp_back_kernel, size, layer, parts), ou...  94.3 us
    pallas_call x1, Pallas kernels, last_backward(): pl.pallas_call(functools.partial(last_kernel, size, replicas), out_shape=...  63.4 us
    pallas_call x1, Pallas kernels, first_forward(): pl.pallas_call(functools.partial(first_kernel, size, replicas), out_shape...  56.7 us
    pallas_call x1, Pallas kernels, qkv_backward(): pl.pallas_call(functools.partial(qkv_back_kernel, size, layer, parts), ou...  34.3 us
    pallas_call x1, Pallas kernels, qkv_forward(): pl.pallas_call(functools.partial(qkv_kernel, size, layer, columns), out_s...  32 us
  transfers between devices with their start and end apart: 7, of which 0 were waited for; matrix products, arithmetic and copies ran while one was open for 1% of the time, Pallas kernels for 43%

profile of v8, /device:TPU:0, one launch (start us, length us, event | category | flops | bytes accessed | tf_op | source)
XLA Modules:
  0.0 716.6 jit_solution(7120978809788883577)
XLA Ops:
  7.2 0.0 copy-start
  7.2 0.0 copy-start.5
  7.2 0.0 reduce-scatter.5.cloned.1.call-start
  7.3 0.0 copy-start.6
  7.3 1.3 convert_element_type.55
  8.6 0.1 convert_element_type.56
  8.7 0.0 copy-start.9
  8.7 1.1 copy.19.wq_ref
  9.8 0.0 copy-done.5
  9.8 0.9 convert_element_type.59
  10.6 0.0 copy-done.6
  10.6 0.8 convert_element_type.61
  11.5 0.0 copy-done.9
  11.5 0.7 convert_element_type.57
  12.2 0.0 copy-done
  12.2 0.0 copy-start.12
  12.2 0.0 copy-start.13
  12.2 3.0 dynamic-slice_bitcast_fusion
  15.3 0.1 pad.4.clone
  15.3 1.2 select_convert_fusion
  16.6 0.0 copy-done.12
  16.6 0.0 copy-done.13
  16.6 0.7 maximum_maximum_fusion.gain_ref
  17.2 56.7 %shard_map.152 = (bf16[4,512,768]{2,1,0:T(8,128)(2,1)}, f32[2,8,1024]{2,1,0:T(8,128)}, bf16[4,512,1024]{2,1,0:T(8,128)(2,1)}, bf16[1024,768]{1,0:T(8,128)(2,1)},...) custom-call(bf16[512,1024]{1,0:T(8,128)(2,1)} %get-tuple-element.142, ...), custom_call_target="tpu_custom_call" | custom-call | flops 30000001024 | bytes 30000000 | tf_op jit(solution)/shard_map/pallas_call | solution.py:773
  74.0 60.3 %shard_map.153 = (f32[512,1024]{1,0:T(8,128)}, bf16[4,512,256]{2,1,0:T(8,128)(2,1)}, f32[4,4,512]{2,1,0:T(4,128)}, bf16[1024,1024]{1,0:T(8,128)(2,1)}, bf16[1024,1024]{1,0:T(8,128)(2,1)}) custom-call(bf16[4,512,768]{2,1,0:T(8,128)(2,1)} %get-tuple-element.69.refs_0_.refs_1_, bf16[4,512,64]{2,1,0:T(8,128)(2,1)} %get-tuple-element.141.refs_1_.refs_2_, ...), custom_call_target="tpu_custom_call" | custom-call | flops 60000002048 | bytes 20000000 | tf_op jit(solution)/shard_map/pallas_call | solution.py:979
  134.3 66.4 %shard_map.154 = (bf16[512,1024]{1,0:T(8,128)(2,1)}, bf16[4,512,1024]{2,1,0:T(8,128)(2,1)}, bf16[4,512,1024]{2,1,0:T(8,128)(2,1)}, bf16[4,512,1024]{2,1,0:T(8,12...) custom-call(f32[512,1024]{1,0:T(8,128)} %get-tuple-element.73.refs_0_.refs_1_, ...), custom_call_target="tpu_custom_call" | custom-call | flops 49999998976 | bytes 30000000 | tf_op jit(solution)/shard_map/pallas_call | solution.py:1089
  200.7 32.0 %shard_map.155 = (bf16[4,512,768]{2,1,0:T(8,128)(2,1)}, bf16[4,512,1024]{2,1,0:T(8,128)(2,1)}, bf16[4,512,256]{2,1,0:T(8,128)(2,1)}) custom-call(bf16[512,1024]{1,0:T(8,128)(2,1)} %get-tuple-element.79.refs_0_.refs_3_.refs_8_.x_ref, f32[2,8,1024]{2,1,0:T(8,128)} %get-tuple-element.74.refs_1_.refs_2_.gain_ref, ...), custom_call_target="tpu_custom_call" | custom-call | flops 20000000000 | bytes 30000000 | tf_op jit(solution)/shard_map/pallas_call | solution.py:852
  232.7 57.2 %shard_map.156 = (f32[512,1024]{1,0:T(8,128)}, bf16[4,512,256]{2,1,0:T(8,128)(2,1)}, f32[4,4,512]{2,1,0:T(4,128)}, bf16[4,512,1024]{2,1,0:T(8,128)(2,1)}, bf16[1...) custom-call(bf16[4,512,768]{2,1,0:T(8,128)(2,1)} %get-tuple-element.81.refs_0_.refs_1_, ...), custom_call_target="tpu_custom_call" | custom-call | flops 60000002048 | bytes 20000000 | tf_op jit(solution)/shard_map/pallas_call | solution.py:979
  290.0 50.8 %shard_map.157 = (bf16[512,1024]{1,0:T(8,128)(2,1)}, bf16[4,512,1024]{2,1,0:T(8,128)(2,1)}, bf16[4,512,1024]{2,1,0:T(8,128)(2,1)}, bf16[4,512,1024]{2,1,0:T(8,128)(2,1)}) custom-call(f32[512,1024]{1,0:T(8,128)} %get-tuple-element.85.refs_0_.refs_1_, f32[2,8,1024]{2,1,0:T(8,128)} %get-tuple-element.74.refs_1_.refs_2_.gain_ref, ...), custom_call_target="tpu_custom_call" | custom-call | flops 49999998976 | bytes 30000000 | tf_op jit(solution)/shard_map/pallas_call | solution.py:1089
  340.8 41.0 %shard_map.158 = (f32[512,1024]{1,0:T(8,128)}, f32[1,1024]{1,0:T(1,128)}, bf16[4,256,1024]{2,1,0:T(8,128)(2,1)}, bf16[4,1024,256]{2,1,0:T(8,128)(2,1)}, bf16[2,512,1024]{2,1,0:T(8,128)(2,1)}) custom-call(bf16[512,1024]{1,0:T(8,128)(2,1)} %get-tuple-element.143.refs_5_.refs_0_, f32[512,1024]{1,0:T(8,128)} %get-tuple-element.85.refs_0_.refs_1_, ...), custom_call_target="tpu_custom_call" | custom-call | flops 60000002048 | bytes 40000000 | tf_op jit(solution)/shard_map/pallas_call | solution.py:1247
  381.8 0.0 reduce-scatter.5.cloned.1.call-update
  381.8 0.0 reduce-scatter.7.cloned.1.call-start
  381.9 0.7 reduce-scatter.7.cloned.1.call-update
  382.6 0.0 reduce-scatter.9.cloned.1.call-start
  382.6 74.8 %shard_map.159 = (bf16[4,512,768]{2,1,0:T(8,128)(2,1)}, f32[256,256]{1,0:T(8,128)}) custom-call(f32[512,1024]{1,0:T(8,128)} %get-tuple-element.94.refs_0_.mid_ref, bf16[4,512,768]{2,1,0:T(8,128)(2,1)} %get-tuple-element.81.refs_0_.refs_1_, bf16[4,512,64]{2,1,0:T(8,128)(2,1)} %get-tuple-element.141.refs_1_.refs_2_, ...), custom_call_target="tpu_custom_call" | custom-call | flops 89999998976 | bytes 40000000 | tf_op jit(solution)/shard_map/pallas_call | solution.py:1418
  457.4 0.0 copy-start.11
  457.5 34.3 %shard_map.160 = (bf16[512,1024]{1,0:T(8,128)(2,1)}, f32[1,1024]{1,0:T(1,128)}, bf16[4,256,768]{2,1,0:T(8,128)(2,1)}) custom-call(bf16[4,512,768]{2,1,0:T(8,128)(2,1)} %get-tuple-element.97.dqkv_ref, bf16[4,512,1024]{2,1,0:T(8,128)(2,1)} %get-tuple-element.98.a1_ref, bf16[512,1024]{1,0:T(8,128)(2,1)} %get-tuple-element.79.refs_0_.refs_3_.refs_8_.x_ref, ...), custom_call_target="tpu_custom_call" | custom-call | flops 30000001024 | bytes 30000000 | tf_op jit(solution)/shard_map/pallas_call | solution.py:1494
  491.7 0.0 reduce-scatter.9.cloned.1.call-update
  491.8 0.0 reduce-scatter.11.cloned.1.call-start
  491.8 0.0 copy-done.11
  491.8 1.3 pad_maximum_fusion.above_ref
  493.1 53.3 %shard_map.161 = (f32[512,1024]{1,0:T(8,128)}, f32[1,1024]{1,0:T(1,128)}, bf16[4,256,1024]{2,1,0:T(8,128)(2,1)}, bf16[4,1024,256]{2,1,0:T(8,128)(2,1)}) custom-call(bf16[512,1024]{1,0:T(8,128)(2,1)} %get-tuple-element.102.refs_0_.dx1_ref, f32[512,1024]{1,0:T(8,128)} %get-tuple-element.73.refs_0_.refs_1_, ...), custom_call_target="tpu_custom_call" | custom-call | flops 60000002048 | bytes 40000000 | tf_op jit(solution)/shard_map/pallas_call | solution.py:1247
  546.4 0.0 reduce-scatter.9.cloned.1.call-done
  546.5 0.0 copy-start.8
  546.5 2.5 collective-permute-start.2
  549.0 0.0 reduce-scatter.11.cloned.1.call-update
  549.0 0.9 collective-permute-start
  549.9 81.5 %shard_map.162 = (bf16[4,512,768]{2,1,0:T(8,128)(2,1)}, f32[256,256]{1,0:T(8,128)}, f32[1024,256]{1,0:T(8,128)}) custom-call(f32[512,1024]{1,0:T(8,128)} %get-tuple-element.108.refs_0_.mid_ref, bf16[4,512,768]{2,1,0:T(8,128)(2,1)} %get-tuple-element.69.refs_0_.refs_1_, bf16[4,512,64]{2,1,0:T(8,128)(2,1)} %get-tuple-element.141.refs_1_.refs_2_, ...), custom_call_target="tpu_custom_call" | custom-call | flops 89999998976 | bytes 40000000 | tf_op jit(solution)/shard_map/pallas_call | solution.py:1418
  631.4 1.7 broadcast_select_fusion.1
  633.2 0.0 collective-permute-done.2
  633.2 2.3 select_bitcast_fusion
  635.5 0.0 copy-done.4
  635.5 0.9 broadcast_select_fusion
  636.4 0.0 collective-permute-start.1
  636.4 63.4 %shard_map.163 = (f32[8,1024]{1,0:T(8,128)}, f32[256,768]{1,0:T(8,128)}, bf16[2,512,1024]{2,1,0:T(8,128)(2,1)}) custom-call(bf16[4,512,768]{2,1,0:T(8,128)(2,1)} %get-tuple-element.114.dqkv_ref, bf16[4,512,1024]{2,1,0:T(8,128)(2,1)} %get-tuple-element.115.a1_ref, bf16[512,1024]{1,0:T(8,128)(2,1)} %get-tuple-element.142.x_ref.refs_3_, ...), custom_call_target="tpu_custom_call" | custom-call | flops 40000000000 | bytes 30000000 | tf_op jit(solution)/shard_map/pallas_call | solution.py:1668
  699.8 0.0 collective-permute-done
  699.8 1.2 add_select_fusion
  701.1 1.1 copy.20
  702.3 1.4 constant_dynamic-slice_fusion.1
  703.7 0.0 collective-permute-done.1
  703.7 2.4 add_bitcast_fusion
  706.1 1.3 copy.23
  707.4 1.0 copy-done.3
  708.5 1.3 copy.24
  (18 shorter events, 0.1 us)
Async XLA Ops:
  7.2 5.0 copy-start
  7.2 2.6 copy-start.5
  7.2 485.9 %reduce-scatter.5.cloned.1.call-start = ((), (), s32[]{:S(2)}) async-start(), calls=%async_computation.4 | async-start | bytes 2621440 | tf_op jit(solution)/shard_map/reduce_scatter | solution.py:1767
  7.3 3.4 copy-start.6
  8.7 2.8 copy-start.9
  12.2 4.4 copy-start.12
  12.2 4.4 copy-start.13
  381.8 111.3 %reduce-scatter.7.cloned.1.call-start = ((), (), s32[]{:S(2)}) async-start(), calls=%async_computation.5 | async-start | bytes 2621440 | tf_op jit(solution)/shard_map/reduce_scatter | solution.py:1767
  382.6 163.9 %reduce-scatter.9.cloned.1.call-start = ((), (), s32[]{:S(2)}) async-start(), calls=%async_computation.6 | async-start | bytes 1966080 | tf_op jit(solution)/shard_map/reduce_scatter | solution.py:1767
  457.4 34.4 %copy-start.11 = (f32[1,1024]{1,0:T(1,128)S(1)}, f32[1,1024]{1,0:T(1,128)}, u32[]{:S(2)}) copy-start(f32[1,1024]{1,0:T(1,128)} %get-tuple-element.119) | copy-start | bytes 12292
  491.8 143.8 %reduce-scatter.11.cloned.1.call-start = ((), (), s32[]{:S(2)}) async-start(), calls=%async_computation.7 | async-start | bytes 2621440 | tf_op jit(solution)/shard_map/reduce_scatter | solution.py:1767
  493.1 53.3 %copy-start.7 = (bf16[1,1024,256]{2,1,0:T(8,128)(2,1)S(1)}, bf16[1,1024,256]{2,1,0:T(8,128)(2,1)}, u32[]{:S(2)}) copy-start(bf16[1,1024,256]{2,1,0:T(8,128)(2,1)} %reduce-scatter.7.cloned.1.call-done) | copy-start | bytes 1572868
  546.5 2.6 copy-start.8
  546.5 86.7 %collective-permute-start.2 = (bf16[1024,256]{1,0:T(8,128)(2,1)S(1)}, bf16[1024,256]{1,0:T(8,128)(2,1)S(1)}, u32[]{:S(2)}, u32[]{:S(2)}) collective-permute-start(bf16[1024,256]{1,0:T(8,128)(2,1)S(1)} %bitcast.32), channel_id=1, source_target_pairs={{0,16},{16,0},{1,17},{17,1},{2,18},{18,2},{3,19},{19,3},{4,20},{20... | collective-permute-start | bytes 1572872 | tf_op jit(solution)/shard_map/ppermute | solution.py:1708
  549.0 150.8 %collective-permute-start = (bf16[256,768]{1,0:T(8,128)(2,1)S(1)}, bf16[256,768]{1,0:T(8,128)(2,1)S(1)}, u32[]{:S(2)}, u32[]{:S(2)}) collective-permute-start(bf16[256,768]{1,0:T(8,128)(2,1)S(1)} %bitcast.34), channel_id=1, source_target_pairs={{0,16},{16,0},{1,17},{17,1},{2,18},{18,2},{3,19},{19,3},{4,20},{20... | collective-permute-start | bytes 1179656 | tf_op jit(solution)/shard_map/ppermute | solution.py:1708
  549.9 81.5 %copy-start.10 = (f32[256,256]{1,0:T(8,128)S(1)}, f32[256,256]{1,0:T(8,128)}, u32[]{:S(2)}) copy-start(f32[256,256]{1,0:T(8,128)} %get-tuple-element.125) | copy-start | bytes 786436
  631.4 4.1 copy-start.4
  636.4 67.3 %collective-permute-start.1 = (bf16[256,1024]{1,0:T(8,128)(2,1)}, bf16[256,1024]{1,0:T(8,128)(2,1)}, u32[]{:S(2)}, u32[]{:S(2)}) collective-permute-start(bf16[256,1024]{1,0:T(8,128)(2,1)} %broadcast_select_fusion), channel_id=1, source_target_pairs={{0,16},{16,0},{1,17},{17,1},{2,18},{18,2},{3,19},{19,3},{4,20},{20... | collective-permute-start | bytes 1572872 | tf_op jit(solution)/shard_map/ppermute | solution.py:1708
  701.1 5.0 copy-start.2
  706.1 2.3 copy-start.3
  706.1 3.7 copy-start.1
Sparse Core Ops, SparseCore 0:
  382.0 50.4 reduce-scatter.4
  434.9 44.4 reduce-scatter.6
  491.9 35.3 reduce-scatter.8
  549.2 48.8 reduce-scatter.10

commit v9 on v8

--- a/solution.py
+++ b/solution.py
@@ -28,6 +28,10 @@
 
 def chunks(rows):
     return 4 if rows % 64 == 0 else 1
+
+
+def thin_chunks(rows):
+    return 8 if rows % 128 == 0 else chunks(rows)
 
 
 def shape(dims, dtype):
@@ -690,7 +694,7 @@
     a1, w, gains, own_sem, q_sem, o_sem, u_sem, d_sem, gain_sem, *sems
 ):
     rows, width = x_ref.shape
-    n = chunks(rows)
+    n = thin_chunks(rows)
     rc = rows // n
     g = Group(size)
     section = lax.axis_index("section")
@@ -769,7 +773,7 @@
     rows, width = x.shape
     wide = ws[0].shape[2]
     deep = 2 * ws[1].shape[1]
-    n = chunks(rows)
+    n = thin_chunks(rows)
     return pl.pallas_call(
         functools.partial(first_kernel, size, replicas),
         out_shape=[
@@ -798,77 +802,6 @@
         compiler_params=params(0),
         cost_estimate=cost(30e9, 30e6),
     )(x, gains, *ws)
-
-
-def qkv_kernel(size, layer, columns, *refs):
-    m = len(columns)
-    x_ref, gain_ref, w_ref = refs[:3]
-    halves, refs = refs[3 : 3 + m], refs[3 + m :]
-    qkv_ref, a1_out = refs[:2]
-    wholes, refs = refs[2 : 2 + m], refs[2 + m :]
-    a1, w, w_sem, out_sem = refs[:4]
-    sems, refs = refs[4:8], refs[8:]
-    riders = Riders(halves, wholes, columns, refs)
-    rows, width = x_ref.shape
-    n = chunks(rows)
-    rc = rows // n
-    g = Group(size)
-    copy = pltpu.make_async_copy(w_ref, w, w_sem.at[0])
-    copy.start()
-    g.greet(riders.replicas)
-    gather = Gather(g, a1, rc, sems)
-    riders.start()
-
-    def send(j):
-        at = span(j, rc)
-        a = normed(x_ref[at, :].astype(F32))[0] * gain_ref[layer, 0:1, :]
-        a1[g.me, at, :] = a.astype(BF)
-        gather.start(j)
-
-    run(n, send)
-    copy.wait()
-
-    def work(j):
-        at = span(j, rc)
-        gather.relay(j)
-        gather.ready(j)
-        r = dg(flat(a1[:, at, :]), w[...], NN).astype(BF)
-        qkv_ref[:, at, :] = r.reshape(size, rc, r.shape[1])
-        riders.step(j, n)
-
-    run(n, work)
-    out = pltpu.make_async_copy(a1, a1_out, out_sem.at[0])
-    out.start()
-    riders.finish()
-    gather.drain(n)
-    out.wait()
-
-
-def qkv_forward(size, replicas, layer, x, gains, w, riders):
-    rows, width = x.shape
-    wide = w.shape[1]
-    n = chunks(rows)
-    halves, columns, outs, sems = riding(riders, replicas)
-    return pl.pallas_call(
-        functools.partial(qkv_kernel, size, layer, columns),
-        out_shape=[
-            shape((size, rows, wide), BF),
-            shape((size, rows, width), BF),
-        ]
-        + outs,
-        in_specs=[VM, VM, HB] + [HB] * len(riders),
-        out_specs=[VM, HB] + [HB] * len(outs),
-        scratch_shapes=[
-            pltpu.VMEM((size, rows, width), BF),
-            pltpu.VMEM((width, wide), BF),
-            DMA((1,)),
-            DMA((1,)),
-        ]
-        + comm_sems(size, n)
-        + sems,
-        compiler_params=params(layer),
-        cost_estimate=cost(20e9, 30e6),
-    )(x, gains, w, *halves)
 
 
 def attend_kernel(size, layer, columns, *refs):
@@ -1013,7 +946,7 @@
     rows, width = h1_ref.shape
     hidden = wu_ref.shape[1]
     fb = min(256, hidden)
-    n = chunks(rows)
+    n = thin_chunks(rows)
     rc = rows // n
     g = Group(size)
     copies = [
@@ -1084,7 +1017,7 @@
 def mlp_forward(size, replicas, layer, h1, gains, wu, wd, riders):
     rows, width = h1.shape
     hidden = wu.shape[1]
-    n = chunks(rows)
+    n = thin_chunks(rows)
     halves, columns, outs, sems = riding(riders, replicas)
     return pl.pallas_call(
         functools.partial(mlp_kernel, size, layer, columns),
@@ -1114,6 +1047,158 @@
     )(h1, gains, wu, wd, *halves)
 
 
+def turn_kernel(size, columns, *refs):
+    m = len(columns)
+    h1_ref, gain_ref, wu_ref, wd_ref, q_stage = refs[:5]
+    halves, refs = refs[5 : 5 + m], refs[5 + m :]
+    y_ref, qkv_ref, a2_out, hid_out, slope_out, a1_out, wq_out = refs[:7]
+    wholes, refs = refs[7 : 7 + m], refs[7 + m :]
+    a2, hid, slope, wu, wd, a1, wq, w_sem, out_sem = refs[:9]
+    gather_sems, next_sems, refs = refs[9:13], refs[13:17], refs[17:]
+    scratch, refs = refs[:9], refs[9:]
+    spread = Spread(q_stage.at[1], wq, False, refs[:5])
+    riders = Riders(halves, wholes, columns, refs[5:])
+    riders.all.insert(0, spread)
+    riders.replicas = spread.replicas
+    rows, width = h1_ref.shape
+    hidden = wu_ref.shape[1]
+    fb = min(256, hidden)
+    n = thin_chunks(rows)
+    rc = rows // n
+    g = Group(size)
+    copies = [
+        pltpu.make_async_copy(wu_ref, wu, w_sem.at[0]),
+        pltpu.make_async_copy(wd_ref, wd, w_sem.at[1]),
+    ]
+    for copy in copies:
+        copy.start()
+    g.greet(riders.replicas)
+    gather = Gather(g, a2, rc, gather_sems)
+    onward = Gather(g, a1, rc, next_sems)
+    scatter = Scatter(g, rc, scratch)
+
+    def send(j):
+        at = span(j, rc)
+        a = normed(h1_ref[at, :])[0] * gain_ref[0, 1:2, :]
+        a2[g.me, at, :] = a.astype(BF)
+        gather.start(j)
+
+    run(n, send)
+    riders.start()
+    for copy in copies:
+        copy.wait()
+
+    def pass_on(j):
+        at = span(j, rc)
+        y = (h1_ref[at, :] + scatter.third(j)).astype(BF)
+        y_ref[at, :] = y
+        a = normed(y.astype(F32))[0] * gain_ref[1, 0:1, :]
+        a1[g.me, at, :] = a.astype(BF)
+        onward.start(j)
+
+    lag = min(2, n)
+
+    def work(j):
+        at = span(j, rc)
+        gather.relay(j)
+        gather.ready(j)
+        a = flat(a2[:, at, :])
+        for f in range(hidden // fb):
+            cols = slice(f * fb, (f + 1) * fb)
+            u = dg(a, wu[:, cols], NN)
+            half = 0.5 + 0.5 * lax.erf(u * (0.5**0.5))
+            slope[:, at, cols] = (
+                (half + u * jnp.exp(-0.5 * u * u) * ((2 * math.pi) ** -0.5))
+                .astype(BF)
+                .reshape(size, rc, fb)
+            )
+            hid[:, at, cols] = (u * half).astype(BF).reshape(size, rc, fb)
+        held = flat(hid[:, at, :])
+        for f in range(width // 256):
+            cols = slice(f * 256, (f + 1) * 256)
+            scatter.part[:, at, cols] = dg(held, wd[:, cols], NN).reshape(size, rc, 256)
+        scatter.first(j)
+        scatter.second(j)
+
+        @pl.when(j >= lag)
+        def _():
+            pass_on(j - lag)
+
+        riders.step(j, n)
+
+    run(n, work)
+    outs = [
+        pltpu.make_async_copy(a2, a2_out, out_sem.at[0]),
+        pltpu.make_async_copy(hid, hid_out, out_sem.at[1]),
+        pltpu.make_async_copy(slope, slope_out, out_sem.at[2]),
+    ]
+    for out in outs:
+        out.start()
+    for j in range(n - lag, n):
+        pass_on(j)
+    spread.finish()
+    riders.all.pop(0)
+    outs.append(pltpu.make_async_copy(wq, wq_out, out_sem.at[3]))
+    outs[3].start()
+
+    def multiply(j):
+        at = span(j, rc)
+        onward.relay(j)
+        onward.ready(j)
+        r = dg(flat(a1[:, at, :]), wq[...], NN).astype(BF)
+        qkv_ref[:, at, :] = r.reshape(size, rc, r.shape[1])
+
+    run(n, multiply)
+    outs.append(pltpu.make_async_copy(a1, a1_out, out_sem.at[4]))
+    outs[4].start()
+    riders.finish()
+    gather.drain(n)
+    onward.drain(n)
+    scatter.drain(n)
+    for out in outs:
+        out.wait()
+
+
+def turn_forward(size, replicas, h1, gains, wu, wd, stage, riders):
+    rows, width = h1.shape
+    hidden = wu.shape[1]
+    wide = stage.shape[2]
+    n = thin_chunks(rows)
+    halves, columns, outs, sems = riding(riders, replicas)
+    return pl.pallas_call(
+        functools.partial(turn_kernel, size, columns),
+        out_shape=[
+            shape((rows, width), BF),
+            shape((size, rows, wide), BF),
+            shape((size, rows, width), BF),
+            shape((size, rows, hidden), BF),
+            shape((size, rows, hidden), BF),
+            shape((size, rows, width), BF),
+            shape((width, wide), BF),
+        ]
+        + outs,
+        in_specs=[VM, VM] + [HB] * (3 + len(riders)),
+        out_specs=[VM, VM] + [HB] * (5 + len(outs)),
+        scratch_shapes=[
+            pltpu.VMEM((size, rows, width), BF),
+            pltpu.VMEM((size, rows, hidden), BF),
+            pltpu.VMEM((size, rows, hidden), BF),
+            pltpu.VMEM((width, hidden), BF),
+            pltpu.VMEM((hidden, width), BF),
+            pltpu.VMEM((size, rows, width), BF),
+            pltpu.VMEM((width, wide), BF),
+            DMA((2,)),
+            DMA((5,)),
+        ]
+        + comm_sems(size, n) * 2
+        + scatter_scratch(size, rows, width, n)
+        + rider_sems(replicas)
+        + sems,
+        compiler_params=params(4),
+        cost_estimate=cost(50e9, 30e6),
+    )(h1, gains, wu, wd, stage, *halves)
+
+
 def mlp_back_kernel(size, layer, parts, *refs):
     g_ref, h1_ref, gain_ref, a2_ref, hid_ref, slope_ref, wu_ref, wd_ref = refs[:8]
     refs = refs[8:]
@@ -1129,7 +1214,7 @@
     hidden = wu_ref.shape[1]
     depth = width // parts
     fb = min(256, hidden)
-    n = chunks(rows)
+    n = thin_chunks(rows)
     rc = rows // n
     g = Group(size)
     copies = [
@@ -1243,7 +1328,7 @@
     rows, width = h1.shape
     hidden = wu.shape[1]
     parts, depth = replicas, width // replicas
-    n = chunks(rows)
+    n = thin_chunks(rows)
     return pl.pallas_call(
         functools.partial(mlp_back_kernel, size, layer, parts),
         out_shape=[
@@ -1440,16 +1525,21 @@
 
 
 def qkv_back_kernel(
-    size, layer, parts, dqkv_ref, a1_ref, x_ref, mid_ref, gain_ref, w_ref,
-    dx_ref, gain_out, gqkv_ref, w, w_sem, *scratch
+    size, layer, parts, dqkv_ref, gain_ref, a1_in, x_in, mid_in, w_ref,
+    dx_ref, gain_out, gqkv_ref, a1_ref, x_ref, mid_ref, w, w_sem, *scratch
 ):
     rows, width = x_ref.shape
+    late = [
+        pltpu.make_async_copy(a1_in, a1_ref, w_sem.at[1]),
+        pltpu.make_async_copy(x_in, x_ref, w_sem.at[2]),
+        pltpu.make_async_copy(mid_in, mid_ref, w_sem.at[3]),
+    ]
     depth = width // parts
-    n = chunks(rows)
+    n = thin_chunks(rows)
     rc = rows // n
     g = Group(size)
     copies = [pltpu.make_async_copy(w_ref, w, w_sem.at[0])]
-    for copy in copies:
+    for copy in copies + late:
         copy.start()
     g.greet()
     scatter = Scatter(g, rc, scratch)
@@ -1466,6 +1556,8 @@
         scatter.second(j)
 
     run(n, work)
+    for copy in late:
+        copy.wait()
 
     def qkv_grad(z):
         cols = pl.ds(pl.multiple_of(z * depth, depth), depth)
@@ -1490,7 +1582,7 @@
     rows, width = x.shape
     wide = w.shape[1]
     parts, depth = replicas, width // replicas
-    n = chunks(rows)
+    n = thin_chunks(rows)
     return pl.pallas_call(
         functools.partial(qkv_back_kernel, size, layer, parts),
         out_shape=(
@@ -1498,16 +1590,19 @@
             shape((1, width), F32),
             shape((parts, depth, wide), BF),
         ),
-        in_specs=[VM] * 5 + [HB],
+        in_specs=[VM, VM] + [HB] * 4,
         out_specs=(VM, VM, VM),
         scratch_shapes=[
+            pltpu.VMEM((size, rows, width), BF),
+            pltpu.VMEM((rows, width), BF),
+            pltpu.VMEM((rows, width), F32),
             pltpu.VMEM((width, wide), BF),
-            DMA((1,)),
+            DMA((4,)),
         ]
         + scatter_scratch(size, rows, width, n),
         compiler_params=params(11),
         cost_estimate=cost(30e9, 30e6),
-    )(dqkv, a1, x, mid, gains, w)
+    )(dqkv, gains, a1, x, mid, w)
 
 
 def last_kernel(
@@ -1517,7 +1612,7 @@
 ):
     rows, width = x_ref.shape
     depth = width // parts
-    n = chunks(rows)
+    n = thin_chunks(rows)
     rc = rows // n
     g = Group(size)
     section = lax.axis_index("section")
@@ -1663,7 +1758,7 @@
     rows, width = x.shape
     wide = w.shape[1]
     depth = width // replicas
-    n = chunks(rows)
+    n = thin_chunks(rows)
     slots = 1 + (size // 2 - 1) + (replicas - 1) + 1
     return pl.pallas_call(
         functools.partial(last_kernel, size, replicas),
@@ -1744,18 +1839,15 @@
         size, replicas, 0, qkv, qm, km, x, w_out_0,
         [(h_up, "spread", 0, False), (h_down, "spread", 0, True)],
     )
-    y0, a2, hid, slope, w_qkv_1, w_out_1, got_up = mlp_forward(
-        size, replicas, 0, h1, gains, w_up_0, w_down_0,
-        [(h_qkv, "spread", 1, False), (h_out, "spread", 1, True), (h_up, "z", 1, False)],
+    below = (x, a1, qkv, ctx, lse, h1)
+    y0, qkv, a2, hid, slope, a1, w_qkv_1, w_out_1, w_up_1, got_down = turn_forward(
+        size, replicas, h1, gains, w_up_0, w_down_0, h_qkv,
+        [(h_out, "spread", 1, True), (h_up, "spread", 1, False), (h_down, "z", 1, True)],
     )
-    kept = [(x, a1, qkv, ctx, lse, h1, a2, hid, slope)]
-    qkv, a1, got_down = qkv_forward(
-        size, replicas, 1, y0, gains, w_qkv_1, [(h_down, "z", 1, True)]
-    )
+    kept = [below + (a2, hid, slope)]
     grad = lax.dynamic_index_in_dim(cotangent, section, 0, keepdims=False)
-    h1, ctx, lse, grad_all, w_up_1, w_down_1 = attend(
-        size, replicas, 1, qkv, qm, km, y0, w_out_1,
-        [(got_up, "y", 1, False), (got_down, "y", 1, True)], [grad],
+    h1, ctx, lse, grad_all, w_down_1 = attend(
+        size, replicas, 1, qkv, qm, km, y0, w_out_1, [(got_down, "y", 1, True)], [grad]
     )
     y1, a2, hid, slope = mlp_forward(size, replicas, 1, h1, gains, w_up_1, w_down_1, [])
     kept.append((y0, a1, qkv, ctx, lse, h1, a2, hid, slope))

time: 726 us -> 730 us (level)
    pallas_call x1, Pallas kernels: 32 us -> 102 us  [turn_forward(): pl.pallas_call(functools.partial(turn_kernel, size, columns), out_shape=[...]
    pallas_call x2 -> x1, Pallas kernels: 117 us -> 50.6 us  [mlp_forward(): pl.pallas_call(functools.partial(mlp_kernel, size, layer, columns), out_s...]
  transfers between devices with their start and end apart: 7 -> 7, of which waited for: 0 -> 0; matrix products, arithmetic and copies ran while one was open for 1% -> 1% of each run, Pallas kernels for 43% -> 42%
where the time goes in v9:
time: 730 us; the launch traced here: 721 us
  Pallas kernels  676 us (93%)
  other arithmetic  15.5 us (2%)
  between operations  14.5 us (2%)
  local copies, waits for them, and re-layouts  10.6 us (1%)
    pallas_call x2, Pallas kernels, attend_backward(): pl.pallas_call(functools.partial(attend_back_kernel, size, layer, parts),...  154 us
    pallas_call x2, Pallas kernels, attend(): pl.pallas_call(functools.partial(attend_kernel, size, layer, columns), ou...  116 us
    pallas_call x1, Pallas kernels, turn_forward(): pl.pallas_call(functools.partial(turn_kernel, size, columns), out_shape=[...  102 us
    pallas_call x2, Pallas kernels, mlp_backward(): pl.pallas_call(functools.partial(mlp_back_kernel, size, layer, parts), ou...  99.3 us
    pallas_call x1, Pallas kernels, last_backward(): pl.pallas_call(functools.partial(last_kernel, size, replicas), out_shape=...  64 us
    pallas_call x1, Pallas kernels, first_forward(): pl.pallas_call(functools.partial(first_kernel, size, replicas), out_shape...  58.1 us
    pallas_call x1, Pallas kernels, mlp_forward(): pl.pallas_call(functools.partial(mlp_kernel, size, layer, columns), out_s...  50.6 us
    pallas_call x1, Pallas kernels, qkv_backward(): pl.pallas_call(functools.partial(qkv_back_kernel, size, layer, parts), ou...  31.8 us
  transfers between devices with their start and end apart: 7, of which 0 were waited for; matrix products, arithmetic and copies ran while one was open for 1% of the time, Pallas kernels for 42%

profile of v9, /device:TPU:0, one launch (start us, length us, event | category | flops | bytes accessed | tf_op | source)
XLA Modules:
  0.0 721.0 jit_solution(4080060932220233059)
XLA Ops:
  7.2 0.0 copy-start
  7.2 0.0 copy-start.5
  7.2 0.0 reduce-scatter.5.cloned.1.call-start
  7.3 0.0 copy-start.6
  7.3 1.3 convert_element_type.55
  8.6 0.1 convert_element_type.56
  8.7 0.0 copy-start.9
  8.7 1.1 copy.19.wq_ref
  9.8 0.0 copy-done.5
  9.8 0.9 convert_element_type.59
  10.6 0.0 copy-done.6
  10.6 0.8 convert_element_type.61
  11.5 0.0 copy-done.9
  11.5 0.7 convert_element_type.57
  12.2 0.0 copy-done
  12.2 0.0 copy-start.12
  12.2 0.0 copy-start.13
  12.2 3.0 dynamic-slice_bitcast_fusion
  15.3 0.1 pad.4.clone
  15.3 1.2 select_convert_fusion
  16.6 0.0 copy-done.12
  16.6 0.7 maximum_maximum_fusion.gain_ref
  17.3 58.1 %shard_map.152 = (bf16[4,512,768]{2,1,0:T(8,128)(2,1)}, f32[2,8,1024]{2,1,0:T(8,128)}, bf16[4,512,1024]{2,1,0:T(8,128)(2,1)}, bf16[1024,768]{1,0:T(8,128)(2,1)},...) custom-call(bf16[512,1024]{1,0:T(8,128)(2,1)} %get-tuple-element.140, ...), custom_call_target="tpu_custom_call" | custom-call | flops 30000001024 | bytes 30000000 | tf_op jit(solution)/shard_map/pallas_call | solution.py:777
  75.3 60.3 %shard_map.153 = (f32[512,1024]{1,0:T(8,128)}, bf16[4,512,256]{2,1,0:T(8,128)(2,1)}, f32[4,4,512]{2,1,0:T(4,128)}, bf16[1024,1024]{1,0:T(8,128)(2,1)}, bf16[1024,1024]{1,0:T(8,128)(2,1)}) custom-call(bf16[4,512,768]{2,1,0:T(8,128)(2,1)} %get-tuple-element.68.refs_0_.refs_1_, bf16[4,512,64]{2,1,0:T(8,128)(2,1)} %get-tuple-element.139.refs_1_.refs_2_, ...), custom_call_target="tpu_custom_call" | custom-call | flops 60000002048 | bytes 20000000 | tf_op jit(solution)/shard_map/pallas_call | solution.py:912
  135.6 102.0 %shard_map.154 = (bf16[512,1024]{1,0:T(8,128)(2,1)}, bf16[4,512,768]{2,1,0:T(8,128)(2,1)}, bf16[4,512,1024]{2,1,0:T(8,128)(2,1)}, bf16[4,512,1024]{2,1,0:T(8,128...) custom-call(f32[512,1024]{1,0:T(8,128)} %get-tuple-element.72.refs_0, ...), custom_call_target="tpu_custom_call" | custom-call | flops 49999998976 | bytes 30000000 | tf_op jit(solution)/shard_map/pallas_call | solution.py:1168
  237.7 55.8 %shard_map.155 = (f32[512,1024]{1,0:T(8,128)}, bf16[4,512,256]{2,1,0:T(8,128)(2,1)}, f32[4,4,512]{2,1,0:T(4,128)}, bf16[4,512,1024]{2,1,0:T(8,128)(2,1)}, bf16[1024,1024]{1,0:T(8,128)(2,1)}) custom-call(bf16[4,512,768]{2,1,0:T(8,128)(2,1)} %get-tuple-element.78.refs_0_.refs_1_, bf16[4,512,64]{2,1,0:T(8,128)(2,1)} %get-tuple-element.139.refs_1_.refs_2_, ...), custom_call_target="tpu_custom_call" | custom-call | flops 60000002048 | bytes 20000000 | tf_op jit(solution)/shard_map/pallas_call | solution.py:912
  293.5 50.6 %shard_map.156 = (bf16[512,1024]{1,0:T(8,128)(2,1)}, bf16[4,512,1024]{2,1,0:T(8,128)(2,1)}, bf16[4,512,1024]{2,1,0:T(8,128)(2,1)}, bf16[4,512,1024]{2,1,0:T(8,128)(2,1)}) custom-call(f32[512,1024]{1,0:T(8,128)} %get-tuple-element.82.refs_0_.refs_1_, f32[2,8,1024]{2,1,0:T(8,128)} %get-tuple-element.73.refs_1_.refs_2_.gain_ref, ...), custom_call_target="tpu_custom_call" | custom-call | flops 49999998976 | bytes 30000000 | tf_op jit(solution)/shard_map/pallas_call | solution.py:1022
  344.1 45.8 %shard_map.157 = (f32[512,1024]{1,0:T(8,128)}, f32[1,1024]{1,0:T(1,128)}, bf16[4,256,1024]{2,1,0:T(8,128)(2,1)}, bf16[4,1024,256]{2,1,0:T(8,128)(2,1)}, bf16[2,512,1024]{2,1,0:T(8,128)(2,1)}) custom-call(bf16[512,1024]{1,0:T(8,128)(2,1)} %get-tuple-element.141.refs_5_.refs_0_, f32[512,1024]{1,0:T(8,128)} %get-tuple-element.82.refs_0_.refs_1_, ...), custom_call_target="tpu_custom_call" | custom-call | flops 60000002048 | bytes 40000000 | tf_op jit(solution)/shard_map/pallas_call | solution.py:1332
  389.9 0.0 reduce-scatter.5.cloned.1.call-update
  390.0 0.0 reduce-scatter.7.cloned.1.call-start
  390.0 0.7 reduce-scatter.7.cloned.1.call-update
  390.7 0.0 reduce-scatter.9.cloned.1.call-start
  390.8 71.6 %shard_map.158 = (bf16[4,512,768]{2,1,0:T(8,128)(2,1)}, f32[256,256]{1,0:T(8,128)}) custom-call(f32[512,1024]{1,0:T(8,128)} %get-tuple-element.91.refs_0_.mid_in, bf16[4,512,768]{2,1,0:T(8,128)(2,1)} %get-tuple-element.78.refs_0_.refs_1_, bf16[4,512,64]{2,1,0:T(8,128)(2,1)} %get-tuple-element.139.refs_1_.refs_2_, ...), custom_call_target="tpu_custom_call" | custom-call | flops 89999998976 | bytes 40000000 | tf_op jit(solution)/shard_map/pallas_call | solution.py:1503
  462.4 0.0 copy-start.11
  462.4 31.8 %shard_map.159 = (bf16[512,1024]{1,0:T(8,128)(2,1)}, f32[1,1024]{1,0:T(1,128)}, bf16[4,256,768]{2,1,0:T(8,128)(2,1)}) custom-call(bf16[4,512,768]{2,1,0:T(8,128)(2,1)} %get-tuple-element.94.dqkv_ref, f32[2,8,1024]{2,1,0:T(8,128)} %get-tuple-element.73.refs_1_.refs_2_.gain_ref, bf16[4,512,1024]{2,1,0:T(8,128)(2,1)} %get-tuple-element.95.a1_in, ...), custom_call_target="tpu_custom_call" | custom-call | flops 30000001024 | bytes 30000000 | tf_op jit(solution)/shard_map/pallas_call | solution.py:1586
  494.2 0.0 reduce-scatter.9.cloned.1.call-update
  494.2 0.0 reduce-scatter.11.cloned.1.call-start
  494.3 1.3 pad_maximum_fusion.above_ref
  495.6 53.4 %shard_map.160 = (f32[512,1024]{1,0:T(8,128)}, f32[1,1024]{1,0:T(1,128)}, bf16[4,256,1024]{2,1,0:T(8,128)(2,1)}, bf16[4,1024,256]{2,1,0:T(8,128)(2,1)}) custom-call(bf16[512,1024]{1,0:T(8,128)(2,1)} %get-tuple-element.100.refs_0_.dx1_ref, f32[512,1024]{1,0:T(8,128)} %get-tuple-element.72.refs_0_.refs_1_, ...), custom_call_target="tpu_custom_call" | custom-call | flops 60000002048 | bytes 40000000 | tf_op jit(solution)/shard_map/pallas_call | solution.py:1332
  549.0 0.0 reduce-scatter.9.cloned.1.call-done
  549.0 2.6 collective-permute-start.2
  551.6 0.0 reduce-scatter.11.cloned.1.call-update
  551.6 0.0 copy-done.8
  551.6 0.9 collective-permute-start
  552.5 82.6 %shard_map.161 = (bf16[4,512,768]{2,1,0:T(8,128)(2,1)}, f32[256,256]{1,0:T(8,128)}, f32[1024,256]{1,0:T(8,128)}) custom-call(f32[512,1024]{1,0:T(8,128)} %get-tuple-element.106.refs_0_.mid_ref, bf16[4,512,768]{2,1,0:T(8,128)(2,1)} %get-tuple-element.68.refs_0_.refs_1_, bf16[4,512,64]{2,1,0:T(8,128)(2,1)} %get-tuple-element.139.refs_1_.refs_2_, ...), custom_call_target="tpu_custom_call" | custom-call | flops 89999998976 | bytes 40000000 | tf_op jit(solution)/shard_map/pallas_call | solution.py:1503
  635.1 0.0 copy-start.4
  635.1 0.0 copy-done.10
  635.1 1.7 broadcast_select_fusion.1
  636.9 0.0 collective-permute-done.2
  636.9 2.3 select_bitcast_fusion
  639.2 0.9 broadcast_select_fusion
  640.1 0.0 collective-permute-start.1
  640.1 64.0 %shard_map.162 = (f32[8,1024]{1,0:T(8,128)}, f32[256,768]{1,0:T(8,128)}, bf16[2,512,1024]{2,1,0:T(8,128)(2,1)}) custom-call(bf16[4,512,768]{2,1,0:T(8,128)(2,1)} %get-tuple-element.112.dqkv_ref, bf16[4,512,1024]{2,1,0:T(8,128)(2,1)} %get-tuple-element.113.a1_ref, bf16[512,1024]{1,0:T(8,128)(2,1)} %get-tuple-element.140.x_ref.refs_3_, ...), custom_call_target="tpu_custom_call" | custom-call | flops 40000000000 | bytes 30000000 | tf_op jit(solution)/shard_map/pallas_call | solution.py:1763
  704.1 0.0 collective-permute-done
  704.1 1.2 add_select_fusion
  705.4 0.0 copy-start.2
  705.4 1.1 copy.20
  706.5 1.4 constant_dynamic-slice_fusion.1
  708.0 0.0 collective-permute-done.1
  708.0 2.4 add_bitcast_fusion
  710.4 0.0 copy-done.2
  710.4 1.3 copy.23
  711.7 1.0 copy-done.3
  712.8 1.3 copy.24
  (17 shorter events, 0.1 us)
Async XLA Ops:
  7.2 5.0 copy-start
  7.2 2.6 copy-start.5
  7.2 488.4 %reduce-scatter.5.cloned.1.call-start = ((), (), s32[]{:S(2)}) async-start(), calls=%async_computation.4 | async-start | bytes 2621440 | tf_op jit(solution)/shard_map/reduce_scatter | solution.py:1859
  7.3 3.4 copy-start.6
  8.7 2.8 copy-start.9
  12.2 4.4 copy-start.12
  12.2 4.4 copy-start.13
  390.0 105.6 %reduce-scatter.7.cloned.1.call-start = ((), (), s32[]{:S(2)}) async-start(), calls=%async_computation.5 | async-start | bytes 2621440 | tf_op jit(solution)/shard_map/reduce_scatter | solution.py:1859
  390.7 158.3 %reduce-scatter.9.cloned.1.call-start = ((), (), s32[]{:S(2)}) async-start(), calls=%async_computation.6 | async-start | bytes 1966080 | tf_op jit(solution)/shard_map/reduce_scatter | solution.py:1859
  462.4 31.9 %copy-start.11 = (f32[1,1024]{1,0:T(1,128)S(1)}, f32[1,1024]{1,0:T(1,128)}, u32[]{:S(2)}) copy-start(f32[1,1024]{1,0:T(1,128)} %get-tuple-element.117) | copy-start | bytes 12292
  494.2 145.0 %reduce-scatter.11.cloned.1.call-start = ((), (), s32[]{:S(2)}) async-start(), calls=%async_computation.7 | async-start | bytes 2621440 | tf_op jit(solution)/shard_map/reduce_scatter | solution.py:1859
  495.6 53.5 %copy-start.7 = (bf16[1,1024,256]{2,1,0:T(8,128)(2,1)S(1)}, bf16[1,1024,256]{2,1,0:T(8,128)(2,1)}, u32[]{:S(2)}) copy-start(bf16[1,1024,256]{2,1,0:T(8,128)(2,1)} %reduce-scatter.7.cloned.1.call-done) | copy-start | bytes 1572868
  549.0 2.6 copy-start.8
  549.0 87.8 %collective-permute-start.2 = (bf16[1024,256]{1,0:T(8,128)(2,1)S(1)}, bf16[1024,256]{1,0:T(8,128)(2,1)S(1)}, u32[]{:S(2)}, u32[]{:S(2)}) collective-permute-start(bf16[1024,256]{1,0:T(8,128)(2,1)S(1)} %bitcast.32), channel_id=1, source_target_pairs={{0,16},{16,0},{1,17},{17,1},{2,18},{18,2},{3,19},{19,3},{4,20},{20... | collective-permute-start | bytes 1572872 | tf_op jit(solution)/shard_map/ppermute | solution.py:1803
  551.6 152.5 %collective-permute-start = (bf16[256,768]{1,0:T(8,128)(2,1)S(1)}, bf16[256,768]{1,0:T(8,128)(2,1)S(1)}, u32[]{:S(2)}, u32[]{:S(2)}) collective-permute-start(bf16[256,768]{1,0:T(8,128)(2,1)S(1)} %bitcast.34), channel_id=1, source_target_pairs={{0,16},{16,0},{1,17},{17,1},{2,18},{18,2},{3,19},{19,3},{4,20},{20... | collective-permute-start | bytes 1179656 | tf_op jit(solution)/shard_map/ppermute | solution.py:1803
  552.5 82.6 %copy-start.10 = (f32[256,256]{1,0:T(8,128)S(1)}, f32[256,256]{1,0:T(8,128)}, u32[]{:S(2)}) copy-start(f32[256,256]{1,0:T(8,128)} %get-tuple-element.123) | copy-start | bytes 786436
  635.1 4.1 copy-start.4
  640.1 67.9 %collective-permute-start.1 = (bf16[256,1024]{1,0:T(8,128)(2,1)}, bf16[256,1024]{1,0:T(8,128)(2,1)}, u32[]{:S(2)}, u32[]{:S(2)}) collective-permute-start(bf16[256,1024]{1,0:T(8,128)(2,1)} %broadcast_select_fusion), channel_id=1, source_target_pairs={{0,16},{16,0},{1,17},{17,1},{2,18},{18,2},{3,19},{19,3},{4,20},{20... | collective-permute-start | bytes 1572872 | tf_op jit(solution)/shard_map/ppermute | solution.py:1803
  705.4 5.0 copy-start.2
  710.4 2.3 copy-start.3
  710.4 3.7 copy-start.1
Sparse Core Ops, SparseCore 0:
  390.1 48.8 reduce-scatter.4
  441.4 45.2 reduce-scatter.6
  494.3 36.2 reduce-scatter.8
  551.7 50.5 reduce-scatter.10

commit v10 on v9

--- a/solution.py
+++ b/solution.py
@@ -946,7 +946,7 @@
     rows, width = h1_ref.shape
     hidden = wu_ref.shape[1]
     fb = min(256, hidden)
-    n = thin_chunks(rows)
+    n = chunks(rows)
     rc = rows // n
     g = Group(size)
     copies = [
@@ -1017,7 +1017,7 @@
 def mlp_forward(size, replicas, layer, h1, gains, wu, wd, riders):
     rows, width = h1.shape
     hidden = wu.shape[1]
-    n = thin_chunks(rows)
+    n = chunks(rows)
     halves, columns, outs, sems = riding(riders, replicas)
     return pl.pallas_call(
         functools.partial(mlp_kernel, size, layer, columns),
@@ -1058,8 +1058,8 @@
     scratch, refs = refs[:9], refs[9:]
     spread = Spread(q_stage.at[1], wq, False, refs[:5])
     riders = Riders(halves, wholes, columns, refs[5:])
-    riders.all.insert(0, spread)
-    riders.replicas = spread.replicas
+    out_rider, up_rider, down_rider = riders.all
+    stages = len(spread.stages)
     rows, width = h1_ref.shape
     hidden = wu_ref.shape[1]
     fb = min(256, hidden)
@@ -1072,7 +1072,7 @@
     ]
     for copy in copies:
         copy.start()
-    g.greet(riders.replicas)
+    g.greet(spread.replicas)
     gather = Gather(g, a2, rc, gather_sems)
     onward = Gather(g, a1, rc, next_sems)
     scatter = Scatter(g, rc, scratch)
@@ -1084,7 +1084,8 @@
         gather.start(j)
 
     run(n, send)
-    riders.start()
+    spread.start()
+    out_rider.start()
     for copy in copies:
         copy.wait()
 
@@ -1124,7 +1125,19 @@
         def _():
             pass_on(j - lag)
 
-        riders.step(j, n)
+        @pl.when(j == 3 * n // 8)
+        def _():
+            spread.step(0)
+            out_rider.step(0)
+            up_rider.start()
+
+        @pl.when(j == n - 1)
+        def _():
+            for i in range(1, stages):
+                spread.step(i)
+                out_rider.step(i)
+            up_rider.step(0)
+            down_rider.start()
 
     run(n, work)
     outs = [
@@ -1137,7 +1150,6 @@
     for j in range(n - lag, n):
         pass_on(j)
     spread.finish()
-    riders.all.pop(0)
     outs.append(pltpu.make_async_copy(wq, wq_out, out_sem.at[3]))
     outs[3].start()
 
@@ -1151,6 +1163,8 @@
     run(n, multiply)
     outs.append(pltpu.make_async_copy(a1, a1_out, out_sem.at[4]))
     outs[4].start()
+    for i in range(1, stages):
+        up_rider.step(i)
     riders.finish()
     gather.drain(n)
     onward.drain(n)
@@ -1214,7 +1228,7 @@
     hidden = wu_ref.shape[1]
     depth = width // parts
     fb = min(256, hidden)
-    n = thin_chunks(rows)
+    n = chunks(rows)
     rc = rows // n
     g = Group(size)
     copies = [
@@ -1226,7 +1240,7 @@
         pltpu.make_async_copy(hid_ref, hid, w_sem.at[3]),
         pltpu.make_async_copy(a2_ref, a2, w_sem.at[4]),
     ]
-    for copy in copies + late:
+    for copy in copies:
         copy.start()
     g.greet(side=layer == 1)
     section = lax.axis_index("section")
@@ -1267,6 +1281,8 @@
         run(n, send)
     for copy in copies:
         copy.wait()
+    for copy in late:
+        copy.start()
     if layer == 1:
         y_load(ys[0]).wait()
         y_copies(ys[0], ys[1], section)[0].start()
@@ -1328,7 +1344,7 @@
     rows, width = h1.shape
     hidden = wu.shape[1]
     parts, depth = replicas, width // replicas
-    n = thin_chunks(rows)
+    n = chunks(rows)
     return pl.pallas_call(
         functools.partial(mlp_back_kernel, size, layer, parts),
         out_shape=[
@@ -1606,9 +1622,9 @@
 
 
 def last_kernel(
-    size, parts, dqkv_ref, a1_ref, x_ref, mid_ref, gain_ref, w_ref, two_ref, above_ref, dx1_ref,
+    size, parts, dqkv_ref, a1_in, x_in, mid_in, gain_ref, w_ref, two_ref, above_ref, dx1_in,
     gain_out, gqkv_out, dx_out,
-    gqkv, swap_sem, w, dx, gsum, gcame, w_sem, x_sem, x_send, x_recv, g_send, g_recv, *scratch
+    a1_ref, x_ref, mid_ref, dx1_ref, in_sem, gqkv, swap_sem, w, dx, gsum, gcame, w_sem, x_sem, x_send, x_recv, g_send, g_recv, *scratch
 ):
     rows, width = x_ref.shape
     depth = width // parts
@@ -1619,6 +1635,14 @@
     d = lax.axis_index("dp")
     copy = pltpu.make_async_copy(w_ref, w, w_sem.at[0])
     copy.start()
+    late = [
+        pltpu.make_async_copy(a1_in, a1_ref, in_sem.at[0]),
+        pltpu.make_async_copy(mid_in, mid_ref, in_sem.at[1]),
+        pltpu.make_async_copy(x_in, x_ref, in_sem.at[2]),
+        pltpu.make_async_copy(dx1_in, dx1_ref, in_sem.at[3]),
+    ]
+    for one in late:
+        one.start()
     reduce = HalfReduce(0, scratch[:HALF])
     swap = HalfSwap(gqkv, reduce.other, swap_sem)
     scatter = Scatter(g, rc, scratch[HALF:])
@@ -1645,15 +1669,6 @@
     def qkv_grad(z):
         cols = pl.ds(pl.multiple_of(z * depth, depth), depth)
         gqkv[z] = dg(flat(a1_ref[:, :, cols]), flat(dqkv_ref[...]), TN).astype(BF)
-
-    run(parts, qkv_grad)
-    swap.copy().start()
-    load = reduce.loads(gqkv, None)[0]
-    load.start()
-
-    @pl.when(section == 1)
-    def _():
-        keep_upper().start()
 
     copy.wait()
 
@@ -1667,6 +1682,17 @@
         scatter.second(j)
 
     run(n, work)
+    for one in late:
+        one.wait()
+    run(parts, qkv_grad)
+    swap.copy().start()
+    load = reduce.loads(gqkv, None)[0]
+    load.start()
+
+    @pl.when(section == 1)
+    def _():
+        keep_upper().start()
+
     gsum[0] = jnp.zeros_like(gsum[0])
 
     def last(j):
@@ -1767,9 +1793,14 @@
             shape((depth, wide), F32),
             shape((2, rows, width), BF),
         ),
-        in_specs=[VM] * 5 + [HB, VM, VM, VM],
+        in_specs=[VM, HB, HB, HB, VM, HB, VM, VM, HB],
         out_specs=(VM, VM, HB),
         scratch_shapes=[
+            pltpu.VMEM((size, rows, width), BF),
+            pltpu.VMEM((rows, width), BF),
+            pltpu.VMEM((rows, width), F32),
+            pltpu.VMEM((rows, width), BF),
+            DMA((4,)),
             pltpu.VMEM((replicas, depth, wide), BF),
             DMA((2,)),
             pltpu.VMEM((width, wide), BF),

time: 730 us -> 743 us (1.018)
  Pallas kernels: 676 us -> 689 us
    pallas_call x1, Pallas kernels: 64 us -> 76.4 us  [last_backward(): pl.pallas_call(functools.partial(last_kernel, size, replicas), out_shape=...]
    pallas_call x2, Pallas kernels: 99.3 us -> 91.3 us  [mlp_backward(): pl.pallas_call(functools.partial(mlp_back_kernel, size, layer, parts), ou...]
  transfers between devices with their start and end apart: 7 -> 7, of which waited for: 0 -> 0; matrix products, arithmetic and copies ran while one was open for 1% -> 1% of each run, Pallas kernels for 42% -> 43%
where the time goes in v10:
time: 743 us; the launch traced here: 734 us
  Pallas kernels  689 us (93%)
  other arithmetic  15.5 us (2%)
  between operations  14.5 us (2%)
  local copies, waits for them, and re-layouts  10.6 us (1%)
    pallas_call x2, Pallas kernels, attend_backward(): pl.pallas_call(functools.partial(attend_back_kernel, size, layer, parts),...  156 us
    pallas_call x2, Pallas kernels, attend(): pl.pallas_call(functools.partial(attend_kernel, size, layer, columns), ou...  117 us
    pallas_call x1, Pallas kernels, turn_forward(): pl.pallas_call(functools.partial(turn_kernel, size, columns), out_shape=[...  108 us
    pallas_call x2, Pallas kernels, mlp_backward(): pl.pallas_call(functools.partial(mlp_back_kernel, size, layer, parts), ou...  91.3 us
    pallas_call x1, Pallas kernels, last_backward(): pl.pallas_call(functools.partial(last_kernel, size, replicas), out_shape=...  76.4 us
    pallas_call x1, Pallas kernels, first_forward(): pl.pallas_call(functools.partial(first_kernel, size, replicas), out_shape...  58.1 us
    pallas_call x1, Pallas kernels, mlp_forward(): pl.pallas_call(functools.partial(mlp_kernel, size, layer, columns), out_s...  51.3 us
    pallas_call x1, Pallas kernels, qkv_backward(): pl.pallas_call(functools.partial(qkv_back_kernel, size, layer, parts), ou...  31.6 us
  transfers between devices with their start and end apart: 7, of which 0 were waited for; matrix products, arithmetic and copies ran while one was open for 1% of the time, Pallas kernels for 43%

profile of v10, /device:TPU:0, one launch (start us, length us, event | category | flops | bytes accessed | tf_op | source)
XLA Modules:
  0.0 733.7 jit_solution(12300154103899683184)
XLA Ops:
  7.2 0.0 copy-start
  7.2 0.0 copy-start.5
  7.2 0.0 reduce-scatter.5.cloned.1.call-start
  7.3 0.0 copy-start.6
  7.3 1.3 convert_element_type.55
  8.6 0.1 convert_element_type.56
  8.7 0.0 copy-start.9
  8.7 1.1 copy.19.wq_ref
  9.8 0.0 copy-done.5
  9.8 0.9 convert_element_type.59
  10.6 0.0 copy-done.6
  10.6 0.8 convert_element_type.61
  11.5 0.0 copy-done.9
  11.5 0.7 convert_element_type.57
  12.2 0.0 copy-done
  12.2 0.0 copy-start.12
  12.2 0.0 copy-start.13
  12.2 3.0 dynamic-slice_bitcast_fusion
  15.3 0.1 pad.4.clone
  15.3 1.2 select_convert_fusion
  16.6 0.0 copy-done.12
  16.6 0.0 copy-done.13
  16.6 0.7 maximum_maximum_fusion.gain_ref
  17.3 58.1 %shard_map.152 = (bf16[4,512,768]{2,1,0:T(8,128)(2,1)}, f32[2,8,1024]{2,1,0:T(8,128)}, bf16[4,512,1024]{2,1,0:T(8,128)(2,1)}, bf16[1024,768]{1,0:T(8,128)(2,1)},...) custom-call(bf16[512,1024]{1,0:T(8,128)(2,1)} %get-tuple-element.140, ...), custom_call_target="tpu_custom_call" | custom-call | flops 30000001024 | bytes 30000000 | tf_op jit(solution)/shard_map/pallas_call | solution.py:777
  75.3 60.3 %shard_map.153 = (f32[512,1024]{1,0:T(8,128)}, bf16[4,512,256]{2,1,0:T(8,128)(2,1)}, f32[4,4,512]{2,1,0:T(4,128)}, bf16[1024,1024]{1,0:T(8,128)(2,1)}, bf16[1024,1024]{1,0:T(8,128)(2,1)}) custom-call(bf16[4,512,768]{2,1,0:T(8,128)(2,1)} %get-tuple-element.68.refs_0_.refs_1_, bf16[4,512,64]{2,1,0:T(8,128)(2,1)} %get-tuple-element.139.refs_1_.refs_2_, ...), custom_call_target="tpu_custom_call" | custom-call | flops 60000002048 | bytes 20000000 | tf_op jit(solution)/shard_map/pallas_call | solution.py:912
  135.6 107.7 %shard_map.154 = (bf16[512,1024]{1,0:T(8,128)(2,1)}, bf16[4,512,768]{2,1,0:T(8,128)(2,1)}, bf16[4,512,1024]{2,1,0:T(8,128)(2,1)}, bf16[4,512,1024]{2,1,0:T(8,128...) custom-call(f32[512,1024]{1,0:T(8,128)} %get-tuple-element.72.refs_0, ...), custom_call_target="tpu_custom_call" | custom-call | flops 49999998976 | bytes 30000000 | tf_op jit(solution)/shard_map/pallas_call | solution.py:1182
  243.4 56.4 %shard_map.155 = (f32[512,1024]{1,0:T(8,128)}, bf16[4,512,256]{2,1,0:T(8,128)(2,1)}, f32[4,4,512]{2,1,0:T(4,128)}, bf16[4,512,1024]{2,1,0:T(8,128)(2,1)}, bf16[1024,1024]{1,0:T(8,128)(2,1)}) custom-call(bf16[4,512,768]{2,1,0:T(8,128)(2,1)} %get-tuple-element.78.refs_0_.refs_1_, bf16[4,512,64]{2,1,0:T(8,128)(2,1)} %get-tuple-element.139.refs_1_.refs_2_, ...), custom_call_target="tpu_custom_call" | custom-call | flops 60000002048 | bytes 20000000 | tf_op jit(solution)/shard_map/pallas_call | solution.py:912
  299.8 51.3 %shard_map.156 = (bf16[512,1024]{1,0:T(8,128)(2,1)}, bf16[4,512,1024]{2,1,0:T(8,128)(2,1)}, bf16[4,512,1024]{2,1,0:T(8,128)(2,1)}, bf16[4,512,1024]{2,1,0:T(8,128)(2,1)}) custom-call(f32[512,1024]{1,0:T(8,128)} %get-tuple-element.82.refs_0_.refs_1_, f32[2,8,1024]{2,1,0:T(8,128)} %get-tuple-element.73.refs_1_.refs_2_.gain_ref, ...), custom_call_target="tpu_custom_call" | custom-call | flops 49999998976 | bytes 30000000 | tf_op jit(solution)/shard_map/pallas_call | solution.py:1022
  351.1 38.1 %shard_map.157 = (f32[512,1024]{1,0:T(8,128)}, f32[1,1024]{1,0:T(1,128)}, bf16[4,256,1024]{2,1,0:T(8,128)(2,1)}, bf16[4,1024,256]{2,1,0:T(8,128)(2,1)}, bf16[2,512,1024]{2,1,0:T(8,128)(2,1)}) custom-call(bf16[512,1024]{1,0:T(8,128)(2,1)} %get-tuple-element.141.refs_5_.refs_0_, f32[512,1024]{1,0:T(8,128)} %get-tuple-element.82.refs_0_.refs_1_, ...), custom_call_target="tpu_custom_call" | custom-call | flops 60000002048 | bytes 40000000 | tf_op jit(solution)/shard_map/pallas_call | solution.py:1348
  389.1 0.0 reduce-scatter.5.cloned.1.call-update
  389.2 0.0 reduce-scatter.7.cloned.1.call-start
  389.2 0.7 reduce-scatter.7.cloned.1.call-update
  389.9 0.0 reduce-scatter.9.cloned.1.call-start
  390.0 74.1 %shard_map.158 = (bf16[4,512,768]{2,1,0:T(8,128)(2,1)}, f32[256,256]{1,0:T(8,128)}) custom-call(f32[512,1024]{1,0:T(8,128)} %get-tuple-element.91.refs_0_.mid_in, bf16[4,512,768]{2,1,0:T(8,128)(2,1)} %get-tuple-element.78.refs_0_.refs_1_, bf16[4,512,64]{2,1,0:T(8,128)(2,1)} %get-tuple-element.139.refs_1_.refs_2_, ...), custom_call_target="tpu_custom_call" | custom-call | flops 89999998976 | bytes 40000000 | tf_op jit(solution)/shard_map/pallas_call | solution.py:1519
  464.0 0.0 copy-start.11
  464.0 31.6 %shard_map.159 = (bf16[512,1024]{1,0:T(8,128)(2,1)}, f32[1,1024]{1,0:T(1,128)}, bf16[4,256,768]{2,1,0:T(8,128)(2,1)}) custom-call(bf16[4,512,768]{2,1,0:T(8,128)(2,1)} %get-tuple-element.94.dqkv_ref, f32[2,8,1024]{2,1,0:T(8,128)} %get-tuple-element.73.refs_1_.refs_2_.gain_ref, bf16[4,512,1024]{2,1,0:T(8,128)(2,1)} %get-tuple-element.95.a1_in, ...), custom_call_target="tpu_custom_call" | custom-call | flops 30000001024 | bytes 30000000 | tf_op jit(solution)/shard_map/pallas_call | solution.py:1602
  495.6 0.0 reduce-scatter.9.cloned.1.call-update
  495.7 0.0 reduce-scatter.11.cloned.1.call-start
  495.7 0.0 copy-done.11
  495.7 1.3 pad_maximum_fusion.above_ref
  497.0 53.2 %shard_map.160 = (f32[512,1024]{1,0:T(8,128)}, f32[1,1024]{1,0:T(1,128)}, bf16[4,256,1024]{2,1,0:T(8,128)(2,1)}, bf16[4,1024,256]{2,1,0:T(8,128)(2,1)}) custom-call(bf16[512,1024]{1,0:T(8,128)(2,1)} %get-tuple-element.100.refs_0_.dx1_in, f32[512,1024]{1,0:T(8,128)} %get-tuple-element.72.refs_0_.refs_1_, ...), custom_call_target="tpu_custom_call" | custom-call | flops 60000002048 | bytes 40000000 | tf_op jit(solution)/shard_map/pallas_call | solution.py:1348
  550.3 0.0 reduce-scatter.9.cloned.1.call-done
  550.3 0.0 copy-start.8
  550.3 2.5 collective-permute-start.2
  552.9 0.0 reduce-scatter.11.cloned.1.call-update
  552.9 0.9 collective-permute-start
  553.8 81.7 %shard_map.161 = (bf16[4,512,768]{2,1,0:T(8,128)(2,1)}, f32[256,256]{1,0:T(8,128)}, f32[1024,256]{1,0:T(8,128)}) custom-call(f32[512,1024]{1,0:T(8,128)} %get-tuple-element.106.refs_0_.mid_in, bf16[4,512,768]{2,1,0:T(8,128)(2,1)} %get-tuple-element.68.refs_0_.refs_1_, bf16[4,512,64]{2,1,0:T(8,128)(2,1)} %get-tuple-element.139.refs_1_.refs_2_, ...), custom_call_target="tpu_custom_call" | custom-call | flops 89999998976 | bytes 40000000 | tf_op jit(solution)/shard_map/pallas_call | solution.py:1519
  635.5 1.7 broadcast_select_fusion.1
  637.2 0.0 collective-permute-done.2
  637.2 2.3 select_bitcast_fusion
  639.5 0.0 copy-done.4
  639.5 0.9 broadcast_select_fusion
  640.4 0.0 collective-permute-start.1
  640.4 76.4 %shard_map.162 = (f32[8,1024]{1,0:T(8,128)}, f32[256,768]{1,0:T(8,128)}, bf16[2,512,1024]{2,1,0:T(8,128)(2,1)}) custom-call(bf16[4,512,768]{2,1,0:T(8,128)(2,1)} %get-tuple-element.112.dqkv_ref, bf16[4,512,1024]{2,1,0:T(8,128)(2,1)} %get-tuple-element.113.a1_in, bf16[512,1024]{1,0:T(8,128)(2,1)} %get-tuple-element.140.x_ref.refs_3_.x_in, ...), custom_call_target="tpu_custom_call" | custom-call | flops 40000000000 | bytes 30000000 | tf_op jit(solution)/shard_map/pallas_call | solution.py:1789
  716.8 0.0 collective-permute-done
  716.8 1.2 add_select_fusion
  718.0 1.1 copy.20
  719.2 1.4 constant_dynamic-slice_fusion.1
  720.6 0.0 collective-permute-done.1
  720.6 2.4 add_bitcast_fusion
  723.1 0.0 copy-done.2
  723.1 1.3 copy.23
  724.4 1.0 copy-done.3
  725.4 1.3 copy.24
  (17 shorter events, 0.1 us)
Async XLA Ops:
  7.2 5.0 copy-start
  7.2 2.6 copy-start.5
  7.2 489.8 %reduce-scatter.5.cloned.1.call-start = ((), (), s32[]{:S(2)}) async-start(), calls=%async_computation.4 | async-start | bytes 2621440 | tf_op jit(solution)/shard_map/reduce_scatter | solution.py:1890
  7.3 3.4 copy-start.6
  8.7 2.8 copy-start.9
  12.2 4.4 copy-start.12
  12.2 4.4 copy-start.13
  389.2 107.8 %reduce-scatter.7.cloned.1.call-start = ((), (), s32[]{:S(2)}) async-start(), calls=%async_computation.5 | async-start | bytes 2621440 | tf_op jit(solution)/shard_map/reduce_scatter | solution.py:1890
  389.9 160.4 %reduce-scatter.9.cloned.1.call-start = ((), (), s32[]{:S(2)}) async-start(), calls=%async_computation.6 | async-start | bytes 1966080 | tf_op jit(solution)/shard_map/reduce_scatter | solution.py:1890
  464.0 31.7 %copy-start.11 = (f32[1,1024]{1,0:T(1,128)S(1)}, f32[1,1024]{1,0:T(1,128)}, u32[]{:S(2)}) copy-start(f32[1,1024]{1,0:T(1,128)} %get-tuple-element.117) | copy-start | bytes 12292
  495.7 143.9 %reduce-scatter.11.cloned.1.call-start = ((), (), s32[]{:S(2)}) async-start(), calls=%async_computation.7 | async-start | bytes 2621440 | tf_op jit(solution)/shard_map/reduce_scatter | solution.py:1890
  497.0 53.3 %copy-start.7 = (bf16[1,1024,256]{2,1,0:T(8,128)(2,1)S(1)}, bf16[1,1024,256]{2,1,0:T(8,128)(2,1)}, u32[]{:S(2)}) copy-start(bf16[1,1024,256]{2,1,0:T(8,128)(2,1)} %reduce-scatter.7.cloned.1.call-done) | copy-start | bytes 1572868
  550.3 2.6 copy-start.8
  550.3 86.9 %collective-permute-start.2 = (bf16[1024,256]{1,0:T(8,128)(2,1)S(1)}, bf16[1024,256]{1,0:T(8,128)(2,1)S(1)}, u32[]{:S(2)}, u32[]{:S(2)}) collective-permute-start(bf16[1024,256]{1,0:T(8,128)(2,1)S(1)} %bitcast.32), channel_id=1, source_target_pairs={{0,16},{16,0},{1,17},{17,1},{2,18},{18,2},{3,19},{19,3},{4,20},{20... | collective-permute-start | bytes 1572872 | tf_op jit(solution)/shard_map/ppermute | solution.py:1834
  552.9 163.9 %collective-permute-start = (bf16[256,768]{1,0:T(8,128)(2,1)S(1)}, bf16[256,768]{1,0:T(8,128)(2,1)S(1)}, u32[]{:S(2)}, u32[]{:S(2)}) collective-permute-start(bf16[256,768]{1,0:T(8,128)(2,1)S(1)} %bitcast.34), channel_id=1, source_target_pairs={{0,16},{16,0},{1,17},{17,1},{2,18},{18,2},{3,19},{19,3},{4,20},{20... | collective-permute-start | bytes 1179656 | tf_op jit(solution)/shard_map/ppermute | solution.py:1834
  553.8 81.7 %copy-start.10 = (f32[256,256]{1,0:T(8,128)S(1)}, f32[256,256]{1,0:T(8,128)}, u32[]{:S(2)}) copy-start(f32[256,256]{1,0:T(8,128)} %get-tuple-element.123) | copy-start | bytes 786436
  635.4 4.1 copy-start.4
  640.4 80.2 %collective-permute-start.1 = (bf16[256,1024]{1,0:T(8,128)(2,1)}, bf16[256,1024]{1,0:T(8,128)(2,1)}, u32[]{:S(2)}, u32[]{:S(2)}) collective-permute-start(bf16[256,1024]{1,0:T(8,128)(2,1)} %broadcast_select_fusion), channel_id=1, source_target_pairs={{0,16},{16,0},{1,17},{17,1},{2,18},{18,2},{3,19},{19,3},{4,20},{20... | collective-permute-start | bytes 1572872 | tf_op jit(solution)/shard_map/ppermute | solution.py:1834
  718.0 5.0 copy-start.2
  723.1 2.3 copy-start.3
  723.1 3.7 copy-start.1
Sparse Core Ops, SparseCore 0:
  389.3 50.4 reduce-scatter.4
  442.2 45.0 reduce-scatter.6
  495.8 36.0 reduce-scatter.8
  553.0 49.3 reduce-scatter.10

commit v11 on v9

--- a/solution.py
+++ b/solution.py
@@ -874,12 +874,17 @@
             total = acc[e : e + 1]
             found.append((acc[:e] * (1.0 / total)).astype(BF))
             lse_ref[j, h : h + 1, :] = top + jnp.log2(total)
+            if h == heads // 2:
+
+                @pl.when(j > 0)
+                def _():
+                    scatter.second(j - 1)
+
         ctx = (jnp.concatenate(found, axis=0) if heads > 1 else found[0]).T
         ctx_ref[:, at, :] = ctx.reshape(size, rc, heads * e)
         width = x_ref.shape[1]
         scatter.part[:, at, :] = dg(ctx, w[...], NN).reshape(size, rc, width)
         scatter.first(j)
-        scatter.second(j)
         riders.step(j, n)
         if layer == 1:
 
@@ -888,6 +893,7 @@
                 cot.relay(0)
 
     run(n, work)
+    scatter.second(n - 1)
 
     def last(j):
         at = span(j, rc)
@@ -946,7 +952,7 @@
     rows, width = h1_ref.shape
     hidden = wu_ref.shape[1]
     fb = min(256, hidden)
-    n = thin_chunks(rows)
+    n = chunks(rows)
     rc = rows // n
     g = Group(size)
     copies = [
@@ -970,9 +976,10 @@
     for copy in copies:
         copy.wait()
 
+    gather.relay(0)
+
     def work(j):
         at = span(j, rc)
-        gather.relay(j)
         gather.ready(j)
         a = flat(a2[:, at, :])
         for f in range(hidden // fb):
@@ -985,15 +992,24 @@
                 .reshape(size, rc, fb)
             )
             hid[:, at, cols] = (u * half).astype(BF).reshape(size, rc, fb)
+
+        @pl.when(j + 1 < n)
+        def _():
+            gather.relay(j + 1)
+
+        @pl.when(j > 0)
+        def _():
+            scatter.second(j - 1)
+
         held = flat(hid[:, at, :])
         for f in range(width // 256):
             cols = slice(f * 256, (f + 1) * 256)
             scatter.part[:, at, cols] = dg(held, wd[:, cols], NN).reshape(size, rc, 256)
         scatter.first(j)
-        scatter.second(j)
         riders.step(j, n)
 
     run(n, work)
+    scatter.second(n - 1)
     outs = [
         pltpu.make_async_copy(a2, a2_out, out_sem.at[0]),
         pltpu.make_async_copy(hid, hid_out, out_sem.at[1]),
@@ -1017,7 +1033,7 @@
 def mlp_forward(size, replicas, layer, h1, gains, wu, wd, riders):
     rows, width = h1.shape
     hidden = wu.shape[1]
-    n = thin_chunks(rows)
+    n = chunks(rows)
     halves, columns, outs, sems = riding(riders, replicas)
     return pl.pallas_call(
         functools.partial(mlp_kernel, size, layer, columns),
@@ -1058,12 +1074,12 @@
     scratch, refs = refs[:9], refs[9:]
     spread = Spread(q_stage.at[1], wq, False, refs[:5])
     riders = Riders(halves, wholes, columns, refs[5:])
-    riders.all.insert(0, spread)
-    riders.replicas = spread.replicas
+    out_rider, up_rider, down_rider = riders.all
+    stages = len(spread.stages)
     rows, width = h1_ref.shape
     hidden = wu_ref.shape[1]
     fb = min(256, hidden)
-    n = thin_chunks(rows)
+    n = chunks(rows)
     rc = rows // n
     g = Group(size)
     copies = [
@@ -1072,7 +1088,7 @@
     ]
     for copy in copies:
         copy.start()
-    g.greet(riders.replicas)
+    g.greet(spread.replicas)
     gather = Gather(g, a2, rc, gather_sems)
     onward = Gather(g, a1, rc, next_sems)
     scatter = Scatter(g, rc, scratch)
@@ -1084,7 +1100,8 @@
         gather.start(j)
 
     run(n, send)
-    riders.start()
+    spread.start()
+    out_rider.start()
     for copy in copies:
         copy.wait()
 
@@ -1097,10 +1114,10 @@
         onward.start(j)
 
     lag = min(2, n)
+    gather.relay(0)
 
     def work(j):
         at = span(j, rc)
-        gather.relay(j)
         gather.ready(j)
         a = flat(a2[:, at, :])
         for f in range(hidden // fb):
@@ -1113,20 +1130,39 @@
                 .reshape(size, rc, fb)
             )
             hid[:, at, cols] = (u * half).astype(BF).reshape(size, rc, fb)
+
+        @pl.when(j + 1 < n)
+        def _():
+            gather.relay(j + 1)
+
+        @pl.when(j > 0)
+        def _():
+            scatter.second(j - 1)
+
         held = flat(hid[:, at, :])
         for f in range(width // 256):
             cols = slice(f * 256, (f + 1) * 256)
             scatter.part[:, at, cols] = dg(held, wd[:, cols], NN).reshape(size, rc, 256)
         scatter.first(j)
-        scatter.second(j)
 
         @pl.when(j >= lag)
         def _():
             pass_on(j - lag)
 
-        riders.step(j, n)
+        @pl.when(j == n // 2)
+        def _():
+            spread.step(0)
+            out_rider.step(0)
+            up_rider.start()
+
+        @pl.when(j == n - 1)
+        def _():
+            for i in range(1, stages):
+                spread.step(i)
+                out_rider.step(i)
 
     run(n, work)
+    scatter.second(n - 1)
     outs = [
         pltpu.make_async_copy(a2, a2_out, out_sem.at[0]),
         pltpu.make_async_copy(hid, hid_out, out_sem.at[1]),
@@ -1136,14 +1172,21 @@
         out.start()
     for j in range(n - lag, n):
         pass_on(j)
+    up_rider.step(0)
+    down_rider.start()
     spread.finish()
-    riders.all.pop(0)
     outs.append(pltpu.make_async_copy(wq, wq_out, out_sem.at[3]))
     outs[3].start()
 
+    onward.relay(0)
+
     def multiply(j):
         at = span(j, rc)
-        onward.relay(j)
+
+        @pl.when(j + 1 < n)
+        def _():
+            onward.relay(j + 1)
+
         onward.ready(j)
         r = dg(flat(a1[:, at, :]), wq[...], NN).astype(BF)
         qkv_ref[:, at, :] = r.reshape(size, rc, r.shape[1])
@@ -1151,6 +1194,8 @@
     run(n, multiply)
     outs.append(pltpu.make_async_copy(a1, a1_out, out_sem.at[4]))
     outs[4].start()
+    for i in range(1, stages):
+        up_rider.step(i)
     riders.finish()
     gather.drain(n)
     onward.drain(n)
@@ -1163,7 +1208,7 @@
     rows, width = h1.shape
     hidden = wu.shape[1]
     wide = stage.shape[2]
-    n = thin_chunks(rows)
+    n = chunks(rows)
     halves, columns, outs, sems = riding(riders, replicas)
     return pl.pallas_call(
         functools.partial(turn_kernel, size, columns),
@@ -1214,7 +1259,7 @@
     hidden = wu_ref.shape[1]
     depth = width // parts
     fb = min(256, hidden)
-    n = thin_chunks(rows)
+    n = chunks(rows)
     rc = rows // n
     g = Group(size)
     copies = [
@@ -1226,7 +1271,7 @@
         pltpu.make_async_copy(hid_ref, hid, w_sem.at[3]),
         pltpu.make_async_copy(a2_ref, a2, w_sem.at[4]),
     ]
-    for copy in copies + late:
+    for copy in copies:
         copy.start()
     g.greet(side=layer == 1)
     section = lax.axis_index("section")
@@ -1267,28 +1312,43 @@
         run(n, send)
     for copy in copies:
         copy.wait()
+    for copy in late:
+        copy.start()
     if layer == 1:
         y_load(ys[0]).wait()
         y_copies(ys[0], ys[1], section)[0].start()
 
+    if layer == 0:
+        gather.relay(0)
+
     def work(j):
         at = span(j, rc)
         if layer == 0:
-            gather.relay(j)
             gather.ready(j)
         held = flat(grad[:, at, :])
         for f in range(hidden // fb):
             cols = slice(f * fb, (f + 1) * fb)
             d = dg(held, wd[cols, :], NT) * flat(dup[:, at, cols]).astype(F32)
             dup[:, at, cols] = d.astype(BF).reshape(size, rc, fb)
+
+        if layer == 0:
+
+            @pl.when(j + 1 < n)
+            def _():
+                gather.relay(j + 1)
+
+        @pl.when(j > 0)
+        def _():
+            scatter.second(j - 1)
+
         held = flat(dup[:, at, :])
         for z in range(parts):
             cols = slice(z * depth, (z + 1) * depth)
             scatter.part[:, at, cols] = dg(held, wu[cols, :], NT).reshape(size, rc, depth)
         scatter.first(j)
-        scatter.second(j)
 
     run(n, work)
+    scatter.second(n - 1)
     for copy in late:
         copy.wait()
 
@@ -1328,7 +1388,7 @@
     rows, width = h1.shape
     hidden = wu.shape[1]
     parts, depth = replicas, width // replicas
-    n = thin_chunks(rows)
+    n = chunks(rows)
     return pl.pallas_call(
         functools.partial(mlp_back_kernel, size, layer, parts),
         out_shape=[
@@ -1546,6 +1606,8 @@
     for copy in copies:
         copy.wait()
 
+    lag = min(2, n)
+
     def work(j):
         at = span(j, rc)
         held = flat(dqkv_ref[:, at, :])
@@ -1553,9 +1615,15 @@
             cols = slice(z * depth, (z + 1) * depth)
             scatter.part[:, at, cols] = dg(held, w[cols, :], NT).reshape(size, rc, depth)
         scatter.first(j)
+
+        @pl.when(j >= lag)
+        def _():
+            scatter.second(j - lag)
+
+
+    run(n, work)
+    for j in range(n - lag, n):
         scatter.second(j)
-
-    run(n, work)
     for copy in late:
         copy.wait()
 
@@ -1657,6 +1725,8 @@
 
     copy.wait()
 
+    lag = min(2, n)
+
     def work(j):
         at = span(j, rc)
         held = flat(dqkv_ref[:, at, :])
@@ -1664,9 +1734,15 @@
             cols = slice(z * depth, (z + 1) * depth)
             scatter.part[:, at, cols] = dg(held, w[cols, :], NT).reshape(size, rc, depth)
         scatter.first(j)
+
+        @pl.when(j >= lag)
+        def _():
+            scatter.second(j - lag)
+
+
+    run(n, work)
+    for j in range(n - lag, n):
         scatter.second(j)
-
-    run(n, work)
     gsum[0] = jnp.zeros_like(gsum[0])
 
     def last(j):

time: 730 us -> 724 us (level)
  no operation moved by 1% of the time
where the time goes in v11:
time: 724 us; the launch traced here: 715 us
  Pallas kernels  670 us (93%)
  other arithmetic  15.5 us (2%)
  between operations  14.3 us (2%)
  local copies, waits for them, and re-layouts  10.6 us (1%)
    pallas_call x2, Pallas kernels, attend_backward(): pl.pallas_call(functools.partial(attend_back_kernel, size, layer, parts),...  153 us
    pallas_call x2, Pallas kernels, attend(): pl.pallas_call(functools.partial(attend_kernel, size, layer, columns), ou...  117 us
    pallas_call x1, Pallas kernels, turn_forward(): pl.pallas_call(functools.partial(turn_kernel, size, columns), out_shape=[...  101 us
    pallas_call x2, Pallas kernels, mlp_backward(): pl.pallas_call(functools.partial(mlp_back_kernel, size, layer, parts), ou...  93.9 us
    pallas_call x1, Pallas kernels, last_backward(): pl.pallas_call(functools.partial(last_kernel, size, replicas), out_shape=...  64 us
    pallas_call x1, Pallas kernels, first_forward(): pl.pallas_call(functools.partial(first_kernel, size, replicas), out_shape...  58.1 us
    pallas_call x1, Pallas kernels, mlp_forward(): pl.pallas_call(functools.partial(mlp_kernel, size, layer, columns), out_s...  49.2 us
    pallas_call x1, Pallas kernels, qkv_backward(): pl.pallas_call(functools.partial(qkv_back_kernel, size, layer, parts), ou...  33.5 us
  transfers between devices with their start and end apart: 7, of which 0 were waited for; matrix products, arithmetic and copies ran while one was open for 1% of the time, Pallas kernels for 42%

profile of v11, /device:TPU:0, one launch (start us, length us, event | category | flops | bytes accessed | tf_op | source)
XLA Modules:
  0.0 714.7 jit_solution(13033972771979780721)
XLA Ops:
  7.2 0.0 copy-start
  7.2 0.0 copy-start.5
  7.2 0.0 reduce-scatter.5.cloned.1.call-start
  7.3 0.0 copy-start.6
  7.3 1.3 convert_element_type.55
  8.6 0.1 convert_element_type.56
  8.7 0.0 copy-start.9
  8.7 1.1 copy.19.wq_ref
  9.8 0.0 copy-done.5
  9.8 0.9 convert_element_type.59
  10.6 0.0 copy-done.6
  10.6 0.8 convert_element_type.61
  11.5 0.0 copy-done.9
  11.5 0.7 convert_element_type.57
  12.2 0.0 copy-done
  12.2 0.0 copy-start.12
  12.2 0.0 copy-start.13
  12.2 3.0 dynamic-slice_bitcast_fusion
  15.3 0.1 pad.4.clone
  15.3 1.2 select_convert_fusion
  16.6 0.0 copy-done.12
  16.6 0.0 copy-done.13
  16.6 0.7 maximum_maximum_fusion.gain_ref
  17.3 58.1 %shard_map.152 = (bf16[4,512,768]{2,1,0:T(8,128)(2,1)}, f32[2,8,1024]{2,1,0:T(8,128)}, bf16[4,512,1024]{2,1,0:T(8,128)(2,1)}, bf16[1024,768]{1,0:T(8,128)(2,1)},...) custom-call(bf16[512,1024]{1,0:T(8,128)(2,1)} %get-tuple-element.140, ...), custom_call_target="tpu_custom_call" | custom-call | flops 30000001024 | bytes 30000000 | tf_op jit(solution)/shard_map/pallas_call | solution.py:777
  75.3 59.3 %shard_map.153 = (f32[512,1024]{1,0:T(8,128)}, bf16[4,512,256]{2,1,0:T(8,128)(2,1)}, f32[4,4,512]{2,1,0:T(4,128)}, bf16[1024,1024]{1,0:T(8,128)(2,1)}, bf16[1024,1024]{1,0:T(8,128)(2,1)}) custom-call(bf16[4,512,768]{2,1,0:T(8,128)(2,1)} %get-tuple-element.68.refs_0_.refs_1_, bf16[4,512,64]{2,1,0:T(8,128)(2,1)} %get-tuple-element.139.refs_1_.refs_2_, ...), custom_call_target="tpu_custom_call" | custom-call | flops 60000002048 | bytes 20000000 | tf_op jit(solution)/shard_map/pallas_call | solution.py:918
  134.6 100.7 %shard_map.154 = (bf16[512,1024]{1,0:T(8,128)(2,1)}, bf16[4,512,768]{2,1,0:T(8,128)(2,1)}, bf16[4,512,1024]{2,1,0:T(8,128)(2,1)}, bf16[4,512,1024]{2,1,0:T(8,128...) custom-call(f32[512,1024]{1,0:T(8,128)} %get-tuple-element.72.refs_0, ...), custom_call_target="tpu_custom_call" | custom-call | flops 49999998976 | bytes 30000000 | tf_op jit(solution)/shard_map/pallas_call | solution.py:1213
  235.4 58.2 %shard_map.155 = (f32[512,1024]{1,0:T(8,128)}, bf16[4,512,256]{2,1,0:T(8,128)(2,1)}, f32[4,4,512]{2,1,0:T(4,128)}, bf16[4,512,1024]{2,1,0:T(8,128)(2,1)}, bf16[1024,1024]{1,0:T(8,128)(2,1)}) custom-call(bf16[4,512,768]{2,1,0:T(8,128)(2,1)} %get-tuple-element.78.refs_0_.refs_1_, bf16[4,512,64]{2,1,0:T(8,128)(2,1)} %get-tuple-element.139.refs_1_.refs_2_, ...), custom_call_target="tpu_custom_call" | custom-call | flops 60000002048 | bytes 20000000 | tf_op jit(solution)/shard_map/pallas_call | solution.py:918
  293.5 49.2 %shard_map.156 = (bf16[512,1024]{1,0:T(8,128)(2,1)}, bf16[4,512,1024]{2,1,0:T(8,128)(2,1)}, bf16[4,512,1024]{2,1,0:T(8,128)(2,1)}, bf16[4,512,1024]{2,1,0:T(8,128)(2,1)}) custom-call(f32[512,1024]{1,0:T(8,128)} %get-tuple-element.82.refs_0_.refs_1_, f32[2,8,1024]{2,1,0:T(8,128)} %get-tuple-element.73.refs_1_.refs_2_.gain_ref, ...), custom_call_target="tpu_custom_call" | custom-call | flops 49999998976 | bytes 30000000 | tf_op jit(solution)/shard_map/pallas_call | solution.py:1038
  342.7 40.9 %shard_map.157 = (f32[512,1024]{1,0:T(8,128)}, f32[1,1024]{1,0:T(1,128)}, bf16[4,256,1024]{2,1,0:T(8,128)(2,1)}, bf16[4,1024,256]{2,1,0:T(8,128)(2,1)}, bf16[2,512,1024]{2,1,0:T(8,128)(2,1)}) custom-call(bf16[512,1024]{1,0:T(8,128)(2,1)} %get-tuple-element.141.refs_5_.refs_0_, f32[512,1024]{1,0:T(8,128)} %get-tuple-element.82.refs_0_.refs_1_, ...), custom_call_target="tpu_custom_call" | custom-call | flops 60000002048 | bytes 40000000 | tf_op jit(solution)/shard_map/pallas_call | solution.py:1392
  383.7 0.0 reduce-scatter.5.cloned.1.call-update
  383.7 0.0 reduce-scatter.7.cloned.1.call-start
  383.8 0.7 reduce-scatter.7.cloned.1.call-update
  384.5 0.0 reduce-scatter.9.cloned.1.call-start
  384.5 71.7 %shard_map.158 = (bf16[4,512,768]{2,1,0:T(8,128)(2,1)}, f32[256,256]{1,0:T(8,128)}) custom-call(f32[512,1024]{1,0:T(8,128)} %get-tuple-element.91.refs_0_.mid_in, bf16[4,512,768]{2,1,0:T(8,128)(2,1)} %get-tuple-element.78.refs_0_.refs_1_, bf16[4,512,64]{2,1,0:T(8,128)(2,1)} %get-tuple-element.139.refs_1_.refs_2_, ...), custom_call_target="tpu_custom_call" | custom-call | flops 89999998976 | bytes 40000000 | tf_op jit(solution)/shard_map/pallas_call | solution.py:1563
  456.2 0.0 copy-start.11
  456.2 33.5 %shard_map.159 = (bf16[512,1024]{1,0:T(8,128)(2,1)}, f32[1,1024]{1,0:T(1,128)}, bf16[4,256,768]{2,1,0:T(8,128)(2,1)}) custom-call(bf16[4,512,768]{2,1,0:T(8,128)(2,1)} %get-tuple-element.94.dqkv_ref, f32[2,8,1024]{2,1,0:T(8,128)} %get-tuple-element.73.refs_1_.refs_2_.gain_ref, bf16[4,512,1024]{2,1,0:T(8,128)(2,1)} %get-tuple-element.95.a1_in, ...), custom_call_target="tpu_custom_call" | custom-call | flops 30000001024 | bytes 30000000 | tf_op jit(solution)/shard_map/pallas_call | solution.py:1654
  489.7 0.0 reduce-scatter.9.cloned.1.call-update
  489.7 0.0 reduce-scatter.11.cloned.1.call-start
  489.8 0.0 copy-done.11
  489.8 1.3 pad_maximum_fusion.above_ref
  491.1 52.9 %shard_map.160 = (f32[512,1024]{1,0:T(8,128)}, f32[1,1024]{1,0:T(1,128)}, bf16[4,256,1024]{2,1,0:T(8,128)(2,1)}, bf16[4,1024,256]{2,1,0:T(8,128)(2,1)}) custom-call(bf16[512,1024]{1,0:T(8,128)(2,1)} %get-tuple-element.100.refs_0_.dx1_ref, f32[512,1024]{1,0:T(8,128)} %get-tuple-element.72.refs_0_.refs_1_, ...), custom_call_target="tpu_custom_call" | custom-call | flops 60000002048 | bytes 40000000 | tf_op jit(solution)/shard_map/pallas_call | solution.py:1392
  544.0 0.0 reduce-scatter.9.cloned.1.call-done
  544.0 0.0 copy-start.8
  544.1 0.0 copy-done.7
  544.1 2.6 collective-permute-start.2
  546.7 0.0 reduce-scatter.11.cloned.1.call-update
  546.7 0.0 copy-done.8
  546.7 0.9 collective-permute-start
  547.6 81.4 %shard_map.161 = (bf16[4,512,768]{2,1,0:T(8,128)(2,1)}, f32[256,256]{1,0:T(8,128)}, f32[1024,256]{1,0:T(8,128)}) custom-call(f32[512,1024]{1,0:T(8,128)} %get-tuple-element.106.refs_0_.mid_ref, bf16[4,512,768]{2,1,0:T(8,128)(2,1)} %get-tuple-element.68.refs_0_.refs_1_, bf16[4,512,64]{2,1,0:T(8,128)(2,1)} %get-tuple-element.139.refs_1_.refs_2_, ...), custom_call_target="tpu_custom_call" | custom-call | flops 89999998976 | bytes 40000000 | tf_op jit(solution)/shard_map/pallas_call | solution.py:1563
  629.1 1.7 broadcast_select_fusion.1
  630.8 0.0 collective-permute-done.2
  630.8 2.3 select_bitcast_fusion
  633.2 0.9 broadcast_select_fusion
  634.0 0.0 collective-permute-start.1
  634.0 64.0 %shard_map.162 = (f32[8,1024]{1,0:T(8,128)}, f32[256,768]{1,0:T(8,128)}, bf16[2,512,1024]{2,1,0:T(8,128)(2,1)}) custom-call(bf16[4,512,768]{2,1,0:T(8,128)(2,1)} %get-tuple-element.112.dqkv_ref, bf16[4,512,1024]{2,1,0:T(8,128)(2,1)} %get-tuple-element.113.a1_ref, bf16[512,1024]{1,0:T(8,128)(2,1)} %get-tuple-element.140.x_ref.refs_3_, ...), custom_call_target="tpu_custom_call" | custom-call | flops 40000000000 | bytes 30000000 | tf_op jit(solution)/shard_map/pallas_call | solution.py:1839
  698.0 0.0 collective-permute-done
  698.0 1.2 add_select_fusion
  699.3 1.1 copy.20
  700.4 1.4 constant_dynamic-slice_fusion.1
  701.9 0.0 collective-permute-done.1
  701.9 2.4 add_bitcast_fusion
  704.3 1.3 copy.23
  705.6 1.0 copy-done.3
  706.7 1.3 copy.24
  (17 shorter events, 0.1 us)
Async XLA Ops:
  7.2 5.0 copy-start
  7.2 2.6 copy-start.5
  7.2 483.9 %reduce-scatter.5.cloned.1.call-start = ((), (), s32[]{:S(2)}) async-start(), calls=%async_computation.4 | async-start | bytes 2621440 | tf_op jit(solution)/shard_map/reduce_scatter | solution.py:1935
  7.3 3.4 copy-start.6
  8.7 2.8 copy-start.9
  12.2 4.4 copy-start.12
  12.2 4.4 copy-start.13
  383.7 107.3 %reduce-scatter.7.cloned.1.call-start = ((), (), s32[]{:S(2)}) async-start(), calls=%async_computation.5 | async-start | bytes 2621440 | tf_op jit(solution)/shard_map/reduce_scatter | solution.py:1935
  384.5 159.6 %reduce-scatter.9.cloned.1.call-start = ((), (), s32[]{:S(2)}) async-start(), calls=%async_computation.6 | async-start | bytes 1966080 | tf_op jit(solution)/shard_map/reduce_scatter | solution.py:1935
  456.2 33.6 %copy-start.11 = (f32[1,1024]{1,0:T(1,128)S(1)}, f32[1,1024]{1,0:T(1,128)}, u32[]{:S(2)}) copy-start(f32[1,1024]{1,0:T(1,128)} %get-tuple-element.117) | copy-start | bytes 12292
  489.7 143.5 %reduce-scatter.11.cloned.1.call-start = ((), (), s32[]{:S(2)}) async-start(), calls=%async_computation.7 | async-start | bytes 2621440 | tf_op jit(solution)/shard_map/reduce_scatter | solution.py:1935
  491.1 53.0 %copy-start.7 = (bf16[1,1024,256]{2,1,0:T(8,128)(2,1)S(1)}, bf16[1,1024,256]{2,1,0:T(8,128)(2,1)}, u32[]{:S(2)}) copy-start(bf16[1,1024,256]{2,1,0:T(8,128)(2,1)} %reduce-scatter.7.cloned.1.call-done) | copy-start | bytes 1572868
  544.0 2.7 copy-start.8
  544.1 86.8 %collective-permute-start.2 = (bf16[1024,256]{1,0:T(8,128)(2,1)S(1)}, bf16[1024,256]{1,0:T(8,128)(2,1)S(1)}, u32[]{:S(2)}, u32[]{:S(2)}) collective-permute-start(bf16[1024,256]{1,0:T(8,128)(2,1)S(1)} %bitcast.32), channel_id=1, source_target_pairs={{0,16},{16,0},{1,17},{17,1},{2,18},{18,2},{3,19},{19,3},{4,20},{20... | collective-permute-start | bytes 1572872 | tf_op jit(solution)/shard_map/ppermute | solution.py:1879
  546.7 151.3 %collective-permute-start = (bf16[256,768]{1,0:T(8,128)(2,1)S(1)}, bf16[256,768]{1,0:T(8,128)(2,1)S(1)}, u32[]{:S(2)}, u32[]{:S(2)}) collective-permute-start(bf16[256,768]{1,0:T(8,128)(2,1)S(1)} %bitcast.34), channel_id=1, source_target_pairs={{0,16},{16,0},{1,17},{17,1},{2,18},{18,2},{3,19},{19,3},{4,20},{20... | collective-permute-start | bytes 1179656 | tf_op jit(solution)/shard_map/ppermute | solution.py:1879
  547.6 81.5 %copy-start.10 = (f32[256,256]{1,0:T(8,128)S(1)}, f32[256,256]{1,0:T(8,128)}, u32[]{:S(2)}) copy-start(f32[256,256]{1,0:T(8,128)} %get-tuple-element.123) | copy-start | bytes 786436
  629.1 4.1 copy-start.4
  634.0 67.8 %collective-permute-start.1 = (bf16[256,1024]{1,0:T(8,128)(2,1)}, bf16[256,1024]{1,0:T(8,128)(2,1)}, u32[]{:S(2)}, u32[]{:S(2)}) collective-permute-start(bf16[256,1024]{1,0:T(8,128)(2,1)} %broadcast_select_fusion), channel_id=1, source_target_pairs={{0,16},{16,0},{1,17},{17,1},{2,18},{18,2},{3,19},{19,3},{4,20},{20... | collective-permute-start | bytes 1572872 | tf_op jit(solution)/shard_map/ppermute | solution.py:1879
  699.3 5.0 copy-start.2
  704.3 2.3 copy-start.3
  704.3 3.7 copy-start.1
Sparse Core Ops, SparseCore 0:
  383.8 50.8 reduce-scatter.4
  437.1 43.5 reduce-scatter.6
  489.8 34.7 reduce-scatter.8
  546.9 48.5 reduce-scatter.10

commit v12 on v11

--- a/solution.py
+++ b/solution.py
@@ -736,14 +736,14 @@
     swaps[0].arrive()
     swaps[1].arrive()
     riders.start()
-    swaps[2].start()
-    swaps[3].start()
 
     def relay(j):
         gather.relay(j)
         riders.step(j, n)
 
     run(n, relay)
+    swaps[2].start()
+    swaps[3].start()
     riders.finish()
     outs = [
         pltpu.make_async_copy(w, wq_out, own_sem.at[0]),
@@ -1074,7 +1074,7 @@
     scratch, refs = refs[:9], refs[9:]
     spread = Spread(q_stage.at[1], wq, False, refs[:5])
     riders = Riders(halves, wholes, columns, refs[5:])
-    out_rider, up_rider, down_rider = riders.all
+    out_rider, up_rider = riders.all
     stages = len(spread.stages)
     rows, width = h1_ref.shape
     hidden = wu_ref.shape[1]
@@ -1173,7 +1173,6 @@
     for j in range(n - lag, n):
         pass_on(j)
     up_rider.step(0)
-    down_rider.start()
     spread.finish()
     outs.append(pltpu.make_async_copy(wq, wq_out, out_sem.at[3]))
     outs[3].start()
@@ -1916,14 +1915,14 @@
         [(h_up, "spread", 0, False), (h_down, "spread", 0, True)],
     )
     below = (x, a1, qkv, ctx, lse, h1)
-    y0, qkv, a2, hid, slope, a1, w_qkv_1, w_out_1, w_up_1, got_down = turn_forward(
+    y0, qkv, a2, hid, slope, a1, w_qkv_1, w_out_1, w_up_1 = turn_forward(
         size, replicas, h1, gains, w_up_0, w_down_0, h_qkv,
-        [(h_out, "spread", 1, True), (h_up, "spread", 1, False), (h_down, "z", 1, True)],
+        [(h_out, "spread", 1, True), (h_up, "spread", 1, False)],
     )
     kept = [below + (a2, hid, slope)]
     grad = lax.dynamic_index_in_dim(cotangent, section, 0, keepdims=False)
     h1, ctx, lse, grad_all, w_down_1 = attend(
-        size, replicas, 1, qkv, qm, km, y0, w_out_1, [(got_down, "y", 1, True)], [grad]
+        size, replicas, 1, qkv, qm, km, y0, w_out_1, [(h_down, "spread", 1, True)], [grad]
     )
     y1, a2, hid, slope = mlp_forward(size, replicas, 1, h1, gains, w_up_1, w_down_1, [])
     kept.append((y0, a1, qkv, ctx, lse, h1, a2, hid, slope))

time: 724 us -> 704 us (0.972)
  Pallas kernels: 670 us -> 650 us
    pallas_call x1, Pallas kernels: 101 us -> 85.2 us  [turn_forward(): pl.pallas_call(functools.partial(turn_kernel, size, columns), out_shape=[...]
  transfers between devices with their start and end apart: 7 -> 7, of which waited for: 0 -> 0; matrix products, arithmetic and copies ran while one was open for 1% -> 1% of each run, Pallas kernels for 42% -> 44%
where the time goes in v12:
time: 704 us; the launch traced here: 695 us
  Pallas kernels  650 us (92%)
  other arithmetic  15.5 us (2%)
  between operations  14.3 us (2%)
  local copies, waits for them, and re-layouts  10.6 us (2%)
    pallas_call x2, Pallas kernels, attend_backward(): pl.pallas_call(functools.partial(attend_back_kernel, size, layer, parts),...  154 us
    pallas_call x2, Pallas kernels, attend(): pl.pallas_call(functools.partial(attend_kernel, size, layer, columns), ou...  114 us
    pallas_call x2, Pallas kernels, mlp_backward(): pl.pallas_call(functools.partial(mlp_back_kernel, size, layer, parts), ou...  92.7 us
    pallas_call x1, Pallas kernels, turn_forward(): pl.pallas_call(functools.partial(turn_kernel, size, columns), out_shape=[...  85.2 us
    pallas_call x1, Pallas kernels, last_backward(): pl.pallas_call(functools.partial(last_kernel, size, replicas), out_shape=...  64 us
    pallas_call x1, Pallas kernels, first_forward(): pl.pallas_call(functools.partial(first_kernel, size, replicas), out_shape...  56.8 us
    pallas_call x1, Pallas kernels, mlp_forward(): pl.pallas_call(functools.partial(mlp_kernel, size, layer, columns), out_s...  50.3 us
    pallas_call x1, Pallas kernels, qkv_backward(): pl.pallas_call(functools.partial(qkv_back_kernel, size, layer, parts), ou...  33 us
  transfers between devices with their start and end apart: 7, of which 0 were waited for; matrix products, arithmetic and copies ran while one was open for 1% of the time, Pallas kernels for 44%

profile of v12, /device:TPU:0, one launch (start us, length us, event | category | flops | bytes accessed | tf_op | source)
XLA Modules:
  0.0 694.5 jit_solution(6448958367508602060)
XLA Ops:
  7.2 0.0 copy-start
  7.2 0.0 copy-start.5
  7.2 0.0 reduce-scatter.5.cloned.1.call-start
  7.3 0.0 copy-start.6
  7.3 1.3 convert_element_type.55
  8.6 0.1 convert_element_type.56
  8.7 0.0 copy-start.9
  8.7 1.1 copy.19.wq_ref
  9.8 0.0 copy-done.5
  9.8 0.9 convert_element_type.59
  10.6 0.0 copy-done.6
  10.6 0.8 convert_element_type.61
  11.5 0.0 copy-done.9
  11.5 0.7 convert_element_type.57
  12.2 0.0 copy-done
  12.2 0.0 copy-start.12
  12.2 0.0 copy-start.13
  12.2 3.0 dynamic-slice_bitcast_fusion
  15.3 0.1 pad.4.clone
  15.3 1.2 select_convert_fusion
  16.6 0.0 copy-done.12
  16.6 0.0 copy-done.13
  16.6 0.7 maximum_maximum_fusion.gain_ref
  17.3 56.8 %shard_map.152 = (bf16[4,512,768]{2,1,0:T(8,128)(2,1)}, f32[2,8,1024]{2,1,0:T(8,128)}, bf16[4,512,1024]{2,1,0:T(8,128)(2,1)}, bf16[1024,768]{1,0:T(8,128)(2,1)},...) custom-call(bf16[512,1024]{1,0:T(8,128)(2,1)} %get-tuple-element.138, ...), custom_call_target="tpu_custom_call" | custom-call | flops 30000001024 | bytes 30000000 | tf_op jit(solution)/shard_map/pallas_call | solution.py:777
  74.1 60.4 %shard_map.153 = (f32[512,1024]{1,0:T(8,128)}, bf16[4,512,256]{2,1,0:T(8,128)(2,1)}, f32[4,4,512]{2,1,0:T(4,128)}, bf16[1024,1024]{1,0:T(8,128)(2,1)}, bf16[1024,1024]{1,0:T(8,128)(2,1)}) custom-call(bf16[4,512,768]{2,1,0:T(8,128)(2,1)} %get-tuple-element.67.refs_0_.refs_1_, bf16[4,512,64]{2,1,0:T(8,128)(2,1)} %get-tuple-element.137.refs_1_.refs_2_, ...), custom_call_target="tpu_custom_call" | custom-call | flops 60000002048 | bytes 20000000 | tf_op jit(solution)/shard_map/pallas_call | solution.py:918
  134.5 85.2 %shard_map.154 = (bf16[512,1024]{1,0:T(8,128)(2,1)}, bf16[4,512,768]{2,1,0:T(8,128)(2,1)}, bf16[4,512,1024]{2,1,0:T(8,128)(2,1)}, bf16[4,512,1024]{2,1,0:T(8,128...) custom-call(f32[512,1024]{1,0:T(8,128)} %get-tuple-element.71.refs_0, ...), custom_call_target="tpu_custom_call" | custom-call | flops 49999998976 | bytes 30000000 | tf_op jit(solution)/shard_map/pallas_call | solution.py:1212
  219.7 53.7 %shard_map.155 = (f32[512,1024]{1,0:T(8,128)}, bf16[4,512,256]{2,1,0:T(8,128)(2,1)}, f32[4,4,512]{2,1,0:T(4,128)}, bf16[4,512,1024]{2,1,0:T(8,128)(2,1)}, bf16[1024,1024]{1,0:T(8,128)(2,1)}) custom-call(bf16[4,512,768]{2,1,0:T(8,128)(2,1)} %get-tuple-element.77.refs_0_.refs_1_, bf16[4,512,64]{2,1,0:T(8,128)(2,1)} %get-tuple-element.137.refs_1_.refs_2_, ...), custom_call_target="tpu_custom_call" | custom-call | flops 60000002048 | bytes 20000000 | tf_op jit(solution)/shard_map/pallas_call | solution.py:918
  273.4 50.3 %shard_map.156 = (bf16[512,1024]{1,0:T(8,128)(2,1)}, bf16[4,512,1024]{2,1,0:T(8,128)(2,1)}, bf16[4,512,1024]{2,1,0:T(8,128)(2,1)}, bf16[4,512,1024]{2,1,0:T(8,128)(2,1)}) custom-call(f32[512,1024]{1,0:T(8,128)} %get-tuple-element.80.refs_0_.refs_1_, f32[2,8,1024]{2,1,0:T(8,128)} %get-tuple-element.72.refs_1_.refs_2_.gain_ref, ...), custom_call_target="tpu_custom_call" | custom-call | flops 49999998976 | bytes 30000000 | tf_op jit(solution)/shard_map/pallas_call | solution.py:1038
  323.7 39.8 %shard_map.157 = (f32[512,1024]{1,0:T(8,128)}, f32[1,1024]{1,0:T(1,128)}, bf16[4,256,1024]{2,1,0:T(8,128)(2,1)}, bf16[4,1024,256]{2,1,0:T(8,128)(2,1)}, bf16[2,512,1024]{2,1,0:T(8,128)(2,1)}) custom-call(bf16[512,1024]{1,0:T(8,128)(2,1)} %get-tuple-element.139.refs_5_.refs_0_, f32[512,1024]{1,0:T(8,128)} %get-tuple-element.80.refs_0_.refs_1_, ...), custom_call_target="tpu_custom_call" | custom-call | flops 60000002048 | bytes 40000000 | tf_op jit(solution)/shard_map/pallas_call | solution.py:1391
  363.5 0.0 reduce-scatter.5.cloned.1.call-update
  363.5 0.0 reduce-scatter.7.cloned.1.call-start
  363.5 0.7 reduce-scatter.7.cloned.1.call-update
  364.2 0.0 reduce-scatter.9.cloned.1.call-start
  364.3 71.9 %shard_map.158 = (bf16[4,512,768]{2,1,0:T(8,128)(2,1)}, f32[256,256]{1,0:T(8,128)}) custom-call(f32[512,1024]{1,0:T(8,128)} %get-tuple-element.89.refs_0_.mid_in, bf16[4,512,768]{2,1,0:T(8,128)(2,1)} %get-tuple-element.77.refs_0_.refs_1_, bf16[4,512,64]{2,1,0:T(8,128)(2,1)} %get-tuple-element.137.refs_1_.refs_2_, ...), custom_call_target="tpu_custom_call" | custom-call | flops 89999998976 | bytes 40000000 | tf_op jit(solution)/shard_map/pallas_call | solution.py:1562
  436.2 0.0 copy-start.11
  436.2 33.0 %shard_map.159 = (bf16[512,1024]{1,0:T(8,128)(2,1)}, f32[1,1024]{1,0:T(1,128)}, bf16[4,256,768]{2,1,0:T(8,128)(2,1)}) custom-call(bf16[4,512,768]{2,1,0:T(8,128)(2,1)} %get-tuple-element.92.dqkv_ref, f32[2,8,1024]{2,1,0:T(8,128)} %get-tuple-element.72.refs_1_.refs_2_.gain_ref, bf16[4,512,1024]{2,1,0:T(8,128)(2,1)} %get-tuple-element.93.a1_in, ...), custom_call_target="tpu_custom_call" | custom-call | flops 30000001024 | bytes 30000000 | tf_op jit(solution)/shard_map/pallas_call | solution.py:1653
  469.2 0.0 reduce-scatter.9.cloned.1.call-update
  469.3 0.0 reduce-scatter.11.cloned.1.call-start
  469.3 0.0 copy-done.11
  469.3 1.3 pad_maximum_fusion.above_ref
  470.6 52.9 %shard_map.160 = (f32[512,1024]{1,0:T(8,128)}, f32[1,1024]{1,0:T(1,128)}, bf16[4,256,1024]{2,1,0:T(8,128)(2,1)}, bf16[4,1024,256]{2,1,0:T(8,128)(2,1)}) custom-call(bf16[512,1024]{1,0:T(8,128)(2,1)} %get-tuple-element.98.refs_0_.dx1_ref, f32[512,1024]{1,0:T(8,128)} %get-tuple-element.71.refs_0_.refs_1_, ...), custom_call_target="tpu_custom_call" | custom-call | flops 60000002048 | bytes 40000000 | tf_op jit(solution)/shard_map/pallas_call | solution.py:1391
  523.6 0.0 reduce-scatter.9.cloned.1.call-done
  523.6 2.6 collective-permute-start.2
  526.2 0.0 reduce-scatter.11.cloned.1.call-update
  526.3 0.9 collective-permute-start
  527.2 81.7 %shard_map.161 = (bf16[4,512,768]{2,1,0:T(8,128)(2,1)}, f32[256,256]{1,0:T(8,128)}, f32[1024,256]{1,0:T(8,128)}) custom-call(f32[512,1024]{1,0:T(8,128)} %get-tuple-element.104.refs_0_.mid_ref, bf16[4,512,768]{2,1,0:T(8,128)(2,1)} %get-tuple-element.67.refs_0_.refs_1_, bf16[4,512,64]{2,1,0:T(8,128)(2,1)} %get-tuple-element.137.refs_1_.refs_2_, ...), custom_call_target="tpu_custom_call" | custom-call | flops 89999998976 | bytes 40000000 | tf_op jit(solution)/shard_map/pallas_call | solution.py:1562
  608.9 1.7 broadcast_select_fusion.1
  610.6 0.0 collective-permute-done.2
  610.6 2.3 select_bitcast_fusion
  613.0 0.0 copy-done.4
  613.0 0.9 broadcast_select_fusion
  613.8 0.0 collective-permute-start.1
  613.8 64.0 %shard_map.162 = (f32[8,1024]{1,0:T(8,128)}, f32[256,768]{1,0:T(8,128)}, bf16[2,512,1024]{2,1,0:T(8,128)(2,1)}) custom-call(bf16[4,512,768]{2,1,0:T(8,128)(2,1)} %get-tuple-element.110.dqkv_ref, bf16[4,512,1024]{2,1,0:T(8,128)(2,1)} %get-tuple-element.111.a1_ref, bf16[512,1024]{1,0:T(8,128)(2,1)} %get-tuple-element.138.x_ref.refs_3_, ...), custom_call_target="tpu_custom_call" | custom-call | flops 40000000000 | bytes 30000000 | tf_op jit(solution)/shard_map/pallas_call | solution.py:1838
  677.8 0.0 collective-permute-done
  677.8 1.2 add_select_fusion
  679.1 0.0 copy-start.2
  679.1 1.1 copy.20
  680.2 1.4 constant_dynamic-slice_fusion.1
  681.7 0.0 collective-permute-done.1
  681.7 2.4 add_bitcast_fusion
  684.1 0.0 copy-done.2
  684.1 1.3 copy.23
  685.4 1.0 copy-done.3
  686.5 1.3 copy.24
  (17 shorter events, 0.1 us)
Async XLA Ops:
  7.2 5.0 copy-start
  7.2 2.6 copy-start.5
  7.2 463.4 %reduce-scatter.5.cloned.1.call-start = ((), (), s32[]{:S(2)}) async-start(), calls=%async_computation.4 | async-start | bytes 2621440 | tf_op jit(solution)/shard_map/reduce_scatter | solution.py:1934
  7.3 3.4 copy-start.6
  8.7 2.8 copy-start.9
  12.2 4.4 copy-start.12
  12.2 4.4 copy-start.13
  363.5 107.1 %reduce-scatter.7.cloned.1.call-start = ((), (), s32[]{:S(2)}) async-start(), calls=%async_computation.5 | async-start | bytes 2621440 | tf_op jit(solution)/shard_map/reduce_scatter | solution.py:1934
  364.2 159.4 %reduce-scatter.9.cloned.1.call-start = ((), (), s32[]{:S(2)}) async-start(), calls=%async_computation.6 | async-start | bytes 1966080 | tf_op jit(solution)/shard_map/reduce_scatter | solution.py:1934
  436.2 33.1 %copy-start.11 = (f32[1,1024]{1,0:T(1,128)S(1)}, f32[1,1024]{1,0:T(1,128)}, u32[]{:S(2)}) copy-start(f32[1,1024]{1,0:T(1,128)} %get-tuple-element.115) | copy-start | bytes 12292
  469.3 143.7 %reduce-scatter.11.cloned.1.call-start = ((), (), s32[]{:S(2)}) async-start(), calls=%async_computation.7 | async-start | bytes 2621440 | tf_op jit(solution)/shard_map/reduce_scatter | solution.py:1934
  470.6 53.0 %copy-start.7 = (bf16[1,1024,256]{2,1,0:T(8,128)(2,1)S(1)}, bf16[1,1024,256]{2,1,0:T(8,128)(2,1)}, u32[]{:S(2)}) copy-start(bf16[1,1024,256]{2,1,0:T(8,128)(2,1)} %reduce-scatter.7.cloned.1.call-done) | copy-start | bytes 1572868
  523.6 2.7 copy-start.8
  523.6 87.0 %collective-permute-start.2 = (bf16[1024,256]{1,0:T(8,128)(2,1)S(1)}, bf16[1024,256]{1,0:T(8,128)(2,1)S(1)}, u32[]{:S(2)}, u32[]{:S(2)}) collective-permute-start(bf16[1024,256]{1,0:T(8,128)(2,1)S(1)} %bitcast.32), channel_id=1, source_target_pairs={{0,16},{16,0},{1,17},{17,1},{2,18},{18,2},{3,19},{19,3},{4,20},{20... | collective-permute-start | bytes 1572872 | tf_op jit(solution)/shard_map/ppermute | solution.py:1878
  526.3 151.5 %collective-permute-start = (bf16[256,768]{1,0:T(8,128)(2,1)S(1)}, bf16[256,768]{1,0:T(8,128)(2,1)S(1)}, u32[]{:S(2)}, u32[]{:S(2)}) collective-permute-start(bf16[256,768]{1,0:T(8,128)(2,1)S(1)} %bitcast.34), channel_id=1, source_target_pairs={{0,16},{16,0},{1,17},{17,1},{2,18},{18,2},{3,19},{19,3},{4,20},{20... | collective-permute-start | bytes 1179656 | tf_op jit(solution)/shard_map/ppermute | solution.py:1878
  527.2 81.7 %copy-start.10 = (f32[256,256]{1,0:T(8,128)S(1)}, f32[256,256]{1,0:T(8,128)}, u32[]{:S(2)}) copy-start(f32[256,256]{1,0:T(8,128)} %get-tuple-element.121) | copy-start | bytes 786436
  608.9 4.1 copy-start.4
  613.8 67.8 %collective-permute-start.1 = (bf16[256,1024]{1,0:T(8,128)(2,1)}, bf16[256,1024]{1,0:T(8,128)(2,1)}, u32[]{:S(2)}, u32[]{:S(2)}) collective-permute-start(bf16[256,1024]{1,0:T(8,128)(2,1)} %broadcast_select_fusion), channel_id=1, source_target_pairs={{0,16},{16,0},{1,17},{17,1},{2,18},{18,2},{3,19},{19,3},{4,20},{20... | collective-permute-start | bytes 1572872 | tf_op jit(solution)/shard_map/ppermute | solution.py:1878
  679.1 5.0 copy-start.2
  684.1 2.3 copy-start.3
  684.1 3.7 copy-start.1
Sparse Core Ops, SparseCore 0:
  363.6 50.8 reduce-scatter.4
  416.9 43.7 reduce-scatter.6
  469.4 35.0 reduce-scatter.8
  526.4 49.1 reduce-scatter.10

commit v13 on v12

--- a/solution.py
+++ b/solution.py
@@ -940,17 +940,14 @@
     )(qkv, qm, km, x, w, *cot, *halves)
 
 
-def mlp_kernel(size, layer, columns, *refs):
-    m = len(columns)
-    h1_ref, gain_ref, wu_ref, wd_ref = refs[:4]
-    halves, refs = refs[4 : 4 + m], refs[4 + m :]
-    y_ref, a2_out, hid_out, slope_out = refs[:4]
-    wholes, refs = refs[4 : 4 + m], refs[4 + m :]
-    a2, hid, slope, wu, wd, w_sem, out_sem = refs[:7]
-    scratch, refs = refs[7:20], refs[20:]
-    riders = Riders(halves, wholes, columns, refs)
+def peak_kernel(
+    size, parts, h1_ref, gain_ref, grad_ref, wu_ref, wd_ref,
+    mid_ref, gain_out, gup_ref, gdown_ref, hid_out,
+    a2, hid, dup, grad, wu, wd, w_sem, out_sem, *scratch
+):
     rows, width = h1_ref.shape
     hidden = wu_ref.shape[1]
+    depth = width // parts
     fb = min(256, hidden)
     n = chunks(rows)
     rc = rows // n
@@ -958,40 +955,38 @@
     copies = [
         pltpu.make_async_copy(wu_ref, wu, w_sem.at[0]),
         pltpu.make_async_copy(wd_ref, wd, w_sem.at[1]),
+        pltpu.make_async_copy(grad_ref, grad, w_sem.at[2]),
     ]
     for copy in copies:
         copy.start()
-    g.greet(riders.replicas)
+    g.greet()
     gather = Gather(g, a2, rc, scratch[:4])
     scatter = Scatter(g, rc, scratch[4:])
 
     def send(j):
         at = span(j, rc)
-        a = normed(h1_ref[at, :])[0] * gain_ref[layer, 1:2, :]
+        a = normed(h1_ref[at, :])[0] * gain_ref[1, 1:2, :]
         a2[g.me, at, :] = a.astype(BF)
         gather.start(j)
 
     run(n, send)
-    riders.start()
     for copy in copies:
         copy.wait()
-
     gather.relay(0)
 
     def work(j):
         at = span(j, rc)
         gather.ready(j)
         a = flat(a2[:, at, :])
+        held = flat(grad[:, at, :])
         for f in range(hidden // fb):
             cols = slice(f * fb, (f + 1) * fb)
             u = dg(a, wu[:, cols], NN)
             half = 0.5 + 0.5 * lax.erf(u * (0.5**0.5))
-            slope[:, at, cols] = (
-                (half + u * jnp.exp(-0.5 * u * u) * ((2 * math.pi) ** -0.5))
-                .astype(BF)
-                .reshape(size, rc, fb)
-            )
+            slope = half + u * jnp.exp(-0.5 * u * u) * ((2 * math.pi) ** -0.5)
             hid[:, at, cols] = (u * half).astype(BF).reshape(size, rc, fb)
+            d = dg(held, wd[cols, :], NT) * slope
+            dup[:, at, cols] = d.astype(BF).reshape(size, rc, fb)
 
         @pl.when(j + 1 < n)
         def _():
@@ -1001,66 +996,75 @@
         def _():
             scatter.second(j - 1)
 
-        held = flat(hid[:, at, :])
-        for f in range(width // 256):
-            cols = slice(f * 256, (f + 1) * 256)
-            scatter.part[:, at, cols] = dg(held, wd[:, cols], NN).reshape(size, rc, 256)
+        held = flat(dup[:, at, :])
+        for z in range(parts):
+            cols = slice(z * depth, (z + 1) * depth)
+            scatter.part[:, at, cols] = dg(held, wu[cols, :], NT).reshape(size, rc, depth)
         scatter.first(j)
-        riders.step(j, n)
 
     run(n, work)
     scatter.second(n - 1)
-    outs = [
-        pltpu.make_async_copy(a2, a2_out, out_sem.at[0]),
-        pltpu.make_async_copy(hid, hid_out, out_sem.at[1]),
-        pltpu.make_async_copy(slope, slope_out, out_sem.at[2]),
-    ]
-    for out in outs:
-        out.start()
+    out = pltpu.make_async_copy(hid, hid_out, out_sem.at[0])
+    out.start()
+
+    def up_grad(z):
+        cols = pl.ds(pl.multiple_of(z * depth, depth), depth)
+        gup_ref[z] = dg(flat(a2[:, :, cols]), flat(dup[...]), TN).astype(BF)
+
+    run(parts, up_grad)
+
+    def down_grad(f):
+        cols = pl.ds(pl.multiple_of(f * fb, fb), fb)
+        r = dg(flat(hid[:, :, cols]), flat(grad[...]), TN).astype(BF)
+        for z in range(parts):
+            gdown_ref[z, cols, :] = r[:, z * depth : (z + 1) * depth]
+
+    run(hidden // fb, down_grad)
+    gain_out[...] = jnp.zeros_like(gain_out)
 
     def last(j):
         at = span(j, rc)
-        y_ref[at, :] = (h1_ref[at, :] + scatter.third(j)).astype(BF)
+        dh, dgain = normed_back(h1_ref[at, :], gain_ref[1, 1:2, :], scatter.third(j))
+        mid_ref[at, :] = grad[g.me, at, :].astype(F32) + dh
+        gain_out[...] += dgain
 
     run(n, last)
-    riders.finish()
     gather.drain(n)
     scatter.drain(n)
-    for out in outs:
-        out.wait()
-
-
-def mlp_forward(size, replicas, layer, h1, gains, wu, wd, riders):
+    out.wait()
+
+
+def peak(size, replicas, h1, gains, grad_all, wu, wd):
     rows, width = h1.shape
     hidden = wu.shape[1]
+    depth = width // replicas
     n = chunks(rows)
-    halves, columns, outs, sems = riding(riders, replicas)
     return pl.pallas_call(
-        functools.partial(mlp_kernel, size, layer, columns),
+        functools.partial(peak_kernel, size, replicas),
         out_shape=[
-            shape((rows, width), BF),
-            shape((size, rows, width), BF),
+            shape((rows, width), F32),
+            shape((1, width), F32),
+            shape((replicas, depth, hidden), BF),
+            shape((replicas, hidden, depth), BF),
             shape((size, rows, hidden), BF),
-            shape((size, rows, hidden), BF),
-        ]
-        + outs,
-        in_specs=[VM, VM, HB, HB] + [HB] * len(riders),
-        out_specs=[VM, HB, HB, HB] + [HB] * len(outs),
+        ],
+        in_specs=[VM, VM, HB, HB, HB],
+        out_specs=[VM, VM, VM, VM, HB],
         scratch_shapes=[
             pltpu.VMEM((size, rows, width), BF),
             pltpu.VMEM((size, rows, hidden), BF),
             pltpu.VMEM((size, rows, hidden), BF),
+            pltpu.VMEM((size, rows, width), BF),
             pltpu.VMEM((width, hidden), BF),
             pltpu.VMEM((hidden, width), BF),
-            DMA((2,)),
             DMA((3,)),
+            DMA((1,)),
         ]
         + comm_sems(size, n)
-        + scatter_scratch(size, rows, width, n)
-        + sems,
-        compiler_params=params(4 + layer),
-        cost_estimate=cost(50e9, 30e6),
-    )(h1, gains, wu, wd, *halves)
+        + scatter_scratch(size, rows, width, n),
+        compiler_params=params(5),
+        cost_estimate=cost(60e9, 30e6),
+    )(h1, gains, grad_all, wu, wd)
 
 
 def turn_kernel(size, columns, *refs):
@@ -1246,12 +1250,10 @@
 def mlp_back_kernel(size, layer, parts, *refs):
     g_ref, h1_ref, gain_ref, a2_ref, hid_ref, slope_ref, wu_ref, wd_ref = refs[:8]
     refs = refs[8:]
-    if layer == 1:
-        ys, whole_ref, refs = refs[:2], refs[2], refs[3:]
+    ys, refs = refs[:2], refs[2:]
     mid_ref, gain_out, gup_ref, gdown_ref = refs[:4]
     refs = refs[4:]
-    if layer == 1:
-        y_out, refs = refs[0], refs[1:]
+    y_out, refs = refs[0], refs[1:]
     grad, a2, hid, dup, wu, wd, w_sem = refs[:7]
     scratch, refs = refs[7:20], refs[20:]
     rows, width = h1_ref.shape
@@ -1272,28 +1274,27 @@
     ]
     for copy in copies:
         copy.start()
-    g.greet(side=layer == 1)
+    g.greet(side=True)
     section = lax.axis_index("section")
-    if layer == 1:
-        y_sem, y_own = refs
-
-        def y_load(own):
-            return pltpu.make_async_copy(own, y_own, y_sem.at[3])
-
-        def y_copies(own, other, at):
-            return (
-                pltpu.make_async_copy(y_own, y_out.at[section], y_sem.at[0]),
-                far_copy(
-                    other, y_out.at[at], y_sem.at[1], y_sem.at[2], {"section": 1 - section}
-                ),
-            )
-
-        for i in range(2):
-
-            @pl.when(section == i)
-            def _(i=i):
-                y_load(ys[i]).start()
-                y_copies(ys[i], ys[1 - i], section)[1].start()
+    y_sem, y_own = refs
+
+    def y_load(own):
+        return pltpu.make_async_copy(own, y_own, y_sem.at[3])
+
+    def y_copies(own, other, at):
+        return (
+            pltpu.make_async_copy(y_own, y_out.at[section], y_sem.at[0]),
+            far_copy(
+                other, y_out.at[at], y_sem.at[1], y_sem.at[2], {"section": 1 - section}
+            ),
+        )
+
+    for i in range(2):
+
+        @pl.when(section == i)
+        def _(i=i):
+            y_load(ys[i]).start()
+            y_copies(ys[i], ys[1 - i], section)[1].start()
 
     gather = Gather(g, grad, rc, scratch[:4])
     scatter = Scatter(g, rc, scratch[4:])
@@ -1303,38 +1304,28 @@
         grad[g.me, at, :] = g_ref[at, :]
         gather.start(j)
 
-    if layer == 1:
-        whole = pltpu.make_async_copy(whole_ref, grad, w_sem.at[5])
-        whole.start()
-        copies.append(whole)
-    else:
-        run(n, send)
+    run(n, send)
     for copy in copies:
         copy.wait()
     for copy in late:
         copy.start()
-    if layer == 1:
-        y_load(ys[0]).wait()
-        y_copies(ys[0], ys[1], section)[0].start()
-
-    if layer == 0:
-        gather.relay(0)
+    y_load(ys[0]).wait()
+    y_copies(ys[0], ys[1], section)[0].start()
+
+    gather.relay(0)
 
     def work(j):
         at = span(j, rc)
-        if layer == 0:
-            gather.ready(j)
+        gather.ready(j)
         held = flat(grad[:, at, :])
         for f in range(hidden // fb):
             cols = slice(f * fb, (f + 1) * fb)
             d = dg(held, wd[cols, :], NT) * flat(dup[:, at, cols]).astype(F32)
             dup[:, at, cols] = d.astype(BF).reshape(size, rc, fb)
 
-        if layer == 0:
-
-            @pl.when(j + 1 < n)
-            def _():
-                gather.relay(j + 1)
+        @pl.when(j + 1 < n)
+        def _():
+            gather.relay(j + 1)
 
         @pl.when(j > 0)
         def _():
@@ -1373,13 +1364,11 @@
         gain_out[...] += dgain
 
     run(n, last)
-    if layer == 1:
-        local, side = y_copies(ys[0], ys[1], 1 - section)
-        local.wait()
-        side.wait_recv()
-        y_copies(ys[0], ys[1], section)[1].wait_send()
-    if layer == 0:
-        gather.drain(n)
+    local, side = y_copies(ys[0], ys[1], 1 - section)
+    local.wait()
+    side.wait_recv()
+    y_copies(ys[0], ys[1], section)[1].wait_send()
+    gather.drain(n)
     scatter.drain(n)
 
 
@@ -1396,9 +1385,9 @@
             shape((parts, depth, hidden), BF),
             shape((parts, hidden, depth), BF),
         ]
-        + [shape((2, rows, width), BF)] * (len(extra) // 3),
+        + [shape((2, rows, width), BF)] * (len(extra) // 2),
         in_specs=[VM, VM, VM] + [HB] * (5 + len(extra)),
-        out_specs=[VM, VM, VM, VM] + [HB] * (len(extra) // 3),
+        out_specs=[VM, VM, VM, VM] + [HB] * (len(extra) // 2),
         scratch_shapes=[
             pltpu.VMEM((size, rows, width), BF),
             pltpu.VMEM((size, rows, width), BF),
@@ -1410,7 +1399,7 @@
         ]
         + comm_sems(size, n)
         + scatter_scratch(size, rows, width, n)
-        + [DMA((4,)), pltpu.VMEM((rows, width), BF)] * (len(extra) // 3),
+        + [DMA((4,)), pltpu.VMEM((rows, width), BF)] * (len(extra) // 2),
         compiler_params=params(6 + layer),
         cost_estimate=cost(60e9, 40e6),
     )(grad, h1, gains, a2, hid, slope, wu, wd, *extra)
@@ -1421,15 +1410,21 @@
     refs = refs[7:]
     if layer == 0:
         gdown_ref, refs = refs[0], refs[1:]
+    else:
+        hid_ref, wd_ref, h1_in, refs = refs[0], refs[1], refs[2], refs[3:]
     dqkv_ref, gout_ref, refs = refs[0], refs[1], refs[2:]
     if layer == 0:
         down_out, refs = refs[0], refs[1:]
+    else:
+        y_ref, refs = refs[0], refs[1:]
     da, ka, va, kt, dk, dv, w, w_sem = refs[:8]
     sems, refs = refs[8:12], refs[12:]
     reduce = Reduce(layer, refs[:9])
     if layer == 0:
         down = HalfReduce(layer, refs[9 : 9 + HALF])
         down_swap = HalfSwap(gdown_ref, down.other, refs[9 + HALF])
+    else:
+        held_hid, wd, h1, y_sem = refs[9:13]
     _, rows, wide = qkv_ref.shape
     length = size * rows
     e = qm_ref.shape[2]
@@ -1448,6 +1443,14 @@
     g.greet(parts)
     gather = Gather(g, da, rc, sems)
     loads = []
+    if layer == 1:
+        scatter = Scatter(g, rc, refs[13:])
+        loads = [
+            pltpu.make_async_copy(wd_ref, wd, y_sem.at[0]),
+            pltpu.make_async_copy(h1_in, h1, y_sem.at[1]),
+        ]
+        for load in loads:
+            load.start()
     if layer == 0:
         down_swap.copy().start()
         loads = down.loads(gdown_ref, None)
@@ -1495,6 +1498,9 @@
                 gather.ready(i)
             reduce.send(out_grad)
 
+        if layer == 1:
+            hid_load = pltpu.make_async_copy(hid_ref.at[:, at], held_hid, y_sem.at[2])
+            hid_load.start()
         qm = flat(qm_ref[:, at, :])
         dctx = dg(flat(da[:, at, :]), w[...], NT).astype(BF)
         ctx = flat(ctx_ref[:, at, :])
@@ -1529,6 +1535,12 @@
                     down_swap.copy().wait_recv()
                     down.middle()
 
+            if layer == 1 and h == heads // 2:
+
+                @pl.when(j > 0)
+                def _():
+                    scatter.second(j - 1)
+
             if layer == 0 and h == heads - 1:
 
                 @pl.when(j == n - 1)
@@ -1536,14 +1548,33 @@
                     down.late()
 
             dqkv_ref[:, at, o : o + e] = (dqt * scale).T.astype(BF).reshape(size, rc, e)
+        if layer == 1:
+            hid_load.wait()
+            width = wd.shape[1]
+            for f in range(width // 256):
+                cols = slice(f * 256, (f + 1) * 256)
+                scatter.part[:, at, cols] = dg(flat(held_hid[...]), wd[:, cols], NN).reshape(
+                    size, rc, 256
+                )
+            scatter.first(j)
 
     run(n, work)
+    if layer == 1:
+        scatter.second(n - 1)
     for h in range(heads):
         o = 3 * e * h
         dqkv_ref[:, :, o + e : o + 2 * e] = (dk[h] * scale).astype(BF).reshape(size, rows, e)
         dqkv_ref[:, :, o + 2 * e : o + 3 * e] = dv[h].astype(BF).reshape(size, rows, e)
 
     reduce.collect()
+    if layer == 1:
+
+        def output(j):
+            at = span(j, rc)
+            y_ref[at, :] = (h1[at, :] + scatter.third(j)).astype(BF)
+
+        run(n, output)
+        scatter.drain(n)
     reduce.finish(gout_ref)
     if layer == 0:
         down.finish(down_out)
@@ -1551,7 +1582,7 @@
     gather.drain(n)
 
 
-def attend_backward(size, replicas, layer, mid, qkv, qm, km, ctx, lse, w, grads):
+def attend_backward(size, replicas, layer, mid, qkv, qm, km, ctx, lse, w, grads, more=()):
     _, rows, wide = qkv.shape
     e = qm.shape[2]
     heads = wide // (3 * e)
@@ -1562,9 +1593,10 @@
     return pl.pallas_call(
         functools.partial(attend_back_kernel, size, layer, parts),
         out_shape=[shape(qkv.shape, BF), shape((heads * e, depth), F32)]
-        + [shape(grad.shape[1:], F32) for grad in grads],
-        in_specs=[VM] * 6 + [HB] * (1 + len(grads)),
-        out_specs=[VM, VM] + [VM] * len(grads),
+        + [shape(grad.shape[1:], F32) for grad in grads]
+        + [shape((rows, width), BF)] * (len(more) // 3),
+        in_specs=[VM] * 6 + [HB] * (1 + len(grads) + len(more)),
+        out_specs=[VM, VM] + [VM] * (len(grads) + len(more) // 3),
         scratch_shapes=[
             pltpu.VMEM((size, rows, width), BF),
             pltpu.VMEM((heads, length, 2 * e), BF),
@@ -1577,10 +1609,21 @@
         ]
         + comm_sems(size, n)
         + reduce_scratch(parts, heads * e, depth)
-        + sum([half_scratch(parts, *grad.shape[1:]) + [DMA((2,))] for grad in grads], []),
+        + sum([half_scratch(parts, *grad.shape[1:]) + [DMA((2,))] for grad in grads], [])
+        + (
+            [
+                pltpu.VMEM((size, rows // n, more[0].shape[2]), BF),
+                pltpu.VMEM(more[1].shape, BF),
+                pltpu.VMEM((rows, width), F32),
+                DMA((3,)),
+            ]
+            + scatter_scratch(size, rows, width, n)
+            if more
+            else []
+        ),
         compiler_params=params(8 + layer),
         cost_estimate=cost(90e9, 40e6),
-    )(mid, qkv, qm, km, ctx, lse, w, *grads)
+    )(mid, qkv, qm, km, ctx, lse, w, *grads, *more)
 
 
 def qkv_back_kernel(
@@ -1924,8 +1967,7 @@
     h1, ctx, lse, grad_all, w_down_1 = attend(
         size, replicas, 1, qkv, qm, km, y0, w_out_1, [(h_down, "spread", 1, True)], [grad]
     )
-    y1, a2, hid, slope = mlp_forward(size, replicas, 1, h1, gains, w_up_1, w_down_1, [])
-    kept.append((y0, a1, qkv, ctx, lse, h1, a2, hid, slope))
+    kept.append((y0, a1, qkv, ctx, lse, h1))
     weights = [
         (w_qkv_0, w_out_0, w_up_0, w_down_0),
         (w_qkv_1, w_out_1, w_up_1, w_down_1),
@@ -1933,12 +1975,12 @@
     def reduce_rows(value):
         return lax.psum_scatter(value, "dp", scatter_dimension=0, tiled=False)
 
-    x, a1, qkv, ctx, lse, h1, a2, hid, slope = kept[1]
+    x, a1, qkv, ctx, lse, h1 = kept[1]
     w_qkv, w_out, w_up, w_down = weights[1]
-    mid, gain_two, g_up, g_down, layer_out = mlp_backward(
-        size, replicas, 1, grad, h1, gains, a2, hid, slope, w_up, w_down, [y0, y1, grad_all]
+    mid, gain_two, g_up, g_down, hid = peak(size, replicas, h1, gains, grad_all, w_up, w_down)
+    d_qkv, out_1, y1 = attend_backward(
+        size, replicas, 1, mid, qkv, qm, km, ctx, lse, w_out, [], [hid, w_down, h1]
     )
-    d_qkv, out_1 = attend_backward(size, replicas, 1, mid, qkv, qm, km, ctx, lse, w_out, [])
     up_1, down_1 = reduce_rows(g_up), reduce_rows(g_down)
     dx1, gain_one, g_qkv = qkv_backward(size, replicas, 1, d_qkv, a1, x, mid, gains, w_qkv)
     gains_above = jnp.concatenate([gain_one, gain_two], axis=0)
@@ -1947,8 +1989,8 @@
 
     x, a1, qkv, ctx, lse, h1, a2, hid, slope = kept[0]
     w_qkv, w_out, w_up, w_down = weights[0]
-    mid, gain_two, g_up, g_down = mlp_backward(
-        size, replicas, 0, dx1, h1, gains, a2, hid, slope, w_up, w_down, []
+    mid, gain_two, g_up, g_down, layer_out = mlp_backward(
+        size, replicas, 0, dx1, h1, gains, a2, hid, slope, w_up, w_down, [y0, y1]
     )
     mid, qkv_1 = lax.optimization_barrier((mid, qkv_1))
     d_qkv, out_0, down_0 = attend_backward(

time: 704 us -> 677 us (0.962)
  Pallas kernels: 650 us -> 624 us
    pallas_call x2 -> x1, Pallas kernels: 92.7 us -> 53.7 us  [mlp_backward(): pl.pallas_call(functools.partial(mlp_back_kernel, size, layer, parts), ou...]
    pallas_call x2, Pallas kernels: 154 us -> 166 us  [attend_backward(): pl.pallas_call(functools.partial(attend_back_kernel, size, layer, parts),...]
  transfers between devices with their start and end apart: 7 -> 7, of which waited for: 0 -> 0; matrix products, arithmetic and copies ran while one was open for 1% -> 2% of each run, Pallas kernels for 44% -> 47%
where the time goes in v13:
time: 677 us; the launch traced here: 668 us
  Pallas kernels  624 us (92%)
  other arithmetic  15.5 us (2%)
  between operations  14.3 us (2%)
  local copies, waits for them, and re-layouts  10.6 us (2%)
    pallas_call x2, Pallas kernels, attend_backward(): pl.pallas_call(functools.partial(attend_back_kernel, size, layer, parts),...  166 us
    pallas_call x2, Pallas kernels, attend(): pl.pallas_call(functools.partial(attend_kernel, size, layer, columns), ou...  114 us
    pallas_call x1, Pallas kernels, turn_forward(): pl.pallas_call(functools.partial(turn_kernel, size, columns), out_shape=[...  85.1 us
    pallas_call x1, Pallas kernels, last_backward(): pl.pallas_call(functools.partial(last_kernel, size, replicas), out_shape=...  63.6 us
    pallas_call x1, Pallas kernels, first_forward(): pl.pallas_call(functools.partial(first_kernel, size, replicas), out_shape...  56.8 us
    pallas_call x1, Pallas kernels, mlp_backward(): pl.pallas_call(functools.partial(mlp_back_kernel, size, layer, parts), ou...  53.7 us
    pallas_call x1, Pallas kernels, peak(): pl.pallas_call(functools.partial(peak_kernel, size, replicas), out_shape=...  52.3 us
    pallas_call x1, Pallas kernels, qkv_backward(): pl.pallas_call(functools.partial(qkv_back_kernel, size, layer, parts), ou...  32.6 us
  transfers between devices with their start and end apart: 7, of which 0 were waited for; matrix products, arithmetic and copies ran while one was open for 2% of the time, Pallas kernels for 47%

profile of v13, /device:TPU:0, one launch (start us, length us, event | category | flops | bytes accessed | tf_op | source)
XLA Modules:
  0.0 667.6 jit_solution(15763985492315960053)
XLA Ops:
  7.2 0.0 copy-start
  7.2 0.0 copy-start.5
  7.2 0.0 reduce-scatter.5.cloned.1.call-start
  7.3 0.0 copy-start.6
  7.3 1.3 convert_element_type.55
  8.6 0.1 convert_element_type.56
  8.7 0.0 copy-start.9
  8.7 1.1 copy.19.wq_ref
  9.8 0.0 copy-done.5
  9.8 0.9 convert_element_type.59
  10.7 0.0 copy-done.6
  10.7 0.8 convert_element_type.61
  11.5 0.0 copy-done.9
  11.5 0.7 convert_element_type.57
  12.2 0.0 copy-done
  12.2 0.0 copy-start.12
  12.2 0.0 copy-start.13
  12.2 3.0 dynamic-slice_bitcast_fusion
  15.3 0.1 pad.4.clone
  15.4 1.2 select_convert_fusion
  16.6 0.0 copy-done.12
  16.6 0.0 copy-done.13
  16.6 0.7 maximum_maximum_fusion.gain_ref
  17.3 56.8 %shard_map.152 = (bf16[4,512,768]{2,1,0:T(8,128)(2,1)}, f32[2,8,1024]{2,1,0:T(8,128)}, bf16[4,512,1024]{2,1,0:T(8,128)(2,1)}, bf16[1024,768]{1,0:T(8,128)(2,1)},...) custom-call(bf16[512,1024]{1,0:T(8,128)(2,1)} %get-tuple-element.135, ...), custom_call_target="tpu_custom_call" | custom-call | flops 30000001024 | bytes 30000000 | tf_op jit(solution)/shard_map/pallas_call | solution.py:777
  74.1 60.5 %shard_map.153 = (f32[512,1024]{1,0:T(8,128)}, bf16[4,512,256]{2,1,0:T(8,128)(2,1)}, f32[4,4,512]{2,1,0:T(4,128)}, bf16[1024,1024]{1,0:T(8,128)(2,1)}, bf16[1024,1024]{1,0:T(8,128)(2,1)}) custom-call(bf16[4,512,768]{2,1,0:T(8,128)(2,1)} %get-tuple-element.65.refs_0_.refs_1_, bf16[4,512,64]{2,1,0:T(8,128)(2,1)} %get-tuple-element.133.refs_1_.refs_2_, ...), custom_call_target="tpu_custom_call" | custom-call | flops 60000002048 | bytes 20000000 | tf_op jit(solution)/shard_map/pallas_call | solution.py:918
  134.6 85.1 %shard_map.154 = (bf16[512,1024]{1,0:T(8,128)(2,1)}, bf16[4,512,768]{2,1,0:T(8,128)(2,1)}, bf16[4,512,1024]{2,1,0:T(8,128)(2,1)}, bf16[4,512,1024]{2,1,0:T(8,128...) custom-call(f32[512,1024]{1,0:T(8,128)} %get-tuple-element.69.refs_0, ...), custom_call_target="tpu_custom_call" | custom-call | flops 49999998976 | bytes 30000000 | tf_op jit(solution)/shard_map/pallas_call | solution.py:1216
  219.7 53.7 %shard_map.155 = (f32[512,1024]{1,0:T(8,128)}, bf16[4,512,256]{2,1,0:T(8,128)(2,1)}, f32[4,4,512]{2,1,0:T(4,128)}, bf16[4,512,1024]{2,1,0:T(8,128)(2,1)}, bf16[1024,1024]{1,0:T(8,128)(2,1)}) custom-call(bf16[4,512,768]{2,1,0:T(8,128)(2,1)} %get-tuple-element.75.refs_0_.refs_1_, bf16[4,512,64]{2,1,0:T(8,128)(2,1)} %get-tuple-element.133.refs_1_.refs_2_, ...), custom_call_target="tpu_custom_call" | custom-call | flops 60000002048 | bytes 20000000 | tf_op jit(solution)/shard_map/pallas_call | solution.py:918
  273.4 52.3 %shard_map.156 = (f32[512,1024]{1,0:T(8,128)}, f32[1,1024]{1,0:T(1,128)}, bf16[4,256,1024]{2,1,0:T(8,128)(2,1)}, bf16[4,1024,256]{2,1,0:T(8,128)(2,1)}, bf16[4,512,1024]{2,1,0:T(8,128)(2,1)}) custom-call(f32[512,1024]{1,0:T(8,128)} %get-tuple-element.78.h1_ref.refs_9_, f32[2,8,1024]{2,1,0:T(8,128)} %get-tuple-element.70.refs_1_.gain_ref.refs_2_, ...), custom_call_target="tpu_custom_call" | custom-call | flops 60000002048 | bytes 30000000 | tf_op jit(solution)/shard_map/pallas_call | solution.py:1042
  325.7 0.0 reduce-scatter.5.cloned.1.call-update
  325.7 0.0 reduce-scatter.7.cloned.1.call-start
  325.7 0.7 reduce-scatter.7.cloned.1.call-update
  326.4 0.0 reduce-scatter.9.cloned.1.call-start
  326.5 84.0 %shard_map.157 = (bf16[4,512,768]{2,1,0:T(8,128)(2,1)}, f32[256,256]{1,0:T(8,128)}, bf16[512,1024]{1,0:T(8,128)(2,1)}) custom-call(f32[512,1024]{1,0:T(8,128)} %get-tuple-element.82.refs_0_.mid_in, bf16[4,512,768]{2,1,0:T(8,128)(2,1)} %get-tuple-element.75.refs_0_.refs_1_, bf16[4,512,64]{2,1,0:T(8,128)(2,1)} %get-tuple-element.133.refs_1_.refs_2_, ...), custom_call_target="tpu_custom_call" | custom-call | flops 89999998976 | bytes 40000000 | tf_op jit(solution)/shard_map/pallas_call | solution.py:1593
  410.4 0.0 copy-start.11
  410.5 32.6 %shard_map.158 = (bf16[512,1024]{1,0:T(8,128)(2,1)}, f32[1,1024]{1,0:T(1,128)}, bf16[4,256,768]{2,1,0:T(8,128)(2,1)}) custom-call(bf16[4,512,768]{2,1,0:T(8,128)(2,1)} %get-tuple-element.86.dqkv_ref, f32[2,8,1024]{2,1,0:T(8,128)} %get-tuple-element.70.refs_1_.gain_ref.refs_2_, bf16[4,512,1024]{2,1,0:T(8,128)(2,1)} %get-tuple-element.87.a1_in, ...), custom_call_target="tpu_custom_call" | custom-call | flops 30000001024 | bytes 30000000 | tf_op jit(solution)/shard_map/pallas_call | solution.py:1696
  443.1 0.0 reduce-scatter.9.cloned.1.call-update
  443.1 0.0 reduce-scatter.11.cloned.1.call-start
  443.2 1.3 pad_maximum_fusion.above_ref
  444.5 53.7 %shard_map.159 = (f32[512,1024]{1,0:T(8,128)}, f32[1,1024]{1,0:T(1,128)}, bf16[4,256,1024]{2,1,0:T(8,128)(2,1)}, bf16[4,1024,256]{2,1,0:T(8,128)(2,1)}, bf16[2,512,1024]{2,1,0:T(8,128)(2,1)}) custom-call(bf16[512,1024]{1,0:T(8,128)(2,1)} %get-tuple-element.92.refs_0_.dx1_ref, f32[512,1024]{1,0:T(8,128)} %get-tuple-element.69.refs_0_.refs_1_, ...), custom_call_target="tpu_custom_call" | custom-call | flops 60000002048 | bytes 40000000 | tf_op jit(solution)/shard_map/pallas_call | solution.py:1380
  498.2 0.0 reduce-scatter.9.cloned.1.call-done
  498.2 0.0 copy-start.8
  498.3 0.0 copy-done.7
  498.3 1.0 collective-permute-start.2
  499.3 0.0 reduce-scatter.11.cloned.1.call-update
  499.3 0.0 copy-done.8
  499.3 1.2 collective-permute-start
  500.5 81.9 %shard_map.160 = (bf16[4,512,768]{2,1,0:T(8,128)(2,1)}, f32[256,256]{1,0:T(8,128)}, f32[1024,256]{1,0:T(8,128)}) custom-call(f32[512,1024]{1,0:T(8,128)} %get-tuple-element.100.refs_0_.mid_ref, bf16[4,512,768]{2,1,0:T(8,128)(2,1)} %get-tuple-element.65.refs_0_.refs_1_, bf16[4,512,64]{2,1,0:T(8,128)(2,1)} %get-tuple-element.133.refs_1_.refs_2_, ...), custom_call_target="tpu_custom_call" | custom-call | flops 89999998976 | bytes 40000000 | tf_op jit(solution)/shard_map/pallas_call | solution.py:1593
  582.4 0.0 copy-start.4
  582.4 0.0 copy-done.10
  582.4 1.7 broadcast_select_fusion.1
  584.1 0.0 collective-permute-done.2
  584.1 2.3 select_bitcast_fusion
  586.5 0.9 broadcast_select_fusion
  587.3 0.0 collective-permute-start.1
  587.3 63.6 %shard_map.161 = (f32[8,1024]{1,0:T(8,128)}, f32[256,768]{1,0:T(8,128)}, bf16[2,512,1024]{2,1,0:T(8,128)(2,1)}) custom-call(bf16[4,512,768]{2,1,0:T(8,128)(2,1)} %get-tuple-element.106.dqkv_ref, bf16[4,512,1024]{2,1,0:T(8,128)(2,1)} %get-tuple-element.107.a1_ref, bf16[512,1024]{1,0:T(8,128)(2,1)} %get-tuple-element.135.x_ref.refs_3_, ...), custom_call_target="tpu_custom_call" | custom-call | flops 40000000000 | bytes 30000000 | tf_op jit(solution)/shard_map/pallas_call | solution.py:1881
  650.9 0.0 collective-permute-done
  650.9 1.2 add_select_fusion
  652.2 1.1 copy.20
  653.3 1.4 constant_dynamic-slice_fusion.1
  654.8 0.0 collective-permute-done.1
  654.8 2.4 add_bitcast_fusion
  657.2 1.3 copy.23
  658.5 1.0 copy-done.3
  659.5 1.3 copy.24
  (16 shorter events, 0.1 us)
Async XLA Ops:
  7.2 5.0 copy-start
  7.2 2.6 copy-start.5
  7.2 437.3 %reduce-scatter.5.cloned.1.call-start = ((), (), s32[]{:S(2)}) async-start(), calls=%async_computation.4 | async-start | bytes 2621440 | tf_op jit(solution)/shard_map/reduce_scatter | solution.py:1976
  7.3 3.4 copy-start.6
  8.7 2.8 copy-start.9
  12.2 4.4 copy-start.12
  12.2 4.4 copy-start.13
  325.7 118.8 %reduce-scatter.7.cloned.1.call-start = ((), (), s32[]{:S(2)}) async-start(), calls=%async_computation.5 | async-start | bytes 2621440 | tf_op jit(solution)/shard_map/reduce_scatter | solution.py:1976
  326.4 171.8 %reduce-scatter.9.cloned.1.call-start = ((), (), s32[]{:S(2)}) async-start(), calls=%async_computation.6 | async-start | bytes 1966080 | tf_op jit(solution)/shard_map/reduce_scatter | solution.py:1976
  410.4 32.7 %copy-start.11 = (f32[1,1024]{1,0:T(1,128)S(1)}, f32[1,1024]{1,0:T(1,128)}, u32[]{:S(2)}) copy-start(f32[1,1024]{1,0:T(1,128)} %get-tuple-element.111) | copy-start | bytes 12292
  443.1 143.3 %reduce-scatter.11.cloned.1.call-start = ((), (), s32[]{:S(2)}) async-start(), calls=%async_computation.7 | async-start | bytes 2621440 | tf_op jit(solution)/shard_map/reduce_scatter | solution.py:1976
  444.5 53.8 %copy-start.7 = (bf16[1,1024,256]{2,1,0:T(8,128)(2,1)S(1)}, bf16[1,1024,256]{2,1,0:T(8,128)(2,1)}, u32[]{:S(2)}) copy-start(bf16[1,1024,256]{2,1,0:T(8,128)(2,1)} %reduce-scatter.7.cloned.1.call-done) | copy-start | bytes 1572868
  498.2 1.0 copy-start.8
  498.3 85.9 %collective-permute-start.2 = (bf16[1024,256]{1,0:T(8,128)(2,1)S(1)}, bf16[1024,256]{1,0:T(8,128)(2,1)S(1)}, u32[]{:S(2)}, u32[]{:S(2)}) collective-permute-start(bf16[1024,256]{1,0:T(8,128)(2,1)S(1)} %bitcast.32), channel_id=1, source_target_pairs={{0,16},{16,0},{1,17},{17,1},{2,18},{18,2},{3,19},{19,3},{4,20},{20... | collective-permute-start | bytes 1572872 | tf_op jit(solution)/shard_map/ppermute | solution.py:1921
  499.3 151.6 %collective-permute-start = (bf16[256,768]{1,0:T(8,128)(2,1)S(1)}, bf16[256,768]{1,0:T(8,128)(2,1)S(1)}, u32[]{:S(2)}, u32[]{:S(2)}) collective-permute-start(bf16[256,768]{1,0:T(8,128)(2,1)S(1)} %bitcast.34), channel_id=1, source_target_pairs={{0,16},{16,0},{1,17},{17,1},{2,18},{18,2},{3,19},{19,3},{4,20},{20... | collective-permute-start | bytes 1179656 | tf_op jit(solution)/shard_map/ppermute | solution.py:1921
  500.5 81.9 %copy-start.10 = (f32[256,256]{1,0:T(8,128)S(1)}, f32[256,256]{1,0:T(8,128)}, u32[]{:S(2)}) copy-start(f32[256,256]{1,0:T(8,128)} %get-tuple-element.117) | copy-start | bytes 786436
  582.4 4.1 copy-start.4
  587.3 67.4 %collective-permute-start.1 = (bf16[256,1024]{1,0:T(8,128)(2,1)}, bf16[256,1024]{1,0:T(8,128)(2,1)}, u32[]{:S(2)}, u32[]{:S(2)}) collective-permute-start(bf16[256,1024]{1,0:T(8,128)(2,1)} %broadcast_select_fusion), channel_id=1, source_target_pairs={{0,16},{16,0},{1,17},{17,1},{2,18},{18,2},{3,19},{19,3},{4,20},{20... | collective-permute-start | bytes 1572872 | tf_op jit(solution)/shard_map/ppermute | solution.py:1921
  652.2 5.0 copy-start.2
  657.2 2.3 copy-start.3
  657.2 3.7 copy-start.1
Sparse Core Ops, SparseCore 0:
  325.8 49.4 reduce-scatter.4
  377.7 44.8 reduce-scatter.6
  443.2 34.4 reduce-scatter.8
  499.4 48.9 reduce-scatter.10

commit v14 on v13

--- a/solution.py
+++ b/solution.py
@@ -611,19 +611,21 @@
         self.replicas = self.all[0].replicas if self.all else 0
 
     def start(self):
-        for one in self.all:
+        for one in self.all[:1]:
             one.start()
 
     def step(self, j, n):
         if not self.all:
             return
         stages = self.replicas // 2
-        for i in range(stages):
-
-            @pl.when(j == n * (i + 1) // stages - 1)
-            def _(i=i):
-                for one in self.all:
-                    one.step(i)
+        turns = len(self.all) * stages
+        for turn in range(turns):
+
+            @pl.when(j == max(n * (turn + 1) // turns - 1, 0))
+            def _(turn=turn):
+                self.all[turn // stages].step(turn % stages)
+                if (turn + 1) % stages == 0 and turn + 1 < turns:
+                    self.all[turn // stages + 1].start()
 
     def finish(self):
         for one in self.all:
@@ -709,9 +711,6 @@
         Spread(q_stage.at[0], w, False, sems[4:9]),
         Spread(o_stage.at[0], wo_out, True, sems[9:14]),
     ]
-    riders = Riders([], [], (), [])
-    riders.all = spreads
-    riders.replicas = replicas
     g.greet(replicas)
 
     def gain_copy(layer):
@@ -735,16 +734,25 @@
     run(n, send)
     swaps[0].arrive()
     swaps[1].arrive()
-    riders.start()
+    for one in spreads:
+        one.start()
+    stages = len(spreads[0].stages)
 
     def relay(j):
         gather.relay(j)
-        riders.step(j, n)
+
+        for i in range(stages):
+
+            @pl.when(j == n * (i + 1) // stages - 1)
+            def _(i=i):
+                for one in spreads:
+                    one.step(i)
 
     run(n, relay)
     swaps[2].start()
     swaps[3].start()
-    riders.finish()
+    for one in spreads:
+        one.finish()
     outs = [
         pltpu.make_async_copy(w, wq_out, own_sem.at[0]),
         pltpu.make_async_copy(a1, a1_out, own_sem.at[1]),
@@ -1153,17 +1161,17 @@
         def _():
             pass_on(j - lag)
 
-        @pl.when(j == n // 2)
+        @pl.when(j == min(1, n - 1))
         def _():
             spread.step(0)
             out_rider.step(0)
-            up_rider.start()
 
         @pl.when(j == n - 1)
         def _():
             for i in range(1, stages):
                 spread.step(i)
                 out_rider.step(i)
+            up_rider.start()
 
     run(n, work)
     scatter.second(n - 1)
@@ -1190,6 +1198,11 @@
         def _():
             onward.relay(j + 1)
 
+        @pl.when(j == n // 2)
+        def _():
+            for i in range(1, stages):
+                up_rider.step(i)
+
         onward.ready(j)
         r = dg(flat(a1[:, at, :]), wq[...], NN).astype(BF)
         qkv_ref[:, at, :] = r.reshape(size, rc, r.shape[1])
@@ -1197,8 +1210,6 @@
     run(n, multiply)
     outs.append(pltpu.make_async_copy(a1, a1_out, out_sem.at[4]))
     outs[4].start()
-    for i in range(1, stages):
-        up_rider.step(i)
     riders.finish()
     gather.drain(n)
     onward.drain(n)

time: 677 us -> 679 us (level)
  no operation moved by 1% of the time
where the time goes in v14:
time: 679 us; the launch traced here: 670 us
  Pallas kernels  626 us (92%)
  other arithmetic  15.5 us (2%)
  between operations  14.3 us (2%)
  local copies, waits for them, and re-layouts  10.6 us (2%)
    pallas_call x2, Pallas kernels, attend_backward(): pl.pallas_call(functools.partial(attend_back_kernel, size, layer, parts),...  167 us
    pallas_call x2, Pallas kernels, attend(): pl.pallas_call(functools.partial(attend_kernel, size, layer, columns), ou...  118 us
    pallas_call x1, Pallas kernels, turn_forward(): pl.pallas_call(functools.partial(turn_kernel, size, columns), out_shape=[...  83.1 us
    pallas_call x1, Pallas kernels, last_backward(): pl.pallas_call(functools.partial(last_kernel, size, replicas), out_shape=...  64 us
    pallas_call x1, Pallas kernels, first_forward(): pl.pallas_call(functools.partial(first_kernel, size, replicas), out_shape...  56.8 us
    pallas_call x1, Pallas kernels, mlp_backward(): pl.pallas_call(functools.partial(mlp_back_kernel, size, layer, parts), ou...  52.8 us
    pallas_call x1, Pallas kernels, peak(): pl.pallas_call(functools.partial(peak_kernel, size, replicas), out_shape=...  51.6 us
    pallas_call x1, Pallas kernels, qkv_backward(): pl.pallas_call(functools.partial(qkv_back_kernel, size, layer, parts), ou...  33.1 us
  transfers between devices with their start and end apart: 7, of which 0 were waited for; matrix products, arithmetic and copies ran while one was open for 2% of the time, Pallas kernels for 47%

profile of v14, /device:TPU:0, one launch (start us, length us, event | category | flops | bytes accessed | tf_op | source)
XLA Modules:
  0.0 669.9 jit_solution(1704880543390873533)
XLA Ops:
  7.2 0.0 copy-start
  7.2 0.0 copy-start.5
  7.2 0.0 reduce-scatter.5.cloned.1.call-start
  7.3 0.0 copy-start.6
  7.3 1.3 convert_element_type.55
  8.6 0.1 convert_element_type.56
  8.7 0.0 copy-start.9
  8.7 1.1 copy.19.wq_ref
  9.8 0.0 copy-done.5
  9.8 0.9 convert_element_type.59
  10.7 0.0 copy-done.6
  10.7 0.8 convert_element_type.61
  11.5 0.0 copy-done.9
  11.5 0.7 convert_element_type.57
  12.2 0.0 copy-done
  12.2 0.0 copy-start.12
  12.2 0.0 copy-start.13
  12.2 3.0 dynamic-slice_bitcast_fusion
  15.3 0.1 pad.4.clone
  15.4 1.2 select_convert_fusion
  16.6 0.0 copy-done.12
  16.6 0.0 copy-done.13
  16.6 0.7 maximum_maximum_fusion.gain_ref
  17.3 56.8 %shard_map.152 = (bf16[4,512,768]{2,1,0:T(8,128)(2,1)}, f32[2,8,1024]{2,1,0:T(8,128)}, bf16[4,512,1024]{2,1,0:T(8,128)(2,1)}, bf16[1024,768]{1,0:T(8,128)(2,1)},...) custom-call(bf16[512,1024]{1,0:T(8,128)(2,1)} %get-tuple-element.135, ...), custom_call_target="tpu_custom_call" | custom-call | flops 30000001024 | bytes 30000000 | tf_op jit(solution)/shard_map/pallas_call | solution.py:785
  74.1 64.8 %shard_map.153 = (f32[512,1024]{1,0:T(8,128)}, bf16[4,512,256]{2,1,0:T(8,128)(2,1)}, f32[4,4,512]{2,1,0:T(4,128)}, bf16[1024,1024]{1,0:T(8,128)(2,1)}, bf16[1024,1024]{1,0:T(8,128)(2,1)}) custom-call(bf16[4,512,768]{2,1,0:T(8,128)(2,1)} %get-tuple-element.65.refs_0_.refs_1_, bf16[4,512,64]{2,1,0:T(8,128)(2,1)} %get-tuple-element.133.refs_1_.refs_2_, ...), custom_call_target="tpu_custom_call" | custom-call | flops 60000002048 | bytes 20000000 | tf_op jit(solution)/shard_map/pallas_call | solution.py:926
  138.9 83.1 %shard_map.154 = (bf16[512,1024]{1,0:T(8,128)(2,1)}, bf16[4,512,768]{2,1,0:T(8,128)(2,1)}, bf16[4,512,1024]{2,1,0:T(8,128)(2,1)}, bf16[4,512,1024]{2,1,0:T(8,128...) custom-call(f32[512,1024]{1,0:T(8,128)} %get-tuple-element.69.refs_0, ...), custom_call_target="tpu_custom_call" | custom-call | flops 49999998976 | bytes 30000000 | tf_op jit(solution)/shard_map/pallas_call | solution.py:1227
  221.9 53.6 %shard_map.155 = (f32[512,1024]{1,0:T(8,128)}, bf16[4,512,256]{2,1,0:T(8,128)(2,1)}, f32[4,4,512]{2,1,0:T(4,128)}, bf16[4,512,1024]{2,1,0:T(8,128)(2,1)}, bf16[1024,1024]{1,0:T(8,128)(2,1)}) custom-call(bf16[4,512,768]{2,1,0:T(8,128)(2,1)} %get-tuple-element.75.refs_0_.refs_1_, bf16[4,512,64]{2,1,0:T(8,128)(2,1)} %get-tuple-element.133.refs_1_.refs_2_, ...), custom_call_target="tpu_custom_call" | custom-call | flops 60000002048 | bytes 20000000 | tf_op jit(solution)/shard_map/pallas_call | solution.py:926
  275.6 51.6 %shard_map.156 = (f32[512,1024]{1,0:T(8,128)}, f32[1,1024]{1,0:T(1,128)}, bf16[4,256,1024]{2,1,0:T(8,128)(2,1)}, bf16[4,1024,256]{2,1,0:T(8,128)(2,1)}, bf16[4,512,1024]{2,1,0:T(8,128)(2,1)}) custom-call(f32[512,1024]{1,0:T(8,128)} %get-tuple-element.78.h1_ref.refs_9_, f32[2,8,1024]{2,1,0:T(8,128)} %get-tuple-element.70.refs_1_.gain_ref.refs_2_, ...), custom_call_target="tpu_custom_call" | custom-call | flops 60000002048 | bytes 30000000 | tf_op jit(solution)/shard_map/pallas_call | solution.py:1050
  327.2 0.0 reduce-scatter.5.cloned.1.call-update
  327.2 0.0 reduce-scatter.7.cloned.1.call-start
  327.3 0.7 reduce-scatter.7.cloned.1.call-update
  328.0 0.0 reduce-scatter.9.cloned.1.call-start
  328.0 84.8 %shard_map.157 = (bf16[4,512,768]{2,1,0:T(8,128)(2,1)}, f32[256,256]{1,0:T(8,128)}, bf16[512,1024]{1,0:T(8,128)(2,1)}) custom-call(f32[512,1024]{1,0:T(8,128)} %get-tuple-element.82.refs_0_.mid_in, bf16[4,512,768]{2,1,0:T(8,128)(2,1)} %get-tuple-element.75.refs_0_.refs_1_, bf16[4,512,64]{2,1,0:T(8,128)(2,1)} %get-tuple-element.133.refs_1_.refs_2_, ...), custom_call_target="tpu_custom_call" | custom-call | flops 89999998976 | bytes 40000000 | tf_op jit(solution)/shard_map/pallas_call | solution.py:1604
  412.9 0.0 copy-start.11
  412.9 33.1 %shard_map.158 = (bf16[512,1024]{1,0:T(8,128)(2,1)}, f32[1,1024]{1,0:T(1,128)}, bf16[4,256,768]{2,1,0:T(8,128)(2,1)}) custom-call(bf16[4,512,768]{2,1,0:T(8,128)(2,1)} %get-tuple-element.86.dqkv_ref, f32[2,8,1024]{2,1,0:T(8,128)} %get-tuple-element.70.refs_1_.gain_ref.refs_2_, bf16[4,512,1024]{2,1,0:T(8,128)(2,1)} %get-tuple-element.87.a1_in, ...), custom_call_target="tpu_custom_call" | custom-call | flops 30000001024 | bytes 30000000 | tf_op jit(solution)/shard_map/pallas_call | solution.py:1707
  446.0 0.0 reduce-scatter.9.cloned.1.call-update
  446.0 0.0 reduce-scatter.11.cloned.1.call-start
  446.1 0.0 copy-done.11
  446.1 1.3 pad_maximum_fusion.above_ref
  447.4 52.8 %shard_map.159 = (f32[512,1024]{1,0:T(8,128)}, f32[1,1024]{1,0:T(1,128)}, bf16[4,256,1024]{2,1,0:T(8,128)(2,1)}, bf16[4,1024,256]{2,1,0:T(8,128)(2,1)}, bf16[2,512,1024]{2,1,0:T(8,128)(2,1)}) custom-call(bf16[512,1024]{1,0:T(8,128)(2,1)} %get-tuple-element.92.refs_0_.dx1_ref, f32[512,1024]{1,0:T(8,128)} %get-tuple-element.69.refs_0_.refs_1_, ...), custom_call_target="tpu_custom_call" | custom-call | flops 60000002048 | bytes 40000000 | tf_op jit(solution)/shard_map/pallas_call | solution.py:1391
  500.2 0.0 reduce-scatter.9.cloned.1.call-done
  500.2 0.0 copy-start.8
  500.3 0.0 copy-done.7
  500.3 1.3 collective-permute-start.2
  501.6 0.0 reduce-scatter.11.cloned.1.call-update
  501.6 0.0 copy-done.8
  501.6 0.9 collective-permute-start
  502.5 81.7 %shard_map.160 = (bf16[4,512,768]{2,1,0:T(8,128)(2,1)}, f32[256,256]{1,0:T(8,128)}, f32[1024,256]{1,0:T(8,128)}) custom-call(f32[512,1024]{1,0:T(8,128)} %get-tuple-element.100.refs_0_.mid_ref, bf16[4,512,768]{2,1,0:T(8,128)(2,1)} %get-tuple-element.65.refs_0_.refs_1_, bf16[4,512,64]{2,1,0:T(8,128)(2,1)} %get-tuple-element.133.refs_1_.refs_2_, ...), custom_call_target="tpu_custom_call" | custom-call | flops 89999998976 | bytes 40000000 | tf_op jit(solution)/shard_map/pallas_call | solution.py:1604
  584.2 1.7 broadcast_select_fusion.1
  585.9 0.0 collective-permute-done.2
  585.9 2.3 select_bitcast_fusion
  588.3 0.0 copy-done.4
  588.3 0.9 broadcast_select_fusion
  589.1 0.0 collective-permute-start.1
  589.1 64.0 %shard_map.161 = (f32[8,1024]{1,0:T(8,128)}, f32[256,768]{1,0:T(8,128)}, bf16[2,512,1024]{2,1,0:T(8,128)(2,1)}) custom-call(bf16[4,512,768]{2,1,0:T(8,128)(2,1)} %get-tuple-element.106.dqkv_ref, bf16[4,512,1024]{2,1,0:T(8,128)(2,1)} %get-tuple-element.107.a1_ref, bf16[512,1024]{1,0:T(8,128)(2,1)} %get-tuple-element.135.x_ref.refs_3_, ...), custom_call_target="tpu_custom_call" | custom-call | flops 40000000000 | bytes 30000000 | tf_op jit(solution)/shard_map/pallas_call | solution.py:1892
  653.2 0.0 collective-permute-done
  653.2 1.2 add_select_fusion
  654.5 1.1 copy.20
  655.6 1.4 constant_dynamic-slice_fusion.1
  657.1 0.0 collective-permute-done.1
  657.1 2.4 add_bitcast_fusion
  659.5 1.3 copy.23
  660.8 1.0 copy-done.3
  661.8 1.3 copy.24
  (16 shorter events, 0.1 us)
Async XLA Ops:
  7.2 5.0 copy-start
  7.2 2.6 copy-start.5
  7.2 440.2 %reduce-scatter.5.cloned.1.call-start = ((), (), s32[]{:S(2)}) async-start(), calls=%async_computation.4 | async-start | bytes 2621440 | tf_op jit(solution)/shard_map/reduce_scatter | solution.py:1987
  7.3 3.4 copy-start.6
  8.7 2.8 copy-start.9
  12.2 4.4 copy-start.12
  12.2 4.4 copy-start.13
  327.2 120.1 %reduce-scatter.7.cloned.1.call-start = ((), (), s32[]{:S(2)}) async-start(), calls=%async_computation.5 | async-start | bytes 2621440 | tf_op jit(solution)/shard_map/reduce_scatter | solution.py:1987
  328.0 172.3 %reduce-scatter.9.cloned.1.call-start = ((), (), s32[]{:S(2)}) async-start(), calls=%async_computation.6 | async-start | bytes 1966080 | tf_op jit(solution)/shard_map/reduce_scatter | solution.py:1987
  412.9 33.2 %copy-start.11 = (f32[1,1024]{1,0:T(1,128)S(1)}, f32[1,1024]{1,0:T(1,128)}, u32[]{:S(2)}) copy-start(f32[1,1024]{1,0:T(1,128)} %get-tuple-element.111) | copy-start | bytes 12292
  446.0 142.3 %reduce-scatter.11.cloned.1.call-start = ((), (), s32[]{:S(2)}) async-start(), calls=%async_computation.7 | async-start | bytes 2621440 | tf_op jit(solution)/shard_map/reduce_scatter | solution.py:1987
  447.4 52.9 %copy-start.7 = (bf16[1,1024,256]{2,1,0:T(8,128)(2,1)S(1)}, bf16[1,1024,256]{2,1,0:T(8,128)(2,1)}, u32[]{:S(2)}) copy-start(bf16[1,1024,256]{2,1,0:T(8,128)(2,1)} %reduce-scatter.7.cloned.1.call-done) | copy-start | bytes 1572868
  500.2 1.4 copy-start.8
  500.3 85.7 %collective-permute-start.2 = (bf16[1024,256]{1,0:T(8,128)(2,1)S(1)}, bf16[1024,256]{1,0:T(8,128)(2,1)S(1)}, u32[]{:S(2)}, u32[]{:S(2)}) collective-permute-start(bf16[1024,256]{1,0:T(8,128)(2,1)S(1)} %bitcast.32), channel_id=1, source_target_pairs={{0,16},{16,0},{1,17},{17,1},{2,18},{18,2},{3,19},{19,3},{4,20},{20... | collective-permute-start | bytes 1572872 | tf_op jit(solution)/shard_map/ppermute | solution.py:1932
  501.6 151.6 %collective-permute-start = (bf16[256,768]{1,0:T(8,128)(2,1)S(1)}, bf16[256,768]{1,0:T(8,128)(2,1)S(1)}, u32[]{:S(2)}, u32[]{:S(2)}) collective-permute-start(bf16[256,768]{1,0:T(8,128)(2,1)S(1)} %bitcast.34), channel_id=1, source_target_pairs={{0,16},{16,0},{1,17},{17,1},{2,18},{18,2},{3,19},{19,3},{4,20},{20... | collective-permute-start | bytes 1179656 | tf_op jit(solution)/shard_map/ppermute | solution.py:1932
  502.5 81.7 %copy-start.10 = (f32[256,256]{1,0:T(8,128)S(1)}, f32[256,256]{1,0:T(8,128)}, u32[]{:S(2)}) copy-start(f32[256,256]{1,0:T(8,128)} %get-tuple-element.117) | copy-start | bytes 786436
  584.2 4.1 copy-start.4
  589.1 67.9 %collective-permute-start.1 = (bf16[256,1024]{1,0:T(8,128)(2,1)}, bf16[256,1024]{1,0:T(8,128)(2,1)}, u32[]{:S(2)}, u32[]{:S(2)}) collective-permute-start(bf16[256,1024]{1,0:T(8,128)(2,1)} %broadcast_select_fusion), channel_id=1, source_target_pairs={{0,16},{16,0},{1,17},{17,1},{2,18},{18,2},{3,19},{19,3},{4,20},{20... | collective-permute-start | bytes 1572872 | tf_op jit(solution)/shard_map/ppermute | solution.py:1932
  654.5 5.0 copy-start.2
  659.5 2.3 copy-start.3
  659.5 3.7 copy-start.1
Sparse Core Ops, SparseCore 0:
  327.3 50.1 reduce-scatter.4
  380.0 44.9 reduce-scatter.6
  446.1 33.6 reduce-scatter.8
  501.7 49.0 reduce-scatter.10

commit v15 on v14

--- a/solution.py
+++ b/solution.py
@@ -611,21 +611,19 @@
         self.replicas = self.all[0].replicas if self.all else 0
 
     def start(self):
-        for one in self.all[:1]:
+        for one in self.all:
             one.start()
 
     def step(self, j, n):
         if not self.all:
             return
         stages = self.replicas // 2
-        turns = len(self.all) * stages
-        for turn in range(turns):
-
-            @pl.when(j == max(n * (turn + 1) // turns - 1, 0))
-            def _(turn=turn):
-                self.all[turn // stages].step(turn % stages)
-                if (turn + 1) % stages == 0 and turn + 1 < turns:
-                    self.all[turn // stages + 1].start()
+        for i in range(stages):
+
+            @pl.when(j == n * (i + 1) // stages - 1)
+            def _(i=i):
+                for one in self.all:
+                    one.step(i)
 
     def finish(self):
         for one in self.all:
@@ -691,8 +689,8 @@
 
 
 def first_kernel(
-    size, replicas, x_ref, gain_ref, wq_ref, wo_ref, wu_ref, wd_ref,
-    qkv_ref, gains_out, a1_out, wq_out, wo_out, q_stage, o_stage, u_stage, d_stage,
+    size, replicas, x_in, gain_ref, wq_ref, wo_ref, wu_ref, wd_ref,
+    qkv_ref, gains_out, x_ref, a1_out, wq_out, wo_out, q_stage, o_stage, u_stage, d_stage,
     a1, w, gains, own_sem, q_sem, o_sem, u_sem, d_sem, gain_sem, *sems
 ):
     rows, width = x_ref.shape
@@ -700,6 +698,8 @@
     rc = rows // n
     g = Group(size)
     section = lax.axis_index("section")
+    x_load = pltpu.make_async_copy(x_in.at[section], x_ref, own_sem.at[2])
+    x_load.start()
     gather = Gather(g, a1, rc, sems[:4])
     swaps = [
         Swap(wq_ref, q_stage, q_sem),
@@ -724,6 +724,7 @@
     gains[section] = gain_ref[...]
     gain_copy(1 - section).wait_recv()
     gains_out[...] = gains[...]
+    x_load.wait()
 
     def send(j):
         at = span(j, rc)
@@ -778,7 +779,7 @@
 
 
 def first_forward(size, replicas, x, gains, ws):
-    rows, width = x.shape
+    _, rows, width = x.shape
     wide = ws[0].shape[2]
     deep = 2 * ws[1].shape[1]
     n = thin_chunks(rows)
@@ -787,18 +788,19 @@
         out_shape=[
             shape((size, rows, wide), BF),
             shape((2,) + gains.shape, F32),
+            shape((rows, width), BF),
             shape((size, rows, width), BF),
             shape((width, wide), BF),
             shape((deep, width), BF),
         ]
         + [shape(w.shape, BF) for w in ws],
-        in_specs=[VM] * 6,
-        out_specs=[VM, VM] + [HB] * 7,
+        in_specs=[HB] + [VM] * 5,
+        out_specs=[VM, VM, VM] + [HB] * 7,
         scratch_shapes=[
             pltpu.VMEM((size, rows, width), BF),
             pltpu.VMEM((width, wide), BF),
             pltpu.VMEM((2,) + gains.shape, F32),
-            DMA((2,)),
+            DMA((3,)),
             DMA((3,)),
             DMA((3,)),
             DMA((3,)),
@@ -827,7 +829,11 @@
     ka, vt, w, w_sem = refs[:4]
     scratch, refs = refs[4:13], refs[13:]
     if layer == 1:
-        cot_sems, cot_sem, refs = refs[:4], refs[4], refs[5:]
+        cot_sems, cot_sem, cot_mine, refs = refs[:4], refs[4], refs[5], refs[6:]
+        cot_load = pltpu.make_async_copy(
+            cot_ref.at[lax.axis_index("section")], cot_mine, cot_sem.at[1]
+        )
+        cot_load.start()
     riders = Riders(halves, wholes, columns, refs)
     _, rows, wide = qkv_ref.shape
     length = size * rows
@@ -845,9 +851,10 @@
     riders.start()
     if layer == 1:
         cot = Gather(g, cot_out, rows, cot_sems)
-        own = pltpu.make_async_copy(cot_ref, cot_out.at[g.me], cot_sem.at[0])
+        own = pltpu.make_async_copy(cot_mine, cot_out.at[g.me], cot_sem.at[0])
+        cot_load.wait()
         own.start()
-        cot.start(0, cot_ref)
+        cot.start(0, cot_mine)
     scatter = Scatter(g, rc, scratch)
     whole = flat(qkv_ref[...])
     for h in range(heads):
@@ -932,7 +939,7 @@
         ]
         + [shape((size, rows, width), BF) for _ in cot]
         + outs,
-        in_specs=[VM, VM, VM, VM, HB] + [VM] * len(cot) + [HB] * len(riders),
+        in_specs=[VM, VM, VM, VM, HB] + [HB] * (len(cot) + len(riders)),
         out_specs=[VM, VM, VM] + [HB] * (len(cot) + len(outs)),
         scratch_shapes=[
             pltpu.VMEM((heads, size * rows, 2 * e), BF),
@@ -941,7 +948,7 @@
             DMA((1,)),
         ]
         + scatter_scratch(size, rows, width, n)
-        + (comm_sems(size, 1) + [DMA((1,))]) * len(cot)
+        + (comm_sems(size, 1) + [DMA((2,)), pltpu.VMEM((rows, width), BF)]) * len(cot)
         + sems,
         compiler_params=params(2 + layer),
         cost_estimate=cost(60e9, 20e6),
@@ -1958,11 +1965,10 @@
         [norm_one_gain, norm_two_gain, jnp.zeros((6, norm_one_gain.shape[1]), F32)], axis=0
     )
     segments = lax.dynamic_index_in_dim(segment_ids, section, 0, keepdims=False)
-    x = lax.dynamic_index_in_dim(block_input, section, 0, keepdims=False)
     head_dim = qkv_weight.shape[3] // 3
     qm, km = scene_masks(segments.reshape((size, -1)), head_dim)
-    qkv, gains, a1, w_qkv_0, w_out_0, h_qkv, h_out, h_up, h_down = first_forward(
-        size, replicas, x, gains, mine
+    qkv, gains, x, a1, w_qkv_0, w_out_0, h_qkv, h_out, h_up, h_down = first_forward(
+        size, replicas, block_input, gains, mine
     )
     h1, ctx, lse, w_up_0, w_down_0 = attend(
         size, replicas, 0, qkv, qm, km, x, w_out_0,
@@ -1974,9 +1980,8 @@
         [(h_out, "spread", 1, True), (h_up, "spread", 1, False)],
     )
     kept = [below + (a2, hid, slope)]
-    grad = lax.dynamic_index_in_dim(cotangent, section, 0, keepdims=False)
     h1, ctx, lse, grad_all, w_down_1 = attend(
-        size, replicas, 1, qkv, qm, km, y0, w_out_1, [(h_down, "spread", 1, True)], [grad]
+        size, replicas, 1, qkv, qm, km, y0, w_out_1, [(h_down, "spread", 1, True)], [cotangent]
     )
     kept.append((y0, a1, qkv, ctx, lse, h1))
     weights = [

time: 679 us -> 669 us (0.985)
  Pallas kernels: 626 us -> 619 us
  transfers between devices with their start and end apart: 7 -> 7, of which waited for: 0 -> 0; matrix products, arithmetic and copies ran while one was open for 2% -> 2% of each run, Pallas kernels for 47% -> 48%
where the time goes in v15:
time: 669 us; the launch traced here: 660 us
  Pallas kernels  619 us (93%)
  other arithmetic  15.5 us (2%)
  between operations  14.2 us (2%)
  local copies, waits for them, and re-layouts  8.85 us (1%)
    pallas_call x2, Pallas kernels, attend_backward(): pl.pallas_call(functools.partial(attend_back_kernel, size, layer, parts),...  165 us
    pallas_call x2, Pallas kernels, attend(): pl.pallas_call(functools.partial(attend_kernel, size, layer, columns), ou...  113 us
    pallas_call x1, Pallas kernels, turn_forward(): pl.pallas_call(functools.partial(turn_kernel, size, columns), out_shape=[...  81 us
    pallas_call x1, Pallas kernels, last_backward(): pl.pallas_call(functools.partial(last_kernel, size, replicas), out_shape=...  64 us
    pallas_call x1, Pallas kernels, first_forward(): pl.pallas_call(functools.partial(first_kernel, size, replicas), out_shape...  56.9 us
    pallas_call x1, Pallas kernels, mlp_backward(): pl.pallas_call(functools.partial(mlp_back_kernel, size, layer, parts), ou...  52.9 us
    pallas_call x1, Pallas kernels, peak(): pl.pallas_call(functools.partial(peak_kernel, size, replicas), out_shape=...  52.6 us
    pallas_call x1, Pallas kernels, qkv_backward(): pl.pallas_call(functools.partial(qkv_back_kernel, size, layer, parts), ou...  33.4 us
  transfers between devices with their start and end apart: 7, of which 0 were waited for; matrix products, arithmetic and copies ran while one was open for 2% of the time, Pallas kernels for 48%

profile of v15, /device:TPU:0, one launch (start us, length us, event | category | flops | bytes accessed | tf_op | source)
XLA Modules:
  0.0 659.8 jit_solution(3405245258770136710)
XLA Ops:
  7.2 0.0 copy-start
  7.2 0.0 copy-start.5
  7.2 0.0 reduce-scatter.5.cloned.1.call-start
  7.3 0.6 copy-done
  7.9 0.0 copy-start.6
  7.9 1.3 convert_element_type.55
  9.2 0.1 convert_element_type.56
  9.3 0.0 copy-start.9
  9.3 1.0 copy.19.wq_ref
  10.4 0.0 copy-done.5
  10.4 0.9 convert_element_type.59
  11.3 0.0 copy-done.6
  11.3 0.8 convert_element_type.61
  12.1 0.0 copy-done.9
  12.1 0.7 convert_element_type.57
  12.8 1.2 select_convert_fusion
  14.0 0.1 pad.4.clone
  14.1 0.0 copy-done.12
  14.1 0.0 copy-done.13
  14.1 0.7 maximum_maximum_fusion.gain_ref
  14.8 56.9 %shard_map.152 = (bf16[4,512,768]{2,1,0:T(8,128)(2,1)}, f32[2,8,1024]{2,1,0:T(8,128)}, bf16[512,1024]{1,0:T(8,128)(2,1)}, bf16[4,512,1024]{2,1,0:T(8,128)(2,1)},...) custom-call(bf16[2,512,1024]{2,1,0:T(8,128)(2,1)} %x_in.1, ...), custom_call_target="tpu_custom_call" | custom-call | flops 30000001024 | bytes 30000000 | tf_op jit(solution)/shard_map/pallas_call | solution.py:786
  71.7 60.4 %shard_map.153 = (f32[512,1024]{1,0:T(8,128)}, bf16[4,512,256]{2,1,0:T(8,128)(2,1)}, f32[4,4,512]{2,1,0:T(4,128)}, bf16[1024,1024]{1,0:T(8,128)(2,1)}, bf16[1024,1024]{1,0:T(8,128)(2,1)}) custom-call(bf16[4,512,768]{2,1,0:T(8,128)(2,1)} %get-tuple-element.66.refs_0_.refs_1_, bf16[4,512,64]{2,1,0:T(8,128)(2,1)} %get-tuple-element.135.refs_1_.refs_2_, ...), custom_call_target="tpu_custom_call" | custom-call | flops 60000002048 | bytes 20000000 | tf_op jit(solution)/shard_map/pallas_call | solution.py:933
  132.1 81.0 %shard_map.154 = (bf16[512,1024]{1,0:T(8,128)(2,1)}, bf16[4,512,768]{2,1,0:T(8,128)(2,1)}, bf16[4,512,1024]{2,1,0:T(8,128)(2,1)}, bf16[4,512,1024]{2,1,0:T(8,128...) custom-call(f32[512,1024]{1,0:T(8,128)} %get-tuple-element.71.refs_0, ...), custom_call_target="tpu_custom_call" | custom-call | flops 49999998976 | bytes 30000000 | tf_op jit(solution)/shard_map/pallas_call | solution.py:1234
  213.2 52.1 %shard_map.155 = (f32[512,1024]{1,0:T(8,128)}, bf16[4,512,256]{2,1,0:T(8,128)(2,1)}, f32[4,4,512]{2,1,0:T(4,128)}, bf16[4,512,1024]{2,1,0:T(8,128)(2,1)}, bf16[1024,1024]{1,0:T(8,128)(2,1)}) custom-call(bf16[4,512,768]{2,1,0:T(8,128)(2,1)} %get-tuple-element.77.refs_0_.refs_1_, bf16[4,512,64]{2,1,0:T(8,128)(2,1)} %get-tuple-element.135.refs_1_.refs_2_, ...), custom_call_target="tpu_custom_call" | custom-call | flops 60000002048 | bytes 20000000 | tf_op jit(solution)/shard_map/pallas_call | solution.py:933
  265.3 52.6 %shard_map.156 = (f32[512,1024]{1,0:T(8,128)}, f32[1,1024]{1,0:T(1,128)}, bf16[4,256,1024]{2,1,0:T(8,128)(2,1)}, bf16[4,1024,256]{2,1,0:T(8,128)(2,1)}, bf16[4,512,1024]{2,1,0:T(8,128)(2,1)}) custom-call(f32[512,1024]{1,0:T(8,128)} %get-tuple-element.80.h1_ref.refs_9_, f32[2,8,1024]{2,1,0:T(8,128)} %get-tuple-element.72.refs_1_.gain_ref.refs_2_, ...), custom_call_target="tpu_custom_call" | custom-call | flops 60000002048 | bytes 30000000 | tf_op jit(solution)/shard_map/pallas_call | solution.py:1057
  318.0 0.0 reduce-scatter.5.cloned.1.call-update
  318.0 0.0 reduce-scatter.7.cloned.1.call-start
  318.0 0.7 reduce-scatter.7.cloned.1.call-update
  318.7 0.0 reduce-scatter.9.cloned.1.call-start
  318.8 83.9 %shard_map.157 = (bf16[4,512,768]{2,1,0:T(8,128)(2,1)}, f32[256,256]{1,0:T(8,128)}, bf16[512,1024]{1,0:T(8,128)(2,1)}) custom-call(f32[512,1024]{1,0:T(8,128)} %get-tuple-element.84.refs_0_.mid_in, bf16[4,512,768]{2,1,0:T(8,128)(2,1)} %get-tuple-element.77.refs_0_.refs_1_, bf16[4,512,64]{2,1,0:T(8,128)(2,1)} %get-tuple-element.135.refs_1_.refs_2_, ...), custom_call_target="tpu_custom_call" | custom-call | flops 89999998976 | bytes 40000000 | tf_op jit(solution)/shard_map/pallas_call | solution.py:1611
  402.7 0.0 copy-start.11
  402.7 33.4 %shard_map.158 = (bf16[512,1024]{1,0:T(8,128)(2,1)}, f32[1,1024]{1,0:T(1,128)}, bf16[4,256,768]{2,1,0:T(8,128)(2,1)}) custom-call(bf16[4,512,768]{2,1,0:T(8,128)(2,1)} %get-tuple-element.88.dqkv_ref, f32[2,8,1024]{2,1,0:T(8,128)} %get-tuple-element.72.refs_1_.gain_ref.refs_2_, bf16[4,512,1024]{2,1,0:T(8,128)(2,1)} %get-tuple-element.89.a1_in, ...), custom_call_target="tpu_custom_call" | custom-call | flops 30000001024 | bytes 30000000 | tf_op jit(solution)/shard_map/pallas_call | solution.py:1714
  436.2 0.0 reduce-scatter.9.cloned.1.call-update
  436.2 0.0 reduce-scatter.11.cloned.1.call-start
  436.3 0.0 copy-done.11
  436.3 1.3 pad_maximum_fusion.above_ref
  437.6 52.9 %shard_map.159 = (f32[512,1024]{1,0:T(8,128)}, f32[1,1024]{1,0:T(1,128)}, bf16[4,256,1024]{2,1,0:T(8,128)(2,1)}, bf16[4,1024,256]{2,1,0:T(8,128)(2,1)}, bf16[2,512,1024]{2,1,0:T(8,128)(2,1)}) custom-call(bf16[512,1024]{1,0:T(8,128)(2,1)} %get-tuple-element.94.refs_0_.dx1_ref, f32[512,1024]{1,0:T(8,128)} %get-tuple-element.71.refs_0_.refs_1_, ...), custom_call_target="tpu_custom_call" | custom-call | flops 60000002048 | bytes 40000000 | tf_op jit(solution)/shard_map/pallas_call | solution.py:1398
  490.5 0.0 reduce-scatter.9.cloned.1.call-done
  490.5 0.0 copy-start.8
  490.6 0.0 copy-done.7
  490.6 0.3 collective-permute-start.2
  490.9 0.0 reduce-scatter.11.cloned.1.call-update
  490.9 0.6 copy-done.8
  491.5 1.2 collective-permute-start
  492.8 81.4 %shard_map.160 = (bf16[4,512,768]{2,1,0:T(8,128)(2,1)}, f32[256,256]{1,0:T(8,128)}, f32[1024,256]{1,0:T(8,128)}) custom-call(f32[512,1024]{1,0:T(8,128)} %get-tuple-element.102.refs_0_.mid_ref, bf16[4,512,768]{2,1,0:T(8,128)(2,1)} %get-tuple-element.66.refs_0_.refs_1_, bf16[4,512,64]{2,1,0:T(8,128)(2,1)} %get-tuple-element.135.refs_1_.refs_2_, ...), custom_call_target="tpu_custom_call" | custom-call | flops 89999998976 | bytes 40000000 | tf_op jit(solution)/shard_map/pallas_call | solution.py:1611
  574.1 0.0 copy-start.4
  574.1 0.0 copy-done.10
  574.1 1.7 broadcast_select_fusion.1
  575.9 0.0 collective-permute-done.2
  575.9 2.3 select_bitcast_fusion
  578.2 0.0 copy-done.4
  578.2 0.9 broadcast_select_fusion
  579.1 0.0 collective-permute-start.1
  579.1 64.0 %shard_map.161 = (f32[8,1024]{1,0:T(8,128)}, f32[256,768]{1,0:T(8,128)}, bf16[2,512,1024]{2,1,0:T(8,128)(2,1)}) custom-call(bf16[4,512,768]{2,1,0:T(8,128)(2,1)} %get-tuple-element.108.dqkv_ref, bf16[4,512,1024]{2,1,0:T(8,128)(2,1)} %get-tuple-element.109.a1_ref, bf16[512,1024]{1,0:T(8,128)(2,1)} %get-tuple-element.67.refs_3_.x_ref, ...), custom_call_target="tpu_custom_call" | custom-call | flops 40000000000 | bytes 30000000 | tf_op jit(solution)/shard_map/pallas_call | solution.py:1899
  643.1 0.0 collective-permute-done
  643.1 1.2 add_select_fusion
  644.4 0.0 copy-start.2
  644.4 1.1 copy.20
  645.5 1.4 constant_dynamic-slice_fusion.1
  647.0 0.0 collective-permute-done.1
  647.0 2.4 add_bitcast_fusion
  649.4 1.3 copy.23
  650.7 1.0 copy-done.3
  651.7 1.3 copy.24
  (15 shorter events, 0.1 us)
Async XLA Ops:
  7.2 0.7 copy-start
  7.2 3.2 copy-start.5
  7.2 430.4 %reduce-scatter.5.cloned.1.call-start = ((), (), s32[]{:S(2)}) async-start(), calls=%async_computation.4 | async-start | bytes 2621440 | tf_op jit(solution)/shard_map/reduce_scatter | solution.py:1992
  7.9 3.3 copy-start.6
  9.3 2.8 copy-start.9
  10.4 3.7 copy-start.12
  10.4 3.7 copy-start.13
  318.0 119.6 %reduce-scatter.7.cloned.1.call-start = ((), (), s32[]{:S(2)}) async-start(), calls=%async_computation.5 | async-start | bytes 2621440 | tf_op jit(solution)/shard_map/reduce_scatter | solution.py:1992
  318.7 171.8 %reduce-scatter.9.cloned.1.call-start = ((), (), s32[]{:S(2)}) async-start(), calls=%async_computation.6 | async-start | bytes 1966080 | tf_op jit(solution)/shard_map/reduce_scatter | solution.py:1992
  402.7 33.5 %copy-start.11 = (f32[1,1024]{1,0:T(1,128)S(1)}, f32[1,1024]{1,0:T(1,128)}, u32[]{:S(2)}) copy-start(f32[1,1024]{1,0:T(1,128)} %get-tuple-element.113) | copy-start | bytes 12292
  436.2 142.0 %reduce-scatter.11.cloned.1.call-start = ((), (), s32[]{:S(2)}) async-start(), calls=%async_computation.7 | async-start | bytes 2621440 | tf_op jit(solution)/shard_map/reduce_scatter | solution.py:1992
  437.6 53.0 %copy-start.7 = (bf16[1,1024,256]{2,1,0:T(8,128)(2,1)S(1)}, bf16[1,1024,256]{2,1,0:T(8,128)(2,1)}, u32[]{:S(2)}) copy-start(bf16[1,1024,256]{2,1,0:T(8,128)(2,1)} %reduce-scatter.7.cloned.1.call-done) | copy-start | bytes 1572868
  490.5 1.0 copy-start.8
  490.6 85.3 %collective-permute-start.2 = (bf16[1024,256]{1,0:T(8,128)(2,1)S(1)}, bf16[1024,256]{1,0:T(8,128)(2,1)S(1)}, u32[]{:S(2)}, u32[]{:S(2)}) collective-permute-start(bf16[1024,256]{1,0:T(8,128)(2,1)S(1)} %bitcast.28), channel_id=1, source_target_pairs={{0,16},{16,0},{1,17},{17,1},{2,18},{18,2},{3,19},{19,3},{4,20},{20... | collective-permute-start | bytes 1572872 | tf_op jit(solution)/shard_map/ppermute | solution.py:1939
  491.5 151.6 %collective-permute-start = (bf16[256,768]{1,0:T(8,128)(2,1)S(1)}, bf16[256,768]{1,0:T(8,128)(2,1)S(1)}, u32[]{:S(2)}, u32[]{:S(2)}) collective-permute-start(bf16[256,768]{1,0:T(8,128)(2,1)S(1)} %bitcast.30), channel_id=1, source_target_pairs={{0,16},{16,0},{1,17},{17,1},{2,18},{18,2},{3,19},{19,3},{4,20},{20... | collective-permute-start | bytes 1179656 | tf_op jit(solution)/shard_map/ppermute | solution.py:1939
  492.8 81.4 %copy-start.10 = (f32[256,256]{1,0:T(8,128)S(1)}, f32[256,256]{1,0:T(8,128)}, u32[]{:S(2)}) copy-start(f32[256,256]{1,0:T(8,128)} %get-tuple-element.119) | copy-start | bytes 786436
  574.1 4.1 copy-start.4
  579.1 67.9 %collective-permute-start.1 = (bf16[256,1024]{1,0:T(8,128)(2,1)}, bf16[256,1024]{1,0:T(8,128)(2,1)}, u32[]{:S(2)}, u32[]{:S(2)}) collective-permute-start(bf16[256,1024]{1,0:T(8,128)(2,1)} %broadcast_select_fusion), channel_id=1, source_target_pairs={{0,16},{16,0},{1,17},{17,1},{2,18},{18,2},{3,19},{19,3},{4,20},{20... | collective-permute-start | bytes 1572872 | tf_op jit(solution)/shard_map/ppermute | solution.py:1939
  644.4 5.0 copy-start.2
  649.4 2.3 copy-start.3
  649.4 3.7 copy-start.1
Sparse Core Ops, SparseCore 0:
  318.1 49.8 reduce-scatter.4
  370.4 44.5 reduce-scatter.6
  436.3 33.6 reduce-scatter.8
  491.0 49.4 reduce-scatter.10

commit v16 on v15

--- a/solution.py
+++ b/solution.py
@@ -1734,8 +1734,8 @@
 
 
 def last_kernel(
-    size, parts, dqkv_ref, a1_ref, x_ref, mid_ref, gain_ref, w_ref, two_ref, above_ref, dx1_ref,
-    gain_out, gqkv_out, dx_out,
+    size, parts, dqkv_ref, a1_ref, x_ref, mid_ref, gain_ref, w_ref, two_ref, up_one_ref, up_two_ref, dx1_ref,
+    one_out, two_out, gqkv_out, dx_out,
     gqkv, swap_sem, w, dx, gsum, gcame, w_sem, x_sem, x_send, x_recv, g_send, g_recv, *scratch
 ):
     rows, width = x_ref.shape
@@ -1835,7 +1835,8 @@
 
     run(n, rest)
     gsum[0, 1:2, :] = two_ref[...]
-    gsum[0, 2:4, :] = above_ref[...]
+    gsum[0, 2:3, :] = up_one_ref[...]
+    gsum[0, 3:4, :] = up_two_ref[...]
 
     targets = [
         [{"tensor": g.sibling}],
@@ -1867,7 +1868,9 @@
     reduce.late()
     exchange(2)
     exchange(3)
-    gain_out[...] = gsum[4]
+    lower_layer = section == 0
+    one_out[...] = jnp.where(lower_layer, gsum[4, 0:1, :], gsum[4, 2:3, :])
+    two_out[...] = jnp.where(lower_layer, gsum[4, 1:2, :], gsum[4, 3:4, :])
 
     @pl.when(section == 0)
     def _():
@@ -1890,7 +1893,7 @@
     scatter.drain(n)
 
 
-def last_backward(size, replicas, dqkv, a1, x, mid, gains, w, two, above, dx1):
+def last_backward(size, replicas, dqkv, a1, x, mid, gains, w, two, up_one, up_two, dx1):
     rows, width = x.shape
     wide = w.shape[1]
     depth = width // replicas
@@ -1899,12 +1902,13 @@
     return pl.pallas_call(
         functools.partial(last_kernel, size, replicas),
         out_shape=(
-            shape((8, width), F32),
+            shape((1, width), F32),
+            shape((1, width), F32),
             shape((depth, wide), F32),
             shape((2, rows, width), BF),
         ),
-        in_specs=[VM] * 5 + [HB, VM, VM, VM],
-        out_specs=(VM, VM, HB),
+        in_specs=[VM] * 5 + [HB, VM, VM, VM, VM],
+        out_specs=(VM, VM, VM, HB),
         scratch_shapes=[
             pltpu.VMEM((replicas, depth, wide), BF),
             DMA((2,)),
@@ -1923,7 +1927,7 @@
         + scatter_scratch(size, rows, width, n),
         compiler_params=params(10),
         cost_estimate=cost(40e9, 30e6),
-    )(dqkv, a1, x, mid, gains, w, two, above, dx1)
+    )(dqkv, a1, x, mid, gains, w, two, up_one, up_two, dx1)
 
 
 def scene_masks(segments, e):
@@ -1999,7 +2003,7 @@
     )
     up_1, down_1 = reduce_rows(g_up), reduce_rows(g_down)
     dx1, gain_one, g_qkv = qkv_backward(size, replicas, 1, d_qkv, a1, x, mid, gains, w_qkv)
-    gains_above = jnp.concatenate([gain_one, gain_two], axis=0)
+    up_one, up_two = gain_one, gain_two
     dx1, up_1, down_1 = lax.optimization_barrier((dx1, up_1, down_1))
     qkv_1 = reduce_rows(g_qkv)
 
@@ -2014,8 +2018,8 @@
     )
     up_0 = reduce_rows(g_up)
     d_qkv, up_0 = lax.optimization_barrier((d_qkv, up_0))
-    gains, qkv_0, input_out = last_backward(
-        size, replicas, d_qkv, a1, x, mid, gains, w_qkv, gain_two, gains_above, dx1
+    one_grad, two_grad, qkv_0, input_out = last_backward(
+        size, replicas, d_qkv, a1, x, mid, gains, w_qkv, gain_two, up_one, up_two, dx1
     )
 
     def finish(zero, one):
@@ -2028,14 +2032,13 @@
     up_grad = finish(up_0, up_1)
     other_down_1 = swap_section(down_1)
     down_grad = jnp.where(section == 0, down_0, down_1.astype(F32) + other_down_1.astype(F32))
-    gains = lax.dynamic_slice_in_dim(gains, 2 * section, 2, 0)
     return (
         layer_out[None],
         input_out[None],
-        gains[0:1],
+        one_grad,
         qkv_grad.reshape(qkv_weight.shape),
         out_grad.reshape(out_weight.shape),
-        gains[1:2],
+        two_grad,
         up_grad[None],
         down_grad[None],
     )

time: 669 us -> 667 us (level)
  transfers between devices with their start and end apart: 7 -> 7, of which waited for: 0 -> 0; matrix products, arithmetic and copies ran while one was open for 2% -> 1% of each run, Pallas kernels for 48% -> 48%
where the time goes in v16:
time: 667 us; the launch traced here: 659 us
  Pallas kernels  617 us (93%)
  other arithmetic  15.1 us (2%)
  between operations  14.2 us (2%)
  local copies, waits for them, and re-layouts  8.96 us (1%)
    pallas_call x2, Pallas kernels, attend_backward(): pl.pallas_call(functools.partial(attend_back_kernel, size, layer, parts),...  165 us
    pallas_call x2, Pallas kernels, attend(): pl.pallas_call(functools.partial(attend_kernel, size, layer, columns), ou...  113 us
    pallas_call x1, Pallas kernels, turn_forward(): pl.pallas_call(functools.partial(turn_kernel, size, columns), out_shape=[...  81 us
    pallas_call x1, Pallas kernels, last_backward(): pl.pallas_call(functools.partial(last_kernel, size, replicas), out_shape=...  62.5 us
    pallas_call x1, Pallas kernels, first_forward(): pl.pallas_call(functools.partial(first_kernel, size, replicas), out_shape...  56.9 us
    pallas_call x1, Pallas kernels, mlp_backward(): pl.pallas_call(functools.partial(mlp_back_kernel, size, layer, parts), ou...  52.9 us
    pallas_call x1, Pallas kernels, peak(): pl.pallas_call(functools.partial(peak_kernel, size, replicas), out_shape=...  52.6 us
    pallas_call x1, Pallas kernels, qkv_backward(): pl.pallas_call(functools.partial(qkv_back_kernel, size, layer, parts), ou...  33.4 us
  transfers between devices with their start and end apart: 7, of which 0 were waited for; matrix products, arithmetic and copies ran while one was open for 1% of the time, Pallas kernels for 48%

profile of v16, /device:TPU:0, one launch (start us, length us, event | category | flops | bytes accessed | tf_op | source)
XLA Modules:
  0.0 658.6 jit_solution(7554998393878272631)
XLA Ops:
  7.2 0.0 copy-start
  7.2 0.0 copy-start.5
  7.2 0.0 reduce-scatter.5.cloned.1.call-start
  7.3 0.6 copy-done
  7.9 1.6 convert_element_type.57
  9.6 1.3 convert_element_type.55
  10.8 0.1 convert_element_type.56
  10.9 1.0 copy.19.wq_ref
  12.0 0.0 copy-done.5
  12.0 0.9 convert_element_type.59
  12.9 0.0 copy-done.6
  12.9 0.8 convert_element_type.61
  13.7 0.1 pad.2.clone
  13.8 1.2 select_convert_fusion
  15.0 0.0 copy-done.12
  15.0 0.0 copy-done.13
  15.0 0.7 maximum_maximum_fusion.gain_ref
  15.7 56.9 %shard_map.152 = (bf16[4,512,768]{2,1,0:T(8,128)(2,1)}, f32[2,8,1024]{2,1,0:T(8,128)}, bf16[512,1024]{1,0:T(8,128)(2,1)}, bf16[4,512,1024]{2,1,0:T(8,128)(2,1)},...) custom-call(bf16[2,512,1024]{2,1,0:T(8,128)(2,1)} %x_in.1, ...), custom_call_target="tpu_custom_call" | custom-call | flops 30000001024 | bytes 30000000 | tf_op jit(solution)/shard_map/pallas_call | solution.py:786
  72.6 60.4 %shard_map.153 = (f32[512,1024]{1,0:T(8,128)}, bf16[4,512,256]{2,1,0:T(8,128)(2,1)}, f32[4,4,512]{2,1,0:T(4,128)}, bf16[1024,1024]{1,0:T(8,128)(2,1)}, bf16[1024,1024]{1,0:T(8,128)(2,1)}) custom-call(bf16[4,512,768]{2,1,0:T(8,128)(2,1)} %get-tuple-element.67.refs_0_.refs_1_, bf16[4,512,64]{2,1,0:T(8,128)(2,1)} %get-tuple-element.135.refs_1_.refs_2_, ...), custom_call_target="tpu_custom_call" | custom-call | flops 60000002048 | bytes 20000000 | tf_op jit(solution)/shard_map/pallas_call | solution.py:933
  133.1 81.0 %shard_map.154 = (bf16[512,1024]{1,0:T(8,128)(2,1)}, bf16[4,512,768]{2,1,0:T(8,128)(2,1)}, bf16[4,512,1024]{2,1,0:T(8,128)(2,1)}, bf16[4,512,1024]{2,1,0:T(8,128...) custom-call(f32[512,1024]{1,0:T(8,128)} %get-tuple-element.72.refs_0, ...), custom_call_target="tpu_custom_call" | custom-call | flops 49999998976 | bytes 30000000 | tf_op jit(solution)/shard_map/pallas_call | solution.py:1234
  214.1 52.1 %shard_map.155 = (f32[512,1024]{1,0:T(8,128)}, bf16[4,512,256]{2,1,0:T(8,128)(2,1)}, f32[4,4,512]{2,1,0:T(4,128)}, bf16[4,512,1024]{2,1,0:T(8,128)(2,1)}, bf16[1024,1024]{1,0:T(8,128)(2,1)}) custom-call(bf16[4,512,768]{2,1,0:T(8,128)(2,1)} %get-tuple-element.78.refs_0_.refs_1_, bf16[4,512,64]{2,1,0:T(8,128)(2,1)} %get-tuple-element.135.refs_1_.refs_2_, ...), custom_call_target="tpu_custom_call" | custom-call | flops 60000002048 | bytes 20000000 | tf_op jit(solution)/shard_map/pallas_call | solution.py:933
  266.2 52.6 %shard_map.156 = (f32[512,1024]{1,0:T(8,128)}, f32[1,1024]{1,0:T(1,128)}, bf16[4,256,1024]{2,1,0:T(8,128)(2,1)}, bf16[4,1024,256]{2,1,0:T(8,128)(2,1)}, bf16[4,512,1024]{2,1,0:T(8,128)(2,1)}) custom-call(f32[512,1024]{1,0:T(8,128)} %get-tuple-element.81.h1_ref.refs_9_, f32[2,8,1024]{2,1,0:T(8,128)} %get-tuple-element.73.refs_1_.gain_ref.refs_2_, ...), custom_call_target="tpu_custom_call" | custom-call | flops 60000002048 | bytes 30000000 | tf_op jit(solution)/shard_map/pallas_call | solution.py:1057
  318.9 0.0 reduce-scatter.5.cloned.1.call-update
  318.9 0.0 reduce-scatter.7.cloned.1.call-start
  318.9 0.7 reduce-scatter.7.cloned.1.call-update
  319.6 0.0 reduce-scatter.9.cloned.1.call-start
  319.7 83.9 %shard_map.157 = (bf16[4,512,768]{2,1,0:T(8,128)(2,1)}, f32[256,256]{1,0:T(8,128)}, bf16[512,1024]{1,0:T(8,128)(2,1)}) custom-call(f32[512,1024]{1,0:T(8,128)} %get-tuple-element.85.refs_0_.mid_in, bf16[4,512,768]{2,1,0:T(8,128)(2,1)} %get-tuple-element.78.refs_0_.refs_1_, bf16[4,512,64]{2,1,0:T(8,128)(2,1)} %get-tuple-element.135.refs_1_.refs_2_, ...), custom_call_target="tpu_custom_call" | custom-call | flops 89999998976 | bytes 40000000 | tf_op jit(solution)/shard_map/pallas_call | solution.py:1611
  403.6 33.4 %shard_map.158 = (bf16[512,1024]{1,0:T(8,128)(2,1)}, f32[1,1024]{1,0:T(1,128)}, bf16[4,256,768]{2,1,0:T(8,128)(2,1)}) custom-call(bf16[4,512,768]{2,1,0:T(8,128)(2,1)} %get-tuple-element.89.dqkv_ref, f32[2,8,1024]{2,1,0:T(8,128)} %get-tuple-element.73.refs_1_.gain_ref.refs_2_, bf16[4,512,1024]{2,1,0:T(8,128)(2,1)} %get-tuple-element.90.a1_in, ...), custom_call_target="tpu_custom_call" | custom-call | flops 30000001024 | bytes 30000000 | tf_op jit(solution)/shard_map/pallas_call | solution.py:1714
  437.1 0.0 reduce-scatter.9.cloned.1.call-update
  437.1 0.0 reduce-scatter.11.cloned.1.call-start
  437.2 0.0 reduce-scatter.5.cloned.1.call-done
  437.2 0.0 reduce-scatter.7.cloned.1.call-done
  437.2 52.9 %shard_map.159 = (f32[512,1024]{1,0:T(8,128)}, f32[1,1024]{1,0:T(1,128)}, bf16[4,256,1024]{2,1,0:T(8,128)(2,1)}, bf16[4,1024,256]{2,1,0:T(8,128)(2,1)}, bf16[2,512,1024]{2,1,0:T(8,128)(2,1)}) custom-call(bf16[512,1024]{1,0:T(8,128)(2,1)} %get-tuple-element.95.refs_0_.dx1_ref, f32[512,1024]{1,0:T(8,128)} %get-tuple-element.72.refs_0_.refs_1_, ...), custom_call_target="tpu_custom_call" | custom-call | flops 60000002048 | bytes 40000000 | tf_op jit(solution)/shard_map/pallas_call | solution.py:1398
  490.2 0.0 copy-start.7
  490.2 0.0 reduce-scatter.9.cloned.1.call-done
  490.2 0.0 copy-start.8
  490.2 0.0 reduce-scatter.11.cloned.1.call-update
  490.2 1.0 copy-done.8
  491.2 0.2 collective-permute-start
  491.5 0.0 copy-done.7
  491.5 1.8 collective-permute-start.2
  493.3 81.3 %shard_map.160 = (bf16[4,512,768]{2,1,0:T(8,128)(2,1)}, f32[256,256]{1,0:T(8,128)}, f32[1024,256]{1,0:T(8,128)}) custom-call(f32[512,1024]{1,0:T(8,128)} %get-tuple-element.103.refs_0_.mid_ref, bf16[4,512,768]{2,1,0:T(8,128)(2,1)} %get-tuple-element.67.refs_0_.refs_1_, bf16[4,512,64]{2,1,0:T(8,128)(2,1)} %get-tuple-element.135.refs_1_.refs_2_, ...), custom_call_target="tpu_custom_call" | custom-call | flops 89999998976 | bytes 40000000 | tf_op jit(solution)/shard_map/pallas_call | solution.py:1611
  574.6 0.0 copy-start.4
  574.6 0.0 copy-done.9
  574.7 1.7 broadcast_select_fusion.1
  576.4 0.0 collective-permute-done.2
  576.4 2.3 select_bitcast_fusion
  578.7 0.0 copy-done.4
  578.7 0.9 broadcast_select_fusion
  579.6 0.0 collective-permute-start.1
  579.6 62.5 %shard_map.161 = (f32[1,1024]{1,0:T(1,128)}, f32[1,1024]{1,0:T(1,128)}, f32[256,768]{1,0:T(8,128)}, bf16[2,512,1024]{2,1,0:T(8,128)(2,1)}) custom-call(bf16[4,512,768]{2,1,0:T(8,128)(2,1)} %get-tuple-element.109.dqkv_ref, bf16[4,512,1024]{2,1,0:T(8,128)(2,1)} %get-tuple-element.110.a1_ref, bf16[512,1024]{1,0:T(8,128)(2,1)} %get-tuple-element.68.refs_3_.x_ref, ...), custom_call_target="tpu_custom_call" | custom-call | flops 40000000000 | bytes 30000000 | tf_op jit(solution)/shard_map/pallas_call | solution.py:1902
  642.1 0.0 collective-permute-done
  642.1 1.2 add_select_fusion
  643.4 0.0 copy-start.2
  643.4 1.1 copy.20
  644.6 0.0 collective-permute-done.1
  644.6 2.4 add_bitcast_fusion
  647.0 0.0 copy-done.2
  647.0 1.3 copy.25
  648.3 1.0 copy-done.3
  649.3 1.3 copy.26
  650.7 0.0 copy-done.11
  650.7 0.6 copy.27
  651.3 0.6 copy.28
  (15 shorter events, 0.1 us)
Async XLA Ops:
  7.2 0.7 copy-start
  7.2 4.8 copy-start.5
  7.2 430.0 %reduce-scatter.5.cloned.1.call-start = ((), (), s32[]{:S(2)}) async-start(), calls=%async_computation.4 | async-start | bytes 2621440 | tf_op jit(solution)/shard_map/reduce_scatter | solution.py:1996
  9.6 3.3 copy-start.6
  12.0 3.0 copy-start.12
  12.0 3.0 copy-start.13
  318.9 118.3 %reduce-scatter.7.cloned.1.call-start = ((), (), s32[]{:S(2)}) async-start(), calls=%async_computation.5 | async-start | bytes 2621440 | tf_op jit(solution)/shard_map/reduce_scatter | solution.py:1996
  319.6 170.5 %reduce-scatter.9.cloned.1.call-start = ((), (), s32[]{:S(2)}) async-start(), calls=%async_computation.6 | async-start | bytes 1966080 | tf_op jit(solution)/shard_map/reduce_scatter | solution.py:1996
  437.1 141.6 %reduce-scatter.11.cloned.1.call-start = ((), (), s32[]{:S(2)}) async-start(), calls=%async_computation.7 | async-start | bytes 2621440 | tf_op jit(solution)/shard_map/reduce_scatter | solution.py:1996
  490.2 1.3 copy-start.7
  490.2 1.0 copy-start.8
  491.2 150.9 %collective-permute-start = (bf16[256,768]{1,0:T(8,128)(2,1)S(1)}, bf16[256,768]{1,0:T(8,128)(2,1)S(1)}, u32[]{:S(2)}, u32[]{:S(2)}) collective-permute-start(bf16[256,768]{1,0:T(8,128)(2,1)S(1)} %bitcast.30), channel_id=1, source_target_pairs={{0,16},{16,0},{1,17},{17,1},{2,18},{18,2},{3,19},{19,3},{4,20},{20... | collective-permute-start | bytes 1179656 | tf_op jit(solution)/shard_map/ppermute | solution.py:1943
  491.5 84.9 %collective-permute-start.2 = (bf16[1024,256]{1,0:T(8,128)(2,1)S(1)}, bf16[1024,256]{1,0:T(8,128)(2,1)S(1)}, u32[]{:S(2)}, u32[]{:S(2)}) collective-permute-start(bf16[1024,256]{1,0:T(8,128)(2,1)S(1)} %bitcast.28), channel_id=1, source_target_pairs={{0,16},{16,0},{1,17},{17,1},{2,18},{18,2},{3,19},{19,3},{4,20},{20... | collective-permute-start | bytes 1572872 | tf_op jit(solution)/shard_map/ppermute | solution.py:1943
  493.3 81.4 %copy-start.9 = (f32[256,256]{1,0:T(8,128)S(1)}, f32[256,256]{1,0:T(8,128)}, u32[]{:S(2)}) copy-start(f32[256,256]{1,0:T(8,128)} %get-tuple-element.120) | copy-start | bytes 786436
  574.6 4.1 copy-start.4
  579.6 65.0 %collective-permute-start.1 = (bf16[256,1024]{1,0:T(8,128)(2,1)}, bf16[256,1024]{1,0:T(8,128)(2,1)}, u32[]{:S(2)}, u32[]{:S(2)}) collective-permute-start(bf16[256,1024]{1,0:T(8,128)(2,1)} %broadcast_select_fusion), channel_id=1, source_target_pairs={{0,16},{16,0},{1,17},{17,1},{2,18},{18,2},{3,19},{19,3},{4,20},{20... | collective-permute-start | bytes 1572872 | tf_op jit(solution)/shard_map/ppermute | solution.py:1943
  643.4 3.6 copy-start.2
  647.0 2.3 copy-start.3
  647.0 4.9 copy-start.1
  649.3 1.3 copy-start.11
  649.3 1.9 copy-start.10
Sparse Core Ops, SparseCore 0:
  319.0 49.8 reduce-scatter.4
  371.3 44.5 reduce-scatter.6
  437.2 33.6 reduce-scatter.8
  490.4 47.3 reduce-scatter.10

commit v17 on v16

--- a/solution.py
+++ b/solution.py
@@ -319,7 +319,7 @@
 
         run(2, one)
 
-    def finish(self, out):
+    def finish(self, out, above=None):
         @pl.when(self.s == self.layer)
         def _():
             self.y_copy(0).wait_recv()
@@ -330,7 +330,7 @@
         def _():
             self.y_copy(0).wait_send()
             self.y_copy(1).wait_send()
-            out[...] = self.own[...]
+            out[...] = self.own[...] if above is None else above[...]
 
         for k in range(1, self.replicas):
             self.z_copy(k, 0).wait_send()
@@ -1427,8 +1427,9 @@
     mid_ref, qkv_ref, qm_ref, km_ref, ctx_ref, lse_ref, w_ref = refs[:7]
     refs = refs[7:]
     if layer == 0:
-        gdown_ref, refs = refs[0], refs[1:]
+        gdown_ref, above_ref, refs = refs[0], refs[1], refs[2:]
     else:
+        above_ref = None
         hid_ref, wd_ref, h1_in, refs = refs[0], refs[1], refs[2], refs[3:]
     dqkv_ref, gout_ref, refs = refs[0], refs[1], refs[2:]
     if layer == 0:
@@ -1593,14 +1594,14 @@
 
         run(n, output)
         scatter.drain(n)
-    reduce.finish(gout_ref)
+    reduce.finish(gout_ref, above_ref)
     if layer == 0:
         down.finish(down_out)
         down_swap.copy().wait_send()
     gather.drain(n)
 
 
-def attend_backward(size, replicas, layer, mid, qkv, qm, km, ctx, lse, w, grads, more=()):
+def attend_backward(size, replicas, layer, mid, qkv, qm, km, ctx, lse, w, grads, more=(), above=()):
     _, rows, wide = qkv.shape
     e = qm.shape[2]
     heads = wide // (3 * e)
@@ -1613,7 +1614,7 @@
         out_shape=[shape(qkv.shape, BF), shape((heads * e, depth), F32)]
         + [shape(grad.shape[1:], F32) for grad in grads]
         + [shape((rows, width), BF)] * (len(more) // 3),
-        in_specs=[VM] * 6 + [HB] * (1 + len(grads) + len(more)),
+        in_specs=[VM] * 6 + [HB] * (1 + len(grads) + len(more)) + [VM] * len(above),
         out_specs=[VM, VM] + [VM] * (len(grads) + len(more) // 3),
         scratch_shapes=[
             pltpu.VMEM((size, rows, width), BF),
@@ -1641,7 +1642,7 @@
         ),
         compiler_params=params(8 + layer),
         cost_estimate=cost(90e9, 40e6),
-    )(mid, qkv, qm, km, ctx, lse, w, *grads, *more)
+    )(mid, qkv, qm, km, ctx, lse, w, *grads, *more, *above)
 
 
 def qkv_back_kernel(
@@ -2014,7 +2015,7 @@
     )
     mid, qkv_1 = lax.optimization_barrier((mid, qkv_1))
     d_qkv, out_0, down_0 = attend_backward(
-        size, replicas, 0, mid, qkv, qm, km, ctx, lse, w_out, [g_down]
+        size, replicas, 0, mid, qkv, qm, km, ctx, lse, w_out, [g_down], (), [out_1]
     )
     up_0 = reduce_rows(g_up)
     d_qkv, up_0 = lax.optimization_barrier((d_qkv, up_0))
@@ -2028,7 +2029,7 @@
 
     other_qkv_1 = swap_section(qkv_1)
     qkv_grad = jnp.where(section == 0, qkv_0, qkv_1.astype(F32) + other_qkv_1.astype(F32))
-    out_grad = jnp.where(section == 0, out_0, out_1)
+    out_grad = out_0
     up_grad = finish(up_0, up_1)
     other_down_1 = swap_section(down_1)
     down_grad = jnp.where(section == 0, down_0, down_1.astype(F32) + other_down_1.astype(F32))

time: 667 us -> 670 us (level)
  no operation moved by 1% of the time
where the time goes in v17:
time: 670 us; the launch traced here: 661 us
  Pallas kernels  621 us (93%)
  between operations  14.2 us (2%)
  other arithmetic  13.4 us (2%)
  local copies, waits for them, and re-layouts  9.63 us (1%)
    pallas_call x2, Pallas kernels, attend_backward(): pl.pallas_call(functools.partial(attend_back_kernel, size, layer, parts),...  166 us
    pallas_call x2, Pallas kernels, attend(): pl.pallas_call(functools.partial(attend_kernel, size, layer, columns), ou...  113 us
    pallas_call x1, Pallas kernels, turn_forward(): pl.pallas_call(functools.partial(turn_kernel, size, columns), out_shape=[...  81 us
    pallas_call x1, Pallas kernels, last_backward(): pl.pallas_call(functools.partial(last_kernel, size, replicas), out_shape=...  65.5 us
    pallas_call x1, Pallas kernels, first_forward(): pl.pallas_call(functools.partial(first_kernel, size, replicas), out_shape...  56.9 us
    pallas_call x1, Pallas kernels, mlp_backward(): pl.pallas_call(functools.partial(mlp_back_kernel, size, layer, parts), ou...  52.9 us
    pallas_call x1, Pallas kernels, peak(): pl.pallas_call(functools.partial(peak_kernel, size, replicas), out_shape=...  52.6 us
    pallas_call x1, Pallas kernels, qkv_backward(): pl.pallas_call(functools.partial(qkv_back_kernel, size, layer, parts), ou...  33.4 us
  transfers between devices with their start and end apart: 7, of which 0 were waited for; matrix products, arithmetic and copies ran while one was open for 1% of the time, Pallas kernels for 48%

profile of v17, /device:TPU:0, one launch (start us, length us, event | category | flops | bytes accessed | tf_op | source)
XLA Modules:
  0.0 661.2 jit_solution(11895651490180760577)
XLA Ops:
  7.2 0.0 copy-start
  7.2 0.0 copy-start.5
  7.2 0.0 reduce-scatter.5.cloned.1.call-start
  7.3 0.6 copy-done
  7.9 1.6 convert_element_type.57
  9.6 1.3 convert_element_type.55
  10.8 0.1 convert_element_type.56
  10.9 1.0 copy.19.wq_ref
  12.0 0.0 copy-done.5
  12.0 0.9 convert_element_type.59
  12.9 0.0 copy-done.6
  12.9 0.8 convert_element_type.61
  13.7 0.1 pad.2.clone
  13.8 1.2 select_convert_fusion
  15.0 0.0 copy-done.12
  15.0 0.0 copy-done.13
  15.0 0.7 maximum_maximum_fusion.gain_ref
  15.7 56.9 %shard_map.152 = (bf16[4,512,768]{2,1,0:T(8,128)(2,1)}, f32[2,8,1024]{2,1,0:T(8,128)}, bf16[512,1024]{1,0:T(8,128)(2,1)}, bf16[4,512,1024]{2,1,0:T(8,128)(2,1)},...) custom-call(bf16[2,512,1024]{2,1,0:T(8,128)(2,1)} %x_in.1, ...), custom_call_target="tpu_custom_call" | custom-call | flops 30000001024 | bytes 30000000 | tf_op jit(solution)/shard_map/pallas_call | solution.py:786
  72.6 60.4 %shard_map.153 = (f32[512,1024]{1,0:T(8,128)}, bf16[4,512,256]{2,1,0:T(8,128)(2,1)}, f32[4,4,512]{2,1,0:T(4,128)}, bf16[1024,1024]{1,0:T(8,128)(2,1)}, bf16[1024,1024]{1,0:T(8,128)(2,1)}) custom-call(bf16[4,512,768]{2,1,0:T(8,128)(2,1)} %get-tuple-element.67.refs_0_.refs_1_, bf16[4,512,64]{2,1,0:T(8,128)(2,1)} %get-tuple-element.135.refs_1_.refs_2_, ...), custom_call_target="tpu_custom_call" | custom-call | flops 60000002048 | bytes 20000000 | tf_op jit(solution)/shard_map/pallas_call | solution.py:933
  133.1 81.0 %shard_map.154 = (bf16[512,1024]{1,0:T(8,128)(2,1)}, bf16[4,512,768]{2,1,0:T(8,128)(2,1)}, bf16[4,512,1024]{2,1,0:T(8,128)(2,1)}, bf16[4,512,1024]{2,1,0:T(8,128...) custom-call(f32[512,1024]{1,0:T(8,128)} %get-tuple-element.72.refs_0, ...), custom_call_target="tpu_custom_call" | custom-call | flops 49999998976 | bytes 30000000 | tf_op jit(solution)/shard_map/pallas_call | solution.py:1234
  214.1 52.1 %shard_map.155 = (f32[512,1024]{1,0:T(8,128)}, bf16[4,512,256]{2,1,0:T(8,128)(2,1)}, f32[4,4,512]{2,1,0:T(4,128)}, bf16[4,512,1024]{2,1,0:T(8,128)(2,1)}, bf16[1024,1024]{1,0:T(8,128)(2,1)}) custom-call(bf16[4,512,768]{2,1,0:T(8,128)(2,1)} %get-tuple-element.78.refs_0_.refs_1_, bf16[4,512,64]{2,1,0:T(8,128)(2,1)} %get-tuple-element.135.refs_1_.refs_2_, ...), custom_call_target="tpu_custom_call" | custom-call | flops 60000002048 | bytes 20000000 | tf_op jit(solution)/shard_map/pallas_call | solution.py:933
  266.2 52.6 %shard_map.156 = (f32[512,1024]{1,0:T(8,128)}, f32[1,1024]{1,0:T(1,128)}, bf16[4,256,1024]{2,1,0:T(8,128)(2,1)}, bf16[4,1024,256]{2,1,0:T(8,128)(2,1)}, bf16[4,512,1024]{2,1,0:T(8,128)(2,1)}) custom-call(f32[512,1024]{1,0:T(8,128)} %get-tuple-element.81.h1_ref.refs_9_, f32[2,8,1024]{2,1,0:T(8,128)} %get-tuple-element.73.refs_1_.gain_ref.refs_2_, ...), custom_call_target="tpu_custom_call" | custom-call | flops 60000002048 | bytes 30000000 | tf_op jit(solution)/shard_map/pallas_call | solution.py:1057
  318.9 0.0 reduce-scatter.5.cloned.1.call-update
  318.9 0.0 reduce-scatter.7.cloned.1.call-start
  318.9 0.7 reduce-scatter.7.cloned.1.call-update
  319.6 0.0 reduce-scatter.9.cloned.1.call-start
  319.7 83.9 %shard_map.157 = (bf16[4,512,768]{2,1,0:T(8,128)(2,1)}, f32[256,256]{1,0:T(8,128)}, bf16[512,1024]{1,0:T(8,128)(2,1)}) custom-call(f32[512,1024]{1,0:T(8,128)} %get-tuple-element.85.refs_0_.mid_in, bf16[4,512,768]{2,1,0:T(8,128)(2,1)} %get-tuple-element.78.refs_0_.refs_1_, bf16[4,512,64]{2,1,0:T(8,128)(2,1)} %get-tuple-element.135.refs_1_.refs_2_, ...), custom_call_target="tpu_custom_call" | custom-call | flops 89999998976 | bytes 40000000 | tf_op jit(solution)/shard_map/pallas_call | solution.py:1612
  403.6 33.4 %shard_map.158 = (bf16[512,1024]{1,0:T(8,128)(2,1)}, f32[1,1024]{1,0:T(1,128)}, bf16[4,256,768]{2,1,0:T(8,128)(2,1)}) custom-call(bf16[4,512,768]{2,1,0:T(8,128)(2,1)} %get-tuple-element.89.dqkv_ref, f32[2,8,1024]{2,1,0:T(8,128)} %get-tuple-element.73.refs_1_.gain_ref.refs_2_, bf16[4,512,1024]{2,1,0:T(8,128)(2,1)} %get-tuple-element.90.a1_in, ...), custom_call_target="tpu_custom_call" | custom-call | flops 30000001024 | bytes 30000000 | tf_op jit(solution)/shard_map/pallas_call | solution.py:1715
  437.1 0.0 reduce-scatter.9.cloned.1.call-update
  437.1 0.0 reduce-scatter.11.cloned.1.call-start
  437.2 0.0 reduce-scatter.5.cloned.1.call-done
  437.2 0.0 reduce-scatter.7.cloned.1.call-done
  437.2 52.9 %shard_map.159 = (f32[512,1024]{1,0:T(8,128)}, f32[1,1024]{1,0:T(1,128)}, bf16[4,256,1024]{2,1,0:T(8,128)(2,1)}, bf16[4,1024,256]{2,1,0:T(8,128)(2,1)}, bf16[2,512,1024]{2,1,0:T(8,128)(2,1)}) custom-call(bf16[512,1024]{1,0:T(8,128)(2,1)} %get-tuple-element.95.refs_0_.dx1_ref, f32[512,1024]{1,0:T(8,128)} %get-tuple-element.72.refs_0_.refs_1_, ...), custom_call_target="tpu_custom_call" | custom-call | flops 60000002048 | bytes 40000000 | tf_op jit(solution)/shard_map/pallas_call | solution.py:1398
  490.2 0.0 copy-start.7
  490.2 0.0 reduce-scatter.9.cloned.1.call-done
  490.2 0.0 reduce-scatter.11.cloned.1.call-update
  490.2 1.0 copy-done.7
  491.2 0.2 collective-permute-start.2
  491.4 81.9 %shard_map.160 = (bf16[4,512,768]{2,1,0:T(8,128)(2,1)}, f32[256,256]{1,0:T(8,128)}, f32[1024,256]{1,0:T(8,128)}) custom-call(f32[512,1024]{1,0:T(8,128)} %get-tuple-element.103.refs_0_.mid_ref, bf16[4,512,768]{2,1,0:T(8,128)(2,1)} %get-tuple-element.67.refs_0_.refs_1_, bf16[4,512,64]{2,1,0:T(8,128)(2,1)} %get-tuple-element.135.refs_1_.refs_2_, ...), custom_call_target="tpu_custom_call" | custom-call | flops 89999998976 | bytes 40000000 | tf_op jit(solution)/shard_map/pallas_call | solution.py:1612
  573.3 0.0 copy-start.4
  573.3 0.0 copy-done.8
  573.3 0.1 collective-permute-start
  573.4 0.0 collective-permute-done.2
  573.4 2.4 select_bitcast_fusion
  575.8 0.0 copy-done.4
  575.8 0.9 broadcast_select_fusion
  576.6 1.8 collective-permute-start.1
  578.4 65.5 %shard_map.161 = (f32[1,1024]{1,0:T(1,128)}, f32[1,1024]{1,0:T(1,128)}, f32[256,768]{1,0:T(8,128)}, bf16[2,512,1024]{2,1,0:T(8,128)(2,1)}) custom-call(bf16[4,512,768]{2,1,0:T(8,128)(2,1)} %get-tuple-element.110.dqkv_ref, bf16[4,512,1024]{2,1,0:T(8,128)(2,1)} %get-tuple-element.111.a1_ref, bf16[512,1024]{1,0:T(8,128)(2,1)} %get-tuple-element.68.refs_3_.x_ref, ...), custom_call_target="tpu_custom_call" | custom-call | flops 40000000000 | bytes 30000000 | tf_op jit(solution)/shard_map/pallas_call | solution.py:1903
  644.0 0.0 collective-permute-done
  644.0 1.2 add_select_fusion
  645.2 0.0 copy-start.2
  645.2 1.1 copy.20
  646.4 0.0 collective-permute-done.1
  646.4 2.4 add_bitcast_fusion
  648.8 0.0 copy-done.2
  648.8 1.3 copy.26
  650.1 1.0 copy-done.3
  651.2 1.3 copy.27
  652.5 0.0 copy-done.11
  652.5 0.6 copy.28
  653.1 0.0 copy-done.9
  653.1 0.7 copy.29
  653.8 0.0 copy-done.10
  653.8 0.6 copy.30
  (15 shorter events, 0.1 us)
Async XLA Ops:
  7.2 0.7 copy-start
  7.2 4.8 copy-start.5
  7.2 430.0 %reduce-scatter.5.cloned.1.call-start = ((), (), s32[]{:S(2)}) async-start(), calls=%async_computation.4 | async-start | bytes 2621440 | tf_op jit(solution)/shard_map/reduce_scatter | solution.py:1997
  9.6 3.3 copy-start.6
  12.0 3.0 copy-start.12
  12.0 3.0 copy-start.13
  318.9 118.3 %reduce-scatter.7.cloned.1.call-start = ((), (), s32[]{:S(2)}) async-start(), calls=%async_computation.5 | async-start | bytes 2621440 | tf_op jit(solution)/shard_map/reduce_scatter | solution.py:1997
  319.6 170.5 %reduce-scatter.9.cloned.1.call-start = ((), (), s32[]{:S(2)}) async-start(), calls=%async_computation.6 | async-start | bytes 1966080 | tf_op jit(solution)/shard_map/reduce_scatter | solution.py:1997
  437.1 138.7 %reduce-scatter.11.cloned.1.call-start = ((), (), s32[]{:S(2)}) async-start(), calls=%async_computation.7 | async-start | bytes 2621440 | tf_op jit(solution)/shard_map/reduce_scatter | solution.py:1997
  490.2 1.0 copy-start.7
  491.2 82.2 %collective-permute-start.2 = (bf16[1024,256]{1,0:T(8,128)(2,1)S(1)}, bf16[1024,256]{1,0:T(8,128)(2,1)S(1)}, u32[]{:S(2)}, u32[]{:S(2)}) collective-permute-start(bf16[1024,256]{1,0:T(8,128)(2,1)S(1)} %bitcast.28), channel_id=1, source_target_pairs={{0,16},{16,0},{1,17},{17,1},{2,18},{18,2},{3,19},{19,3},{4,20},{20... | collective-permute-start | bytes 1572872 | tf_op jit(solution)/shard_map/ppermute | solution.py:1944
  491.4 81.9 %copy-start.8 = (bf16[1,256,768]{2,1,0:T(8,128)(2,1)S(1)}, bf16[1,256,768]{2,1,0:T(8,128)(2,1)}, u32[]{:S(2)}) copy-start(bf16[1,256,768]{2,1,0:T(8,128)(2,1)} %reduce-scatter.9.cloned.1.call-done) | copy-start | bytes 1179652
  573.3 2.5 copy-start.4
  573.3 70.7 %collective-permute-start = (bf16[256,768]{1,0:T(8,128)(2,1)S(1)}, bf16[256,768]{1,0:T(8,128)(2,1)S(1)}, u32[]{:S(2)}, u32[]{:S(2)}) collective-permute-start(bf16[256,768]{1,0:T(8,128)(2,1)S(1)} %bitcast.30), channel_id=1, source_target_pairs={{0,16},{16,0},{1,17},{17,1},{2,18},{18,2},{3,19},{19,3},{4,20},{20... | collective-permute-start | bytes 1179656 | tf_op jit(solution)/shard_map/ppermute | solution.py:1944
  576.6 69.7 %collective-permute-start.1 = (bf16[256,1024]{1,0:T(8,128)(2,1)}, bf16[256,1024]{1,0:T(8,128)(2,1)}, u32[]{:S(2)}, u32[]{:S(2)}) collective-permute-start(bf16[256,1024]{1,0:T(8,128)(2,1)} %broadcast_select_fusion), channel_id=1, source_target_pairs={{0,16},{16,0},{1,17},{17,1},{2,18},{18,2},{3,19},{19,3},{4,20},{20... | collective-permute-start | bytes 1572872 | tf_op jit(solution)/shard_map/ppermute | solution.py:1944
  645.2 3.6 copy-start.2
  648.8 2.3 copy-start.3
  648.8 5.6 copy-start.1
  651.2 1.3 copy-start.11
  651.2 1.9 copy-start.9
  651.2 2.6 copy-start.10
Sparse Core Ops, SparseCore 0:
  319.0 49.8 reduce-scatter.4
  371.3 44.5 reduce-scatter.6
  437.2 33.6 reduce-scatter.8
  490.3 48.6 reduce-scatter.10
